TPU v7x, 256 devices: a whole 4x4x8 slice. The times are simulated.
256 devices in a mesh: dp: 32 (over y_hi, z, core), space: 8 (over x, y_lo).
Axes of the slice: x: 4, y: 4 (y_hi: 2, y_lo: 2; y = y_hi * 2 + y_lo), z: 8, core: 2. Of those that a mesh axis runs over, the one named last changes fastest.
Arguments:
- clip_qkv: bfloat16 [32, 16, 256, 4992], P('dp', None, 'space'), may hold values from -48 to 48
- temporal_qk: bfloat16 [32, 16, 256, 3328], P('dp', None, 'space'), may hold values from -48 to 48
- proj_weight: bfloat16 [1664, 512], replicated, may hold values from -0.15625 to 0.15625
- caption_tokens: bfloat16 [32, 77, 512], P('dp'), may hold values from -18 to 18
- caption_lens: int32 [32], P('dp'), may hold values from 8 to 77, as said below
- positive: int32 [32], P('dp'), may hold values from 0 to 31, each once
Outputs:
- video_emb: bfloat16 [32, 16, 256, 512], P('dp', None, 'space')
- caption_grad: float32 [32, 77, 512], P('dp')
- clip_loss: float32 [32], P('dp')
Inputs may be any that keep to these rules, and one draw needn't show every extreme that they name: `caption_lens`: some caption fills all 77 slots in every draw.
All inputs are finite; a program needn't handle non-finite values.
Results may differ from a plain program's by a relative error of at most 0.029.
Values may be sent and summed in bfloat16 or wider, within the bound.
No kernel may reach another device: no remote copies, remote signals or barrier semaphores. Data moves between devices by JAX's collectives and lax.ppermute only.
A program may use at most 192 MiB of HBM per device.

v0:
```python
import jax
import jax.numpy as jnp
from jax import lax
from jax.sharding import PartitionSpec as P

HEADS = 13
HD = 128


SHARPNESS = 4.0
LOGIT_SCALE = 10.0


def merged(value, axis, join):
    pieces = jax.tree.map(lambda part: lax.all_gather(part, axis), value)
    head = jax.tree.map(lambda part: part[0], pieces)
    tail = jax.tree.map(lambda part: part[1:], pieces)
    so_far, _ = lax.scan(lambda so_far, piece: (join(so_far, piece), None), head, tail)
    return so_far


def heads_first(block, rows, length):
    return jnp.transpose(block.reshape(rows, length, HEADS, HD), (0, 2, 1, 3)).reshape(
        rows * HEADS, length, HD
    )


def frame_attention(frame_block):
    frame_count, patch_count, triple = frame_block.shape
    features = triple // 3
    query_matrix = heads_first(frame_block[..., :features], frame_count, patch_count)
    key_matrix = heads_first(frame_block[..., features : 2 * features], frame_count, patch_count)
    value_matrix = heads_first(frame_block[..., 2 * features :], frame_count, patch_count)
    attention_logits = jnp.einsum(
        "fyu,fhu->fyh", query_matrix, key_matrix, preferred_element_type=jnp.float32
    ) * HD ** (-0.5)
    row_max = jnp.max(attention_logits, axis=-1, keepdims=True)
    expo_terms = jnp.exp(attention_logits - row_max)
    row_total = jnp.sum(expo_terms, axis=-1, keepdims=True)
    attended = jnp.einsum(
        "vhz,vzn->vhn",
        expo_terms.astype(jnp.bfloat16),
        value_matrix,
        preferred_element_type=jnp.float32,
    )
    attended = (attended / row_total).astype(jnp.bfloat16)
    attended = jnp.transpose(attended.reshape(frame_count, HEADS, patch_count, HD), (0, 2, 1, 3))
    return attended.reshape(frame_count, patch_count, features)


def on_device(clip_qkv, temporal_qk, proj_weight, caption_tokens, caption_lens, positive):
    clip_count, frames, local_patches, triple = clip_qkv.shape
    features = triple // 3
    groups = lax.axis_size("space")
    blocks = clip_qkv.reshape(groups, clip_count * frames // groups, local_patches, triple)
    frame_block = lax.all_to_all(blocks, "space", split_axis=0, concat_axis=2, tiled=True)
    item_count = frame_block.shape[1]
    attended = frame_attention(frame_block.reshape(item_count, frame_block.shape[2], triple))
    spatial = lax.all_to_all(
        attended.reshape(1, item_count, -1, features),
        "space",
        split_axis=2,
        concat_axis=0,
        tiled=True,
    )
    spatial = spatial.reshape(clip_count, frames, local_patches, features)

    def time_major(block):
        shaped = block.reshape(clip_count, frames, local_patches, HEADS, HD)
        return jnp.transpose(shaped, (0, 2, 3, 1, 4)).reshape(
            clip_count * local_patches * HEADS, frames, HD
        )

    time_query = time_major(temporal_qk[..., :features])
    time_key = time_major(temporal_qk[..., features:])
    time_value = time_major(spatial)
    attention_logits = jnp.einsum(
        "bfd,bgd->bfg", time_query, time_key, preferred_element_type=jnp.float32
    ) * HD ** (-0.5)
    row_max = jnp.max(attention_logits, axis=-1, keepdims=True)
    expo_terms = jnp.exp(attention_logits - row_max)
    row_total = jnp.sum(expo_terms, axis=-1, keepdims=True)
    temporal_out = jnp.einsum(
        "bfg,bgd->bfd",
        expo_terms.astype(jnp.bfloat16),
        time_value,
        preferred_element_type=jnp.float32,
    )
    temporal_out = temporal_out / row_total
    temporal_out = jnp.transpose(
        temporal_out.reshape(clip_count, local_patches, HEADS, frames, HD), (0, 3, 1, 2, 4)
    )
    combined = (
        spatial.astype(jnp.float32)
        + temporal_out.reshape(clip_count, frames, local_patches, features)
    ).astype(jnp.bfloat16)
    projected = jnp.dot(
        combined.reshape(-1, features), proj_weight, preferred_element_type=jnp.float32
    )
    scaled = projected * lax.rsqrt(jnp.mean(projected * projected, axis=-1, keepdims=True) + 1e-06)
    embed_width = proj_weight.shape[1]
    video_rows = scaled.astype(jnp.bfloat16).reshape(clip_count, -1, embed_width)
    all_tokens, all_lens = (
        lax.all_gather(caption_tokens, "dp", axis=0, tiled=True),
        lax.all_gather(caption_lens, "dp", axis=0, tiled=True),
    )
    captions, cap_slots, embed_width = all_tokens.shape
    flattened_caption = all_tokens.reshape(captions * cap_slots, embed_width)
    similarity = jnp.einsum(
        "cne,ke->cnk", video_rows, flattened_caption, preferred_element_type=jnp.float32
    )
    local_max = jnp.max(similarity, axis=1)
    local_total = jnp.sum(jnp.exp(SHARPNESS * (similarity - local_max[:, None, :])), axis=1)

    def combine(earlier, second):
        merged_max = jnp.maximum(earlier[0], second[0])
        merged_total = earlier[1] * jnp.exp(SHARPNESS * (earlier[0] - merged_max)) + second[
            1
        ] * jnp.exp(SHARPNESS * (second[0] - merged_max))
        return (merged_max, merged_total)

    global_max, global_total = merged((local_max, local_total), "space", combine)
    soft_max = global_max + jnp.log(global_total) / SHARPNESS
    token_mask = (jnp.arange(cap_slots, dtype=jnp.int32)[None, :] < all_lens[:, None]).astype(
        jnp.float32
    )
    length_float = all_lens.astype(jnp.float32)
    caption_score = (
        jnp.sum(soft_max.reshape(clip_count, captions, cap_slots) * token_mask[None], axis=-1)
        / length_float[None, :]
    )
    logit_matrix = LOGIT_SCALE * caption_score
    logit_max = jnp.max(logit_matrix, axis=-1, keepdims=True)
    log_total = logit_max[:, 0] + jnp.log(jnp.sum(jnp.exp(logit_matrix - logit_max), axis=-1))
    onehot = (jnp.arange(captions, dtype=jnp.int32)[None, :] == positive[:, None]).astype(
        jnp.float32
    )
    clip_loss = log_total - jnp.sum(logit_matrix * onehot, axis=-1)
    grad_logit = LOGIT_SCALE * (jnp.exp(logit_matrix - log_total[:, None]) - onehot)
    token_coef = (grad_logit[:, :, None] * token_mask[None] / length_float[None, :, None]).reshape(
        clip_count, captions * cap_slots
    )
    weights = (
        jnp.exp(SHARPNESS * (similarity - soft_max[:, None, :])) * token_coef[:, None, :]
    ).astype(jnp.bfloat16)
    local_sum = lax.psum_scatter(
        jnp.einsum("cnk,cne->ke", weights, video_rows, preferred_element_type=jnp.float32).astype(
            jnp.bfloat16
        ),
        "dp",
        scatter_dimension=0,
        tiled=True,
    )
    caption_grad = lax.psum(local_sum, "space").astype(jnp.float32).reshape(caption_tokens.shape)
    video_emb = video_rows.reshape(clip_count, frames, local_patches, embed_width)
    return (video_emb, caption_grad, clip_loss)


def solution(mesh):
    return jax.shard_map(
        on_device,
        mesh=mesh,
        in_specs=(
            P("dp", None, "space", None),
            P("dp", None, "space", None),
            P(),
            P("dp", None, None),
            P("dp"),
            P("dp"),
        ),
        out_specs=(P("dp", None, "space", None), P("dp", None, None), P("dp")),
        check_vma=False,
    )
```

profile of v0, /device:TPU:32, one launch (start us, length us, event | category | flops | bytes accessed | tf_op | source)
XLA Modules:
  0.0 434.8 jit_solution(5550810836195385153)
XLA Ops:
  7.2 5.5 %all-to-all-start = ((bf16[8,2,32,4992]{3,2,1,0:T(8,128)(2,1)}), bf16[8,2,32,4992]{3,2,1,0:T(8,128)(2,1)}, u32[]{:S(2)}, u32[]{:S(2)}) async-start(bf16[8,2,32,4992]{3,2,1,0:T(8,128)(2,1)} %bitcast.104), calls=%async_computation | async-start | bytes 10223616 | tf_op jit(solution)/shard_map/all_to_all | solution.py:56
  13.4 71.2 %all-to-all-done = bf16[8,2,32,4992]{3,2,1,0:T(8,128)(2,1)} async-done(((bf16[8,2,32,4992]{3,2,1,0:T(8,128)(2,1)}), bf16[8,2,32,4992]{3,2,1,0:T(8,128)(2,1)}, u32[]{:S(2)}, u32[]{:S(2)}) %all-to-all-start) | async-done | bytes 5111840 | tf_op jit(solution)/shard_map/all_to_all | solution.py:56
  84.5 2.9 copy.45
  87.4 2.4 fusion.28
  89.8 2.8 copy.46
  92.7 3.7 copy.48
  96.3 3.6 copy.50
  100.0 2.6 multiply_reduce_fusion
  105.6 3.7 copy.52
  109.3 3.7 all-to-all-start.1
  113.1 4.1 fusion.29
  117.2 4.1 reshape.251
  121.4 4.8 %copy.55 = bf16[1,32,13,16,128]{4,3,2,1,0:T(8,128)(2,1)} copy(bf16[1,32,13,16,128]{4,2,1,3,0:T(8,128)(2,1)} %bitcast.97) | data formatting | bytes 3407872 | tf_op jit(solution)/shard_map/transpose | solution.py:70
  126.1 4.1 reshape.253
  130.3 4.8 %copy.56 = bf16[1,32,13,16,128]{4,3,2,1,0:T(8,128)(2,1)} copy(bf16[1,32,13,16,128]{4,2,1,3,0:T(8,128)(2,1)} %bitcast.98) | data formatting | bytes 3407872 | tf_op jit(solution)/shard_map/transpose | solution.py:70
  136.3 3.0 multiply_reduce_fusion.1
  139.4 1.7 copy-done.3
  141.2 1.9 fusion.11
  143.1 4.3 reshape.258
  147.8 2.1 copy.54
  149.9 2.2 reshape_reshape.10
  152.1 3.7 copy.58
  155.9 2.9 convolution_divide_fusion
  165.3 2.2 copy-done.1
  173.0 19.9 %all-reduce.2 = s32[32]{0:T(128)S(1)} all-reduce(s32[32]{0:T(128)S(1)} %dynamic-update-slice.2), channel_id=1, replica_groups=mesh['dp'=32,'space'=8] {'dp'}, use_global_device_ids=true, to_apply=%add.2 | all-reduce | flops 32 | bytes 256
  193.2 57.3 %all-reduce.11.cloned.1.call-done = (f32[19712]{0:T(1024)}, f32[19712]{0:T(1024)}) async-done(((f32[19712]{0:T(1024)}, f32[19712]{0:T(1024)}), (f32[19712]{0:T(1024)}, f32[19712]{0:T(1024)})) %all-reduce.11.cloned.1.call-update) | async-done | bytes 157712
  258.7 5.6 %convolution_convert_fusion = bf16[2464,512]{1,0:T(8,128)(2,1)} fusion(bf16[512,512]{1,0:T(8,128)(2,1)S(1)} %multiply_convert_fusion.2, f32[512,2464]{0,1:T(8,128)} %copy-done.1, f32[2464]{0:T(1024)S(1)} %select_divide_fusion, f32[2464]{0:T(1024)S(1)} %add_reduce_fusion), kind=kOutput, calls=%fused_computation.12 | convolution fusion | flops 1298153472 | bytes 8113408 | tf_op jit(solution)/shard_map/cnk,cne->ke/dot_general | solution.py:147
  264.4 76.5 %fusion = bf16[80,512]{1,0:T(8,128)(2,1)S(1)} fusion(bf16[2464,512]{1,0:T(8,128)(2,1)} %convolution_convert_fusion), kind=kCustom, calls=%all-reduce-scatter | all-reduce-scatter fusion | flops 1310721 | bytes 2606080
  340.9 1.9 collective-permute-start
  342.9 1.9 collective-permute-start.1
  345.5 6.2 %collective-permute-done.1 = bf16[13,512]{1,0:T(8,128)(2,1)S(1)} collective-permute-done((bf16[13,512]{1,0:T(8,128)(2,1)S(1)}, bf16[13,512]{1,0:T(8,128)(2,1)S(1)}, u32[]{:S(2)}, u32[]{:S(2)}) %collective-permute-start.1) | collective-permute-done | bytes 13344
  353.4 72.1 %all-reduce.9.cloned.1.call-done = bf16[1,77,512]{2,1,0:T(8,128)(2,1)} async-done(((bf16[1,77,512]{2,1,0:T(8,128)(2,1)}), bf16[1,77,512]{2,1,0:T(8,128)(2,1)}) %all-reduce.9.cloned.1.call-update) | async-done | bytes 78864 | tf_op jit(solution)/shard_map/psum | solution.py:154
  (89 shorter events, 25.9 us)
Async XLA Ops:
  7.2 154.8 %copy-start = (bf16[1664,512]{1,0:T(8,128)(2,1)S(1)}, bf16[1664,512]{1,0:T(8,128)(2,1)}, u32[]{:S(2)}) copy-start(bf16[1664,512]{1,0:T(8,128)(2,1)} %param.10) | copy-start | bytes 5111812
  7.2 77.4 %all-to-all-start = ((bf16[8,2,32,4992]{3,2,1,0:T(8,128)(2,1)}), bf16[8,2,32,4992]{3,2,1,0:T(8,128)(2,1)}, u32[]{:S(2)}, u32[]{:S(2)}) async-start(bf16[8,2,32,4992]{3,2,1,0:T(8,128)(2,1)} %bitcast.104), calls=%async_computation | async-start | bytes 10223616 | tf_op jit(solution)/shard_map/all_to_all | solution.py:56
  12.6 130.5 %all-gather.4.cloned.1.call-start = ((), (), s32[]{:S(2)}) async-start(), calls=%async_computation.2 | async-start | bytes 2703360 | tf_op jit(solution)/shard_map/all_gather | solution.py:104
  102.5 1.5 copy-start.7
  109.3 38.2 %all-to-all-start.1 = ((bf16[1,2,256,1664]{3,1,0,2:T(2,128)(2,1)}), bf16[1,2,256,1664]{3,1,0,2:T(2,128)(2,1)S(1)}, u32[]{:S(2)}, u32[]{:S(2)}) async-start(bf16[1,2,256,1664]{3,1,0,2:T(2,128)(2,1)} %copy.52), calls=%async_computation.1 | async-start | bytes 3407872 | tf_op jit(solution)/shard_map/all_to_all | solution.py:59
  112.9 137.7 %all-reduce.11.cloned.1.call-start = ((), (), s32[]{:S(2)}) async-start(), calls=%async_computation.4 | async-start | bytes 327680
  126.1 9.0 %copy-start.13 = (u32[256]{0:T(256)S(1)}, u32[256]{0:T(256)}, u32[]{:S(2)}) copy-start(u32[256]{0:T(256)} %constant.41) | copy-start | bytes 3076
  139.4 1.7 copy-start.3
  139.4 1.8 copy-start.8
  152.1 3.7 copy-start.4
  152.1 3.7 copy-start.9
  158.8 2.0 copy-start.2
  162.0 1.7 copy-start.5
  163.7 95.0 %copy-start.6 = (bf16[512,512]{1,0:T(8,128)(2,1)}, bf16[512,512]{1,0:T(8,128)(2,1)S(1)}, u32[]{:S(2)}) copy-start(bf16[512,512]{1,0:T(8,128)(2,1)S(1)} %multiply_convert_fusion.2) | copy-start | bytes 1572868
  165.3 2.2 copy-start.1
  165.3 6.3 %copy-start.12 = (u32[256]{0:T(256)S(1)}, u32[256]{0:T(256)}, u32[]{:S(2)}) copy-start(u32[256]{0:T(256)} %constant.51) | copy-start | bytes 3076
  169.2 0.6 copy-start.11
  169.6 0.6 copy-start.10
  170.3 255.2 %all-reduce.9.cloned.1.call-start = ((), (), s32[]{:S(2)}) async-start(), calls=%async_computation.3 | async-start | bytes 163840 | tf_op jit(solution)/shard_map/psum | solution.py:154
  340.9 10.8 %collective-permute-start = (bf16[80,512]{1,0:T(8,128)(2,1)S(1)}, bf16[80,512]{1,0:T(8,128)(2,1)S(1)}, u32[]{:S(2)}, u32[]{:S(2)}) collective-permute-start(bf16[80,512]{1,0:T(8,128)(2,1)S(1)} %fusion), channel_id=1, source_target_pairs={{0,8},{8,16},{16,24},{24,32},{32,40},{40,48},{48,56},{56,64},{64,7... | collective-permute-start | bytes 245768
  342.9 8.8 %collective-permute-start.1 = (bf16[13,512]{1,0:T(8,128)(2,1)S(1)}, bf16[13,512]{1,0:T(8,128)(2,1)S(1)}, u32[]{:S(2)}, u32[]{:S(2)}) collective-permute-start(bf16[13,512]{1,0:T(8,128)(2,1)S(1)} %slice.47), channel_id=1, source_target_pairs={{0,16},{8,24},{16,32},{24,40},{32,48},{40,56},{48,64},{56,72},{64,... | collective-permute-start | bytes 39944
Sparse Core Ops, SparseCore 0:
  16.2 92.5 all-gather.3
  170.4 80.1 all-reduce.10
  353.0 72.4 all-reduce.8
where the time goes:
time: 437 us; the launch traced here: 435 us
  waiting for transfers between devices  208 us (48%)
  blocking collectives  96.4 us (22%)
  local copies, waits for them, and re-layouts  70.8 us (16%)
  between operations  19.8 us (5%)
  matrix products  18.5 us (4%)
  starting transfers between devices  13.2 us (3%)
  other arithmetic  8.38 us (2%)
    unnamed x2, blocking collectives  96.4 us
    psum x1, waiting for transfers between devices, on_device(): lax.psum(local_sum, 'space').astype(jnp.float32)  72.1 us
    all_to_all x1, waiting for transfers between devices, on_device(): lax.all_to_all(blocks, 'space', split_axis=0, concat_axis=2, tiled=True)  71.2 us
    unnamed x6, waiting for transfers between devices  64.3 us
    transpose x3, local copies, waits for them, and re-layouts, time_major(): jnp.transpose(shaped, (0, 2, 3, 1, 4))  13.3 us
    unnamed x39, local copies, waits for them, and re-layouts  10.8 us
  transfers between devices with their start and end apart: 7, of which 4 were waited for; matrix products, arithmetic and copies ran while one was open for 13% of the time, Pallas kernels for 0%

commit v1 on v0

v1 whole, which is shorter than its diff:
```python
import math

import jax
import jax.numpy as jnp
from jax import lax
from jax.experimental import pallas as pl
from jax.experimental.pallas import tpu as pltpu
from jax.sharding import PartitionSpec as P

HEADS = 13
HD = 128
FEATURES = HEADS * HD
EMB = 512
FRAMES = 16
PATCHES = 256
LOCAL = 32
SLOTS = 77
PADDED = 80
CAPTIONS = 32
SHARPNESS = 4.0
LOGIT_SCALE = 10.0
LOG2E = math.log2(math.e)
SCORE_LOG2 = HD ** (-0.5) * LOG2E
SHARP_LOG2 = SHARPNESS * LOG2E
MIB = 1 << 20


def nt(a, b):
    return lax.dot_general(a, b, (((1,), (1,)), ((), ())), preferred_element_type=jnp.float32)


def spatial_kernel(qkv_ref, out_ref):
    for h in range(HEADS):
        q = qkv_ref[:, 0, :, pl.ds(h * HD, HD)].reshape(PATCHES, HD)
        k = qkv_ref[:, 0, :, pl.ds(FEATURES + h * HD, HD)].reshape(PATCHES, HD)
        v = qkv_ref[:, 0, :, pl.ds(2 * FEATURES + h * HD, HD)].reshape(PATCHES, HD)
        s = nt(q, k)
        m = jnp.max(s, axis=-1, keepdims=True)
        e = jnp.exp2((s - m) * SCORE_LOG2)
        total = jnp.sum(e, axis=-1, keepdims=True)
        o = jnp.dot(e.astype(jnp.bfloat16), v, preferred_element_type=jnp.float32)
        o = (o / total).astype(jnp.bfloat16)
        out_ref[:, 0, :, pl.ds(h * HD, HD)] = o.reshape(8, LOCAL, HD)


def spatial_attention(blocks):
    frames = blocks.shape[1]
    return pl.pallas_call(
        spatial_kernel,
        grid=(frames,),
        in_specs=[pl.BlockSpec((8, 1, LOCAL, 3 * FEATURES), lambda f: (0, f, 0, 0))],
        out_specs=pl.BlockSpec((8, 1, LOCAL, FEATURES), lambda f: (0, f, 0, 0)),
        out_shape=jax.ShapeDtypeStruct((8, frames, LOCAL, FEATURES), jnp.bfloat16),
        compiler_params=pltpu.CompilerParams(vmem_limit_bytes=32 * MIB),
        cost_estimate=pl.CostEstimate(
            flops=4 * frames * HEADS * PATCHES * PATCHES * HD,
            bytes_accessed=frames * PATCHES * 4 * FEATURES * 2,
            transcendentals=frames * HEADS * PATCHES * PATCHES,
        ),
        name="spatial_attention",
    )(blocks)


def token_kernel(s_ref, tqk_ref, proj_ref, cap_ref, emb_ref, stats_ref, grad_ref, comb):
    rows = FRAMES * 16
    r = lax.broadcasted_iota(jnp.int32, (rows, rows), 0)
    c = lax.broadcasted_iota(jnp.int32, (rows, rows), 1)
    bias = jnp.where((r & 15) == (c & 15), 0.0, -1e30).astype(jnp.float32)
    for g in range(LOCAL // 16):
        part = pl.ds(g * 16, 16)
        for h in range(HEADS):
            q = tqk_ref[:, part, pl.ds(h * HD, HD)].reshape(rows, HD)
            k = tqk_ref[:, part, pl.ds(FEATURES + h * HD, HD)].reshape(rows, HD)
            v = s_ref[:, part, pl.ds(h * HD, HD)].reshape(rows, HD)
            s = nt(q, k) + bias
            m = jnp.max(s, axis=-1, keepdims=True)
            e = jnp.exp2((s - m) * SCORE_LOG2)
            total = jnp.sum(e, axis=-1, keepdims=True)
            o = jnp.dot(e.astype(jnp.bfloat16), v, preferred_element_type=jnp.float32)
            o = (v.astype(jnp.float32) + o / total).astype(jnp.bfloat16)
            comb[:, part, pl.ds(h * HD, HD)] = o.reshape(FRAMES, 16, HD)
    tokens = FRAMES * LOCAL
    projected = jnp.dot(
        comb[...].reshape(tokens, FEATURES), proj_ref[...], preferred_element_type=jnp.float32
    )
    scale = lax.rsqrt(jnp.mean(projected * projected, axis=-1, keepdims=True) + 1e-06)
    video = (projected * scale).astype(jnp.bfloat16)
    emb_ref[...] = video.reshape(FRAMES, LOCAL, EMB)

    eye = lax.broadcasted_iota(jnp.int32, (PADDED, 128), 0) == lax.broadcasted_iota(
        jnp.int32, (PADDED, 128), 1
    )
    group = 8
    for j0 in range(0, CAPTIONS, group):
        caps = cap_ref[pl.ds(j0, group)].reshape(group * PADDED, EMB)
        sim = nt(caps, video)
        top = jnp.max(sim, axis=-1, keepdims=True)
        w = jnp.exp2((sim - top) * SHARP_LOG2)
        total = jnp.sum(w, axis=-1, keepdims=True)
        for j in range(group):
            rng = slice(j * PADDED, (j + 1) * PADDED)
            stats_ref[0, pl.ds(j0 + j, 1), :] = jnp.sum(
                jnp.where(eye, top[rng], 0.0), axis=0, keepdims=True
            )
            stats_ref[1, pl.ds(j0 + j, 1), :] = jnp.sum(
                jnp.where(eye, total[rng], 0.0), axis=0, keepdims=True
            )
        grad_ref[pl.ds(j0, group)] = jnp.dot(
            w.astype(jnp.bfloat16), video, preferred_element_type=jnp.float32
        ).reshape(group, PADDED, EMB)


def token_part(spatial, temporal_qk, proj_weight, caps):
    vmem = pl.BlockSpec(memory_space=pltpu.VMEM)
    return pl.pallas_call(
        token_kernel,
        in_specs=[vmem] * 4,
        out_specs=[vmem] * 3,
        out_shape=[
            jax.ShapeDtypeStruct((FRAMES, LOCAL, EMB), jnp.bfloat16),
            jax.ShapeDtypeStruct((2, CAPTIONS, 128), jnp.float32),
            jax.ShapeDtypeStruct((CAPTIONS, PADDED, EMB), jnp.float32),
        ],
        scratch_shapes=[pltpu.VMEM((FRAMES, LOCAL, FEATURES), jnp.bfloat16)],
        compiler_params=pltpu.CompilerParams(vmem_limit_bytes=48 * MIB),
        cost_estimate=pl.CostEstimate(
            flops=4_400_000_000, bytes_accessed=16_000_000, transcendentals=3_000_000
        ),
        name="token_part",
    )(spatial, temporal_qk, proj_weight, caps)


def coef_kernel(pos_ref, me_ref, stats_ref, lens_ref, grad_ref, out_ref, loss_ref):
    tops = stats_ref[:, 0]
    totals = stats_ref[:, 1]
    top = jnp.max(tops, axis=0)
    total = jnp.sum(totals * jnp.exp2((tops - top[None]) * SHARP_LOG2), axis=0)
    soft = top + jnp.log(total) / SHARPNESS
    slot = lax.broadcasted_iota(jnp.int32, (CAPTIONS, 128), 1).astype(jnp.float32)
    lens = lens_ref[...].astype(jnp.float32)
    live = slot < lens
    lens_col = lens[:, :1]
    score = jnp.sum(jnp.where(live, soft, 0.0), axis=-1, keepdims=True) / lens_col
    logits = LOGIT_SCALE * score
    peak = jnp.max(logits, axis=0, keepdims=True)
    log_total = peak + jnp.log(jnp.sum(jnp.exp(logits - peak), axis=0, keepdims=True))
    onehot = lax.broadcasted_iota(jnp.int32, (CAPTIONS, 1), 0) == pos_ref[0]
    loss_ref[...] = log_total - jnp.sum(jnp.where(onehot, logits, 0.0), axis=0, keepdims=True)
    grad_logit = LOGIT_SCALE * (jnp.exp(logits - log_total) - onehot.astype(jnp.float32))
    coef = jnp.where(live, grad_logit / lens_col, 0.0)
    mine = stats_ref[me_ref[0], 0]
    factor = coef * jnp.exp2((mine - soft) * SHARP_LOG2)
    eye = lax.broadcasted_iota(jnp.int32, (PADDED, 128), 0) == lax.broadcasted_iota(
        jnp.int32, (PADDED, 128), 1
    )
    for j in range(CAPTIONS):
        col = jnp.sum(jnp.where(eye, factor[j : j + 1, :], 0.0), axis=-1, keepdims=True)
        out_ref[j] = (grad_ref[j] * col).astype(jnp.bfloat16)


def coef_part(pos, me, stats, lens, grad):
    vmem = pl.BlockSpec(memory_space=pltpu.VMEM)
    smem = pl.BlockSpec(memory_space=pltpu.SMEM)
    return pl.pallas_call(
        coef_kernel,
        in_specs=[smem, smem, vmem, vmem, vmem],
        out_specs=[vmem, vmem],
        out_shape=[
            jax.ShapeDtypeStruct((CAPTIONS, PADDED, EMB), jnp.bfloat16),
            jax.ShapeDtypeStruct((1, 1), jnp.float32),
        ],
        compiler_params=pltpu.CompilerParams(vmem_limit_bytes=32 * MIB),
        cost_estimate=pl.CostEstimate(
            flops=4_000_000, bytes_accessed=8_000_000, transcendentals=100_000
        ),
        name="coef_part",
    )(pos, me, stats, lens, grad)


def on_device(clip_qkv, temporal_qk, proj_weight, caption_tokens, caption_lens, positive):
    groups = lax.axis_size("space")
    lens_row = jnp.broadcast_to(
        caption_lens.astype(jnp.bfloat16)[:, None, None], (1, PADDED - SLOTS, EMB)
    )
    caps = lax.all_gather(
        jnp.concatenate([caption_tokens, lens_row], axis=1), "dp", axis=0, tiled=True
    )
    blocks = clip_qkv.reshape(groups, FRAMES // groups, LOCAL, 3 * FEATURES)
    blocks = lax.all_to_all(blocks, "space", split_axis=0, concat_axis=0, tiled=True)
    attended = spatial_attention(blocks)
    spatial = lax.all_to_all(attended, "space", split_axis=0, concat_axis=0, tiled=True)
    video, stats, grad = token_part(
        spatial.reshape(FRAMES, LOCAL, FEATURES),
        temporal_qk.reshape(FRAMES, LOCAL, 2 * FEATURES),
        proj_weight,
        caps,
    )
    stats = lax.all_gather(stats, "space", axis=0)
    me = lax.axis_index("space").astype(jnp.int32)[None]
    scaled, loss = coef_part(positive, me, stats, caps[:, SLOTS, :128], grad)
    mine = lax.psum_scatter(scaled, "dp", scatter_dimension=0, tiled=True)
    mine = lax.psum(mine, "space")
    caption_grad = mine[:, :SLOTS].astype(jnp.float32)
    return video[None], caption_grad, loss.reshape(1)


def solution(mesh):
    return jax.shard_map(
        on_device,
        mesh=mesh,
        in_specs=(
            P("dp", None, "space", None),
            P("dp", None, "space", None),
            P(),
            P("dp", None, None),
            P("dp"),
            P("dp"),
        ),
        out_specs=(P("dp", None, "space", None), P("dp", None, None), P("dp")),
        check_vma=False,
    )
```

time: 437 us -> 370 us (0.85)
  waiting for transfers between devices: 208 us -> 289 us
  blocking collectives: 96.4 us -> 28.4 us
  local copies, waits for them, and re-layouts: 70.8 us -> 6.57 us
  Pallas kernels: 0 us -> 19.1 us
  matrix products: 18.5 us -> 0 us
  other arithmetic: 8.38 us -> 0.9 us
  between operations: 19.8 us -> 15.1 us
    reduce_scatter x0 -> x1, waiting for transfers between devices: none -> 120 us  [on_device(): mine = lax.psum_scatter(scaled, 'dp', scatter_dimension=0, tiled=True)]
    unnamed x2 -> x0, blocking collectives: 96.4 us -> none
    unnamed x6 -> x3, waiting for transfers between devices: 64.3 us -> 0.05 us
    all_gather x0 -> x1, blocking collectives: none -> 28.4 us  [on_device(): stats = lax.all_gather(stats, 'space', axis=0)]
    slice x11 -> x1, local copies, waits for them, and re-layouts: 20.2 us -> 0.86 us  [on_device(): scaled, loss = coef_part(positive, me, stats, caps[:, SLOTS, :128], grad)]
    pallas_call x0 -> x3, Pallas kernels: none -> 19.1 us  [the longest x1 11.2 us: token_part(): pl.pallas_call(token_kernel, in_specs=[vmem] * 4, out_specs=[vmem] * 3, o...]
    dot_general x7 -> x0, matrix products: 18.5 us -> none  [the longest x1 5.65 us: on_device(): jnp.einsum('cnk,cne->ke', weights, video_rows, preferred_element_type=jnp...]
    reshape x6 -> x0, local copies, waits for them, and re-layouts: 14.5 us -> none  [the longest x2 8.26 us: time_major(): shaped = block.reshape(clip_count, frames, local_patches, HEADS, HD)]
  transfers between devices with their start and end apart: 7 -> 5, of which waited for: 4 -> 5; matrix products, arithmetic and copies ran while one was open for 13% -> 0% of each run, Pallas kernels for 0% -> 2%
where the time goes in v1:
time: 370 us; the launch traced here: 368 us
  waiting for transfers between devices  289 us (78%)
  blocking collectives  28.4 us (8%)
  Pallas kernels  19.1 us (5%)
  between operations  15.1 us (4%)
  starting transfers between devices  9.32 us (3%)
  local copies, waits for them, and re-layouts  6.57 us (2%)
    reduce_scatter x1, waiting for transfers between devices, on_device(): mine = lax.psum_scatter(scaled, 'dp', scatter_dimension=0, tiled=True)  120 us
    psum x1, waiting for transfers between devices, on_device(): mine = lax.psum(mine, 'space')  75.4 us
    all_to_all x1, waiting for transfers between devices, on_device(): lax.all_to_all(blocks, 'space', split_axis=0, concat_axis=0, tiled=True)  70.5 us
    all_gather x1, blocking collectives, on_device(): stats = lax.all_gather(stats, 'space', axis=0)  28.4 us
    all_gather x1, waiting for transfers between devices, on_device(): lax.all_gather(jnp.concatenate([caption_tokens, lens_row], axis=1), 'dp',...  14.1 us
    pallas_call x1, Pallas kernels, token_part(): pl.pallas_call(token_kernel, in_specs=[vmem] * 4, out_specs=[vmem] * 3, o...  11.2 us
    all_to_all x1, waiting for transfers between devices, on_device(): lax.all_to_all(attended, 'space', split_axis=0, concat_axis=0, tiled=True)  8.65 us
  transfers between devices with their start and end apart: 5, of which 5 were waited for; matrix products, arithmetic and copies ran while one was open for 0% of the time, Pallas kernels for 2%

profile of v1, /device:TPU:32, one launch (start us, length us, event | category | flops | bytes accessed | tf_op | source)
XLA Modules:
  0.0 368.4 jit_solution(10500852989792689101)
XLA Ops:
  7.2 0.0 copy-start.3
  7.2 5.5 %all-to-all-start = ((bf16[8,2,32,4992]{3,2,1,0:T(8,128)(2,1)}), bf16[8,2,32,4992]{3,2,1,0:T(8,128)(2,1)}, u32[]{:S(2)}, u32[]{:S(2)}) async-start(bf16[8,2,32,4992]{3,2,1,0:T(8,128)(2,1)} %bitcast.14), calls=%async_computation | async-start | bytes 10223616 | tf_op jit(solution)/shard_map/all_to_all | solution.py:189
  12.6 0.0 all-gather.3.cloned.1.call-start
  13.3 0.0 copy-done.3
  13.3 0.6 concatenate.3
  14.0 0.0 all-gather.3.cloned.1.call-update
  14.0 70.5 %all-to-all-done.qkv_ref = bf16[8,2,32,4992]{3,2,1,0:T(8,128)(2,1)} async-done(((bf16[8,2,32,4992]{3,2,1,0:T(8,128)(2,1)}), bf16[8,2,32,4992]{3,2,1,0:T(8,128)(2,1)}, u32[]{:S(2)}, u32[]{:S(2)}) %all-to-all-start) | async-done | bytes 5111840 | tf_op jit(solution)/shard_map/all_to_all | solution.py:189
  84.5 5.8 %spatial_attention.1 = bf16[8,2,32,1664]{3,2,1,0:T(8,128)(2,1)} custom-call(bf16[8,2,32,4992]{3,2,1,0:T(8,128)(2,1)} %all-to-all-done.qkv_ref), custom_call_target="tpu_custom_call" | custom-call | flops 872415232 | bytes 6815744 | tf_op jit(solution)/shard_map/spatial_attention/pallas_call | solution.py:48
  90.3 0.0 copy-start.2
  90.3 3.7 %all-to-all-start.1 = ((bf16[8,2,32,1664]{3,2,1,0:T(8,128)(2,1)}), bf16[8,2,32,1664]{3,2,1,0:T(8,128)(2,1)S(1)}, u32[]{:S(2)}, u32[]{:S(2)}) async-start(bf16[8,2,32,1664]{3,2,1,0:T(8,128)(2,1)} %spatial_attention.1), calls=%async_computation.1 | async-start | bytes 3407872 | tf_op jit(solution)/shard_map/all_to_all | solution.py:191
  94.1 0.0 reduce-scatter.2.cloned.1.call-start
  94.7 14.1 %all-gather.3.cloned.1.call-done.cap_ref = bf16[32,80,512]{2,1,0:T(8,128)(2,1)} async-done(((bf16[1,80,512]{2,1,0:T(8,128)(2,1)}), bf16[32,80,512]{2,1,0:T(8,128)(2,1)}) %all-gather.3.cloned.1.call-update) | async-done | bytes 2621456 | tf_op jit(solution)/shard_map/all_gather | solution.py:185
  108.8 0.9 slice.8
  109.7 8.7 %all-to-all-done.1 = bf16[8,2,32,1664]{3,2,1,0:T(8,128)(2,1)S(1)} async-done(((bf16[8,2,32,1664]{3,2,1,0:T(8,128)(2,1)}), bf16[8,2,32,1664]{3,2,1,0:T(8,128)(2,1)S(1)}, u32[]{:S(2)}, u32[]{:S(2)}) %all-to-all-start.1) | async-done | bytes 1703968 | tf_op jit(solution)/shard_map/all_to_all | solution.py:191
  118.3 0.0 copy-done.2
  118.3 0.0 copy-start.1
  118.3 1.7 copy-done.1
  120.1 11.2 %token_part.1 = (bf16[16,32,512]{2,1,0:T(8,128)(2,1)}, f32[2,32,128]{2,1,0:T(8,128)S(1)}, f32[32,80,512]{2,1,0:T(8,128)}) custom-call(bf16[16,32,1664]{2,1,0:T(8,128)(2,1)S(1)} %bitcast.11, bf16[16,32,3328]{2,1,0:T(8,128)(2,1)} %bitcast.15, bf16[1664,512]{1,0:T(8,128)(2,1)S(1)} %copy-done.2, bf16[32,80,512]{2,1,0:T(8,128)(2,1)S(1)} %copy-done.1), custom_call_target="tpu_custom_call" | custom-call | flops 4400000000 | bytes 16000000 | tf_op jit(solution)/shard_map/token_part/pallas_call | solution.py:115
  131.2 28.4 %all-gather = f32[16,32,128]{2,1,0:T(8,128)S(1)} all-gather(f32[2,32,128]{2,1,0:T(8,128)S(1)} %get-tuple-element.9), channel_id=2, replica_groups=mesh['dp'=32,'space'=8] {'space'}, dimensions={0}, use_global_device_ids=true | all-gather | bytes 294912 | tf_op jit(solution)/shard_map/all_gather | solution.py:198
  159.6 0.0 copy-start
  159.6 2.5 copy-done
  162.1 2.2 coef_part.1
  164.3 0.0 reduce-scatter.2.cloned.1.call-update
  164.3 0.0 all-reduce.3.cloned.1.call-start
  164.4 120.3 %reduce-scatter.2.cloned.1.call-done = bf16[1,80,512]{2,1,0:T(8,128)(2,1)} async-done(((bf16[32,80,512]{2,1,0:T(8,128)(2,1)}), bf16[1,80,512]{2,1,0:T(8,128)(2,1)}) %reduce-scatter.2.cloned.1.call-update) | async-done | bytes 81936 | tf_op jit(solution)/shard_map/reduce_scatter | solution.py:201
  284.7 0.0 all-reduce.3.cloned.1.call-update
  284.7 75.4 %all-reduce.3.cloned.1.call-done = bf16[1,80,512]{2,1,0:T(8,128)(2,1)} async-done(((bf16[1,80,512]{2,1,0:T(8,128)(2,1)}), bf16[1,80,512]{2,1,0:T(8,128)(2,1)}) %all-reduce.3.cloned.1.call-update) | async-done | bytes 81936 | tf_op jit(solution)/shard_map/psum | solution.py:202
  360.2 0.9 slice_convert_fusion
  361.1 0.8 copy.13
  (1 shorter events, 0.0 us)
Async XLA Ops:
  7.2 6.2 %copy-start.3 = (bf16[1,77,512]{2,1,0:T(8,128)(2,1)S(1)}, bf16[1,77,512]{2,1,0:T(8,128)(2,1)}, u32[]{:S(2)}) copy-start(bf16[1,77,512]{2,1,0:T(8,128)(2,1)} %param.9) | copy-start | bytes 236548
  7.2 77.4 %all-to-all-start = ((bf16[8,2,32,4992]{3,2,1,0:T(8,128)(2,1)}), bf16[8,2,32,4992]{3,2,1,0:T(8,128)(2,1)}, u32[]{:S(2)}, u32[]{:S(2)}) async-start(bf16[8,2,32,4992]{3,2,1,0:T(8,128)(2,1)} %bitcast.14), calls=%async_computation | async-start | bytes 10223616 | tf_op jit(solution)/shard_map/all_to_all | solution.py:189
  12.6 96.2 %all-gather.3.cloned.1.call-start = ((), (), s32[]{:S(2)}) async-start(), calls=%async_computation.3 | async-start | bytes 2703360 | tf_op jit(solution)/shard_map/all_gather | solution.py:185
  90.3 28.0 %copy-start.2 = (bf16[1664,512]{1,0:T(8,128)(2,1)S(1)}, bf16[1664,512]{1,0:T(8,128)(2,1)}, u32[]{:S(2)}) copy-start(bf16[1664,512]{1,0:T(8,128)(2,1)} %proj_ref.1) | copy-start | bytes 5111812
  90.3 28.0 %all-to-all-start.1 = ((bf16[8,2,32,1664]{3,2,1,0:T(8,128)(2,1)}), bf16[8,2,32,1664]{3,2,1,0:T(8,128)(2,1)S(1)}, u32[]{:S(2)}, u32[]{:S(2)}) async-start(bf16[8,2,32,1664]{3,2,1,0:T(8,128)(2,1)} %spatial_attention.1), calls=%async_computation.1 | async-start | bytes 3407872 | tf_op jit(solution)/shard_map/all_to_all | solution.py:191
  94.1 190.7 %reduce-scatter.2.cloned.1.call-start = ((), (), s32[]{:S(2)}) async-start(), calls=%async_computation.4 | async-start | bytes 2703360 | tf_op jit(solution)/shard_map/reduce_scatter | solution.py:201
  118.3 1.7 copy-start.1
  159.6 2.5 copy-start
  164.3 195.8 %all-reduce.3.cloned.1.call-start = ((), (), s32[]{:S(2)}) async-start(), calls=%async_computation.5 | async-start | bytes 163840 | tf_op jit(solution)/shard_map/psum | solution.py:202
Sparse Core Ops, SparseCore 0:
  16.8 91.9 all-gather.2
  164.4 120.2 reduce-scatter.1
  287.5 72.5 all-reduce.2

commit v2 on v1

v2 whole, which is shorter than its diff:
```python
import math

import jax
import jax.numpy as jnp
from jax import lax
from jax.experimental import pallas as pl
from jax.experimental.pallas import tpu as pltpu
from jax.sharding import PartitionSpec as P

HEADS = 13
HD = 128
FEATURES = HEADS * HD
EMB = 512
FRAMES = 16
PATCHES = 256
LOCAL = 32
SLOTS = 77
PADDED = 80
CAPTIONS = 32
SHARPNESS = 4.0
LOGIT_SCALE = 10.0
LOG2E = math.log2(math.e)
SCORE_LOG2 = HD ** (-0.5) * LOG2E
SHARP_LOG2 = SHARPNESS * LOG2E
MIB = 1 << 20
VMEM = pl.BlockSpec(memory_space=pltpu.VMEM)
SMEM = pl.BlockSpec(memory_space=pltpu.SMEM)

NEAR = ((0, 1), (1, 0), (3, 0), (1, 1), (3, 1))
FAR = ((2, 0), (2, 1))


def moved(dx, dy):
    return [(s, (s // 2 + dx) % 4 * 2 + (s % 2 ^ dy)) for s in range(8)]


def nt(a, b):
    return lax.dot_general(a, b, (((1,), (1,)), ((), ())), preferred_element_type=jnp.float32)


def exchange(block):
    east = lax.ppermute(jnp.stack([block(2, 0)[0], block(2, 1)[0]]), "space", moved(1, 0))
    west = lax.ppermute(jnp.stack([block(2, 0)[1], block(2, 1)[1]]), "space", moved(3, 0))
    got = {}
    for dx, dy in NEAR:
        back = ((4 - dx) % 4, dy)
        pair = lax.ppermute(block(dx, dy), "space", moved(dx, dy))
        got[back] = [pair]
    for i, (dx, dy) in enumerate(FAR):
        got[(dx, dy)] = [
            lax.ppermute(east[i : i + 1], "space", moved(1, dy)),
            lax.ppermute(west[i : i + 1], "space", moved(3, dy)),
        ]
    return got


ORDER = ((0, 0),) + NEAR + FAR


def frame_view(refs, f):
    views = [refs[i].at[f] for i in range(6)]
    return views + [refs[6 + 2 * i + f].at[0] for i in range(2)]


def spatial_kernel(*refs):
    ins, outs = refs[:10], refs[10:]
    for f in range(2):
        src, dst = frame_view(ins, f), frame_view(outs, f)

        def rows(offset):
            return jnp.concatenate([r[:, pl.ds(offset, HD)] for r in src], axis=0)

        for h in range(HEADS):
            q = rows(h * HD)
            k = rows(FEATURES + h * HD)
            v = rows(2 * FEATURES + h * HD)
            s = nt(q, k)
            m = jnp.max(s, axis=-1, keepdims=True)
            e = jnp.exp2((s - m) * SCORE_LOG2)
            total = jnp.sum(e, axis=-1, keepdims=True)
            o = jnp.dot(e.astype(jnp.bfloat16), v, preferred_element_type=jnp.float32)
            o = (o / total).astype(jnp.bfloat16)
            for i in range(8):
                dst[i][:, pl.ds(h * HD, HD)] = o[i * LOCAL : (i + 1) * LOCAL]


def spatial_attention(pieces):
    shapes = [(2, LOCAL, FEATURES)] * 6 + [(1, LOCAL, FEATURES)] * 4
    return pl.pallas_call(
        spatial_kernel,
        in_specs=[VMEM] * 10,
        out_specs=[VMEM] * 10,
        out_shape=[jax.ShapeDtypeStruct(s, jnp.bfloat16) for s in shapes],
        compiler_params=pltpu.CompilerParams(vmem_limit_bytes=24 * MIB),
        cost_estimate=pl.CostEstimate(
            flops=8 * HEADS * PATCHES * PATCHES * HD,
            bytes_accessed=2 * PATCHES * 4 * FEATURES * 2,
            transcendentals=2 * HEADS * PATCHES * PATCHES,
        ),
        name="spatial_attention",
    )(*pieces)


def time_kernel(tqk_ref, out_ref):
    rows = FRAMES * 16
    r = lax.broadcasted_iota(jnp.int32, (rows, rows), 0)
    c = lax.broadcasted_iota(jnp.int32, (rows, rows), 1)
    bias = jnp.where((r & 15) == (c & 15), 0.0, -1e30).astype(jnp.float32)
    for g in range(LOCAL // 16):
        part = pl.ds(g * 16, 16)
        for h in range(HEADS):
            q = tqk_ref[:, part, pl.ds(h * HD, HD)].reshape(rows, HD)
            k = tqk_ref[:, part, pl.ds(FEATURES + h * HD, HD)].reshape(rows, HD)
            s = nt(q, k) + bias
            m = jnp.max(s, axis=-1, keepdims=True)
            e = jnp.exp2((s - m) * SCORE_LOG2)
            total = jnp.sum(e, axis=-1, keepdims=True)
            out_ref[g * HEADS + h] = (e * (1.0 / total)).astype(jnp.bfloat16)


def time_weights(temporal_qk):
    rows = FRAMES * 16
    return pl.pallas_call(
        time_kernel,
        in_specs=[VMEM],
        out_specs=VMEM,
        out_shape=jax.ShapeDtypeStruct((2 * HEADS, rows, rows), jnp.bfloat16),
        compiler_params=pltpu.CompilerParams(vmem_limit_bytes=24 * MIB),
        cost_estimate=pl.CostEstimate(
            flops=4 * HEADS * rows * rows * HD,
            bytes_accessed=7_000_000,
            transcendentals=2 * HEADS * rows * rows,
        ),
        name="time_weights",
    )(temporal_qk)


def gathered_kernel(place_ref, mine_ref, other_ref, out_ref):
    y_hi, core = place_ref[0], place_ref[1]
    for z in range(8):
        for k in range(2):
            at = (y_hi ^ k) * 16 + z * 2
            out_ref[at + core] = mine_ref[z, k]
            out_ref[at + 1 - core] = other_ref[z, k]


def gather_captions(caps, place):
    far = lax.ppermute(caps, "dp", [(i, i ^ 16) for i in range(32)])
    pair = jnp.stack([caps, far])
    groups = [[a * 16 + z * 2 + c for z in range(8)] for a in range(2) for c in range(2)]
    mine = lax.all_to_all(
        jnp.broadcast_to(pair[None], (8,) + pair.shape),
        "dp", split_axis=0, concat_axis=0, axis_index_groups=groups, tiled=True,
    )
    other = lax.ppermute(mine, "dp", [(i, i ^ 1) for i in range(32)])
    return pl.pallas_call(
        gathered_kernel,
        in_specs=[SMEM, VMEM, VMEM],
        out_specs=VMEM,
        out_shape=jax.ShapeDtypeStruct((CAPTIONS, PADDED, EMB), jnp.bfloat16),
        compiler_params=pltpu.CompilerParams(vmem_limit_bytes=16 * MIB),
        cost_estimate=pl.CostEstimate(flops=0, bytes_accessed=5_200_000, transcendentals=0),
        name="gathered",
    )(place, mine, other)


def token_kernel(place_ref, *refs):
    pieces = refs[:10]
    time_ref, proj_ref, cap_ref, emb_ref, stats_ref, grad_ref, value, comb = refs[10:]
    x, y = place_ref[2], place_ref[3]
    for i, (dx, dy) in enumerate(ORDER):
        at = ((x + dx) & 3) * 4 + (y ^ dy) * 2
        for f in range(2):
            value[at + f] = frame_view(pieces, f)[i][...]
    rows = FRAMES * 16
    for g in range(LOCAL // 16):
        part = pl.ds(g * 16, 16)
        for h in range(HEADS):
            cols = pl.ds(h * HD, HD)
            v = value[:, part, cols].reshape(rows, HD)
            o = jnp.dot(time_ref[g * HEADS + h], v, preferred_element_type=jnp.float32)
            o = (v.astype(jnp.float32) + o).astype(jnp.bfloat16)
            comb[:, part, cols] = o.reshape(FRAMES, 16, HD)
    tokens = FRAMES * LOCAL
    projected = jnp.dot(
        comb[...].reshape(tokens, FEATURES), proj_ref[...], preferred_element_type=jnp.float32
    )
    scale = lax.rsqrt(jnp.mean(projected * projected, axis=-1, keepdims=True) + 1e-06)
    video = (projected * scale).astype(jnp.bfloat16)
    emb_ref[...] = video.reshape(FRAMES, LOCAL, EMB)

    eye = lax.broadcasted_iota(jnp.int32, (PADDED, 128), 0) == lax.broadcasted_iota(
        jnp.int32, (PADDED, 128), 1
    )
    group = 8
    for j0 in range(0, CAPTIONS, group):
        caps = cap_ref[pl.ds(j0, group)].reshape(group * PADDED, EMB)
        sim = nt(caps, video)
        top = jnp.max(sim, axis=-1, keepdims=True)
        w = jnp.exp2((sim - top) * SHARP_LOG2)
        total = jnp.sum(w, axis=-1, keepdims=True)
        for j in range(group):
            rng = slice(j * PADDED, (j + 1) * PADDED)
            top_row = jnp.sum(jnp.where(eye, top[rng], 0.0), axis=0, keepdims=True)
            total_row = jnp.sum(jnp.where(eye, total[rng], 0.0), axis=0, keepdims=True)
            for k in range(8):
                stats_ref[k, 0, pl.ds(j0 + j, 1), :] = top_row
                stats_ref[k, 1, pl.ds(j0 + j, 1), :] = total_row
        grad_ref[pl.ds(j0, group)] = jnp.dot(
            w.astype(jnp.bfloat16), video, preferred_element_type=jnp.float32
        ).reshape(group, PADDED, EMB)


def token_part(place, pieces, time, proj_weight, caps):
    return pl.pallas_call(
        token_kernel,
        in_specs=[SMEM] + [VMEM] * 13,
        out_specs=[VMEM] * 3,
        out_shape=[
            jax.ShapeDtypeStruct((FRAMES, LOCAL, EMB), jnp.bfloat16),
            jax.ShapeDtypeStruct((8, 2, CAPTIONS, 128), jnp.float32),
            jax.ShapeDtypeStruct((CAPTIONS, PADDED, EMB), jnp.float32),
        ],
        scratch_shapes=[pltpu.VMEM((FRAMES, LOCAL, FEATURES), jnp.bfloat16)] * 2,
        compiler_params=pltpu.CompilerParams(vmem_limit_bytes=40 * MIB),
        cost_estimate=pl.CostEstimate(
            flops=4_000_000_000, bytes_accessed=16_000_000, transcendentals=1_300_000
        ),
        name="token_part",
    )(place, *pieces, time, proj_weight, caps)


def coef_kernel(place_ref, pos_ref, stats_ref, lens_ref, grad_ref, send_ref, keep_ref, loss_ref, hold):
    tops = stats_ref[:, 0]
    totals = stats_ref[:, 1]
    top = jnp.max(tops, axis=0)
    total = jnp.sum(totals * jnp.exp2((tops - top[None]) * SHARP_LOG2), axis=0)
    soft = top + jnp.log(total) / SHARPNESS
    slot = lax.broadcasted_iota(jnp.int32, (CAPTIONS, 128), 1).astype(jnp.float32)
    lens = lens_ref[...].astype(jnp.float32)
    live = slot < lens
    lens_col = lens[:, :1]
    score = jnp.sum(jnp.where(live, soft, 0.0), axis=-1, keepdims=True) / lens_col
    logits = LOGIT_SCALE * score
    peak = jnp.max(logits, axis=0, keepdims=True)
    log_total = peak + jnp.log(jnp.sum(jnp.exp(logits - peak), axis=0, keepdims=True))
    onehot = lax.broadcasted_iota(jnp.int32, (CAPTIONS, 1), 0) == pos_ref[0]
    loss_ref[...] = log_total - jnp.sum(jnp.where(onehot, logits, 0.0), axis=0, keepdims=True)
    grad_logit = LOGIT_SCALE * (jnp.exp(logits - log_total) - onehot.astype(jnp.float32))
    coef = jnp.where(live, grad_logit / lens_col, 0.0)
    mine = stats_ref[place_ref[2] * 2 + place_ref[3], 0]
    hold[...] = coef * jnp.exp2((mine - soft) * SHARP_LOG2)
    eye = lax.broadcasted_iota(jnp.int32, (PADDED, 128), 0) == lax.broadcasted_iota(
        jnp.int32, (PADDED, 128), 1
    )
    core = place_ref[1]
    for m in range(CAPTIONS // 2):
        for j, ref in ((2 * m + 1 - core, send_ref), (2 * m + core, keep_ref)):
            col = jnp.sum(jnp.where(eye, hold[pl.ds(j, 1), :], 0.0), axis=-1, keepdims=True)
            ref[m] = (grad_ref[j] * col).astype(jnp.bfloat16)


def coef_part(place, pos, stats, lens, grad):
    half = jax.ShapeDtypeStruct((CAPTIONS // 2, PADDED, EMB), jnp.bfloat16)
    return pl.pallas_call(
        coef_kernel,
        in_specs=[SMEM, SMEM, VMEM, VMEM, VMEM],
        out_specs=[VMEM] * 3,
        out_shape=[half, half, jax.ShapeDtypeStruct((1, 1), jnp.float32)],
        scratch_shapes=[pltpu.VMEM((CAPTIONS, 128), jnp.float32)],
        compiler_params=pltpu.CompilerParams(vmem_limit_bytes=16 * MIB),
        cost_estimate=pl.CostEstimate(
            flops=4_000_000, bytes_accessed=8_000_000, transcendentals=100_000
        ),
        name="coef_part",
    )(place, pos, stats, lens, grad)


def small_call(kernel, name, operands, out_shapes, specs=None):
    return pl.pallas_call(
        kernel,
        in_specs=specs or [VMEM] * len(operands),
        out_specs=[VMEM] * len(out_shapes),
        out_shape=[jax.ShapeDtypeStruct(s, d) for s, d in out_shapes],
        compiler_params=pltpu.CompilerParams(vmem_limit_bytes=16 * MIB),
        cost_estimate=pl.CostEstimate(flops=0, bytes_accessed=2_000_000, transcendentals=0),
        name=name,
    )(*operands)


def added(a, b):
    return (a.astype(jnp.float32) + b.astype(jnp.float32)).astype(jnp.bfloat16)


def first_sum_kernel(place_ref, keep_ref, got_ref, a_keep, a_send, b_keep, b_send):
    x = place_ref[2]
    plan = (
        (0, ((a_keep, 0, 0), (a_send, 0, 1), (a_send, 1, 2), (a_keep, 1, 3))),
        (8, ((b_keep, 0, 0), (b_keep, 1, 1), (b_send, 1, 2), (b_send, 0, 3))),
    )
    for start, parts in plan:
        for ref, at, flip in parts:
            cols = pl.ds(pl.multiple_of((x ^ flip) * 128, 128), 128)
            for m in range(8):
                ref[m, :, pl.ds(at * 128, 128)] = added(
                    keep_ref[start + m, :, cols], got_ref[start + m, :, cols]
                )


def second_sum_kernel(a_keep, a_got, b_keep, b_got, a_mine, a_send, b_mine, b_send):
    for keep, got, mine, send in ((a_keep, a_got, a_mine, a_send), (b_keep, b_got, b_mine, b_send)):
        mine[...] = added(keep[:, :, :128], got[:, :, :128])
        send[...] = added(keep[:, :, 128:], got[:, :, 128:])


def third_sum_kernel(a_mine, a_got, b_mine, b_got, out):
    out[pl.ds(0, 8)] = added(a_mine[...], a_got[...])
    out[pl.ds(8, 8)] = added(b_mine[...], b_got[...])


def fourth_sum_kernel(parts, out):
    total = jnp.sum(parts[...].astype(jnp.float32), axis=0).astype(jnp.bfloat16)
    for k in range(8):
        out[k] = total


def last_sum_kernel(parts, out):
    for x in range(4):
        total = parts[2 * x].astype(jnp.float32) + parts[2 * x + 1].astype(jnp.float32)
        out[0, :, pl.ds(x * 128, 128)] = total[:SLOTS]


def reduce_gradient(place, send, keep):
    bf16 = jnp.bfloat16
    one = [(s, s ^ 2) for s in range(8)]
    three = [(s, s ^ 6) for s in range(8)]
    got = lax.ppermute(send, "dp", [(i, i ^ 1) for i in range(32)])
    a_keep, a_send, b_keep, b_send = small_call(
        first_sum_kernel, "first_sum", (place, keep, got), [((8, PADDED, 256), bf16)] * 4,
        [SMEM, VMEM, VMEM],
    )
    a_got = lax.ppermute(a_send, "space", one)
    b_got = lax.ppermute(b_send, "space", three)
    a_mine, a_send, b_mine, b_send = small_call(
        second_sum_kernel, "second_sum", (a_keep, a_got, b_keep, b_got),
        [((8, PADDED, 128), bf16)] * 4,
    )
    a_got = lax.ppermute(a_send, "space", three)
    b_got = lax.ppermute(b_send, "space", one)
    (parts,) = small_call(
        third_sum_kernel, "third_sum", (a_mine, a_got, b_mine, b_got), [((16, PADDED, 128), bf16)]
    )
    parts = lax.all_to_all(
        parts, "dp", split_axis=0, concat_axis=0, tiled=True,
        axis_index_groups=[[2 * m + c for m in range(16)] for c in range(2)],
    )
    (parts,) = small_call(fourth_sum_kernel, "fourth_sum", (parts,), [((8, PADDED, 128), bf16)])
    parts = lax.all_to_all(parts, "space", split_axis=0, concat_axis=0, tiled=True)
    return small_call(last_sum_kernel, "last_sum", (parts,), [((1, SLOTS, EMB), jnp.float32)])[0]


def on_device(clip_qkv, temporal_qk, proj_weight, caption_tokens, caption_lens, positive):
    dp = lax.axis_index("dp")
    space = lax.axis_index("space")
    x, y = space >> 1, space & 1
    place = jnp.stack([dp >> 4, dp & 1, x, y]).astype(jnp.int32)

    def frames_of(dx, dy):
        owner = ((x + dx) & 3) * 2 + (y ^ dy)
        return lax.dynamic_slice_in_dim(
            clip_qkv[0], owner * 2, 2, axis=0, allow_negative_indices=False
        )

    got = exchange(frames_of)
    lens_row = jnp.broadcast_to(
        caption_lens.astype(jnp.bfloat16)[:, None], (PADDED - SLOTS, EMB)
    )
    caps = gather_captions(jnp.concatenate([caption_tokens[0], lens_row], axis=0), place)
    time = time_weights(temporal_qk[0])
    pieces = [frames_of(0, 0)] + [piece for key in ORDER[1:] for piece in got[key]]
    attended = spatial_attention(pieces)
    sent = dict(zip(ORDER[1:6], attended[1:6]))
    sent[(2, 0)] = (attended[6][0], attended[7][0])
    sent[(2, 1)] = (attended[8][0], attended[9][0])
    got = exchange(lambda dx, dy: sent[(dx, dy)])
    pieces = [attended[0]] + [piece for key in ORDER[1:] for piece in got[key]]
    video, stats, grad = token_part(place, pieces, time, proj_weight, caps)
    stats = lax.all_to_all(stats, "space", split_axis=0, concat_axis=0, tiled=True)
    send, keep, loss = coef_part(place, positive, stats, caps[:, SLOTS, :128], grad)
    caption_grad = reduce_gradient(place, send, keep)
    return video[None], caption_grad, loss.reshape(1)


def solution(mesh):
    return jax.shard_map(
        on_device,
        mesh=mesh,
        in_specs=(
            P("dp", None, "space", None),
            P("dp", None, "space", None),
            P(),
            P("dp", None, None),
            P("dp"),
            P("dp"),
        ),
        out_specs=(P("dp", None, "space", None), P("dp", None, None), P("dp")),
        check_vma=False,
    )
```

time: 370 us -> 209 us (0.56)
  waiting for transfers between devices: 289 us -> 72.1 us
  starting transfers between devices: 9.32 us -> 56.1 us
  local copies, waits for them, and re-layouts: 6.57 us -> 25.7 us
  between operations: 15.1 us -> 2.17 us
    reduce_scatter x1 -> x0, waiting for transfers between devices: 120 us -> none  [on_device(): mine = lax.psum_scatter(scaled, 'dp', scatter_dimension=0, tiled=True)]
    psum x1 -> x0, waiting for transfers between devices: 75.4 us -> none  [on_device(): mine = lax.psum(mine, 'space')]
    all_to_all x2, waiting for transfers between devices: 79.2 us -> 5.35 us  [the longest x1 5.35 us: on_device(): lax.all_to_all(stats, 'space', split_axis=0, concat_axis=0, tiled=True)]
    ppermute x0 -> x29, waiting for transfers between devices: none -> 66.7 us  [the longest x10 25 us: exchange(): pair = lax.ppermute(block(dx, dy), 'space', moved(dx, dy))]
    ppermute x0 -> x29, starting transfers between devices: none -> 44.2 us  [the longest x10 15.4 us: exchange(): pair = lax.ppermute(block(dx, dy), 'space', moved(dx, dy))]
    all_to_all x0 -> x2, blocking collectives: none -> 29 us  [the longest x1 19.5 us: reduce_gradient(): lax.all_to_all(parts, 'dp', split_axis=0, concat_axis=0, tiled=True, axis...]
    all_gather x1 -> x0, blocking collectives: 28.4 us -> none  [on_device(): stats = lax.all_gather(stats, 'space', axis=0)]
    all_gather x1 -> x0, waiting for transfers between devices: 14.1 us -> none  [on_device(): lax.all_gather(jnp.concatenate([caption_tokens, lens_row], axis=1), 'dp',...]
  transfers between devices with their start and end apart: 5 -> 31, of which waited for: 5 -> 15; matrix products, arithmetic and copies ran while one was open for 0% -> 6% of each run, Pallas kernels for 2% -> 4%
where the time goes in v2:
time: 209 us; the launch traced here: 208 us
  waiting for transfers between devices  72.1 us (34%)
  starting transfers between devices  56.1 us (27%)
  blocking collectives  29 us (14%)
  local copies, waits for them, and re-layouts  25.7 us (12%)
  Pallas kernels  19.1 us (9%)
  other arithmetic  3.9 us (2%)
  between operations  2.17 us (1%)
    ppermute x10, waiting for transfers between devices, exchange(): pair = lax.ppermute(block(dx, dy), 'space', moved(dx, dy))  25 us
    all_to_all x1, blocking collectives, reduce_gradient(): lax.all_to_all(parts, 'dp', split_axis=0, concat_axis=0, tiled=True, axis...  19.5 us
    ppermute x10, starting transfers between devices, exchange(): pair = lax.ppermute(block(dx, dy), 'space', moved(dx, dy))  15.4 us
    unnamed x42, local copies, waits for them, and re-layouts  14.5 us
    ppermute x1, waiting for transfers between devices, gather_captions(): far = lax.ppermute(caps, 'dp', [(i, i ^ 16) for i in range(32)])  11.8 us
    ppermute x4, starting transfers between devices, exchange(): lax.ppermute(west[i:i + 1], 'space', moved(3, dy))  10.9 us
    ppermute x2, starting transfers between devices, exchange(): lax.ppermute(jnp.stack([block(2, 0)[1], block(2, 1)[1]]), 'space', moved(...  9.77 us
    all_to_all x1, blocking collectives, reduce_gradient(): lax.all_to_all(parts, 'space', split_axis=0, concat_axis=0, tiled=True)  9.43 us
  transfers between devices with their start and end apart: 31, of which 15 were waited for; matrix products, arithmetic and copies ran while one was open for 6% of the time, Pallas kernels for 4%

profile of v2, /device:TPU:32, one launch (start us, length us, event | category | flops | bytes accessed | tf_op | source)
XLA Modules:
  0.0 208.0 jit_solution(9455991124538753941)
XLA Ops:
  3.0 2.8 %collective-permute-start.7 = (bf16[2,32,4992]{2,1,0:T(8,128)(2,1)}, bf16[2,32,4992]{2,1,0:T(8,128)(2,1)}, u32[]{:S(2)}, u32[]{:S(2)}) collective-permute-start(bf16[2,32,4992]{2,1,0:T(8,128)(2,1)} %pad_maximum_fusion.1), channel_id=1, source_target_pairs={{0,6},{1,7},{2,0},{3,1},{4,2},{5,3},{6,4},{7,5},{8,14},{9,15},{10,... | collective-permute-start | bytes 1916936 | tf_op jit(solution)/shard_map/ppermute | solution.py:43
  6.6 3.8 %dynamic-slice_bitcast_fusion = (bf16[2,32,4992]{2,1,0:T(8,128)(2,1)}, bf16[2,32,4992]{2,1,0:T(8,128)(2,1)}, bf16[2,32,4992]{2,1,0:T(8,128)(2,1)}, bf16[2,32,499...) fusion(bf16[1,16,32,4992]{3,2,1,0:T(8,128)(2,1)} %param.6, s32[]{:T(128)S(6)} %mul.52, ...), kind=kLoop, calls=%fused_computation.2 | loop fusion | bytes 7667736 | tf_op jit(solution)/shard_map/dynamic_slice | solution.py:370
  12.0 3.2 %collective-permute-start.1 = (bf16[2,32,4992]{2,1,0:T(8,128)(2,1)}, bf16[2,32,4992]{2,1,0:T(8,128)(2,1)S(1)}, u32[]{:S(2)}, u32[]{:S(2)}) collective-permute-start(bf16[2,32,4992]{2,1,0:T(8,128)(2,1)} %get-tuple-element.61), channel_id=1, source_target_pairs={{0,6},{1,7},{2,0},{3,1},{4,2},{5,3},{6,4},{7,5},{8,14},{9,15},{10,... | collective-permute-start | bytes 1916936 | tf_op jit(solution)/shard_map/ppermute | solution.py:47
  15.9 3.0 %collective-permute-start.22 = (bf16[80,512]{1,0:T(8,128)(2,1)S(1)}, bf16[80,512]{1,0:T(8,128)(2,1)S(1)}, u32[]{:S(2)}, u32[]{:S(2)}) collective-permute-start(bf16[80,512]{1,0:T(8,128)(2,1)S(1)} %concatenate.3), channel_id=1, source_target_pairs={{0,128},{8,136},{16,144},{24,152},{32,160},{40,168},{48,176},{56,1... | collective-permute-start | bytes 245768 | tf_op jit(solution)/shard_map/ppermute | solution.py:148
  18.9 11.8 %collective-permute-done.22 = bf16[80,512]{1,0:T(8,128)(2,1)S(1)} collective-permute-done((bf16[80,512]{1,0:T(8,128)(2,1)S(1)}, bf16[80,512]{1,0:T(8,128)(2,1)S(1)}, u32[]{:S(2)}, u32[]{:S(2)}) %collective-permute-start.22) | collective-permute-done | bytes 81952 | tf_op jit(solution)/shard_map/ppermute | solution.py:148
  32.4 8.6 %all-to-all-start = ((bf16[8,2,80,512]{3,2,1,0:T(8,128)(2,1)}), bf16[8,2,80,512]{3,2,1,0:T(8,128)(2,1)S(1)}, u32[]{:S(2)}, u32[]{:S(2)}) async-start(bf16[8,2,80,512]{3,2,1,0:T(8,128)(2,1)} %broadcast_in_dim.7), calls=%async_computation | async-start | bytes 2621440 | tf_op jit(solution)/shard_map/all_to_all | solution.py:151
  41.0 2.3 %collective-permute-start.3 = (bf16[2,32,4992]{2,1,0:T(8,128)(2,1)}, bf16[2,32,4992]{2,1,0:T(8,128)(2,1)S(1)}, u32[]{:S(2)}, u32[]{:S(2)}) collective-permute-start(bf16[2,32,4992]{2,1,0:T(8,128)(2,1)} %get-tuple-element.59), channel_id=1, source_target_pairs={{0,7},{1,6},{2,1},{3,0},{4,3},{5,2},{6,5},{7,4},{8,15},{9,14},{10,... | collective-permute-start | bytes 1916936 | tf_op jit(solution)/shard_map/ppermute | solution.py:47
  43.3 2.0 fusion
  45.9 1.9 fusion.1
  47.8 3.5 %collective-permute-start.10 = (bf16[1,32,4992]{2,1,0:T(8,128)(2,1)}, bf16[1,32,4992]{2,1,0:T(8,128)(2,1)S(1)}, u32[]{:S(2)}, u32[]{:S(2)}) collective-permute-start(bf16[1,32,4992]{2,1,0:T(8,128)(2,1)} %get-tuple-element.64), channel_id=1, source_target_pairs={{0,7},{1,6},{2,1},{3,0},{4,3},{5,2},{6,5},{7,4},{8,15},{9,14},{10,... | collective-permute-start | bytes 958472 | tf_op jit(solution)/shard_map/ppermute | solution.py:52
  51.4 3.2 %collective-permute-start.8 = (bf16[1,32,4992]{2,1,0:T(8,128)(2,1)}, bf16[1,32,4992]{2,1,0:T(8,128)(2,1)}, u32[]{:S(2)}, u32[]{:S(2)}) collective-permute-start(bf16[1,32,4992]{2,1,0:T(8,128)(2,1)} %get-tuple-element.65), channel_id=1, source_target_pairs={{0,6},{1,7},{2,0},{3,1},{4,2},{5,3},{6,4},{7,5},{8,14},{9,15},{10,... | collective-permute-start | bytes 958472 | tf_op jit(solution)/shard_map/ppermute | solution.py:52
  54.6 19.4 %collective-permute-done.3.refs_4_ = bf16[2,32,4992]{2,1,0:T(8,128)(2,1)S(1)} collective-permute-done((bf16[2,32,4992]{2,1,0:T(8,128)(2,1)}, bf16[2,32,4992]{2,1,0:T(8,128)(2,1)S(1)}, u32[]{:S(2)}, u32[]{:S(2)}) %collective-permute-start.3) | collective-permute-done | bytes 639008 | tf_op jit(solution)/shard_map/ppermute | solution.py:47
  75.7 2.0 copy-done.1
  77.7 3.1 %time_weights.1.refs_10_ = bf16[26,256,256]{2,1,0:T(8,128)(2,1)S(1)} custom-call(bf16[16,32,3328]{2,1,0:T(8,128)(2,1)S(1)} %bitcast.35), custom_call_target="tpu_custom_call" | custom-call | flops 436207616 | bytes 7000000 | tf_op jit(solution)/shard_map/time_weights/pallas_call | solution.py:123
  84.3 4.1 %spatial_attention.1 = (bf16[2,32,1664]{2,1,0:T(8,128)(2,1)S(1)}, bf16[2,32,1664]{2,1,0:T(8,128)(2,1)S(1)}, bf16[2,32,1664]{2,1,0:T(8,128)(2,1)S(1)}, bf16[2,32,...) custom-call(bf16[2,32,4992]{2,1,0:T(8,128)(2,1)S(1)} %get-tuple-elem, ...), custom_call_target="tpu_custom_call" | custom-call | flops 872415232 | bytes 6815744 | tf_op jit(solution)/shard_map/spatial_attention/pallas_call | solution.py:89
  96.0 7.0 %collective-permute-start.18 = (bf16[2,32,1664]{2,1,0:T(8,128)(2,1)S(1)}, bf16[2,32,1664]{2,1,0:T(8,128)(2,1)S(1)}, u32[]{:S(2)}, u32[]{:S(2)}) collective-permute-start(bf16[2,32,1664]{2,1,0:T(8,128)(2,1)S(1)} %pad_maximum_fusion.3), channel_id=1, source_target_pairs={{0,6},{1,7},{2,0},{3,1},{4,2},{5,3},{6,4},{7,5},{8,14},{9,15},{10,... | collective-permute-start | bytes 638984 | tf_op jit(solution)/shard_map/ppermute | solution.py:43
  105.3 3.1 %collective-permute-start.12 = (bf16[2,32,1664]{2,1,0:T(8,128)(2,1)}, bf16[2,32,1664]{2,1,0:T(8,128)(2,1)S(1)}, u32[]{:S(2)}, u32[]{:S(2)}) collective-permute-start(bf16[2,32,1664]{2,1,0:T(8,128)(2,1)} %copy-done.17), channel_id=1, source_target_pairs={{0,6},{1,7},{2,0},{3,1},{4,2},{5,3},{6,4},{7,5},{8,14},{9,15},{10,... | collective-permute-start | bytes 638984 | tf_op jit(solution)/shard_map/ppermute | solution.py:47
  108.4 4.3 %collective-permute-done.16 = bf16[2,32,1664]{2,1,0:T(8,128)(2,1)S(1)} collective-permute-done((bf16[2,32,1664]{2,1,0:T(8,128)(2,1)S(1)}, bf16[2,32,1664]{2,1,0:T(8,128)(2,1)S(1)}, u32[]{:S(2)}, u32[]{:S(2)}) %collective-permute-start.16) | collective-permute-done | bytes 213024 | tf_op jit(solution)/shard_map/ppermute | solution.py:42
  112.7 2.9 %collective-permute-start.15 = (bf16[2,32,1664]{2,1,0:T(8,128)(2,1)}, bf16[2,32,1664]{2,1,0:T(8,128)(2,1)S(1)}, u32[]{:S(2)}, u32[]{:S(2)}) collective-permute-start(bf16[2,32,1664]{2,1,0:T(8,128)(2,1)} %copy-done.14), channel_id=1, source_target_pairs={{0,3},{1,2},{2,5},{3,4},{4,7},{5,6},{6,1},{7,0},{8,11},{9,10},{10,... | collective-permute-start | bytes 638984 | tf_op jit(solution)/shard_map/ppermute | solution.py:47
  117.8 3.0 %collective-permute-start.21 = (bf16[1,32,1664]{2,1,0:T(8,128)(2,1)S(1)}, bf16[1,32,1664]{2,1,0:T(8,128)(2,1)S(1)}, u32[]{:S(2)}, u32[]{:S(2)}) collective-permute-start(bf16[1,32,1664]{2,1,0:T(8,128)(2,1)S(1)} %get-tuple-element.68), channel_id=1, source_target_pairs={{0,7},{1,6},{2,1},{3,0},{4,3},{5,2},{6,5},{7,4},{8,15},{9,14},{10,... | collective-permute-start | bytes 319496 | tf_op jit(solution)/shard_map/ppermute | solution.py:52
  120.8 4.6 %collective-permute-done.14.refs_4_ = bf16[2,32,1664]{2,1,0:T(8,128)(2,1)S(1)} collective-permute-done((bf16[2,32,1664]{2,1,0:T(8,128)(2,1)}, bf16[2,32,1664]{2,1,0:T(8,128)(2,1)S(1)}, u32[]{:S(2)}, u32[]{:S(2)}) %collective-permute-start.14) | collective-permute-done | bytes 213024 | tf_op jit(solution)/shard_map/ppermute | solution.py:47
  126.5 1.8 collective-permute-done.21.refs_9_
  128.3 3.0 %collective-permute-done.17.refs_6_ = bf16[1,32,1664]{2,1,0:T(8,128)(2,1)S(1)} collective-permute-done((bf16[1,32,1664]{2,1,0:T(8,128)(2,1)S(1)}, bf16[1,32,1664]{2,1,0:T(8,128)(2,1)S(1)}, u32[]{:S(2)}, u32[]{:S(2)}) %collective-permute-start.17) | collective-permute-done | bytes 106528 | tf_op jit(solution)/shard_map/ppermute | solution.py:51
  133.0 8.5 %token_part.1 = (bf16[16,32,512]{2,1,0:T(8,128)(2,1)}, f32[8,2,32,128]{3,2,1,0:T(8,128)}, f32[32,80,512]{2,1,0:T(8,128)}) custom-call(s32[4]{0:T(128)S(1)} %pad_add_fusion.place_ref, bf16[2,32,1664]{2,1,0:T(8,128)(2,1)S(1)} %copy-done.13, bf16[2,32,1664]{2,1,0:T(8,128)(2,1)S(1)} %collective-permute-done.11.refs_1_, ...), custom_call_target="tpu_custom_call" | custom-call | flops 4000000000 | bytes 16000000 | tf_op jit(solution)/shard_map/token_part/pallas_call | solution.py:215
  141.5 3.4 %all-to-all-start.1 = ((f32[8,2,32,128]{3,2,1,0:T(8,128)}), f32[8,2,32,128]{3,2,1,0:T(8,128)S(1)}, u32[]{:S(2)}, u32[]{:S(2)}) async-start(f32[8,2,32,128]{3,2,1,0:T(8,128)} %get-tuple-element.38), calls=%async_computation.1 | async-start | bytes 524288 | tf_op jit(solution)/shard_map/all_to_all | solution.py:388
  146.4 5.3 %all-to-all-done.1.stats_ref = f32[8,2,32,128]{3,2,1,0:T(8,128)S(1)} async-done(((f32[8,2,32,128]{3,2,1,0:T(8,128)}), f32[8,2,32,128]{3,2,1,0:T(8,128)S(1)}, u32[]{:S(2)}, u32[]{:S(2)}) %all-to-all-start.1) | async-done | bytes 262176 | tf_op jit(solution)/shard_map/all_to_all | solution.py:388
  151.8 2.5 %copy-done = f32[32,80,512]{2,1,0:T(8,128)S(1)} copy-done((f32[32,80,512]{2,1,0:T(8,128)S(1)}, f32[32,80,512]{2,1,0:T(8,128)}, u32[]{:S(2)}) %copy-start) | copy-done | bytes 5242904
  155.8 3.0 %collective-permute-done.24.got_ref = bf16[16,80,512]{2,1,0:T(8,128)(2,1)S(1)} collective-permute-done((bf16[16,80,512]{2,1,0:T(8,128)(2,1)S(1)}, bf16[16,80,512]{2,1,0:T(8,128)(2,1)S(1)}, u32[]{:S(2)}, u32[]{:S(2)}) %collective-permute-start.24) | collective-permute-done | bytes 1310752 | tf_op jit(solution)/shard_map/ppermute | solution.py:337
  161.8 7.7 %collective-permute-done.25.a_got = bf16[8,80,256]{2,1,0:T(8,128)(2,1)S(1)} collective-permute-done((bf16[8,80,256]{2,1,0:T(8,128)(2,1)S(1)}, bf16[8,80,256]{2,1,0:T(8,128)(2,1)S(1)}, u32[]{:S(2)}, u32[]{:S(2)}) %collective-permute-start.25) | collective-permute-done | bytes 327712 | tf_op jit(solution)/shard_map/ppermute | solution.py:342
  172.8 4.9 %collective-permute-done.27.a_got = bf16[8,80,128]{2,1,0:T(8,128)(2,1)S(1)} collective-permute-done((bf16[8,80,128]{2,1,0:T(8,128)(2,1)S(1)}, bf16[8,80,128]{2,1,0:T(8,128)(2,1)S(1)}, u32[]{:S(2)}, u32[]{:S(2)}) %collective-permute-start.27) | collective-permute-done | bytes 163872 | tf_op jit(solution)/shard_map/ppermute | solution.py:348
  178.2 19.5 %all_to_all.20.parts = bf16[16,80,128]{2,1,0:T(8,128)(2,1)S(1)} all-to-all(bf16[16,80,128]{2,1,0:T(8,128)(2,1)S(1)} %third_sum.1), channel_id=1, replica_groups={{0,16,32,48,64,80,96,112,128,144,160,176,192,208,224,240},{8,24,40,56,7..., dimensions={0} | all-to-all | bytes 655360 | tf_op jit(solution)/shard_map/all_to_all | solution.py:353
  197.8 9.4 %all_to_all.21.parts = bf16[8,80,128]{2,1,0:T(8,128)(2,1)S(1)} all-to-all(bf16[8,80,128]{2,1,0:T(8,128)(2,1)S(1)} %fourth_sum.1), channel_id=1, replica_groups=mesh['dp'=32,'space'=8] {'space'}, dimensions={0} | all-to-all | bytes 327680 | tf_op jit(solution)/shard_map/all_to_all | solution.py:358
  (100 shorter events, 37.2 us)
Async XLA Ops:
  3.0 38.0 %collective-permute-start.7 = (bf16[2,32,4992]{2,1,0:T(8,128)(2,1)}, bf16[2,32,4992]{2,1,0:T(8,128)(2,1)}, u32[]{:S(2)}, u32[]{:S(2)}) collective-permute-start(bf16[2,32,4992]{2,1,0:T(8,128)(2,1)} %pad_maximum_fusion.1), channel_id=1, source_target_pairs={{0,6},{1,7},{2,0},{3,1},{4,2},{5,3},{6,4},{7,5},{8,14},{9,15},{10,... | collective-permute-start | bytes 1916936 | tf_op jit(solution)/shard_map/ppermute | solution.py:43
  6.6 38.7 %collective-permute-start.5 = (bf16[2,32,4992]{2,1,0:T(8,128)(2,1)}, bf16[2,32,4992]{2,1,0:T(8,128)(2,1)}, u32[]{:S(2)}, u32[]{:S(2)}) collective-permute-start(bf16[2,32,4992]{2,1,0:T(8,128)(2,1)} %pad_maximum_fusion), channel_id=1, source_target_pairs={{0,2},{1,3},{2,4},{3,5},{4,6},{5,7},{6,0},{7,1},{8,10},{9,11},{10,... | collective-permute-start | bytes 1916936 | tf_op jit(solution)/shard_map/ppermute | solution.py:42
  10.4 37.4 %collective-permute-start = (bf16[2,32,4992]{2,1,0:T(8,128)(2,1)}, bf16[2,32,4992]{2,1,0:T(8,128)(2,1)S(1)}, u32[]{:S(2)}, u32[]{:S(2)}) collective-permute-start(bf16[2,32,4992]{2,1,0:T(8,128)(2,1)} %get-tuple-element.62), channel_id=1, source_target_pairs={{0,1},{1,0},{2,3},{3,2},{4,5},{5,4},{6,7},{7,6},{8,9},{9,8},{10,11... | collective-permute-start | bytes 1916936 | tf_op jit(solution)/shard_map/ppermute | solution.py:47
  12.0 39.4 %collective-permute-start.1 = (bf16[2,32,4992]{2,1,0:T(8,128)(2,1)}, bf16[2,32,4992]{2,1,0:T(8,128)(2,1)S(1)}, u32[]{:S(2)}, u32[]{:S(2)}) collective-permute-start(bf16[2,32,4992]{2,1,0:T(8,128)(2,1)} %get-tuple-element.61), channel_id=1, source_target_pairs={{0,6},{1,7},{2,0},{3,1},{4,2},{5,3},{6,4},{7,5},{8,14},{9,15},{10,... | collective-permute-start | bytes 1916936 | tf_op jit(solution)/shard_map/ppermute | solution.py:47
  15.9 14.8 %collective-permute-start.22 = (bf16[80,512]{1,0:T(8,128)(2,1)S(1)}, bf16[80,512]{1,0:T(8,128)(2,1)S(1)}, u32[]{:S(2)}, u32[]{:S(2)}) collective-permute-start(bf16[80,512]{1,0:T(8,128)(2,1)S(1)} %concatenate.3), channel_id=1, source_target_pairs={{0,128},{8,136},{16,144},{24,152},{32,160},{40,168},{48,176},{56,1... | collective-permute-start | bytes 245768 | tf_op jit(solution)/shard_map/ppermute | solution.py:148
  30.7 20.7 %collective-permute-start.2 = (bf16[2,32,4992]{2,1,0:T(8,128)(2,1)}, bf16[2,32,4992]{2,1,0:T(8,128)(2,1)}, u32[]{:S(2)}, u32[]{:S(2)}) collective-permute-start(bf16[2,32,4992]{2,1,0:T(8,128)(2,1)} %get-tuple-element.60), channel_id=1, source_target_pairs={{0,2},{1,3},{2,4},{3,5},{4,6},{5,7},{6,0},{7,1},{8,10},{9,11},{10,... | collective-permute-start | bytes 1916936 | tf_op jit(solution)/shard_map/ppermute | solution.py:47
  32.4 62.6 %all-to-all-start = ((bf16[8,2,80,512]{3,2,1,0:T(8,128)(2,1)}), bf16[8,2,80,512]{3,2,1,0:T(8,128)(2,1)S(1)}, u32[]{:S(2)}, u32[]{:S(2)}) async-start(bf16[8,2,80,512]{3,2,1,0:T(8,128)(2,1)} %broadcast_in_dim.7), calls=%async_computation | async-start | bytes 2621440 | tf_op jit(solution)/shard_map/all_to_all | solution.py:151
  41.0 33.1 %collective-permute-start.3 = (bf16[2,32,4992]{2,1,0:T(8,128)(2,1)}, bf16[2,32,4992]{2,1,0:T(8,128)(2,1)S(1)}, u32[]{:S(2)}, u32[]{:S(2)}) collective-permute-start(bf16[2,32,4992]{2,1,0:T(8,128)(2,1)} %get-tuple-element.59), channel_id=1, source_target_pairs={{0,7},{1,6},{2,1},{3,0},{4,3},{5,2},{6,5},{7,4},{8,15},{9,14},{10,... | collective-permute-start | bytes 1916936 | tf_op jit(solution)/shard_map/ppermute | solution.py:47
  45.3 37.2 %collective-permute-start.4 = (bf16[2,32,4992]{2,1,0:T(8,128)(2,1)}, bf16[2,32,4992]{2,1,0:T(8,128)(2,1)}, u32[]{:S(2)}, u32[]{:S(2)}) collective-permute-start(bf16[2,32,4992]{2,1,0:T(8,128)(2,1)} %get-tuple-element.58), channel_id=1, source_target_pairs={{0,3},{1,2},{2,5},{3,4},{4,7},{5,6},{6,1},{7,0},{8,11},{9,10},{10,... | collective-permute-start | bytes 1916936 | tf_op jit(solution)/shard_map/ppermute | solution.py:47
  47.8 34.6 %collective-permute-start.10 = (bf16[1,32,4992]{2,1,0:T(8,128)(2,1)}, bf16[1,32,4992]{2,1,0:T(8,128)(2,1)S(1)}, u32[]{:S(2)}, u32[]{:S(2)}) collective-permute-start(bf16[1,32,4992]{2,1,0:T(8,128)(2,1)} %get-tuple-element.64), channel_id=1, source_target_pairs={{0,7},{1,6},{2,1},{3,0},{4,3},{5,2},{6,5},{7,4},{8,15},{9,14},{10,... | collective-permute-start | bytes 958472 | tf_op jit(solution)/shard_map/ppermute | solution.py:52
  51.4 31.1 %collective-permute-start.6 = (bf16[1,32,4992]{2,1,0:T(8,128)(2,1)}, bf16[1,32,4992]{2,1,0:T(8,128)(2,1)}, u32[]{:S(2)}, u32[]{:S(2)}) collective-permute-start(bf16[1,32,4992]{2,1,0:T(8,128)(2,1)} %get-tuple-element.67), channel_id=1, source_target_pairs={{0,2},{1,3},{2,4},{3,5},{4,6},{5,7},{6,0},{7,1},{8,10},{9,11},{10,... | collective-permute-start | bytes 958472 | tf_op jit(solution)/shard_map/ppermute | solution.py:51
  51.4 31.1 %collective-permute-start.8 = (bf16[1,32,4992]{2,1,0:T(8,128)(2,1)}, bf16[1,32,4992]{2,1,0:T(8,128)(2,1)}, u32[]{:S(2)}, u32[]{:S(2)}) collective-permute-start(bf16[1,32,4992]{2,1,0:T(8,128)(2,1)} %get-tuple-element.65), channel_id=1, source_target_pairs={{0,6},{1,7},{2,0},{3,1},{4,2},{5,3},{6,4},{7,5},{8,14},{9,15},{10,... | collective-permute-start | bytes 958472 | tf_op jit(solution)/shard_map/ppermute | solution.py:52
  74.9 9.4 %collective-permute-start.9 = (bf16[1,32,4992]{2,1,0:T(8,128)(2,1)}, bf16[1,32,4992]{2,1,0:T(8,128)(2,1)}, u32[]{:S(2)}, u32[]{:S(2)}) collective-permute-start(bf16[1,32,4992]{2,1,0:T(8,128)(2,1)} %get-tuple-element.66), channel_id=1, source_target_pairs={{0,3},{1,2},{2,5},{3,4},{4,7},{5,6},{6,1},{7,0},{8,11},{9,10},{10,... | collective-permute-start | bytes 958472 | tf_op jit(solution)/shard_map/ppermute | solution.py:51
  95.0 30.4 %collective-permute-start.23 = (bf16[8,2,80,512]{3,2,1,0:T(8,128)(2,1)S(1)}, bf16[8,2,80,512]{3,2,1,0:T(8,128)(2,1)S(1)}, u32[]{:S(2)}, u32[]{:S(2)}) collective-permute-start(bf16[8,2,80,512]{3,2,1,0:T(8,128)(2,1)S(1)} %all-to-all-done.mine_ref), channel_id=1, source_target_pairs={{0,8},{8,0},{16,24},{24,16},{32,40},{40,32},{48,56},{56,48},{64,72... | collective-permute-start | bytes 3932168 | tf_op jit(solution)/shard_map/ppermute | solution.py:155
  96.0 12.4 %collective-permute-start.18 = (bf16[2,32,1664]{2,1,0:T(8,128)(2,1)S(1)}, bf16[2,32,1664]{2,1,0:T(8,128)(2,1)S(1)}, u32[]{:S(2)}, u32[]{:S(2)}) collective-permute-start(bf16[2,32,1664]{2,1,0:T(8,128)(2,1)S(1)} %pad_maximum_fusion.3), channel_id=1, source_target_pairs={{0,6},{1,7},{2,0},{3,1},{4,2},{5,3},{6,4},{7,5},{8,14},{9,15},{10,... | collective-permute-start | bytes 638984 | tf_op jit(solution)/shard_map/ppermute | solution.py:43
  104.0 8.7 %collective-permute-start.16 = (bf16[2,32,1664]{2,1,0:T(8,128)(2,1)S(1)}, bf16[2,32,1664]{2,1,0:T(8,128)(2,1)S(1)}, u32[]{:S(2)}, u32[]{:S(2)}) collective-permute-start(bf16[2,32,1664]{2,1,0:T(8,128)(2,1)S(1)} %pad_maximum_fusion.2), channel_id=1, source_target_pairs={{0,2},{1,3},{2,4},{3,5},{4,6},{5,7},{6,0},{7,1},{8,10},{9,11},{10,... | collective-permute-start | bytes 638984 | tf_op jit(solution)/shard_map/ppermute | solution.py:42
  104.1 8.6 %collective-permute-start.11 = (bf16[2,32,1664]{2,1,0:T(8,128)(2,1)}, bf16[2,32,1664]{2,1,0:T(8,128)(2,1)S(1)}, u32[]{:S(2)}, u32[]{:S(2)}) collective-permute-start(bf16[2,32,1664]{2,1,0:T(8,128)(2,1)} %copy-done.18), channel_id=1, source_target_pairs={{0,1},{1,0},{2,3},{3,2},{4,5},{5,4},{6,7},{7,6},{8,9},{9,8},{10,11... | collective-permute-start | bytes 638984 | tf_op jit(solution)/shard_map/ppermute | solution.py:47
  105.3 10.4 %collective-permute-start.12 = (bf16[2,32,1664]{2,1,0:T(8,128)(2,1)}, bf16[2,32,1664]{2,1,0:T(8,128)(2,1)S(1)}, u32[]{:S(2)}, u32[]{:S(2)}) collective-permute-start(bf16[2,32,1664]{2,1,0:T(8,128)(2,1)} %copy-done.17), channel_id=1, source_target_pairs={{0,6},{1,7},{2,0},{3,1},{4,2},{5,3},{6,4},{7,5},{8,14},{9,15},{10,... | collective-permute-start | bytes 638984 | tf_op jit(solution)/shard_map/ppermute | solution.py:47
  108.4 9.4 %collective-permute-start.13 = (bf16[2,32,1664]{2,1,0:T(8,128)(2,1)}, bf16[2,32,1664]{2,1,0:T(8,128)(2,1)S(1)}, u32[]{:S(2)}, u32[]{:S(2)}) collective-permute-start(bf16[2,32,1664]{2,1,0:T(8,128)(2,1)} %copy-done.16), channel_id=1, source_target_pairs={{0,2},{1,3},{2,4},{3,5},{4,6},{5,7},{6,0},{7,1},{8,10},{9,11},{10,... | collective-permute-start | bytes 638984 | tf_op jit(solution)/shard_map/ppermute | solution.py:47
  112.7 12.7 %collective-permute-start.14 = (bf16[2,32,1664]{2,1,0:T(8,128)(2,1)}, bf16[2,32,1664]{2,1,0:T(8,128)(2,1)S(1)}, u32[]{:S(2)}, u32[]{:S(2)}) collective-permute-start(bf16[2,32,1664]{2,1,0:T(8,128)(2,1)} %copy-done.15), channel_id=1, source_target_pairs={{0,7},{1,6},{2,1},{3,0},{4,3},{5,2},{6,5},{7,4},{8,15},{9,14},{10,... | collective-permute-start | bytes 638984 | tf_op jit(solution)/shard_map/ppermute | solution.py:47
  112.7 13.8 %collective-permute-start.15 = (bf16[2,32,1664]{2,1,0:T(8,128)(2,1)}, bf16[2,32,1664]{2,1,0:T(8,128)(2,1)S(1)}, u32[]{:S(2)}, u32[]{:S(2)}) collective-permute-start(bf16[2,32,1664]{2,1,0:T(8,128)(2,1)} %copy-done.14), channel_id=1, source_target_pairs={{0,3},{1,2},{2,5},{3,4},{4,7},{5,6},{6,1},{7,0},{8,11},{9,10},{10,... | collective-permute-start | bytes 638984 | tf_op jit(solution)/shard_map/ppermute | solution.py:47
  115.6 17.4 %copy-start.13 = (bf16[2,32,1664]{2,1,0:T(8,128)(2,1)S(1)}, bf16[2,32,1664]{2,1,0:T(8,128)(2,1)}, u32[]{:S(2)}) copy-start(bf16[2,32,1664]{2,1,0:T(8,128)(2,1)} %copy-done.12) | copy-start | bytes 638980
  115.6 10.9 %collective-permute-start.19 = (bf16[1,32,1664]{2,1,0:T(8,128)(2,1)S(1)}, bf16[1,32,1664]{2,1,0:T(8,128)(2,1)S(1)}, u32[]{:S(2)}, u32[]{:S(2)}) collective-permute-start(bf16[1,32,1664]{2,1,0:T(8,128)(2,1)S(1)} %get-tuple-element.69), channel_id=1, source_target_pairs={{0,6},{1,7},{2,0},{3,1},{4,2},{5,3},{6,4},{7,5},{8,14},{9,15},{10,... | collective-permute-start | bytes 319496 | tf_op jit(solution)/shard_map/ppermute | solution.py:52
  117.8 10.5 %collective-permute-start.21 = (bf16[1,32,1664]{2,1,0:T(8,128)(2,1)S(1)}, bf16[1,32,1664]{2,1,0:T(8,128)(2,1)S(1)}, u32[]{:S(2)}, u32[]{:S(2)}) collective-permute-start(bf16[1,32,1664]{2,1,0:T(8,128)(2,1)S(1)} %get-tuple-element.68), channel_id=1, source_target_pairs={{0,7},{1,6},{2,1},{3,0},{4,3},{5,2},{6,5},{7,4},{8,15},{9,14},{10,... | collective-permute-start | bytes 319496 | tf_op jit(solution)/shard_map/ppermute | solution.py:52
  125.4 5.9 %collective-permute-start.17 = (bf16[1,32,1664]{2,1,0:T(8,128)(2,1)S(1)}, bf16[1,32,1664]{2,1,0:T(8,128)(2,1)S(1)}, u32[]{:S(2)}, u32[]{:S(2)}) collective-permute-start(bf16[1,32,1664]{2,1,0:T(8,128)(2,1)S(1)} %get-tuple-element.71), channel_id=1, source_target_pairs={{0,2},{1,3},{2,4},{3,5},{4,6},{5,7},{6,0},{7,1},{8,10},{9,11},{10,... | collective-permute-start | bytes 319496 | tf_op jit(solution)/shard_map/ppermute | solution.py:51
  125.4 7.6 %collective-permute-start.20 = (bf16[1,32,1664]{2,1,0:T(8,128)(2,1)S(1)}, bf16[1,32,1664]{2,1,0:T(8,128)(2,1)S(1)}, u32[]{:S(2)}, u32[]{:S(2)}) collective-permute-start(bf16[1,32,1664]{2,1,0:T(8,128)(2,1)S(1)} %get-tuple-element.70), channel_id=1, source_target_pairs={{0,3},{1,2},{2,5},{3,4},{4,7},{5,6},{6,1},{7,0},{8,11},{9,10},{10,... | collective-permute-start | bytes 319496 | tf_op jit(solution)/shard_map/ppermute | solution.py:51
  141.5 10.3 %all-to-all-start.1 = ((f32[8,2,32,128]{3,2,1,0:T(8,128)}), f32[8,2,32,128]{3,2,1,0:T(8,128)S(1)}, u32[]{:S(2)}, u32[]{:S(2)}) async-start(f32[8,2,32,128]{3,2,1,0:T(8,128)} %get-tuple-element.38), calls=%async_computation.1 | async-start | bytes 524288 | tf_op jit(solution)/shard_map/all_to_all | solution.py:388
  155.8 3.0 %collective-permute-start.24 = (bf16[16,80,512]{2,1,0:T(8,128)(2,1)S(1)}, bf16[16,80,512]{2,1,0:T(8,128)(2,1)S(1)}, u32[]{:S(2)}, u32[]{:S(2)}) collective-permute-start(bf16[16,80,512]{2,1,0:T(8,128)(2,1)S(1)} %get-tuple-element.41), channel_id=1, source_target_pairs={{0,8},{8,0},{16,24},{24,16},{32,40},{40,32},{48,56},{56,48},{64,72... | collective-permute-start | bytes 3932168 | tf_op jit(solution)/shard_map/ppermute | solution.py:337
  159.7 9.8 %collective-permute-start.25 = (bf16[8,80,256]{2,1,0:T(8,128)(2,1)S(1)}, bf16[8,80,256]{2,1,0:T(8,128)(2,1)S(1)}, u32[]{:S(2)}, u32[]{:S(2)}) collective-permute-start(bf16[8,80,256]{2,1,0:T(8,128)(2,1)S(1)} %get-tuple-element.43), channel_id=1, source_target_pairs={{0,2},{1,3},{2,0},{3,1},{4,6},{5,7},{6,4},{7,5},{8,10},{9,11},{10,... | collective-permute-start | bytes 983048 | tf_op jit(solution)/shard_map/ppermute | solution.py:342
  160.1 10.8 %collective-permute-start.26 = (bf16[8,80,256]{2,1,0:T(8,128)(2,1)S(1)}, bf16[8,80,256]{2,1,0:T(8,128)(2,1)S(1)}, u32[]{:S(2)}, u32[]{:S(2)}) collective-permute-start(bf16[8,80,256]{2,1,0:T(8,128)(2,1)S(1)} %get-tuple-element.45), channel_id=1, source_target_pairs={{0,6},{1,7},{2,4},{3,5},{4,2},{5,3},{6,0},{7,1},{8,14},{9,15},{10,... | collective-permute-start | bytes 983048 | tf_op jit(solution)/shard_map/ppermute | solution.py:343
  171.0 6.6 %collective-permute-start.27 = (bf16[8,80,128]{2,1,0:T(8,128)(2,1)S(1)}, bf16[8,80,128]{2,1,0:T(8,128)(2,1)S(1)}, u32[]{:S(2)}, u32[]{:S(2)}) collective-permute-start(bf16[8,80,128]{2,1,0:T(8,128)(2,1)S(1)} %get-tuple-element.47), channel_id=1, source_target_pairs={{0,6},{1,7},{2,4},{3,5},{4,2},{5,3},{6,0},{7,1},{8,14},{9,15},{10,... | collective-permute-start | bytes 491528 | tf_op jit(solution)/shard_map/ppermute | solution.py:348
  172.8 5.3 %collective-permute-start.28 = (bf16[8,80,128]{2,1,0:T(8,128)(2,1)S(1)}, bf16[8,80,128]{2,1,0:T(8,128)(2,1)S(1)}, u32[]{:S(2)}, u32[]{:S(2)}) collective-permute-start(bf16[8,80,128]{2,1,0:T(8,128)(2,1)S(1)} %get-tuple-element.49), channel_id=1, source_target_pairs={{0,2},{1,3},{2,0},{3,1},{4,6},{5,7},{6,4},{7,5},{8,10},{9,11},{10,... | collective-permute-start | bytes 491528 | tf_op jit(solution)/shard_map/ppermute | solution.py:349
  (19 other events, 59.0 us)

commit v3 on v2

--- a/solution.py
+++ b/solution.py
@@ -39,17 +39,19 @@
 
 
 def exchange(block):
-    east = lax.ppermute(jnp.stack([block(2, 0)[0], block(2, 1)[0]]), "space", moved(1, 0))
-    west = lax.ppermute(jnp.stack([block(2, 0)[1], block(2, 1)[1]]), "space", moved(3, 0))
+    ways = (1, 3)
+    first = {
+        (far, f): lax.ppermute(block(*far)[f : f + 1], "space", moved(ways[f], 0))
+        for far in FAR
+        for f in range(2)
+    }
     got = {}
     for dx, dy in NEAR:
         back = ((4 - dx) % 4, dy)
-        pair = lax.ppermute(block(dx, dy), "space", moved(dx, dy))
-        got[back] = [pair]
-    for i, (dx, dy) in enumerate(FAR):
-        got[(dx, dy)] = [
-            lax.ppermute(east[i : i + 1], "space", moved(1, dy)),
-            lax.ppermute(west[i : i + 1], "space", moved(3, dy)),
+        got[back] = [lax.ppermute(block(dx, dy), "space", moved(dx, dy))]
+    for far in FAR:
+        got[far] = [
+            lax.ppermute(first[(far, f)], "space", moved(ways[f], far[1])) for f in range(2)
         ]
     return got
 
@@ -62,10 +64,11 @@
     return views + [refs[6 + 2 * i + f].at[0] for i in range(2)]
 
 
-def spatial_kernel(*refs):
-    ins, outs = refs[:10], refs[10:]
+def spatial_kernel(place_ref, *refs):
+    ins, out_ref = refs[:10], refs[10]
+    x, y = place_ref[2], place_ref[3]
     for f in range(2):
-        src, dst = frame_view(ins, f), frame_view(outs, f)
+        src = frame_view(ins, f)
 
         def rows(offset):
             return jnp.concatenate([r[:, pl.ds(offset, HD)] for r in src], axis=0)
@@ -80,25 +83,25 @@
             total = jnp.sum(e, axis=-1, keepdims=True)
             o = jnp.dot(e.astype(jnp.bfloat16), v, preferred_element_type=jnp.float32)
             o = (o / total).astype(jnp.bfloat16)
-            for i in range(8):
-                dst[i][:, pl.ds(h * HD, HD)] = o[i * LOCAL : (i + 1) * LOCAL]
-
-
-def spatial_attention(pieces):
-    shapes = [(2, LOCAL, FEATURES)] * 6 + [(1, LOCAL, FEATURES)] * 4
+            for i, (dx, dy) in enumerate(ORDER):
+                at = ((x + dx) & 3) * 2 + (y ^ dy)
+                out_ref[at, f, :, pl.ds(h * HD, HD)] = o[i * LOCAL : (i + 1) * LOCAL]
+
+
+def spatial_attention(place, pieces):
     return pl.pallas_call(
         spatial_kernel,
-        in_specs=[VMEM] * 10,
-        out_specs=[VMEM] * 10,
-        out_shape=[jax.ShapeDtypeStruct(s, jnp.bfloat16) for s in shapes],
-        compiler_params=pltpu.CompilerParams(vmem_limit_bytes=24 * MIB),
+        in_specs=[SMEM] + [VMEM] * 10,
+        out_specs=VMEM,
+        out_shape=jax.ShapeDtypeStruct((8, 2, LOCAL, FEATURES), jnp.bfloat16),
+        compiler_params=pltpu.CompilerParams(vmem_limit_bytes=12 * MIB),
         cost_estimate=pl.CostEstimate(
             flops=8 * HEADS * PATCHES * PATCHES * HD,
             bytes_accessed=2 * PATCHES * 4 * FEATURES * 2,
             transcendentals=2 * HEADS * PATCHES * PATCHES,
         ),
         name="spatial_attention",
-    )(*pieces)
+    )(place, *pieces)
 
 
 def time_kernel(tqk_ref, out_ref):
@@ -125,7 +128,7 @@
         in_specs=[VMEM],
         out_specs=VMEM,
         out_shape=jax.ShapeDtypeStruct((2 * HEADS, rows, rows), jnp.bfloat16),
-        compiler_params=pltpu.CompilerParams(vmem_limit_bytes=24 * MIB),
+        compiler_params=pltpu.CompilerParams(vmem_limit_bytes=12 * MIB),
         cost_estimate=pl.CostEstimate(
             flops=4 * HEADS * rows * rows * HD,
             bytes_accessed=7_000_000,
@@ -136,42 +139,30 @@
 
 
 def gathered_kernel(place_ref, mine_ref, other_ref, out_ref):
-    y_hi, core = place_ref[0], place_ref[1]
-    for z in range(8):
-        for k in range(2):
-            at = (y_hi ^ k) * 16 + z * 2
-            out_ref[at + core] = mine_ref[z, k]
-            out_ref[at + 1 - core] = other_ref[z, k]
+    core = place_ref[1]
+    for m in range(CAPTIONS // 2):
+        out_ref[2 * m + core] = mine_ref[m]
+        out_ref[2 * m + 1 - core] = other_ref[m]
 
 
 def gather_captions(caps, place):
-    far = lax.ppermute(caps, "dp", [(i, i ^ 16) for i in range(32)])
-    pair = jnp.stack([caps, far])
-    groups = [[a * 16 + z * 2 + c for z in range(8)] for a in range(2) for c in range(2)]
-    mine = lax.all_to_all(
-        jnp.broadcast_to(pair[None], (8,) + pair.shape),
-        "dp", split_axis=0, concat_axis=0, axis_index_groups=groups, tiled=True,
-    )
+    groups = [[2 * m + c for m in range(16)] for c in range(2)]
+    mine = lax.all_gather(caps, "dp", axis=0, axis_index_groups=groups)
     other = lax.ppermute(mine, "dp", [(i, i ^ 1) for i in range(32)])
     return pl.pallas_call(
         gathered_kernel,
         in_specs=[SMEM, VMEM, VMEM],
         out_specs=VMEM,
         out_shape=jax.ShapeDtypeStruct((CAPTIONS, PADDED, EMB), jnp.bfloat16),
-        compiler_params=pltpu.CompilerParams(vmem_limit_bytes=16 * MIB),
+        compiler_params=pltpu.CompilerParams(vmem_limit_bytes=10 * MIB),
         cost_estimate=pl.CostEstimate(flops=0, bytes_accessed=5_200_000, transcendentals=0),
         name="gathered",
     )(place, mine, other)
 
 
-def token_kernel(place_ref, *refs):
-    pieces = refs[:10]
-    time_ref, proj_ref, cap_ref, emb_ref, stats_ref, grad_ref, value, comb = refs[10:]
-    x, y = place_ref[2], place_ref[3]
-    for i, (dx, dy) in enumerate(ORDER):
-        at = ((x + dx) & 3) * 4 + (y ^ dy) * 2
-        for f in range(2):
-            value[at + f] = frame_view(pieces, f)[i][...]
+def token_kernel(
+    value, time_ref, proj_ref, cap_ref, emb_ref, stats_ref, grad_ref, comb
+):
     rows = FRAMES * 16
     for g in range(LOCAL // 16):
         part = pl.ds(g * 16, 16)
@@ -211,23 +202,23 @@
         ).reshape(group, PADDED, EMB)
 
 
-def token_part(place, pieces, time, proj_weight, caps):
+def token_part(spatial, time, proj_weight, caps):
     return pl.pallas_call(
         token_kernel,
-        in_specs=[SMEM] + [VMEM] * 13,
+        in_specs=[VMEM] * 4,
         out_specs=[VMEM] * 3,
         out_shape=[
             jax.ShapeDtypeStruct((FRAMES, LOCAL, EMB), jnp.bfloat16),
             jax.ShapeDtypeStruct((8, 2, CAPTIONS, 128), jnp.float32),
             jax.ShapeDtypeStruct((CAPTIONS, PADDED, EMB), jnp.float32),
         ],
-        scratch_shapes=[pltpu.VMEM((FRAMES, LOCAL, FEATURES), jnp.bfloat16)] * 2,
-        compiler_params=pltpu.CompilerParams(vmem_limit_bytes=40 * MIB),
+        scratch_shapes=[pltpu.VMEM((FRAMES, LOCAL, FEATURES), jnp.bfloat16)],
+        compiler_params=pltpu.CompilerParams(vmem_limit_bytes=24 * MIB),
         cost_estimate=pl.CostEstimate(
             flops=4_000_000_000, bytes_accessed=16_000_000, transcendentals=1_300_000
         ),
         name="token_part",
-    )(place, *pieces, time, proj_weight, caps)
+    )(spatial, time, proj_weight, caps)
 
 
 def coef_kernel(place_ref, pos_ref, stats_ref, lens_ref, grad_ref, send_ref, keep_ref, loss_ref, hold):
@@ -378,13 +369,11 @@
     caps = gather_captions(jnp.concatenate([caption_tokens[0], lens_row], axis=0), place)
     time = time_weights(temporal_qk[0])
     pieces = [frames_of(0, 0)] + [piece for key in ORDER[1:] for piece in got[key]]
-    attended = spatial_attention(pieces)
-    sent = dict(zip(ORDER[1:6], attended[1:6]))
-    sent[(2, 0)] = (attended[6][0], attended[7][0])
-    sent[(2, 1)] = (attended[8][0], attended[9][0])
-    got = exchange(lambda dx, dy: sent[(dx, dy)])
-    pieces = [attended[0]] + [piece for key in ORDER[1:] for piece in got[key]]
-    video, stats, grad = token_part(place, pieces, time, proj_weight, caps)
+    attended = spatial_attention(place, pieces)
+    spatial = lax.all_to_all(attended, "space", split_axis=0, concat_axis=0, tiled=True)
+    video, stats, grad = token_part(
+        spatial.reshape(FRAMES, LOCAL, FEATURES), time, proj_weight, caps
+    )
     stats = lax.all_to_all(stats, "space", split_axis=0, concat_axis=0, tiled=True)
     send, keep, loss = coef_part(place, positive, stats, caps[:, SLOTS, :128], grad)
     caption_grad = reduce_gradient(place, send, keep)

time: 209 us -> 214 us (1.024)
  starting transfers between devices: 56.1 us -> 31.3 us
  waiting for transfers between devices: 72.1 us -> 95.7 us
  between operations: 2.17 us -> 15.5 us
  local copies, waits for them, and re-layouts: 25.7 us -> 19.7 us
  other arithmetic: 3.9 us -> 0.08 us
  blocking collectives: 29 us -> 32.4 us
    ppermute x23 -> x13, starting transfers between devices: 40.3 us -> 19.1 us  [the longest x5 9.77 us: exchange(): got[back] = [lax.ppermute(block(dx, dy), 'space', moved(dx, dy))]]
    all_gather x0 -> x1, waiting for transfers between devices: none -> 13.7 us  [gather_captions(): mine = lax.all_gather(caps, 'dp', axis=0, axis_index_groups=groups)]
    ppermute x23 -> x13, waiting for transfers between devices: 49.3 us -> 56.8 us  [the longest x5 26.3 us: exchange(): got[back] = [lax.ppermute(block(dx, dy), 'space', moved(dx, dy))]]
    slice x5 -> x1, local copies, waits for them, and re-layouts: 5.31 us -> 1.36 us  [exchange(): block(*far)[f:f + 1]]
    another operation x5 -> x0, other arithmetic: 3.82 us -> none  [the longest x2 1.93 us: exchange(): jnp.stack([block(2, 0)[1], block(2, 1)[1]])]
    all_to_all x1, blocking collectives: 19.5 us -> 23 us  [reduce_gradient(): lax.all_to_all(parts, 'dp', split_axis=0, concat_axis=0, tiled=True, axis...]
    all_to_all x1, starting transfers between devices: 8.57 us -> 5.25 us  [on_device(): lax.all_to_all(attended, 'space', split_axis=0, concat_axis=0, tiled=True)]
    unnamed x42 -> x24, local copies, waits for them, and re-layouts: 14.5 us -> 12.8 us
  transfers between devices with their start and end apart: 31 -> 22, of which waited for: 15 -> 16; matrix products, arithmetic and copies ran while one was open for 6% -> 3% of each run, Pallas kernels for 4% -> 4%
where the time goes in v3:
time: 214 us; the launch traced here: 213 us
  waiting for transfers between devices  95.7 us (45%)
  blocking collectives  32.4 us (15%)
  starting transfers between devices  31.3 us (15%)
  local copies, waits for them, and re-layouts  19.7 us (9%)
  Pallas kernels  18.4 us (9%)
  between operations  15.5 us (7%)
    ppermute x5, waiting for transfers between devices, exchange(): got[back] = [lax.ppermute(block(dx, dy), 'space', moved(dx, dy))]  26.3 us
    all_to_all x1, blocking collectives, reduce_gradient(): lax.all_to_all(parts, 'dp', split_axis=0, concat_axis=0, tiled=True, axis...  23 us
    ppermute x4, waiting for transfers between devices, exchange(): lax.ppermute(block(*far)[f:f + 1], 'space', moved(ways[f], 0))  17.1 us
    all_gather x1, waiting for transfers between devices, gather_captions(): mine = lax.all_gather(caps, 'dp', axis=0, axis_index_groups=groups)  13.7 us
    ppermute x4, waiting for transfers between devices, exchange(): lax.ppermute(first[far, f], 'space', moved(ways[f], far[1]))  13.5 us
    unnamed x24, local copies, waits for them, and re-layouts  12.8 us
    ppermute x5, starting transfers between devices, exchange(): got[back] = [lax.ppermute(block(dx, dy), 'space', moved(dx, dy))]  9.77 us
    all_to_all x1, blocking collectives, reduce_gradient(): lax.all_to_all(parts, 'space', split_axis=0, concat_axis=0, tiled=True)  9.43 us
  transfers between devices with their start and end apart: 22, of which 16 were waited for; matrix products, arithmetic and copies ran while one was open for 3% of the time, Pallas kernels for 4%

profile of v3, /device:TPU:32, one launch (start us, length us, event | category | flops | bytes accessed | tf_op | source)
XLA Modules:
  0.0 213.1 jit_solution(10466655504582022458)
XLA Ops:
  10.8 1.6 collective-permute-start.9
  12.4 1.7 collective-permute-start.11
  14.4 3.2 %dynamic-slice_bitcast_fusion = (bf16[2,32,4992]{2,1,0:T(8,128)(2,1)}, bf16[2,32,4992]{2,1,0:T(8,128)(2,1)S(1)}, bf16[2,32,4992]{2,1,0:T(8,128)(2,1)S(1)}, bf16[...) fusion(bf16[1,16,32,4992]{3,2,1,0:T(8,128)(2,1)} %param.6, ...), kind=kLoop, calls=%fused_computation | loop fusion | bytes 7667736 | tf_op jit(solution)/shard_map/dynamic_slice | solution.py:361
  17.5 1.6 collective-permute-start
  19.1 3.0 %collective-permute-start.1 = (bf16[2,32,4992]{2,1,0:T(8,128)(2,1)S(1)}, bf16[2,32,4992]{2,1,0:T(8,128)(2,1)S(1)}, u32[]{:S(2)}, u32[]{:S(2)}) collective-permute-start(bf16[2,32,4992]{2,1,0:T(8,128)(2,1)S(1)} %get-tuple-element.41), channel_id=1, source_target_pairs={{0,6},{1,7},{2,0},{3,1},{4,2},{5,3},{6,4},{7,5},{8,14},{9,15},{10,... | collective-permute-start | bytes 1916936 | tf_op jit(solution)/shard_map/ppermute | solution.py:51
  24.5 4.9 %collective-permute-done.5 = bf16[1,32,4992]{2,1,0:T(8,128)(2,1)} collective-permute-done((bf16[1,32,4992]{2,1,0:T(8,128)(2,1)S(1)}, bf16[1,32,4992]{2,1,0:T(8,128)(2,1)}, u32[]{:S(2)}, u32[]{:S(2)}) %collective-permute-start.5) | collective-permute-done | bytes 319520 | tf_op jit(solution)/shard_map/ppermute | solution.py:44
  29.4 2.6 %collective-permute-start.3 = (bf16[2,32,4992]{2,1,0:T(8,128)(2,1)S(1)}, bf16[2,32,4992]{2,1,0:T(8,128)(2,1)S(1)}, u32[]{:S(2)}, u32[]{:S(2)}) collective-permute-start(bf16[2,32,4992]{2,1,0:T(8,128)(2,1)S(1)} %get-tuple-element.39), channel_id=1, source_target_pairs={{0,7},{1,6},{2,1},{3,0},{4,3},{5,2},{6,5},{7,4},{8,15},{9,14},{10,... | collective-permute-start | bytes 1916936 | tf_op jit(solution)/shard_map/ppermute | solution.py:51
  32.0 11.8 %collective-permute-done.7 = bf16[1,32,4992]{2,1,0:T(8,128)(2,1)} collective-permute-done((bf16[1,32,4992]{2,1,0:T(8,128)(2,1)S(1)}, bf16[1,32,4992]{2,1,0:T(8,128)(2,1)}, u32[]{:S(2)}, u32[]{:S(2)}) %collective-permute-start.7) | collective-permute-done | bytes 319520 | tf_op jit(solution)/shard_map/ppermute | solution.py:44
  43.8 2.2 %collective-permute-start.4 = (bf16[2,32,4992]{2,1,0:T(8,128)(2,1)}, bf16[2,32,4992]{2,1,0:T(8,128)(2,1)}, u32[]{:S(2)}, u32[]{:S(2)}) collective-permute-start(bf16[2,32,4992]{2,1,0:T(8,128)(2,1)} %get-tuple-element.38), channel_id=1, source_target_pairs={{0,3},{1,2},{2,5},{3,4},{4,7},{5,6},{6,1},{7,0},{8,11},{9,10},{10,... | collective-permute-start | bytes 1916936 | tf_op jit(solution)/shard_map/ppermute | solution.py:51
  47.0 3.1 %collective-permute-start.12 = (bf16[1,32,4992]{2,1,0:T(8,128)(2,1)}, bf16[1,32,4992]{2,1,0:T(8,128)(2,1)}, u32[]{:S(2)}, u32[]{:S(2)}) collective-permute-start(bf16[1,32,4992]{2,1,0:T(8,128)(2,1)} %collective-permute-done.11), channel_id=1, source_target_pairs={{0,7},{1,6},{2,1},{3,0},{4,3},{5,2},{6,5},{7,4},{8,15},{9,14},{10,... | collective-permute-start | bytes 958472 | tf_op jit(solution)/shard_map/ppermute | solution.py:54
  50.1 26.3 %collective-permute-done.3.refs_4_ = bf16[2,32,4992]{2,1,0:T(8,128)(2,1)S(1)} collective-permute-done((bf16[2,32,4992]{2,1,0:T(8,128)(2,1)S(1)}, bf16[2,32,4992]{2,1,0:T(8,128)(2,1)S(1)}, u32[]{:S(2)}, u32[]{:S(2)}) %collective-permute-start.3) | collective-permute-done | bytes 639008 | tf_op jit(solution)/shard_map/ppermute | solution.py:51
  76.5 7.3 %collective-permute-done.10.refs_8_ = bf16[1,32,4992]{2,1,0:T(8,128)(2,1)S(1)} collective-permute-done((bf16[1,32,4992]{2,1,0:T(8,128)(2,1)}, bf16[1,32,4992]{2,1,0:T(8,128)(2,1)S(1)}, u32[]{:S(2)}, u32[]{:S(2)}) %collective-permute-start.10) | collective-permute-done | bytes 319520 | tf_op jit(solution)/shard_map/ppermute | solution.py:54
  83.7 1.9 collective-permute-done.12.refs_9_
  85.6 2.5 %collective-permute-done.6.refs_6_ = bf16[1,32,4992]{2,1,0:T(8,128)(2,1)} collective-permute-done((bf16[1,32,4992]{2,1,0:T(8,128)(2,1)}, bf16[1,32,4992]{2,1,0:T(8,128)(2,1)}, u32[]{:S(2)}, u32[]{:S(2)}) %collective-permute-start.6) | collective-permute-done | bytes 319520 | tf_op jit(solution)/shard_map/ppermute | solution.py:54
  88.1 1.8 collective-permute-done.8.refs_7_
  89.9 5.1 %spatial_attention.1 = bf16[8,2,32,1664]{3,2,1,0:T(8,128)(2,1)} custom-call(s32[4]{0:T(128)S(1)} %pad_add_fusion.place_ref, bf16[2,32,4992]{2,1,0:T(8,128)(2,1)S(1)} %get-tuple-element.43.refs_0_, bf16[2,32,4992]{2,1,0:T(8,128)(2,1)S(1)} %collective-permute-done.refs_1_, bf16[2,32,4992]{2,1,0:T(8,128)(2,1)S(1)} %collective-permute-done.1.refs_2_, ...), custom_call_target="tpu_custom_call" | custom-call | flops 872415232 | bytes 6815744 | tf_op jit(solution)/shard_map/spatial_attention/pallas_call | solution.py:92
  95.0 5.3 %all-to-all-start = ((bf16[8,2,32,1664]{3,2,1,0:T(8,128)(2,1)}), bf16[8,2,32,1664]{3,2,1,0:T(8,128)(2,1)}, u32[]{:S(2)}, u32[]{:S(2)}) async-start(bf16[8,2,32,1664]{3,2,1,0:T(8,128)(2,1)} %spatial_attention.1), calls=%async_computation | async-start | bytes 3407872 | tf_op jit(solution)/shard_map/all_to_all | solution.py:373
  100.3 13.7 %all-gather.3.cloned.1.call-done = bf16[1280,512]{1,0:T(8,128)(2,1)} async-done(((bf16[80,512]{1,0:T(8,128)(2,1)}), bf16[1280,512]{1,0:T(8,128)(2,1)}) %all-gather.3.cloned.1.call-update) | async-done | bytes 1310736 | tf_op jit(solution)/shard_map/all_gather | solution.py:150
  114.0 3.1 %time_weights.1.time_ref = bf16[26,256,256]{2,1,0:T(8,128)(2,1)S(1)} custom-call(bf16[16,32,3328]{2,1,0:T(8,128)(2,1)S(1)} %bitcast.34), custom_call_target="tpu_custom_call" | custom-call | flops 436207616 | bytes 7000000 | tf_op jit(solution)/shard_map/time_weights/pallas_call | solution.py:126
  117.1 1.7 copy-done.3
  121.0 2.1 all-to-all-done
  123.2 1.7 copy-done.6
  126.4 6.8 %token_part.1 = (bf16[16,32,512]{2,1,0:T(8,128)(2,1)}, f32[8,2,32,128]{3,2,1,0:T(8,128)S(1)}, f32[32,80,512]{2,1,0:T(8,128)S(1)}) custom-call(bf16[16,32,1664]{2,1,0:T(8,128)(2,1)} %bitcast.14.value, bf16[26,256,256]{2,1,0:T(8,128)(2,1)S(1)} %copy-done.4, bf16[1664,512]{1,0:T(8,128)(2,1)S(1)} %copy-done.9, bf16[32,80,512]{2,1,0:T(8,128)(2,1)S(1)} %copy-done.6), custom_call_target="tpu_custom_call" | custom-call | flops 4000000000 | bytes 16000000 | tf_op jit(solution)/shard_map/token_part/pallas_call | solution.py:206
  133.2 2.3 %copy-done = f32[32,80,512]{2,1,0:T(8,128)} copy-done((f32[32,80,512]{2,1,0:T(8,128)}, f32[32,80,512]{2,1,0:T(8,128)S(1)}, u32[]{:S(2)}) %copy-start) | copy-done | bytes 5242904
  136.3 3.4 %all-to-all-start.1 = ((f32[8,2,32,128]{3,2,1,0:T(8,128)}), f32[8,2,32,128]{3,2,1,0:T(8,128)S(1)}, u32[]{:S(2)}, u32[]{:S(2)}) async-start(f32[8,2,32,128]{3,2,1,0:T(8,128)} %copy-done.8), calls=%async_computation.1 | async-start | bytes 524288 | tf_op jit(solution)/shard_map/all_to_all | solution.py:377
  141.2 5.4 %all-to-all-done.1.stats_ref = f32[8,2,32,128]{3,2,1,0:T(8,128)S(1)} async-done(((f32[8,2,32,128]{3,2,1,0:T(8,128)}), f32[8,2,32,128]{3,2,1,0:T(8,128)S(1)}, u32[]{:S(2)}, u32[]{:S(2)}) %all-to-all-start.1) | async-done | bytes 262176 | tf_op jit(solution)/shard_map/all_to_all | solution.py:377
  146.7 2.5 %copy-done.1 = f32[32,80,512]{2,1,0:T(8,128)S(1)} copy-done((f32[32,80,512]{2,1,0:T(8,128)S(1)}, f32[32,80,512]{2,1,0:T(8,128)}, u32[]{:S(2)}) %copy-start.1) | copy-done | bytes 5242904
  150.7 3.0 %collective-permute-done.14.got_ref = bf16[16,80,512]{2,1,0:T(8,128)(2,1)S(1)} collective-permute-done((bf16[16,80,512]{2,1,0:T(8,128)(2,1)S(1)}, bf16[16,80,512]{2,1,0:T(8,128)(2,1)S(1)}, u32[]{:S(2)}, u32[]{:S(2)}) %collective-permute-start.14) | collective-permute-done | bytes 1310752 | tf_op jit(solution)/shard_map/ppermute | solution.py:328
  156.6 7.8 %collective-permute-done.15.a_got = bf16[8,80,256]{2,1,0:T(8,128)(2,1)S(1)} collective-permute-done((bf16[8,80,256]{2,1,0:T(8,128)(2,1)S(1)}, bf16[8,80,256]{2,1,0:T(8,128)(2,1)S(1)}, u32[]{:S(2)}, u32[]{:S(2)}) %collective-permute-start.15) | collective-permute-done | bytes 327712 | tf_op jit(solution)/shard_map/ppermute | solution.py:333
  167.6 5.1 %collective-permute-done.17.a_got = bf16[8,80,128]{2,1,0:T(8,128)(2,1)S(1)} collective-permute-done((bf16[8,80,128]{2,1,0:T(8,128)(2,1)S(1)}, bf16[8,80,128]{2,1,0:T(8,128)(2,1)S(1)}, u32[]{:S(2)}, u32[]{:S(2)}) %collective-permute-start.17) | collective-permute-done | bytes 163872 | tf_op jit(solution)/shard_map/ppermute | solution.py:339
  172.9 23.0 %all_to_all.20.parts = bf16[16,80,128]{2,1,0:T(8,128)(2,1)S(1)} all-to-all(bf16[16,80,128]{2,1,0:T(8,128)(2,1)S(1)} %third_sum.1), channel_id=1, replica_groups={{0,16,32,48,64,80,96,112,128,144,160,176,192,208,224,240},{8,24,40,56,7..., dimensions={0} | all-to-all | bytes 655360 | tf_op jit(solution)/shard_map/all_to_all | solution.py:344
  196.0 9.4 %all_to_all.21.parts = bf16[8,80,128]{2,1,0:T(8,128)(2,1)S(1)} all-to-all(bf16[8,80,128]{2,1,0:T(8,128)(2,1)S(1)} %fourth_sum.1), channel_id=1, replica_groups=mesh['dp'=32,'space'=8] {'space'}, dimensions={0} | all-to-all | bytes 327680 | tf_op jit(solution)/shard_map/all_to_all | solution.py:349
  (54 shorter events, 20.8 us)
Async XLA Ops:
  7.2 106.8 %all-gather.3.cloned.1.call-start = ((), (), s32[]{:S(2)}) async-start(), calls=%async_computation.4 | async-start | bytes 1392640 | tf_op jit(solution)/shard_map/all_gather | solution.py:150
  10.8 11.7 %collective-permute-start.9 = (bf16[1,32,4992]{2,1,0:T(8,128)(2,1)S(1)}, bf16[1,32,4992]{2,1,0:T(8,128)(2,1)S(1)}, u32[]{:S(2)}, u32[]{:S(2)}) collective-permute-start(bf16[1,32,4992]{2,1,0:T(8,128)(2,1)S(1)} %get-tuple-element.35), channel_id=1, source_target_pairs={{0,2},{1,3},{2,4},{3,5},{4,6},{5,7},{6,0},{7,1},{8,10},{9,11},{10,... | collective-permute-start | bytes 958472 | tf_op jit(solution)/shard_map/ppermute | solution.py:44
  12.4 11.7 %collective-permute-start.11 = (bf16[1,32,4992]{2,1,0:T(8,128)(2,1)S(1)}, bf16[1,32,4992]{2,1,0:T(8,128)(2,1)}, u32[]{:S(2)}, u32[]{:S(2)}) collective-permute-start(bf16[1,32,4992]{2,1,0:T(8,128)(2,1)S(1)} %get-tuple-element.34), channel_id=1, source_target_pairs={{0,6},{1,7},{2,0},{3,1},{4,2},{5,3},{6,4},{7,5},{8,14},{9,15},{10,... | collective-permute-start | bytes 958472 | tf_op jit(solution)/shard_map/ppermute | solution.py:44
  14.1 15.3 %collective-permute-start.5 = (bf16[1,32,4992]{2,1,0:T(8,128)(2,1)S(1)}, bf16[1,32,4992]{2,1,0:T(8,128)(2,1)}, u32[]{:S(2)}, u32[]{:S(2)}) collective-permute-start(bf16[1,32,4992]{2,1,0:T(8,128)(2,1)S(1)} %get-tuple-element.36), channel_id=1, source_target_pairs={{0,2},{1,3},{2,4},{3,5},{4,6},{5,7},{6,0},{7,1},{8,10},{9,11},{10,... | collective-permute-start | bytes 958472 | tf_op jit(solution)/shard_map/ppermute | solution.py:44
  17.5 28.4 %collective-permute-start = (bf16[2,32,4992]{2,1,0:T(8,128)(2,1)S(1)}, bf16[2,32,4992]{2,1,0:T(8,128)(2,1)S(1)}, u32[]{:S(2)}, u32[]{:S(2)}) collective-permute-start(bf16[2,32,4992]{2,1,0:T(8,128)(2,1)S(1)} %get-tuple-element.42), channel_id=1, source_target_pairs={{0,1},{1,0},{2,3},{3,2},{4,5},{5,4},{6,7},{7,6},{8,9},{9,8},{10,11... | collective-permute-start | bytes 1916936 | tf_op jit(solution)/shard_map/ppermute | solution.py:51
  19.1 27.9 %collective-permute-start.1 = (bf16[2,32,4992]{2,1,0:T(8,128)(2,1)S(1)}, bf16[2,32,4992]{2,1,0:T(8,128)(2,1)S(1)}, u32[]{:S(2)}, u32[]{:S(2)}) collective-permute-start(bf16[2,32,4992]{2,1,0:T(8,128)(2,1)S(1)} %get-tuple-element.41), channel_id=1, source_target_pairs={{0,6},{1,7},{2,0},{3,1},{4,2},{5,3},{6,4},{7,5},{8,14},{9,15},{10,... | collective-permute-start | bytes 1916936 | tf_op jit(solution)/shard_map/ppermute | solution.py:51
  22.5 1.6 copy-start.10
  22.5 21.3 %collective-permute-start.7 = (bf16[1,32,4992]{2,1,0:T(8,128)(2,1)S(1)}, bf16[1,32,4992]{2,1,0:T(8,128)(2,1)}, u32[]{:S(2)}, u32[]{:S(2)}) collective-permute-start(bf16[1,32,4992]{2,1,0:T(8,128)(2,1)S(1)} %get-tuple-element.37), channel_id=1, source_target_pairs={{0,6},{1,7},{2,0},{3,1},{4,2},{5,3},{6,4},{7,5},{8,14},{9,15},{10,... | collective-permute-start | bytes 958472 | tf_op jit(solution)/shard_map/ppermute | solution.py:44
  24.1 26.1 %collective-permute-start.2 = (bf16[2,32,4992]{2,1,0:T(8,128)(2,1)S(1)}, bf16[2,32,4992]{2,1,0:T(8,128)(2,1)S(1)}, u32[]{:S(2)}, u32[]{:S(2)}) collective-permute-start(bf16[2,32,4992]{2,1,0:T(8,128)(2,1)S(1)} %get-tuple-element.40), channel_id=1, source_target_pairs={{0,2},{1,3},{2,4},{3,5},{4,6},{5,7},{6,0},{7,1},{8,10},{9,11},{10,... | collective-permute-start | bytes 1916936 | tf_op jit(solution)/shard_map/ppermute | solution.py:51
  29.4 46.9 %collective-permute-start.3 = (bf16[2,32,4992]{2,1,0:T(8,128)(2,1)S(1)}, bf16[2,32,4992]{2,1,0:T(8,128)(2,1)S(1)}, u32[]{:S(2)}, u32[]{:S(2)}) collective-permute-start(bf16[2,32,4992]{2,1,0:T(8,128)(2,1)S(1)} %get-tuple-element.39), channel_id=1, source_target_pairs={{0,7},{1,6},{2,1},{3,0},{4,3},{5,2},{6,5},{7,4},{8,15},{9,14},{10,... | collective-permute-start | bytes 1916936 | tf_op jit(solution)/shard_map/ppermute | solution.py:51
  43.8 32.7 %collective-permute-start.4 = (bf16[2,32,4992]{2,1,0:T(8,128)(2,1)}, bf16[2,32,4992]{2,1,0:T(8,128)(2,1)}, u32[]{:S(2)}, u32[]{:S(2)}) collective-permute-start(bf16[2,32,4992]{2,1,0:T(8,128)(2,1)} %get-tuple-element.38), channel_id=1, source_target_pairs={{0,3},{1,2},{2,5},{3,4},{4,7},{5,6},{6,1},{7,0},{8,11},{9,10},{10,... | collective-permute-start | bytes 1916936 | tf_op jit(solution)/shard_map/ppermute | solution.py:51
  46.0 37.8 %collective-permute-start.10 = (bf16[1,32,4992]{2,1,0:T(8,128)(2,1)}, bf16[1,32,4992]{2,1,0:T(8,128)(2,1)S(1)}, u32[]{:S(2)}, u32[]{:S(2)}) collective-permute-start(bf16[1,32,4992]{2,1,0:T(8,128)(2,1)} %copy-done.10), channel_id=1, source_target_pairs={{0,3},{1,2},{2,5},{3,4},{4,7},{5,6},{6,1},{7,0},{8,11},{9,10},{10,... | collective-permute-start | bytes 958472 | tf_op jit(solution)/shard_map/ppermute | solution.py:54
  47.0 38.6 %collective-permute-start.12 = (bf16[1,32,4992]{2,1,0:T(8,128)(2,1)}, bf16[1,32,4992]{2,1,0:T(8,128)(2,1)}, u32[]{:S(2)}, u32[]{:S(2)}) collective-permute-start(bf16[1,32,4992]{2,1,0:T(8,128)(2,1)} %collective-permute-done.11), channel_id=1, source_target_pairs={{0,7},{1,6},{2,1},{3,0},{4,3},{5,2},{6,5},{7,4},{8,15},{9,14},{10,... | collective-permute-start | bytes 958472 | tf_op jit(solution)/shard_map/ppermute | solution.py:54
  50.1 38.0 %collective-permute-start.6 = (bf16[1,32,4992]{2,1,0:T(8,128)(2,1)}, bf16[1,32,4992]{2,1,0:T(8,128)(2,1)}, u32[]{:S(2)}, u32[]{:S(2)}) collective-permute-start(bf16[1,32,4992]{2,1,0:T(8,128)(2,1)} %collective-permute-done.5), channel_id=1, source_target_pairs={{0,2},{1,3},{2,4},{3,5},{4,6},{5,7},{6,0},{7,1},{8,10},{9,11},{10,... | collective-permute-start | bytes 958472 | tf_op jit(solution)/shard_map/ppermute | solution.py:54
  76.4 13.6 %collective-permute-start.8 = (bf16[1,32,4992]{2,1,0:T(8,128)(2,1)}, bf16[1,32,4992]{2,1,0:T(8,128)(2,1)}, u32[]{:S(2)}, u32[]{:S(2)}) collective-permute-start(bf16[1,32,4992]{2,1,0:T(8,128)(2,1)} %collective-permute-done.7), channel_id=1, source_target_pairs={{0,6},{1,7},{2,0},{3,1},{4,2},{5,3},{6,4},{7,5},{8,14},{9,15},{10,... | collective-permute-start | bytes 958472 | tf_op jit(solution)/shard_map/ppermute | solution.py:54
  95.0 19.0 %copy-start.2 = (bf16[1,16,32,3328]{3,2,1,0:T(8,128)(2,1)S(1)}, bf16[1,16,32,3328]{3,2,1,0:T(8,128)(2,1)}, u32[]{:S(2)}) copy-start(bf16[1,16,32,3328]{3,2,1,0:T(8,128)(2,1)} %param.7) | copy-start | bytes 10223620
  95.0 28.1 %all-to-all-start = ((bf16[8,2,32,1664]{3,2,1,0:T(8,128)(2,1)}), bf16[8,2,32,1664]{3,2,1,0:T(8,128)(2,1)}, u32[]{:S(2)}, u32[]{:S(2)}) async-start(bf16[8,2,32,1664]{3,2,1,0:T(8,128)(2,1)} %spatial_attention.1), calls=%async_computation | async-start | bytes 3407872 | tf_op jit(solution)/shard_map/all_to_all | solution.py:373
  114.0 4.8 %collective-permute-start.13 = (bf16[16,80,512]{2,1,0:T(8,128)(2,1)}, bf16[16,80,512]{2,1,0:T(8,128)(2,1)S(1)}, u32[]{:S(2)}, u32[]{:S(2)}) collective-permute-start(bf16[16,80,512]{2,1,0:T(8,128)(2,1)} %bitcast.35), channel_id=1, source_target_pairs={{0,8},{8,0},{16,24},{24,16},{32,40},{40,32},{48,56},{56,48},{64,72... | collective-permute-start | bytes 3932168 | tf_op jit(solution)/shard_map/ppermute | solution.py:151
  114.0 4.8 %copy-start.7 = (bf16[1280,512]{1,0:T(8,128)(2,1)S(1)}, bf16[1280,512]{1,0:T(8,128)(2,1)}, u32[]{:S(2)}) copy-start(bf16[1280,512]{1,0:T(8,128)(2,1)} %all-gather.3.cloned.1.call-done) | copy-start | bytes 3932164
  117.1 1.7 copy-start.3
  118.8 4.4 %copy-start.4 = (bf16[26,256,256]{2,1,0:T(8,128)(2,1)S(1)}, bf16[26,256,256]{2,1,0:T(8,128)(2,1)}, u32[]{:S(2)}) copy-start(bf16[26,256,256]{2,1,0:T(8,128)(2,1)} %copy-done.3) | copy-start | bytes 10223620
  119.5 1.5 copy-start.5
  123.2 1.7 copy-start.6
  124.9 1.5 copy-start.9
  133.2 2.3 %copy-start = (f32[32,80,512]{2,1,0:T(8,128)}, f32[32,80,512]{2,1,0:T(8,128)S(1)}, u32[]{:S(2)}) copy-start(f32[32,80,512]{2,1,0:T(8,128)S(1)} %get-tuple-element.19.grad_ref) | copy-start | bytes 15728644
  136.3 10.4 %all-to-all-start.1 = ((f32[8,2,32,128]{3,2,1,0:T(8,128)}), f32[8,2,32,128]{3,2,1,0:T(8,128)S(1)}, u32[]{:S(2)}, u32[]{:S(2)}) async-start(f32[8,2,32,128]{3,2,1,0:T(8,128)} %copy-done.8), calls=%async_computation.1 | async-start | bytes 524288 | tf_op jit(solution)/shard_map/all_to_all | solution.py:377
  146.7 2.5 %copy-start.1 = (f32[32,80,512]{2,1,0:T(8,128)S(1)}, f32[32,80,512]{2,1,0:T(8,128)}, u32[]{:S(2)}) copy-start(f32[32,80,512]{2,1,0:T(8,128)} %copy-done) | copy-start | bytes 15728644
  150.7 3.0 %collective-permute-start.14 = (bf16[16,80,512]{2,1,0:T(8,128)(2,1)S(1)}, bf16[16,80,512]{2,1,0:T(8,128)(2,1)S(1)}, u32[]{:S(2)}, u32[]{:S(2)}) collective-permute-start(bf16[16,80,512]{2,1,0:T(8,128)(2,1)S(1)} %get-tuple-element.21), channel_id=1, source_target_pairs={{0,8},{8,0},{16,24},{24,16},{32,40},{40,32},{48,56},{56,48},{64,72... | collective-permute-start | bytes 3932168 | tf_op jit(solution)/shard_map/ppermute | solution.py:328
  154.6 9.8 %collective-permute-start.15 = (bf16[8,80,256]{2,1,0:T(8,128)(2,1)S(1)}, bf16[8,80,256]{2,1,0:T(8,128)(2,1)S(1)}, u32[]{:S(2)}, u32[]{:S(2)}) collective-permute-start(bf16[8,80,256]{2,1,0:T(8,128)(2,1)S(1)} %get-tuple-element.23), channel_id=1, source_target_pairs={{0,2},{1,3},{2,0},{3,1},{4,6},{5,7},{6,4},{7,5},{8,10},{9,11},{10,... | collective-permute-start | bytes 983048 | tf_op jit(solution)/shard_map/ppermute | solution.py:333
  155.2 10.7 %collective-permute-start.16 = (bf16[8,80,256]{2,1,0:T(8,128)(2,1)S(1)}, bf16[8,80,256]{2,1,0:T(8,128)(2,1)S(1)}, u32[]{:S(2)}, u32[]{:S(2)}) collective-permute-start(bf16[8,80,256]{2,1,0:T(8,128)(2,1)S(1)} %get-tuple-element.25), channel_id=1, source_target_pairs={{0,6},{1,7},{2,4},{3,5},{4,2},{5,3},{6,0},{7,1},{8,14},{9,15},{10,... | collective-permute-start | bytes 983048 | tf_op jit(solution)/shard_map/ppermute | solution.py:334
  166.0 6.6 %collective-permute-start.17 = (bf16[8,80,128]{2,1,0:T(8,128)(2,1)S(1)}, bf16[8,80,128]{2,1,0:T(8,128)(2,1)S(1)}, u32[]{:S(2)}, u32[]{:S(2)}) collective-permute-start(bf16[8,80,128]{2,1,0:T(8,128)(2,1)S(1)} %get-tuple-element.27), channel_id=1, source_target_pairs={{0,6},{1,7},{2,4},{3,5},{4,2},{5,3},{6,0},{7,1},{8,14},{9,15},{10,... | collective-permute-start | bytes 491528 | tf_op jit(solution)/shard_map/ppermute | solution.py:339
  167.5 5.3 %collective-permute-start.18 = (bf16[8,80,128]{2,1,0:T(8,128)(2,1)S(1)}, bf16[8,80,128]{2,1,0:T(8,128)(2,1)S(1)}, u32[]{:S(2)}, u32[]{:S(2)}) collective-permute-start(bf16[8,80,128]{2,1,0:T(8,128)(2,1)S(1)} %get-tuple-element.29), channel_id=1, source_target_pairs={{0,2},{1,3},{2,0},{3,1},{4,6},{5,7},{6,4},{7,5},{8,10},{9,11},{10,... | collective-permute-start | bytes 491528 | tf_op jit(solution)/shard_map/ppermute | solution.py:340
  (1 other events, 0.8 us)
Sparse Core Ops, SparseCore 0:
  11.2 102.7 all-gather.2

commit v4 on v3

v4 whole, which is shorter than its diff:
```python
import math

import jax
import jax.numpy as jnp
from jax import lax
from jax.experimental import pallas as pl
from jax.experimental.pallas import tpu as pltpu
from jax.sharding import PartitionSpec as P

HEADS = 13
HD = 128
FEATURES = HEADS * HD
EMB = 512
FRAMES = 16
PATCHES = 256
LOCAL = 32
SLOTS = 77
PADDED = 80
CAPTIONS = 32
SHARPNESS = 4.0
LOGIT_SCALE = 10.0
LOG2E = math.log2(math.e)
SCORE_LOG2 = HD ** (-0.5) * LOG2E
SHARP_LOG2 = SHARPNESS * LOG2E
MIB = 1 << 20
VMEM = pl.BlockSpec(memory_space=pltpu.VMEM)
SMEM = pl.BlockSpec(memory_space=pltpu.SMEM)

ANY = pl.BlockSpec(memory_space=pltpu.HBM)


def owner(g1, g0, y):
    return (g1 * 2 + (g0 ^ g1)) * 2 + y


QUADS = [[owner(g1, g0, y) for g0 in range(2) for y in range(2)] for g1 in range(2)]
ACROSS = [(s, s ^ 6) for s in range(8)]


def frame_place(frame):
    if frame < 8:
        quad, g1 = divmod(frame, 2)
        return owner(g1, quad // 2, quad % 2), 0
    g1, quad = divmod(frame - 8, 4)
    return owner(g1, quad // 2, quad % 2), 1


def nt(a, b):
    return lax.dot_general(a, b, (((1,), (1,)), ((), ())), preferred_element_type=jnp.float32)


def quad_exchange(blocks):
    return lax.all_to_all(
        blocks, "space", split_axis=0, concat_axis=0, axis_index_groups=QUADS, tiled=True
    )


def bring_frames(clip, g1):
    across = lax.ppermute(
        lax.dynamic_slice_in_dim(clip, 12 - 4 * g1, 4, allow_negative_indices=False),
        "space", ACROSS,
    )
    quad = quad_exchange(clip[:8].reshape(4, 2, LOCAL, 3 * FEATURES))
    turned = lax.dynamic_index_in_dim(
        quad, 1 - g1, axis=1, keepdims=False, allow_negative_indices=False
    )
    turned = lax.ppermute(turned, "space", ACROSS)
    far = quad_exchange(across)
    mine = lax.dynamic_slice_in_dim(clip, 8 + 4 * g1, 4, allow_negative_indices=False)
    mine, _ = lax.optimization_barrier((mine, across[0, 0, :128]))
    near = quad_exchange(mine)
    return quad, turned, near, far


def spatial_kernel(place_ref, quad_ref, turned_ref, near_ref, far_ref, out_ref, buf, res, sems):
    g1 = place_ref[2] >> 1
    arrivals = (
        (quad_ref.at[:, g1], buf.at[0, pl.ds(0, 4)]),
        (turned_ref, buf.at[0, pl.ds(4, 4)]),
        (near_ref, buf.at[1, pl.ds(0, 4)]),
        (far_ref, buf.at[1, pl.ds(4, 4)]),
    )
    loads = [
        pltpu.make_async_copy(src, dst, sems.at[i]) for i, (src, dst) in enumerate(arrivals)
    ]
    for load in loads:
        load.start()
    stores = [
        pltpu.make_async_copy(res.at[f], out_ref.at[:, f], sems.at[4 + f]) for f in range(2)
    ]
    for f in range(2):
        loads[2 * f].wait()
        loads[2 * f + 1].wait()
        for h in range(HEADS):
            q = buf[f, :, :, pl.ds(h * HD, HD)].reshape(PATCHES, HD)
            k = buf[f, :, :, pl.ds(FEATURES + h * HD, HD)].reshape(PATCHES, HD)
            v = buf[f, :, :, pl.ds(2 * FEATURES + h * HD, HD)].reshape(PATCHES, HD)
            s = nt(q, k)
            m = jnp.max(s, axis=-1, keepdims=True)
            e = jnp.exp2((s - m) * SCORE_LOG2)
            total = jnp.sum(e, axis=-1, keepdims=True)
            o = jnp.dot(e.astype(jnp.bfloat16), v, preferred_element_type=jnp.float32)
            o = (o / total).astype(jnp.bfloat16)
            for i in range(8):
                side = g1 if i < 4 else 1 - g1
                at = owner(side, (i & 3) >> 1, i & 1)
                res[f, at, :, pl.ds(h * HD, HD)] = o[i * LOCAL : (i + 1) * LOCAL]
        stores[f].start()
    for store in stores:
        store.wait()


def spatial_attention(place, pieces):
    return pl.pallas_call(
        spatial_kernel,
        in_specs=[SMEM] + [ANY] * 4,
        out_specs=ANY,
        out_shape=jax.ShapeDtypeStruct((8, 2, LOCAL, FEATURES), jnp.bfloat16),
        scratch_shapes=[
            pltpu.VMEM((2, 8, LOCAL, 3 * FEATURES), jnp.bfloat16),
            pltpu.VMEM((2, 8, LOCAL, FEATURES), jnp.bfloat16),
            pltpu.SemaphoreType.DMA((6,)),
        ],
        compiler_params=pltpu.CompilerParams(vmem_limit_bytes=24 * MIB),
        cost_estimate=pl.CostEstimate(
            flops=8 * HEADS * PATCHES * PATCHES * HD,
            bytes_accessed=2 * PATCHES * 4 * FEATURES * 2,
            transcendentals=2 * HEADS * PATCHES * PATCHES,
        ),
        name="spatial_attention",
    )(place, *pieces)


def time_kernel(tqk_ref, out_ref, tqk, weights, load_sem, sems):
    load = pltpu.make_async_copy(tqk_ref, tqk, load_sem)
    load.start()
    load.wait()
    rows = FRAMES * 16
    r = lax.broadcasted_iota(jnp.int32, (rows, rows), 0)
    c = lax.broadcasted_iota(jnp.int32, (rows, rows), 1)
    bias = jnp.where((r & 15) == (c & 15), 0.0, -1e30).astype(jnp.float32)
    stores = []
    for h in range(HEADS):
        for g in range(LOCAL // 16):
            part = pl.ds(g * 16, 16)
            q = tqk[:, part, pl.ds(h * HD, HD)].reshape(rows, HD)
            k = tqk[:, part, pl.ds(FEATURES + h * HD, HD)].reshape(rows, HD)
            s = nt(q, k) + bias
            m = jnp.max(s, axis=-1, keepdims=True)
            e = jnp.exp2((s - m) * SCORE_LOG2)
            total = jnp.sum(e, axis=-1, keepdims=True)
            weights[h, g] = (e * (1.0 / total)).astype(jnp.bfloat16)
        stores.append(pltpu.make_async_copy(weights.at[h], out_ref.at[h], sems.at[h]))
        stores[-1].start()
    for store in stores:
        store.wait()


def time_weights(temporal_qk):
    rows = FRAMES * 16
    return pl.pallas_call(
        time_kernel,
        in_specs=[ANY],
        out_specs=ANY,
        out_shape=jax.ShapeDtypeStruct((HEADS, 2, rows, rows), jnp.bfloat16),
        scratch_shapes=[
            pltpu.VMEM((FRAMES, LOCAL, 2 * FEATURES), jnp.bfloat16),
            pltpu.VMEM((HEADS, 2, rows, rows), jnp.bfloat16),
            pltpu.SemaphoreType.DMA,
            pltpu.SemaphoreType.DMA((HEADS,)),
        ],
        compiler_params=pltpu.CompilerParams(vmem_limit_bytes=24 * MIB),
        cost_estimate=pl.CostEstimate(
            flops=4 * HEADS * rows * rows * HD,
            bytes_accessed=7_000_000,
            transcendentals=2 * HEADS * rows * rows,
        ),
        name="time_weights",
    )(temporal_qk)


def gathered_kernel(place_ref, mine_ref, other_ref, out_ref, sems):
    y_hi, core, z = place_ref[0], place_ref[1], place_ref[4]
    copies = []
    for m in range(CAPTIONS // 2):
        at = (y_hi ^ (m & 1)) * 16
        flips = (m >> 3 & 1) + (m >> 2 & 1) * 2 + (m >> 1 & 1) * 4
        at = at + (z ^ flips) * 2
        for i, (ref, c) in enumerate(((mine_ref, core), (other_ref, 1 - core))):
            copies.append(
                pltpu.make_async_copy(ref.at[m], out_ref.at[at + c], sems.at[2 * m + i])
            )
            copies[-1].start()
    for copy in copies:
        copy.wait()


def flip(value, bit):
    return lax.ppermute(value, "dp", [(i, i ^ bit) for i in range(32)])


def doubled(value, bit):
    return jnp.concatenate([value, flip(value, bit)], axis=0)


def after(value, *others):
    return lax.optimization_barrier((value,) + others)[0]


def gather_captions(caps, place, first, second, third):
    got = doubled(caps, 16)
    got = doubled(after(got, first), 8)
    got = doubled(after(got, second), 4)
    got = doubled(got, 2)
    got = after(got, third)
    other = flip(got, 1)
    return pl.pallas_call(
        gathered_kernel,
        in_specs=[SMEM, ANY, ANY],
        out_specs=ANY,
        out_shape=jax.ShapeDtypeStruct((CAPTIONS, PADDED, EMB), jnp.bfloat16),
        scratch_shapes=[pltpu.SemaphoreType.DMA((CAPTIONS,))],
        compiler_params=pltpu.CompilerParams(vmem_limit_bytes=4 * MIB),
        cost_estimate=pl.CostEstimate(flops=0, bytes_accessed=5_200_000, transcendentals=0),
        name="gathered",
    )(place, got, other)


SPLIT = 7


def token_kernel(
    value_ref, time_ref, proj_ref, cap_ref, emb_ref, stats_ref, w_ref,
    value, time, proj, caps, comb, video, weights, value_sems, time_sems, sems, w_sems,
):
    cut = pl.ds(0, SPLIT * HD), pl.ds(SPLIT * HD, (HEADS - SPLIT) * HD)
    value_loads = [
        pltpu.make_async_copy(value_ref.at[:, :, :, c], value.at[:, :, :, c], value_sems.at[i])
        for i, c in enumerate(cut)
    ]
    time_loads = [
        pltpu.make_async_copy(time_ref.at[h], time.at[h], time_sems.at[h]) for h in range(HEADS)
    ]
    proj_load = pltpu.make_async_copy(proj_ref, proj, sems.at[0])
    cap_load = pltpu.make_async_copy(cap_ref, caps, sems.at[1])
    value_loads[0].start()
    for h in range(SPLIT):
        time_loads[h].start()
    value_loads[1].start()
    for h in range(SPLIT, HEADS):
        time_loads[h].start()
    proj_load.start()
    cap_load.start()
    rows = FRAMES * 16
    for h in range(HEADS):
        if h in (0, SPLIT):
            value_loads[h // SPLIT].wait()
        time_loads[h].wait()
        cols = pl.ds(h * HD, HD)
        for g in range(LOCAL // 16):
            part = pl.ds(g * 16, 16)
            v = jnp.concatenate(
                [value[at, f, part, cols] for at, f in map(frame_place, range(FRAMES))], axis=0
            )
            o = jnp.dot(time[h, g], v, preferred_element_type=jnp.float32)
            o = (v.astype(jnp.float32) + o).astype(jnp.bfloat16)
            comb[:, part, cols] = o.reshape(FRAMES, 16, HD)
    tokens = FRAMES * LOCAL
    proj_load.wait()
    projected = jnp.dot(
        comb[...].reshape(tokens, FEATURES), proj[...], preferred_element_type=jnp.float32
    )
    scale = lax.rsqrt(jnp.mean(projected * projected, axis=-1, keepdims=True) + 1e-06)
    emb = (projected * scale).astype(jnp.bfloat16)
    video[...] = emb.reshape(FRAMES, LOCAL, EMB)
    emb_store = pltpu.make_async_copy(video, emb_ref, sems.at[2])
    emb_store.start()
    cap_load.wait()

    eye = lax.broadcasted_iota(jnp.int32, (PADDED, 128), 0) == lax.broadcasted_iota(
        jnp.int32, (PADDED, 128), 1
    )
    group = 8
    stores = []
    for j0 in range(0, CAPTIONS, group):
        block = pl.ds(j0, group)
        sim = nt(caps[block].reshape(group * PADDED, EMB), emb)
        top = jnp.max(sim, axis=-1, keepdims=True)
        w = jnp.exp2((sim - top) * SHARP_LOG2)
        total = jnp.sum(w, axis=-1, keepdims=True)
        weights[block] = w.astype(jnp.bfloat16).reshape(group, PADDED, EMB)
        stores.append(
            pltpu.make_async_copy(weights.at[block], w_ref.at[block], w_sems.at[j0 // group])
        )
        stores[-1].start()
        for j in range(group):
            rng = slice(j * PADDED, (j + 1) * PADDED)
            top_row = jnp.sum(jnp.where(eye, top[rng], 0.0), axis=0, keepdims=True)
            total_row = jnp.sum(jnp.where(eye, total[rng], 0.0), axis=0, keepdims=True)
            for k in range(8):
                stats_ref[k, 0, pl.ds(j0 + j, 1), :] = top_row
                stats_ref[k, 1, pl.ds(j0 + j, 1), :] = total_row
    emb_store.wait()
    for store in stores:
        store.wait()


def token_part(spatial, time, proj_weight, caps):
    bf16 = jnp.bfloat16
    return pl.pallas_call(
        token_kernel,
        in_specs=[ANY] * 4,
        out_specs=[ANY, VMEM, ANY],
        out_shape=[
            jax.ShapeDtypeStruct((FRAMES, LOCAL, EMB), bf16),
            jax.ShapeDtypeStruct((8, 2, CAPTIONS, 128), jnp.float32),
            jax.ShapeDtypeStruct((CAPTIONS, PADDED, FRAMES * LOCAL), bf16),
        ],
        scratch_shapes=[
            pltpu.VMEM((8, 2, LOCAL, FEATURES), bf16),
            pltpu.VMEM((HEADS, 2, FRAMES * 16, FRAMES * 16), bf16),
            pltpu.VMEM((FEATURES, EMB), bf16),
            pltpu.VMEM((CAPTIONS, PADDED, EMB), bf16),
            pltpu.VMEM((FRAMES, LOCAL, FEATURES), bf16),
            pltpu.VMEM((FRAMES, LOCAL, EMB), bf16),
            pltpu.VMEM((CAPTIONS, PADDED, FRAMES * LOCAL), bf16),
            pltpu.SemaphoreType.DMA((2,)),
            pltpu.SemaphoreType.DMA((HEADS,)),
            pltpu.SemaphoreType.DMA((3,)),
            pltpu.SemaphoreType.DMA((4,)),
        ],
        compiler_params=pltpu.CompilerParams(vmem_limit_bytes=40 * MIB),
        cost_estimate=pl.CostEstimate(
            flops=2_700_000_000, bytes_accessed=13_000_000, transcendentals=1_300_000
        ),
        name="token_part",
    )(spatial, time, proj_weight, caps)


def product_kernel(w_ref, video_ref, out_ref):
    group = w_ref.shape[0]
    video = video_ref[...].reshape(FRAMES * LOCAL, EMB)
    g = jnp.dot(
        w_ref[...].reshape(group * PADDED, FRAMES * LOCAL), video,
        preferred_element_type=jnp.float32,
    )
    out_ref[...] = g.astype(jnp.bfloat16).reshape(group, PADDED, EMB)


def gradient_product(w, video):
    group = 8
    return pl.pallas_call(
        product_kernel,
        grid=(CAPTIONS // group,),
        in_specs=[
            pl.BlockSpec((group, PADDED, FRAMES * LOCAL), lambda i: (i, 0, 0)),
            pl.BlockSpec((FRAMES, LOCAL, EMB), lambda i: (0, 0, 0)),
        ],
        out_specs=pl.BlockSpec((group, PADDED, EMB), lambda i: (i, 0, 0)),
        out_shape=jax.ShapeDtypeStruct((CAPTIONS, PADDED, EMB), jnp.bfloat16),
        compiler_params=pltpu.CompilerParams(vmem_limit_bytes=16 * MIB),
        cost_estimate=pl.CostEstimate(
            flops=1_340_000_000, bytes_accessed=6_000_000, transcendentals=0
        ),
        name="gradient_product",
    )(w, video)


def coef_kernel(place_ref, pos_ref, stats_ref, lens_ref, grad_ref, send_ref, keep_ref, loss_ref, hold):
    @pl.when(pl.program_id(0) == 0)
    def _():
        tops = stats_ref[:, 0]
        totals = stats_ref[:, 1]
        top = jnp.max(tops, axis=0)
        total = jnp.sum(totals * jnp.exp2((tops - top[None]) * SHARP_LOG2), axis=0)
        soft = top + jnp.log(total) / SHARPNESS
        slot = lax.broadcasted_iota(jnp.int32, (CAPTIONS, 128), 1).astype(jnp.float32)
        lens = lens_ref[...].astype(jnp.float32)
        live = slot < lens
        lens_col = lens[:, :1]
        score = jnp.sum(jnp.where(live, soft, 0.0), axis=-1, keepdims=True) / lens_col
        logits = LOGIT_SCALE * score
        peak = jnp.max(logits, axis=0, keepdims=True)
        log_total = peak + jnp.log(jnp.sum(jnp.exp(logits - peak), axis=0, keepdims=True))
        onehot = lax.broadcasted_iota(jnp.int32, (CAPTIONS, 1), 0) == pos_ref[0]
        loss_ref[...] = log_total - jnp.sum(jnp.where(onehot, logits, 0.0), axis=0, keepdims=True)
        grad_logit = LOGIT_SCALE * (jnp.exp(logits - log_total) - onehot.astype(jnp.float32))
        coef = jnp.where(live, grad_logit / lens_col, 0.0)
        mine = stats_ref[place_ref[2] * 2 + place_ref[3], 0]
        hold[...] = coef * jnp.exp2((mine - soft) * SHARP_LOG2)

    eye = lax.broadcasted_iota(jnp.int32, (PADDED, 128), 0) == lax.broadcasted_iota(
        jnp.int32, (PADDED, 128), 1
    )
    core = place_ref[1]
    half = send_ref.shape[0]
    start = pl.program_id(0) * 2 * half
    for m in range(half):
        for j, ref in ((2 * m + 1 - core, send_ref), (2 * m + core, keep_ref)):
            row = hold[pl.ds(start + j, 1), :]
            col = jnp.sum(jnp.where(eye, row, 0.0), axis=-1, keepdims=True)
            ref[m] = (grad_ref[j].astype(jnp.float32) * col).astype(jnp.bfloat16)


def coef_part(place, pos, stats, lens, grad):
    half = jax.ShapeDtypeStruct((CAPTIONS // 2, PADDED, EMB), jnp.bfloat16)
    steps = 4
    some = CAPTIONS // 2 // steps
    return pl.pallas_call(
        coef_kernel,
        grid=(steps,),
        in_specs=[
            SMEM,
            SMEM,
            pl.BlockSpec((8, 2, CAPTIONS, 128), lambda i: (0, 0, 0, 0)),
            pl.BlockSpec((CAPTIONS, 128), lambda i: (0, 0)),
            pl.BlockSpec((2 * some, PADDED, EMB), lambda i: (i, 0, 0)),
        ],
        out_specs=[
            pl.BlockSpec((some, PADDED, EMB), lambda i: (i, 0, 0)),
            pl.BlockSpec((some, PADDED, EMB), lambda i: (i, 0, 0)),
            pl.BlockSpec((1, 1), lambda i: (0, 0)),
        ],
        out_shape=[half, half, jax.ShapeDtypeStruct((1, 1), jnp.float32)],
        scratch_shapes=[pltpu.VMEM((CAPTIONS, 128), jnp.float32)],
        compiler_params=pltpu.CompilerParams(vmem_limit_bytes=16 * MIB),
        cost_estimate=pl.CostEstimate(
            flops=4_000_000, bytes_accessed=6_000_000, transcendentals=100_000
        ),
        name="coef_part",
    )(place, pos, stats, lens, grad)


def small_call(kernel, name, operands, out_shapes, specs=None):
    return pl.pallas_call(
        kernel,
        in_specs=specs or [VMEM] * len(operands),
        out_specs=[VMEM] * len(out_shapes),
        out_shape=[jax.ShapeDtypeStruct(s, d) for s, d in out_shapes],
        compiler_params=pltpu.CompilerParams(vmem_limit_bytes=16 * MIB),
        cost_estimate=pl.CostEstimate(flops=0, bytes_accessed=2_000_000, transcendentals=0),
        name=name,
    )(*operands)


def added(a, b):
    return (a.astype(jnp.float32) + b.astype(jnp.float32)).astype(jnp.bfloat16)


def first_sum_kernel(place_ref, keep_ref, got_ref, a_keep, a_send, b_keep, b_send):
    x = place_ref[2]
    plan = (
        (0, ((a_keep, 0, 0), (a_send, 0, 1), (a_send, 1, 2), (a_keep, 1, 3))),
        (8, ((b_keep, 0, 0), (b_keep, 1, 1), (b_send, 1, 2), (b_send, 0, 3))),
    )
    for start, parts in plan:
        for ref, at, flip in parts:
            cols = pl.ds(pl.multiple_of((x ^ flip) * 128, 128), 128)
            for m in range(8):
                ref[m, :, pl.ds(at * 128, 128)] = added(
                    keep_ref[start + m, :, cols], got_ref[start + m, :, cols]
                )


def second_sum_kernel(a_keep, a_got, b_keep, b_got, a_mine, a_send, b_mine, b_send):
    for keep, got, mine, send in ((a_keep, a_got, a_mine, a_send), (b_keep, b_got, b_mine, b_send)):
        mine[...] = added(keep[:, :, :128], got[:, :, :128])
        send[...] = added(keep[:, :, 128:], got[:, :, 128:])


def third_sum_kernel(a_mine, a_got, b_mine, b_got, out):
    out[pl.ds(0, 8)] = added(a_mine[...], a_got[...])
    out[pl.ds(8, 8)] = added(b_mine[...], b_got[...])


def fourth_sum_kernel(parts, out):
    total = jnp.sum(parts[...].astype(jnp.float32), axis=0).astype(jnp.bfloat16)
    for k in range(8):
        out[k] = total


def last_sum_kernel(parts, out):
    for x in range(4):
        total = parts[2 * x].astype(jnp.float32) + parts[2 * x + 1].astype(jnp.float32)
        out[0, :, pl.ds(x * 128, 128)] = total[:SLOTS]


def reduce_gradient(place, send, keep):
    bf16 = jnp.bfloat16
    one = [(s, s ^ 2) for s in range(8)]
    three = [(s, s ^ 6) for s in range(8)]
    got = lax.ppermute(send, "dp", [(i, i ^ 1) for i in range(32)])
    a_keep, a_send, b_keep, b_send = small_call(
        first_sum_kernel, "first_sum", (place, keep, got), [((8, PADDED, 256), bf16)] * 4,
        [SMEM, VMEM, VMEM],
    )
    a_got = lax.ppermute(a_send, "space", one)
    b_got = lax.ppermute(b_send, "space", three)
    a_mine, a_send, b_mine, b_send = small_call(
        second_sum_kernel, "second_sum", (a_keep, a_got, b_keep, b_got),
        [((8, PADDED, 128), bf16)] * 4,
    )
    a_got = lax.ppermute(a_send, "space", three)
    b_got = lax.ppermute(b_send, "space", one)
    (parts,) = small_call(
        third_sum_kernel, "third_sum", (a_mine, a_got, b_mine, b_got), [((16, PADDED, 128), bf16)]
    )
    parts = lax.all_to_all(
        parts, "dp", split_axis=0, concat_axis=0, tiled=True,
        axis_index_groups=[[2 * m + c for m in range(16)] for c in range(2)],
    )
    (parts,) = small_call(fourth_sum_kernel, "fourth_sum", (parts,), [((8, PADDED, 128), bf16)])
    parts = lax.all_to_all(parts, "space", split_axis=0, concat_axis=0, tiled=True)
    return small_call(last_sum_kernel, "last_sum", (parts,), [((1, SLOTS, EMB), jnp.float32)])[0]


def on_device(clip_qkv, temporal_qk, proj_weight, caption_tokens, caption_lens, positive):
    dp = lax.axis_index("dp")
    space = lax.axis_index("space")
    x, y = space >> 1, space & 1
    place = jnp.stack([dp >> 4, dp & 1, x, y, (dp >> 1) & 7]).astype(jnp.int32)
    lens_row = jnp.broadcast_to(
        caption_lens.astype(jnp.bfloat16)[:, None, None], (1, PADDED - SLOTS, EMB)
    )
    caps = jnp.concatenate([caption_tokens, lens_row], axis=1)
    pieces = bring_frames(clip_qkv[0], space >> 2)
    time = time_weights(temporal_qk[0])
    attended = spatial_attention(place, pieces)
    caps = gather_captions(
        caps, place, time[0, 0, 0, :128], pieces[0][0, 0, 0, :128], attended[0, 0, 0, :128]
    )
    spatial = lax.all_to_all(attended, "space", split_axis=0, concat_axis=0, tiled=True)
    video, stats, weights = token_part(spatial, time, proj_weight, caps)
    stats = lax.all_to_all(stats, "space", split_axis=0, concat_axis=0, tiled=True)
    grad = gradient_product(weights, video)
    send, keep, loss = coef_part(place, positive, stats, caps[:, SLOTS, :128], grad)
    caption_grad = reduce_gradient(place, send, keep)
    return video[None], caption_grad, loss.reshape(1)


def solution(mesh):
    return jax.shard_map(
        on_device,
        mesh=mesh,
        in_specs=(
            P("dp", None, "space", None),
            P("dp", None, "space", None),
            P(),
            P("dp", None, None),
            P("dp"),
            P("dp"),
        ),
        out_specs=(P("dp", None, "space", None), P("dp", None, None), P("dp")),
        check_vma=False,
    )
```

time: 214 us -> 199 us (0.930)
  waiting for transfers between devices: 95.7 us -> 61 us
  starting transfers between devices: 31.3 us -> 47.5 us
  between operations: 15.5 us -> 2.16 us
  Pallas kernels: 18.4 us -> 29.5 us
  local copies, waits for them, and re-layouts: 19.7 us -> 22.4 us
  other arithmetic: 0.08 us -> 2.41 us
    ppermute x14 -> x7, waiting for transfers between devices: 56.8 us -> 8.88 us  [the longest x5 7.29 us: flip(): return lax.ppermute(value, 'dp', [(i, i ^ bit) for i in range(32)])]
    all_to_all x0 -> x3, waiting for transfers between devices: none -> 28.1 us  [quad_exchange(): lax.all_to_all(blocks, 'space', split_axis=0, concat_axis=0, axis_index_g...]
    all_gather x1 -> x0, waiting for transfers between devices: 13.7 us -> none  [gather_captions(): mine = lax.all_gather(caps, 'dp', axis=0, axis_index_groups=groups)]
    all_to_all x0 -> x3, starting transfers between devices: none -> 12.4 us  [quad_exchange(): lax.all_to_all(blocks, 'space', split_axis=0, concat_axis=0, axis_index_g...]
    pallas_call x5 -> x6, Pallas kernels: 17.3 us -> 28.3 us  [the longest x1 9.21 us: token_part(): pl.pallas_call(token_kernel, in_specs=[ANY] * 4, out_specs=[ANY, VMEM, AN...]
    all_to_all x1, waiting for transfers between devices: 5.44 us -> 0.52 us  [on_device(): lax.all_to_all(stats, 'space', split_axis=0, concat_axis=0, tiled=True)]
    all_to_all x1, waiting for transfers between devices: 2.13 us -> 6.61 us  [on_device(): lax.all_to_all(attended, 'space', split_axis=0, concat_axis=0, tiled=True)]
    concatenate x0 -> x4, other arithmetic: none -> 2.41 us  [doubled(): return jnp.concatenate([value, flip(value, bit)], axis=0)]
  transfers between devices with their start and end apart: 22 -> 17, of which waited for: 16 -> 13; matrix products, arithmetic and copies ran while one was open for 3% -> 4% of each run, Pallas kernels for 4% -> 9%
where the time goes in v4:
time: 199 us; the launch traced here: 198 us
  waiting for transfers between devices  61 us (31%)
  starting transfers between devices  47.5 us (24%)
  blocking collectives  32.7 us (16%)
  Pallas kernels  29.5 us (15%)
  local copies, waits for them, and re-layouts  22.4 us (11%)
  other arithmetic  2.41 us (1%)
  between operations  2.16 us (1%)
    all_to_all x3, waiting for transfers between devices, quad_exchange(): lax.all_to_all(blocks, 'space', split_axis=0, concat_axis=0, axis_index_g...  28.1 us
    all_to_all x1, blocking collectives, reduce_gradient(): lax.all_to_all(parts, 'dp', split_axis=0, concat_axis=0, tiled=True, axis...  23.5 us
    ppermute x5, starting transfers between devices, flip(): return lax.ppermute(value, 'dp', [(i, i ^ bit) for i in range(32)])  15.1 us
    unnamed x30, local copies, waits for them, and re-layouts  13.5 us
    all_to_all x3, starting transfers between devices, quad_exchange(): lax.all_to_all(blocks, 'space', split_axis=0, concat_axis=0, axis_index_g...  12.4 us
    pallas_call x1, Pallas kernels, token_part(): pl.pallas_call(token_kernel, in_specs=[ANY] * 4, out_specs=[ANY, VMEM, AN...  9.21 us
    all_to_all x1, blocking collectives, reduce_gradient(): lax.all_to_all(parts, 'space', split_axis=0, concat_axis=0, tiled=True)  9.15 us
    ppermute x5, waiting for transfers between devices, flip(): return lax.ppermute(value, 'dp', [(i, i ^ bit) for i in range(32)])  7.29 us
  transfers between devices with their start and end apart: 17, of which 13 were waited for; matrix products, arithmetic and copies ran while one was open for 4% of the time, Pallas kernels for 9%

profile of v4, /device:TPU:32, one launch (start us, length us, event | category | flops | bytes accessed | tf_op | source)
XLA Modules:
  0.0 197.7 jit_solution(17638111333660753790)
XLA Ops:
  0.6 3.4 %slice.5 = bf16[1,8,32,4992]{3,2,1,0:T(8,128)(2,1)} slice(bf16[1,16,32,4992]{3,2,1,0:T(8,128)(2,1)} %param.6), slice={[0:1], [0:8], [0:32], [0:4992]} | slice | bytes 5111808 | tf_op jit(solution)/shard_map/slice | solution.py:63
  4.0 3.8 %all-to-all-start = ((bf16[4,2,32,4992]{3,2,1,0:T(8,128)(2,1)}), bf16[4,2,32,4992]{3,2,1,0:T(8,128)(2,1)S(1)}, u32[]{:S(2)}, u32[]{:S(2)}) async-start(bf16[4,2,32,4992]{3,2,1,0:T(8,128)(2,1)} %bitcast.22), calls=%async_computation | async-start | bytes 5111808 | tf_op jit(solution)/shard_map/all_to_all | solution.py:53
  7.8 3.4 %dynamic-slice_bitcast_fusion = (bf16[4,32,4992]{2,1,0:T(8,128)(2,1)}, bf16[4,32,4992]{2,1,0:T(8,128)(2,1)}) fusion(bf16[1,16,32,4992]{3,2,1,0:T(8,128)(2,1)} %param.6, s32[]{:T(128)S(6)} %sub.7, s32[]{:T(128)S(6)} %add_shard_map.3), kind=kLoop, calls=%fused_computation.1 | loop fusion | bytes 5111816 | tf_op jit(solution)/shard_map/dynamic_slice | solution.py:60
  11.2 2.7 %collective-permute-start.1 = (bf16[4,32,4992]{2,1,0:T(8,128)(2,1)}, bf16[4,32,4992]{2,1,0:T(8,128)(2,1)}, u32[]{:S(2)}, u32[]{:S(2)}) collective-permute-start(bf16[4,32,4992]{2,1,0:T(8,128)(2,1)} %get-tuple-element.34), channel_id=1, source_target_pairs={{0,6},{1,7},{2,4},{3,5},{4,2},{5,3},{6,0},{7,1},{8,14},{9,15},{10,... | collective-permute-start | bytes 3833864 | tf_op jit(solution)/shard_map/ppermute | solution.py:59
  14.6 3.3 %collective-permute-start.2 = (bf16[1,80,512]{2,1,0:T(8,128)(2,1)S(1)}, bf16[1,80,512]{2,1,0:T(8,128)(2,1)S(1)}, u32[]{:S(2)}, u32[]{:S(2)}) collective-permute-start(bf16[1,80,512]{2,1,0:T(8,128)(2,1)S(1)} %concatenate.16), channel_id=1, source_target_pairs={{0,128},{8,136},{16,144},{24,152},{32,160},{40,168},{48,176},{56,1... | collective-permute-start | bytes 245768 | tf_op jit(solution)/shard_map/ppermute | solution.py:199
  17.8 20.7 %all-to-all-done.quad_ref = bf16[4,2,32,4992]{3,2,1,0:T(8,128)(2,1)S(1)} async-done(((bf16[4,2,32,4992]{3,2,1,0:T(8,128)(2,1)}), bf16[4,2,32,4992]{3,2,1,0:T(8,128)(2,1)S(1)}, u32[]{:S(2)}, u32[]{:S(2)}) %all-to-all-start) | async-done | bytes 2555936 | tf_op jit(solution)/shard_map/all_to_all | solution.py:53
  38.5 4.3 %all-to-all-start.1 = ((bf16[4,32,4992]{2,1,0:T(8,128)(2,1)}), bf16[4,32,4992]{2,1,0:T(8,128)(2,1)}, u32[]{:S(2)}, u32[]{:S(2)}) async-start(bf16[4,32,4992]{2,1,0:T(8,128)(2,1)} %get-tuple-element.35), calls=%async_computation.1 | async-start | bytes 2555904 | tf_op jit(solution)/shard_map/all_to_all | solution.py:53
  42.9 6.4 %collective-permute-start.3 = (bf16[2,80,512]{2,1,0:T(8,128)(2,1)S(1)}, bf16[2,80,512]{2,1,0:T(8,128)(2,1)S(1)}, u32[]{:S(2)}, u32[]{:S(2)}) collective-permute-start(bf16[2,80,512]{2,1,0:T(8,128)(2,1)S(1)} %pad_maximum_fusion.3), channel_id=1, source_target_pairs={{0,64},{8,72},{16,80},{24,88},{32,96},{40,104},{48,112},{56,120},{... | collective-permute-start | bytes 491528 | tf_op jit(solution)/shard_map/ppermute | solution.py:199
  50.4 2.8 %collective-permute-start = (bf16[4,32,4992]{2,1,0:T(8,128)(2,1)}, bf16[4,32,4992]{2,1,0:T(8,128)(2,1)}, u32[]{:S(2)}, u32[]{:S(2)}) collective-permute-start(bf16[4,32,4992]{2,1,0:T(8,128)(2,1)} %dynamic-slice_bitcast_fusion.2), channel_id=1, source_target_pairs={{0,6},{1,7},{2,4},{3,5},{4,2},{5,3},{6,0},{7,1},{8,14},{9,15},{10,... | collective-permute-start | bytes 3833864 | tf_op jit(solution)/shard_map/ppermute | solution.py:67
  54.5 2.7 %collective-permute-start.4 = (bf16[4,80,512]{2,1,0:T(8,128)(2,1)S(1)}, bf16[4,80,512]{2,1,0:T(8,128)(2,1)S(1)}, u32[]{:S(2)}, u32[]{:S(2)}) collective-permute-start(bf16[4,80,512]{2,1,0:T(8,128)(2,1)S(1)} %pad_maximum_fusion.2), channel_id=1, source_target_pairs={{0,32},{8,40},{16,48},{24,56},{32,0},{40,8},{48,16},{56,24},{64,96... | collective-permute-start | bytes 983048 | tf_op jit(solution)/shard_map/ppermute | solution.py:199
  58.4 4.3 %all-to-all-start.2 = ((bf16[4,32,4992]{2,1,0:T(8,128)(2,1)}), bf16[4,32,4992]{2,1,0:T(8,128)(2,1)}, u32[]{:S(2)}, u32[]{:S(2)}) async-start(bf16[4,32,4992]{2,1,0:T(8,128)(2,1)} %collective-permute-done.1), calls=%async_computation.2 | async-start | bytes 2555904 | tf_op jit(solution)/shard_map/all_to_all | solution.py:53
  62.7 6.0 %collective-permute-done.4 = bf16[4,80,512]{2,1,0:T(8,128)(2,1)S(1)} collective-permute-done((bf16[4,80,512]{2,1,0:T(8,128)(2,1)S(1)}, bf16[4,80,512]{2,1,0:T(8,128)(2,1)S(1)}, u32[]{:S(2)}, u32[]{:S(2)}) %collective-permute-start.4) | collective-permute-done | bytes 327712 | tf_op jit(solution)/shard_map/ppermute | solution.py:199
  69.7 2.5 %collective-permute-start.5 = (bf16[8,80,512]{2,1,0:T(8,128)(2,1)}, bf16[8,80,512]{2,1,0:T(8,128)(2,1)}, u32[]{:S(2)}, u32[]{:S(2)}) collective-permute-start(bf16[8,80,512]{2,1,0:T(8,128)(2,1)} %pad_maximum_fusion.1), channel_id=1, source_target_pairs={{0,16},{8,24},{16,0},{24,8},{32,48},{40,56},{48,32},{56,40},{64,80... | collective-permute-start | bytes 1966088 | tf_op jit(solution)/shard_map/ppermute | solution.py:199
  72.2 6.1 %all-to-all-done.2.far_ref = bf16[4,32,4992]{2,1,0:T(8,128)(2,1)} async-done(((bf16[4,32,4992]{2,1,0:T(8,128)(2,1)}), bf16[4,32,4992]{2,1,0:T(8,128)(2,1)}, u32[]{:S(2)}, u32[]{:S(2)}) %all-to-all-start.2) | async-done | bytes 1277984 | tf_op jit(solution)/shard_map/all_to_all | solution.py:53
  80.0 5.0 %spatial_attention.1 = bf16[8,2,32,1664]{3,2,1,0:T(8,128)(2,1)S(1)} custom-call(s32[5]{0:T(128)S(1)} %stack.23.place_ref, bf16[4,2,32,4992]{3,2,1,0:T(8,128)(2,1)S(1)} %all-to-all-done.quad_ref, bf16[4,32,4992]{2,1,0:T(8,128)(2,1)} %collective-permute-done.turned_ref, bf16[4,32,4992]{2,1,0:T(8,128)(2,1)} %all-to-all-done.1.near_ref, ...), custom_call_target="tpu_custom_call" | custom-call | flops 872415232 | bytes 6815744 | tf_op jit(solution)/shard_map/spatial_attention/pallas_call | solution.py:114
  86.2 5.4 %all-to-all-start.3 = ((bf16[8,2,32,1664]{3,2,1,0:T(8,128)(2,1)}), bf16[8,2,32,1664]{3,2,1,0:T(8,128)(2,1)}, u32[]{:S(2)}, u32[]{:S(2)}) async-start(bf16[8,2,32,1664]{3,2,1,0:T(8,128)(2,1)} %copy-done), calls=%async_computation.3 | async-start | bytes 3407872 | tf_op jit(solution)/shard_map/all_to_all | solution.py:532
  93.3 5.8 %time_weights.1.time_ref = bf16[13,2,256,256]{3,2,1,0:T(8,128)(2,1)S(1)} custom-call(bf16[16,32,3328]{2,1,0:T(8,128)(2,1)S(1)} %bitcast.19), custom_call_target="tpu_custom_call" | custom-call | flops 436207616 | bytes 7000000 | tf_op jit(solution)/shard_map/time_weights/pallas_call | solution.py:161
  99.1 1.8 copy-done.2
  100.9 4.3 %gathered.1.cap_ref = bf16[32,80,512]{2,1,0:T(8,128)(2,1)S(1)} custom-call(s32[5]{0:T(128)S(1)} %stack.23.place_ref, bf16[16,80,512]{2,1,0:T(8,128)(2,1)S(1)} %pad_maximum_fusion.mine_ref, bf16[16,80,512]{2,1,0:T(8,128)(2,1)S(1)} %collective-permute-done.6.other_ref), custom_call_target="tpu_custom_call" | custom-call | bytes 5200000 | tf_op jit(solution)/shard_map/gathered/pallas_call | solution.py:217
  106.8 6.6 %all-to-all-done.3.value_ref = bf16[8,2,32,1664]{3,2,1,0:T(8,128)(2,1)} async-done(((bf16[8,2,32,1664]{3,2,1,0:T(8,128)(2,1)}), bf16[8,2,32,1664]{3,2,1,0:T(8,128)(2,1)}, u32[]{:S(2)}, u32[]{:S(2)}) %all-to-all-start.3) | async-done | bytes 1703968 | tf_op jit(solution)/shard_map/all_to_all | solution.py:532
  116.6 9.2 %token_part.1 = (bf16[16,32,512]{2,1,0:T(8,128)(2,1)}, f32[8,2,32,128]{3,2,1,0:T(8,128)S(1)}, bf16[32,80,512]{2,1,0:T(8,128)(2,1)S(1)}) custom-call(bf16[8,2,32,1664]{3,2,1,0:T(8,128)(2,1)} %all-to-all-done.3.value_ref, bf16[13,2,256,256]{3,2,1,0:T(8,128)(2,1)S(1)} %copy-done.3, bf16[1664,512]{1,0:T(8,128)(2,1)S(1)} %copy-done.10, ...), custom_call_target="tpu_custom_call" | custom-call | flops 2700000000 | bytes 13000000 | tf_op jit(solution)/shard_map/token_part/pallas_call | solution.py:310
  128.0 3.4 %all-to-all-start.4 = ((f32[8,2,32,128]{3,2,1,0:T(8,128)}), f32[8,2,32,128]{3,2,1,0:T(8,128)S(1)}, u32[]{:S(2)}, u32[]{:S(2)}) async-start(f32[8,2,32,128]{3,2,1,0:T(8,128)} %copy-done.9), calls=%async_computation.4 | async-start | bytes 524288 | tf_op jit(solution)/shard_map/all_to_all | solution.py:534
  135.7 2.0 %gradient_product.1.grad_ref = bf16[32,80,512]{2,1,0:T(8,128)(2,1)S(1)} custom-call(bf16[32,80,512]{2,1,0:T(8,128)(2,1)S(1)} %copy-done.7, bf16[16,32,512]{2,1,0:T(8,128)(2,1)S(1)} %copy-done.8), custom_call_target="tpu_custom_call" | custom-call | flops 1340000000 | bytes 6000000 | tf_op jit(solution)/shard_map/gradient_product/pallas_call | solution.py:352
  138.3 2.0 %coef_part.1 = (bf16[16,80,512]{2,1,0:T(8,128)(2,1)S(1)}, bf16[16,80,512]{2,1,0:T(8,128)(2,1)S(1)}, f32[1,1]{1,0:T(1,128)}) custom-call(s32[5]{0:T(128)S(1)} %stack.23.place_ref, s32[1]{0:T(128)S(6)} %copy.15.pos_ref, f32[8,2,32,128]{3,2,1,0:T(8,128)S(1)} %all-to-all-done.4.stats_ref, bf16[32,128]{1,0:T(8,128)(2,1)S(1)} %bitcast.21, ...), custom_call_target="tpu_custom_call" | custom-call | flops 4000000 | bytes 6000000 | tf_op jit(solution)/shard_map/coef_part/pallas_call | solution.py:409
  140.3 3.0 %collective-permute-done.7.got_ref = bf16[16,80,512]{2,1,0:T(8,128)(2,1)S(1)} collective-permute-done((bf16[16,80,512]{2,1,0:T(8,128)(2,1)S(1)}, bf16[16,80,512]{2,1,0:T(8,128)(2,1)S(1)}, u32[]{:S(2)}, u32[]{:S(2)}) %collective-permute-start.7) | collective-permute-done | bytes 1310752 | tf_op jit(solution)/shard_map/ppermute | solution.py:492
  145.7 2.1 %collective-permute-start.9 = (bf16[8,80,256]{2,1,0:T(8,128)(2,1)S(1)}, bf16[8,80,256]{2,1,0:T(8,128)(2,1)S(1)}, u32[]{:S(2)}, u32[]{:S(2)}) collective-permute-start(bf16[8,80,256]{2,1,0:T(8,128)(2,1)S(1)} %get-tuple-element.25), channel_id=1, source_target_pairs={{0,6},{1,7},{2,4},{3,5},{4,2},{5,3},{6,0},{7,1},{8,14},{9,15},{10,... | collective-permute-start | bytes 983048 | tf_op jit(solution)/shard_map/ppermute | solution.py:498
  147.8 6.2 %collective-permute-done.8.a_got = bf16[8,80,256]{2,1,0:T(8,128)(2,1)S(1)} collective-permute-done((bf16[8,80,256]{2,1,0:T(8,128)(2,1)S(1)}, bf16[8,80,256]{2,1,0:T(8,128)(2,1)S(1)}, u32[]{:S(2)}, u32[]{:S(2)}) %collective-permute-start.8) | collective-permute-done | bytes 327712 | tf_op jit(solution)/shard_map/ppermute | solution.py:497
  154.0 2.4 %collective-permute-done.9.b_got = bf16[8,80,256]{2,1,0:T(8,128)(2,1)S(1)} collective-permute-done((bf16[8,80,256]{2,1,0:T(8,128)(2,1)S(1)}, bf16[8,80,256]{2,1,0:T(8,128)(2,1)S(1)}, u32[]{:S(2)}, u32[]{:S(2)}) %collective-permute-start.9) | collective-permute-done | bytes 327712 | tf_op jit(solution)/shard_map/ppermute | solution.py:498
  156.6 2.2 %collective-permute-start.10 = (bf16[8,80,128]{2,1,0:T(8,128)(2,1)S(1)}, bf16[8,80,128]{2,1,0:T(8,128)(2,1)S(1)}, u32[]{:S(2)}, u32[]{:S(2)}) collective-permute-start(bf16[8,80,128]{2,1,0:T(8,128)(2,1)S(1)} %get-tuple-element.27), channel_id=1, source_target_pairs={{0,6},{1,7},{2,4},{3,5},{4,2},{5,3},{6,0},{7,1},{8,14},{9,15},{10,... | collective-permute-start | bytes 491528 | tf_op jit(solution)/shard_map/ppermute | solution.py:503
  158.7 4.4 %collective-permute-done.10.a_got = bf16[8,80,128]{2,1,0:T(8,128)(2,1)S(1)} collective-permute-done((bf16[8,80,128]{2,1,0:T(8,128)(2,1)S(1)}, bf16[8,80,128]{2,1,0:T(8,128)(2,1)S(1)}, u32[]{:S(2)}, u32[]{:S(2)}) %collective-permute-start.10) | collective-permute-done | bytes 163872 | tf_op jit(solution)/shard_map/ppermute | solution.py:503
  164.1 23.5 %all_to_all.35.parts = bf16[16,80,128]{2,1,0:T(8,128)(2,1)S(1)} all-to-all(bf16[16,80,128]{2,1,0:T(8,128)(2,1)S(1)} %third_sum.1), channel_id=1, replica_groups={{0,16,32,48,64,80,96,112,128,144,160,176,192,208,224,240},{8,24,40,56,7..., dimensions={0} | all-to-all | bytes 655360 | tf_op jit(solution)/shard_map/all_to_all | solution.py:508
  187.7 9.1 %all_to_all.36.parts = bf16[8,80,128]{2,1,0:T(8,128)(2,1)S(1)} all-to-all(bf16[8,80,128]{2,1,0:T(8,128)(2,1)S(1)} %fourth_sum.1), channel_id=1, replica_groups=mesh['dp'=32,'space'=8] {'space'}, dimensions={0} | all-to-all | bytes 327680 | tf_op jit(solution)/shard_map/all_to_all | solution.py:513
  (55 shorter events, 24.7 us)
Async XLA Ops:
  4.0 34.5 %all-to-all-start = ((bf16[4,2,32,4992]{3,2,1,0:T(8,128)(2,1)}), bf16[4,2,32,4992]{3,2,1,0:T(8,128)(2,1)S(1)}, u32[]{:S(2)}, u32[]{:S(2)}) async-start(bf16[4,2,32,4992]{3,2,1,0:T(8,128)(2,1)} %bitcast.22), calls=%async_computation | async-start | bytes 5111808 | tf_op jit(solution)/shard_map/all_to_all | solution.py:53
  7.8 6.7 %copy-start.13 = (bf16[1,77,512]{2,1,0:T(8,128)(2,1)S(1)}, bf16[1,77,512]{2,1,0:T(8,128)(2,1)}, u32[]{:S(2)}) copy-start(bf16[1,77,512]{2,1,0:T(8,128)(2,1)} %param.9) | copy-start | bytes 236548
  11.2 47.2 %collective-permute-start.1 = (bf16[4,32,4992]{2,1,0:T(8,128)(2,1)}, bf16[4,32,4992]{2,1,0:T(8,128)(2,1)}, u32[]{:S(2)}, u32[]{:S(2)}) collective-permute-start(bf16[4,32,4992]{2,1,0:T(8,128)(2,1)} %get-tuple-element.34), channel_id=1, source_target_pairs={{0,6},{1,7},{2,4},{3,5},{4,2},{5,3},{6,0},{7,1},{8,14},{9,15},{10,... | collective-permute-start | bytes 3833864 | tf_op jit(solution)/shard_map/ppermute | solution.py:59
  14.6 28.3 %collective-permute-start.2 = (bf16[1,80,512]{2,1,0:T(8,128)(2,1)S(1)}, bf16[1,80,512]{2,1,0:T(8,128)(2,1)S(1)}, u32[]{:S(2)}, u32[]{:S(2)}) collective-permute-start(bf16[1,80,512]{2,1,0:T(8,128)(2,1)S(1)} %concatenate.16), channel_id=1, source_target_pairs={{0,128},{8,136},{16,144},{24,152},{32,160},{40,168},{48,176},{56,1... | collective-permute-start | bytes 245768 | tf_op jit(solution)/shard_map/ppermute | solution.py:199
  38.5 19.9 %all-to-all-start.1 = ((bf16[4,32,4992]{2,1,0:T(8,128)(2,1)}), bf16[4,32,4992]{2,1,0:T(8,128)(2,1)}, u32[]{:S(2)}, u32[]{:S(2)}) async-start(bf16[4,32,4992]{2,1,0:T(8,128)(2,1)} %get-tuple-element.35), calls=%async_computation.1 | async-start | bytes 2555904 | tf_op jit(solution)/shard_map/all_to_all | solution.py:53
  42.9 11.6 %collective-permute-start.3 = (bf16[2,80,512]{2,1,0:T(8,128)(2,1)S(1)}, bf16[2,80,512]{2,1,0:T(8,128)(2,1)S(1)}, u32[]{:S(2)}, u32[]{:S(2)}) collective-permute-start(bf16[2,80,512]{2,1,0:T(8,128)(2,1)S(1)} %pad_maximum_fusion.3), channel_id=1, source_target_pairs={{0,64},{8,72},{16,80},{24,88},{32,96},{40,104},{48,112},{56,120},{... | collective-permute-start | bytes 491528 | tf_op jit(solution)/shard_map/ppermute | solution.py:199
  50.4 29.5 %collective-permute-start = (bf16[4,32,4992]{2,1,0:T(8,128)(2,1)}, bf16[4,32,4992]{2,1,0:T(8,128)(2,1)}, u32[]{:S(2)}, u32[]{:S(2)}) collective-permute-start(bf16[4,32,4992]{2,1,0:T(8,128)(2,1)} %dynamic-slice_bitcast_fusion.2), channel_id=1, source_target_pairs={{0,6},{1,7},{2,4},{3,5},{4,2},{5,3},{6,0},{7,1},{8,14},{9,15},{10,... | collective-permute-start | bytes 3833864 | tf_op jit(solution)/shard_map/ppermute | solution.py:67
  54.5 15.2 %copy-start.11 = (bf16[4,80,512]{2,1,0:T(8,128)(2,1)}, bf16[4,80,512]{2,1,0:T(8,128)(2,1)S(1)}, u32[]{:S(2)}) copy-start(bf16[4,80,512]{2,1,0:T(8,128)(2,1)S(1)} %pad_maximum_fusion.2) | copy-start | bytes 983044
  54.5 14.2 %collective-permute-start.4 = (bf16[4,80,512]{2,1,0:T(8,128)(2,1)S(1)}, bf16[4,80,512]{2,1,0:T(8,128)(2,1)S(1)}, u32[]{:S(2)}, u32[]{:S(2)}) collective-permute-start(bf16[4,80,512]{2,1,0:T(8,128)(2,1)S(1)} %pad_maximum_fusion.2), channel_id=1, source_target_pairs={{0,32},{8,40},{16,48},{24,56},{32,0},{40,8},{48,16},{56,24},{64,96... | collective-permute-start | bytes 983048 | tf_op jit(solution)/shard_map/ppermute | solution.py:199
  58.4 20.0 %all-to-all-start.2 = ((bf16[4,32,4992]{2,1,0:T(8,128)(2,1)}), bf16[4,32,4992]{2,1,0:T(8,128)(2,1)}, u32[]{:S(2)}, u32[]{:S(2)}) async-start(bf16[4,32,4992]{2,1,0:T(8,128)(2,1)} %collective-permute-done.1), calls=%async_computation.2 | async-start | bytes 2555904 | tf_op jit(solution)/shard_map/all_to_all | solution.py:53
  68.7 11.2 %copy-start.12 = (bf16[4,80,512]{2,1,0:T(8,128)(2,1)}, bf16[4,80,512]{2,1,0:T(8,128)(2,1)S(1)}, u32[]{:S(2)}) copy-start(bf16[4,80,512]{2,1,0:T(8,128)(2,1)S(1)} %collective-permute-done.4) | copy-start | bytes 983044
  69.7 21.9 %collective-permute-start.5 = (bf16[8,80,512]{2,1,0:T(8,128)(2,1)}, bf16[8,80,512]{2,1,0:T(8,128)(2,1)}, u32[]{:S(2)}, u32[]{:S(2)}) collective-permute-start(bf16[8,80,512]{2,1,0:T(8,128)(2,1)} %pad_maximum_fusion.1), channel_id=1, source_target_pairs={{0,16},{8,24},{16,0},{24,8},{32,48},{40,56},{48,32},{56,40},{64,80... | collective-permute-start | bytes 1966088 | tf_op jit(solution)/shard_map/ppermute | solution.py:199
  85.0 1.2 copy-start
  86.2 7.1 %copy-start.1 = (bf16[1,16,32,3328]{3,2,1,0:T(8,128)(2,1)S(1)}, bf16[1,16,32,3328]{3,2,1,0:T(8,128)(2,1)}, u32[]{:S(2)}) copy-start(bf16[1,16,32,3328]{3,2,1,0:T(8,128)(2,1)} %param.7) | copy-start | bytes 10223620
  86.2 27.2 %all-to-all-start.3 = ((bf16[8,2,32,1664]{3,2,1,0:T(8,128)(2,1)}), bf16[8,2,32,1664]{3,2,1,0:T(8,128)(2,1)}, u32[]{:S(2)}, u32[]{:S(2)}) async-start(bf16[8,2,32,1664]{3,2,1,0:T(8,128)(2,1)} %copy-done), calls=%async_computation.3 | async-start | bytes 3407872 | tf_op jit(solution)/shard_map/all_to_all | solution.py:532
  93.0 7.9 %collective-permute-start.6 = (bf16[16,80,512]{2,1,0:T(8,128)(2,1)S(1)}, bf16[16,80,512]{2,1,0:T(8,128)(2,1)S(1)}, u32[]{:S(2)}, u32[]{:S(2)}) collective-permute-start(bf16[16,80,512]{2,1,0:T(8,128)(2,1)S(1)} %pad_maximum_fusion.mine_ref), channel_id=1, source_target_pairs={{0,8},{8,0},{16,24},{24,16},{32,40},{40,32},{48,56},{56,48},{64,72... | collective-permute-start | bytes 3932168 | tf_op jit(solution)/shard_map/ppermute | solution.py:199
  99.1 1.8 copy-start.2
  100.9 12.5 %copy-start.3 = (bf16[13,2,256,256]{3,2,1,0:T(8,128)(2,1)S(1)}, bf16[13,2,256,256]{3,2,1,0:T(8,128)(2,1)}, u32[]{:S(2)}) copy-start(bf16[13,2,256,256]{3,2,1,0:T(8,128)(2,1)} %copy-done.2) | copy-start | bytes 10223620
  105.2 1.5 copy-start.4
  113.4 1.7 copy-start.5
  115.1 1.5 copy-start.10
  125.8 1.5 copy-start.6
  127.3 0.7 copy-start.9
  128.0 10.3 %all-to-all-start.4 = ((f32[8,2,32,128]{3,2,1,0:T(8,128)}), f32[8,2,32,128]{3,2,1,0:T(8,128)S(1)}, u32[]{:S(2)}, u32[]{:S(2)}) async-start(f32[8,2,32,128]{3,2,1,0:T(8,128)} %copy-done.9), calls=%async_computation.4 | async-start | bytes 524288 | tf_op jit(solution)/shard_map/all_to_all | solution.py:534
  132.9 1.7 copy-start.7
  134.7 1.0 copy-start.8
  140.3 3.0 %collective-permute-start.7 = (bf16[16,80,512]{2,1,0:T(8,128)(2,1)S(1)}, bf16[16,80,512]{2,1,0:T(8,128)(2,1)S(1)}, u32[]{:S(2)}, u32[]{:S(2)}) collective-permute-start(bf16[16,80,512]{2,1,0:T(8,128)(2,1)S(1)} %get-tuple-element.21), channel_id=1, source_target_pairs={{0,8},{8,0},{16,24},{24,16},{32,40},{40,32},{48,56},{56,48},{64,72... | collective-permute-start | bytes 3932168 | tf_op jit(solution)/shard_map/ppermute | solution.py:492
  144.2 9.8 %collective-permute-start.8 = (bf16[8,80,256]{2,1,0:T(8,128)(2,1)S(1)}, bf16[8,80,256]{2,1,0:T(8,128)(2,1)S(1)}, u32[]{:S(2)}, u32[]{:S(2)}) collective-permute-start(bf16[8,80,256]{2,1,0:T(8,128)(2,1)S(1)} %get-tuple-element.23), channel_id=1, source_target_pairs={{0,2},{1,3},{2,0},{3,1},{4,6},{5,7},{6,4},{7,5},{8,10},{9,11},{10,... | collective-permute-start | bytes 983048 | tf_op jit(solution)/shard_map/ppermute | solution.py:497
  145.7 10.7 %collective-permute-start.9 = (bf16[8,80,256]{2,1,0:T(8,128)(2,1)S(1)}, bf16[8,80,256]{2,1,0:T(8,128)(2,1)S(1)}, u32[]{:S(2)}, u32[]{:S(2)}) collective-permute-start(bf16[8,80,256]{2,1,0:T(8,128)(2,1)S(1)} %get-tuple-element.25), channel_id=1, source_target_pairs={{0,6},{1,7},{2,4},{3,5},{4,2},{5,3},{6,0},{7,1},{8,14},{9,15},{10,... | collective-permute-start | bytes 983048 | tf_op jit(solution)/shard_map/ppermute | solution.py:498
  156.6 6.6 %collective-permute-start.10 = (bf16[8,80,128]{2,1,0:T(8,128)(2,1)S(1)}, bf16[8,80,128]{2,1,0:T(8,128)(2,1)S(1)}, u32[]{:S(2)}, u32[]{:S(2)}) collective-permute-start(bf16[8,80,128]{2,1,0:T(8,128)(2,1)S(1)} %get-tuple-element.27), channel_id=1, source_target_pairs={{0,6},{1,7},{2,4},{3,5},{4,2},{5,3},{6,0},{7,1},{8,14},{9,15},{10,... | collective-permute-start | bytes 491528 | tf_op jit(solution)/shard_map/ppermute | solution.py:503
  158.7 5.3 %collective-permute-start.11 = (bf16[8,80,128]{2,1,0:T(8,128)(2,1)S(1)}, bf16[8,80,128]{2,1,0:T(8,128)(2,1)S(1)}, u32[]{:S(2)}, u32[]{:S(2)}) collective-permute-start(bf16[8,80,128]{2,1,0:T(8,128)(2,1)S(1)} %get-tuple-element.29), channel_id=1, source_target_pairs={{0,2},{1,3},{2,0},{3,1},{4,6},{5,7},{6,4},{7,5},{8,10},{9,11},{10,... | collective-permute-start | bytes 491528 | tf_op jit(solution)/shard_map/ppermute | solution.py:504

commit v5 on v3

v5 whole, which is shorter than its diff:
```python
import math

import jax
import jax.numpy as jnp
from jax import lax
from jax.experimental import pallas as pl
from jax.experimental.pallas import tpu as pltpu
from jax.sharding import PartitionSpec as P

HEADS = 13
HD = 128
FEATURES = HEADS * HD
EMB = 512
FRAMES = 16
PATCHES = 256
LOCAL = 32
SLOTS = 77
PADDED = 80
CAPTIONS = 32
SHARPNESS = 4.0
LOGIT_SCALE = 10.0
LOG2E = math.log2(math.e)
SCORE_LOG2 = HD ** (-0.5) * LOG2E
SHARP_LOG2 = SHARPNESS * LOG2E
MIB = 1 << 20
GRANT = pltpu.CompilerParams(vmem_limit_bytes=24 * MIB)
VMEM = pl.BlockSpec(memory_space=pltpu.VMEM)
SMEM = pl.BlockSpec(memory_space=pltpu.SMEM)

FAR_OFF = pl.BlockSpec(memory_space=pltpu.HBM)
ANY = pl.BlockSpec(memory_space=pl.ANY)

def held(value):
    return pltpu.with_memory_space_constraint(value, pltpu.HBM)


def nt(a, b):
    return lax.dot_general(a, b, (((1,), (1,)), ((), ())), preferred_element_type=jnp.float32)


SPLIT = 7


def spatial_kernel(qkv_ref, out_ref):
    for h in range(HEADS):
        q = qkv_ref[:, 0, :, pl.ds(h * HD, HD)].reshape(PATCHES, HD)
        k = qkv_ref[:, 0, :, pl.ds(FEATURES + h * HD, HD)].reshape(PATCHES, HD)
        v = qkv_ref[:, 0, :, pl.ds(2 * FEATURES + h * HD, HD)].reshape(PATCHES, HD)
        s = nt(q, k)
        m = jnp.max(s, axis=-1, keepdims=True)
        e = jnp.exp2((s - m) * SCORE_LOG2)
        total = jnp.sum(e, axis=-1, keepdims=True)
        o = jnp.dot(e.astype(jnp.bfloat16), v, preferred_element_type=jnp.float32)
        o = (o * (1.0 / total)).astype(jnp.bfloat16)
        out_ref[:, 0, :, pl.ds(h * HD, HD)] = o.reshape(8, LOCAL, HD)


def spatial_attention(blocks):
    return pl.pallas_call(
        spatial_kernel,
        grid=(2,),
        in_specs=[pl.BlockSpec((8, 1, LOCAL, 3 * FEATURES), lambda f: (0, f, 0, 0))],
        out_specs=pl.BlockSpec((8, 1, LOCAL, FEATURES), lambda f: (0, f, 0, 0)),
        out_shape=pltpu.HBM((8, 2, LOCAL, FEATURES), jnp.bfloat16),
        compiler_params=GRANT,
        cost_estimate=pl.CostEstimate(
            flops=8 * HEADS * PATCHES * PATCHES * HD,
            bytes_accessed=2 * PATCHES * 4 * FEATURES * 2,
            transcendentals=2 * HEADS * PATCHES * PATCHES,
        ),
        name="spatial_attention",
    )(blocks)


ROWS = FRAMES * 16


def time_kernel(tqk_ref, out_ref, tqk, weights, load_sem, sems):
    load = pltpu.make_async_copy(tqk_ref, tqk, load_sem)
    load.start()
    load.wait()
    r = lax.broadcasted_iota(jnp.int32, (ROWS, ROWS), 0)
    c = lax.broadcasted_iota(jnp.int32, (ROWS, ROWS), 1)
    bias = jnp.where((r & 15) == (c & 15), 0.0, -1e30).astype(jnp.float32)
    stores = []
    for h in range(HEADS):
        for g in range(LOCAL // 16):
            part = pl.ds(g * 16, 16)
            q = tqk[:, part, pl.ds(h * HD, HD)].reshape(ROWS, HD)
            k = tqk[:, part, pl.ds(FEATURES + h * HD, HD)].reshape(ROWS, HD)
            s = nt(q, k) + bias
            m = jnp.max(s, axis=-1, keepdims=True)
            e = jnp.exp2((s - m) * SCORE_LOG2)
            total = jnp.sum(e, axis=-1, keepdims=True)
            weights[h, g] = (e * (1.0 / total)).astype(jnp.bfloat16)
        stores.append(pltpu.make_async_copy(weights.at[h], out_ref.at[h], sems.at[h]))
        stores[-1].start()
    for store in stores:
        store.wait()


def time_weights(temporal_qk):
    return pl.pallas_call(
        time_kernel,
        in_specs=[FAR_OFF],
        out_specs=FAR_OFF,
        out_shape=pltpu.HBM((HEADS, 2, ROWS, ROWS), jnp.bfloat16),
        scratch_shapes=[
            pltpu.VMEM((FRAMES, LOCAL, 2 * FEATURES), jnp.bfloat16),
            pltpu.VMEM((HEADS, 2, ROWS, ROWS), jnp.bfloat16),
            pltpu.SemaphoreType.DMA,
            pltpu.SemaphoreType.DMA((HEADS,)),
        ],
        compiler_params=GRANT,
        cost_estimate=pl.CostEstimate(
            flops=4 * HEADS * ROWS * ROWS * HD,
            bytes_accessed=7_000_000,
            transcendentals=2 * HEADS * ROWS * ROWS,
        ),
        name="time_weights",
    )(held(temporal_qk))


def flip(value, bit):
    return lax.ppermute(value, "dp", [(i, i ^ bit) for i in range(32)])


def join_kernel(*refs):
    refs[-1][0] = refs[0][...]
    refs[-1][1] = refs[1][...]


def doubled(value, bit, *behind):
    both = pl.pallas_call(
        join_kernel,
        in_specs=[VMEM] * 2 + [ANY] * len(behind),
        out_specs=VMEM,
        out_shape=jax.ShapeDtypeStruct((2,) + value.shape, value.dtype),
        compiler_params=pltpu.CompilerParams(vmem_limit_bytes=8 * MIB),
        cost_estimate=pl.CostEstimate(flops=0, bytes_accessed=1_000_000, transcendentals=0),
        name="join",
    )(value, flip(value, bit), *behind)
    return both.reshape((-1,) + value.shape[1:])


def token_kernel(
    place_ref, value, time_ref, proj_ref, mine_ref, other_ref,
    emb_ref, stats_ref, grad_ref, lens_ref,
    proj, mine, comb, video, grads, sems, grad_sems,
):
    proj_load = pltpu.make_async_copy(proj_ref, proj, sems.at[0])
    mine_load = pltpu.make_async_copy(mine_ref, mine, sems.at[1])
    proj_load.start()
    mine_load.start()
    for h in range(HEADS):
        cols = pl.ds(h * HD, HD)
        for g in range(LOCAL // 16):
            part = pl.ds(g * 16, 16)
            v = value[:, :, part, cols].reshape(ROWS, HD)
            o = jnp.dot(time_ref[h, g], v, preferred_element_type=jnp.float32)
            o = (v.astype(jnp.float32) + o).astype(jnp.bfloat16)
            comb[:, part, cols] = o.reshape(FRAMES, 16, HD)
    tokens = FRAMES * LOCAL
    proj_load.wait()
    projected = jnp.dot(
        comb[...].reshape(tokens, FEATURES), proj[...], preferred_element_type=jnp.float32
    )
    scale = lax.rsqrt(jnp.mean(projected * projected, axis=-1, keepdims=True) + 1e-06)
    emb = (projected * scale).astype(jnp.bfloat16)
    video[...] = emb.reshape(FRAMES, LOCAL, EMB)
    emb_store = pltpu.make_async_copy(video, emb_ref, sems.at[2])
    emb_store.start()
    mine_load.wait()

    eye = lax.broadcasted_iota(jnp.int32, (PADDED, 128), 0) == lax.broadcasted_iota(
        jnp.int32, (PADDED, 128), 1
    )
    y_hi, core, z = place_ref[0], place_ref[1], place_ref[4]
    group = 8
    stores = []
    for i, (ref, c) in enumerate(((mine, core), (other_ref, 1 - core))):
        for m0 in range(0, CAPTIONS // 2, group):
            sim = nt(ref[pl.ds(m0, group)].reshape(group * PADDED, EMB), emb)
            top = jnp.max(sim, axis=-1, keepdims=True)
            w = jnp.exp2((sim - top) * SHARP_LOG2)
            total = jnp.sum(w, axis=-1, keepdims=True)
            product = jnp.dot(w.astype(jnp.bfloat16), emb, preferred_element_type=jnp.float32)
            slot = i * CAPTIONS // 2 + m0
            grads[pl.ds(slot, group)] = product.astype(jnp.bfloat16).reshape(group, PADDED, EMB)
            for j in range(group):
                m = m0 + j
                flips = (m >> 3 & 1) + (m >> 2 & 1) * 2 + (m >> 1 & 1) * 4
                at = (y_hi ^ (m & 1)) * 16 + (z ^ flips) * 2 + c
                stores.append(
                    pltpu.make_async_copy(
                        grads.at[slot + j], grad_ref.at[at], grad_sems.at[slot + j]
                    )
                )
                stores[-1].start()
                rng = slice(j * PADDED, (j + 1) * PADDED)
                top_row = jnp.sum(jnp.where(eye, top[rng], 0.0), axis=0, keepdims=True)
                total_row = jnp.sum(jnp.where(eye, total[rng], 0.0), axis=0, keepdims=True)
                for k in range(8):
                    stats_ref[k, 0, pl.ds(at, 1), :] = top_row
                    stats_ref[k, 1, pl.ds(at, 1), :] = total_row
                lens_ref[pl.ds(at, 1), :] = ref[m, SLOTS : SLOTS + 1, :128].astype(jnp.float32)
    emb_store.wait()
    for store in stores:
        store.wait()


def token_part(place, spatial, time, proj_weight, mine, other):
    bf16 = jnp.bfloat16
    return pl.pallas_call(
        token_kernel,
        in_specs=[SMEM, VMEM, VMEM, FAR_OFF, FAR_OFF, VMEM],
        out_specs=[FAR_OFF, VMEM, FAR_OFF, VMEM],
        out_shape=[
            pltpu.HBM((FRAMES, LOCAL, EMB), bf16),
            jax.ShapeDtypeStruct((8, 2, CAPTIONS, 128), jnp.float32),
            pltpu.HBM((CAPTIONS, PADDED, EMB), bf16),
            jax.ShapeDtypeStruct((CAPTIONS, 128), jnp.float32),
        ],
        scratch_shapes=[
            pltpu.VMEM((FEATURES, EMB), bf16),
            pltpu.VMEM((CAPTIONS // 2, PADDED, EMB), bf16),
            pltpu.VMEM((FRAMES, LOCAL, FEATURES), bf16),
            pltpu.VMEM((FRAMES, LOCAL, EMB), bf16),
            pltpu.VMEM((CAPTIONS, PADDED, EMB), bf16),
            pltpu.SemaphoreType.DMA((3,)),
            pltpu.SemaphoreType.DMA((CAPTIONS,)),
        ],
        compiler_params=GRANT,
        cost_estimate=pl.CostEstimate(
            flops=4_500_000_000, bytes_accessed=12_000_000, transcendentals=1_300_000
        ),
        name="token_part",
    )(place, spatial, time, held(proj_weight), held(mine), other)


def coef_kernel(
    place_ref, pos_ref, stats_ref, lens_ref, grad_ref, send_ref, keep_ref, loss_ref, hold, grad, sems
):
    group = 8
    loads = [
        pltpu.make_async_copy(
            grad_ref.at[pl.ds(group * i, group)], grad.at[pl.ds(group * i, group)], sems.at[i]
        )
        for i in range(CAPTIONS // group)
    ]
    for load in loads:
        load.start()
    tops = stats_ref[:, 0]
    totals = stats_ref[:, 1]
    top = jnp.max(tops, axis=0)
    total = jnp.sum(totals * jnp.exp2((tops - top[None]) * SHARP_LOG2), axis=0)
    soft = top + jnp.log(total) / SHARPNESS
    slot = lax.broadcasted_iota(jnp.int32, (CAPTIONS, 128), 1).astype(jnp.float32)
    lens = lens_ref[...]
    live = slot < lens
    lens_col = lens[:, :1]
    score = jnp.sum(jnp.where(live, soft, 0.0), axis=-1, keepdims=True) / lens_col
    logits = LOGIT_SCALE * score
    peak = jnp.max(logits, axis=0, keepdims=True)
    log_total = peak + jnp.log(jnp.sum(jnp.exp(logits - peak), axis=0, keepdims=True))
    onehot = lax.broadcasted_iota(jnp.int32, (CAPTIONS, 1), 0) == pos_ref[0]
    loss_ref[...] = log_total - jnp.sum(jnp.where(onehot, logits, 0.0), axis=0, keepdims=True)
    grad_logit = LOGIT_SCALE * (jnp.exp(logits - log_total) - onehot.astype(jnp.float32))
    coef = jnp.where(live, grad_logit / lens_col, 0.0)
    mine = stats_ref[place_ref[2] * 2 + place_ref[3], 0]
    hold[...] = coef * jnp.exp2((mine - soft) * SHARP_LOG2)

    eye = lax.broadcasted_iota(jnp.int32, (PADDED, 128), 0) == lax.broadcasted_iota(
        jnp.int32, (PADDED, 128), 1
    )
    core = place_ref[1]
    for m in range(CAPTIONS // 2):
        if 2 * m % group == 0:
            loads[2 * m // group].wait()
        for j, ref in ((2 * m + 1 - core, send_ref), (2 * m + core, keep_ref)):
            col = jnp.sum(jnp.where(eye, hold[pl.ds(j, 1), :], 0.0), axis=-1, keepdims=True)
            ref[m] = (grad[j].astype(jnp.float32) * col).astype(jnp.bfloat16)


def coef_part(place, pos, stats, lens, grad):
    half = jax.ShapeDtypeStruct((CAPTIONS // 2, PADDED, EMB), jnp.bfloat16)
    return pl.pallas_call(
        coef_kernel,
        in_specs=[SMEM, SMEM, VMEM, VMEM, FAR_OFF],
        out_specs=[VMEM] * 3,
        out_shape=[half, half, jax.ShapeDtypeStruct((1, 1), jnp.float32)],
        scratch_shapes=[
            pltpu.VMEM((CAPTIONS, 128), jnp.float32),
            pltpu.VMEM((CAPTIONS, PADDED, EMB), jnp.bfloat16),
            pltpu.SemaphoreType.DMA((4,)),
        ],
        compiler_params=pltpu.CompilerParams(vmem_limit_bytes=12 * MIB),
        cost_estimate=pl.CostEstimate(
            flops=4_000_000, bytes_accessed=6_000_000, transcendentals=100_000
        ),
        name="coef_part",
    )(place, pos, stats, lens, held(grad))


def small_call(kernel, name, operands, out_shapes, specs=None):
    return pl.pallas_call(
        kernel,
        in_specs=specs or [VMEM] * len(operands),
        out_specs=[VMEM] * len(out_shapes),
        out_shape=[jax.ShapeDtypeStruct(s, d) for s, d in out_shapes],
        compiler_params=pltpu.CompilerParams(vmem_limit_bytes=16 * MIB),
        cost_estimate=pl.CostEstimate(flops=0, bytes_accessed=2_000_000, transcendentals=0),
        name=name,
    )(*operands)


def added(a, b):
    return (a.astype(jnp.float32) + b.astype(jnp.float32)).astype(jnp.bfloat16)


def first_sum_kernel(place_ref, keep_ref, got_ref, a_keep, a_send, b_keep, b_send):
    x = place_ref[2]
    plan = (
        (0, ((a_keep, 0, 0), (a_send, 0, 1), (a_send, 1, 2), (a_keep, 1, 3))),
        (8, ((b_keep, 0, 0), (b_keep, 1, 1), (b_send, 1, 2), (b_send, 0, 3))),
    )
    for start, parts in plan:
        for ref, at, flip in parts:
            cols = pl.ds(pl.multiple_of((x ^ flip) * 128, 128), 128)
            for m in range(8):
                ref[m, :, pl.ds(at * 128, 128)] = added(
                    keep_ref[start + m, :, cols], got_ref[start + m, :, cols]
                )


def second_sum_kernel(a_keep, a_got, b_keep, b_got, a_mine, a_send, b_mine, b_send):
    for keep, got, mine, send in ((a_keep, a_got, a_mine, a_send), (b_keep, b_got, b_mine, b_send)):
        mine[...] = added(keep[:, :, :128], got[:, :, :128])
        send[...] = added(keep[:, :, 128:], got[:, :, 128:])


def third_sum_kernel(a_mine, a_got, b_mine, b_got, out):
    out[pl.ds(0, 8)] = added(a_mine[...], a_got[...])
    out[pl.ds(8, 8)] = added(b_mine[...], b_got[...])


def owned_sum_kernel(parts, out):
    total = jnp.sum(parts[...].astype(jnp.float32), axis=0).astype(jnp.bfloat16)
    for k in range(8):
        out[k] = total


def last_sum_kernel(parts, out):
    for x in range(4):
        total = parts[2 * x].astype(jnp.float32) + parts[2 * x + 1].astype(jnp.float32)
        out[:, 0, pl.ds(x * 128, 128)] = total[:SLOTS]


def reduce_gradient(place, send, keep):
    bf16 = jnp.bfloat16
    one = [(s, s ^ 2) for s in range(8)]
    three = [(s, s ^ 6) for s in range(8)]
    got = lax.ppermute(send, "dp", [(i, i ^ 1) for i in range(32)])
    a_keep, a_send, b_keep, b_send = small_call(
        first_sum_kernel, "first_sum", (place, keep, got), [((8, PADDED, 256), bf16)] * 4,
        [SMEM, VMEM, VMEM],
    )
    a_got = lax.ppermute(a_send, "space", one)
    b_got = lax.ppermute(b_send, "space", three)
    a_mine, a_send, b_mine, b_send = small_call(
        second_sum_kernel, "second_sum", (a_keep, a_got, b_keep, b_got),
        [((8, PADDED, 128), bf16)] * 4,
    )
    a_got = lax.ppermute(a_send, "space", three)
    b_got = lax.ppermute(b_send, "space", one)
    (parts,) = small_call(
        third_sum_kernel, "third_sum", (a_mine, a_got, b_mine, b_got), [((16, PADDED, 128), bf16)]
    )
    parts = lax.all_to_all(
        parts, "dp", split_axis=0, concat_axis=0, tiled=True,
        axis_index_groups=[[2 * m + c for m in range(16)] for c in range(2)],
    )
    (parts,) = small_call(owned_sum_kernel, "owned_sum", (parts,), [((8, PADDED, 128), bf16)])
    parts = lax.all_to_all(parts, "space", split_axis=0, concat_axis=0, tiled=True)
    (total,) = small_call(last_sum_kernel, "last_sum", (parts,), [((SLOTS, 1, EMB), jnp.float32)])
    return total.reshape(1, SLOTS, EMB)


def on_device(clip_qkv, temporal_qk, proj_weight, caption_tokens, caption_lens, positive):
    dp = lax.axis_index("dp")
    space = lax.axis_index("space")
    x, y = space >> 1, space & 1
    place = jnp.stack([dp >> 4, dp & 1, x, y, (dp >> 1) & 7]).astype(jnp.int32)
    lens_row = jnp.broadcast_to(
        caption_lens.astype(jnp.bfloat16)[:, None, None], (1, PADDED - SLOTS, EMB)
    )
    caps = jnp.concatenate([caption_tokens, lens_row], axis=1)
    blocks = clip_qkv.reshape(8, 2, LOCAL, 3 * FEATURES)
    blocks = lax.all_to_all(blocks, "space", split_axis=0, concat_axis=0, tiled=True)
    time = time_weights(temporal_qk[0])
    caps = doubled(caps, 16)
    caps = doubled(caps, 8)
    caps = doubled(caps, 4)
    caps = doubled(caps, 2)
    other = flip(caps, 1)
    attended = spatial_attention(blocks)
    spatial = lax.all_to_all(held(attended), "space", split_axis=0, concat_axis=0, tiled=True)
    video, stats, grad, lens = token_part(
        place, spatial, time, proj_weight, caps, other
    )
    stats = lax.all_to_all(stats, "space", split_axis=0, concat_axis=0, tiled=True)
    send, keep, loss = coef_part(place, positive, stats, lens, grad)
    caption_grad = reduce_gradient(place, send, keep)
    return video[None], caption_grad, loss.reshape(1)


def solution(mesh):
    return jax.shard_map(
        on_device,
        mesh=mesh,
        in_specs=(
            P("dp", None, "space", None),
            P("dp", None, "space", None),
            P(),
            P("dp", None, None),
            P("dp"),
            P("dp"),
        ),
        out_specs=(P("dp", None, "space", None), P("dp", None, None), P("dp")),
        check_vma=False,
    )
```

time: 214 us -> 210 us (0.981)
  local copies, waits for them, and re-layouts: 19.7 us -> 2.06 us
  starting transfers between devices: 31.3 us -> 48.4 us
  between operations: 15.5 us -> 2.09 us
  Pallas kernels: 18.4 us -> 26.9 us
  waiting for transfers between devices: 95.7 us -> 101 us
  blocking collectives: 32.4 us -> 29.6 us
    all_to_all x1 -> x2, starting transfers between devices: 5.25 us -> 25.9 us  [the longest x1 20.5 us: on_device(): lax.all_to_all(held(attended), 'space', split_axis=0, concat_axis=0, tile...]
    all_to_all x1 -> x2, waiting for transfers between devices: 2.13 us -> 17 us  [the longest x1 17 us: on_device(): lax.all_to_all(held(attended), 'space', split_axis=0, concat_axis=0, tile...]
    all_gather x1 -> x0, waiting for transfers between devices: 13.7 us -> none  [gather_captions(): mine = lax.all_gather(caps, 'dp', axis=0, axis_index_groups=groups)]
    unnamed x24 -> x6, local copies, waits for them, and re-layouts: 12.8 us -> 1.97 us
    pallas_call x5 -> x8, Pallas kernels: 17.3 us -> 25 us  [the longest x1 10.3 us: token_part(): pl.pallas_call(token_kernel, in_specs=[SMEM, VMEM, VMEM, FAR_OFF, FAR_OFF...]
    ppermute x14 -> x5, starting transfers between devices: 19.1 us -> 15.1 us  [flip(): return lax.ppermute(value, 'dp', [(i, i ^ bit) for i in range(32)])]
    ppermute x14 -> x5, waiting for transfers between devices: 56.8 us -> 60.1 us  [flip(): return lax.ppermute(value, 'dp', [(i, i ^ bit) for i in range(32)])]
    dynamic_slice x1 -> x0, local copies, waits for them, and re-layouts: 3.16 us -> none  [frames_of(): lax.dynamic_slice_in_dim(clip_qkv[0], owner * 2, 2, axis=0, allow_negativ...]
  transfers between devices with their start and end apart: 22 -> 13, of which waited for: 16 -> 10; matrix products, arithmetic and copies ran while one was open for 3% -> 0% of each run, Pallas kernels for 4% -> 6%
where the time goes in v5:
time: 210 us
  waiting for transfers between devices  101 us (48%)
  starting transfers between devices  48.4 us (23%)
  blocking collectives  29.6 us (14%)
  Pallas kernels  26.9 us (13%)
    ppermute x5, waiting for transfers between devices, flip(): return lax.ppermute(value, 'dp', [(i, i ^ bit) for i in range(32)])  60.1 us
    all_to_all x1, starting transfers between devices, on_device(): lax.all_to_all(held(attended), 'space', split_axis=0, concat_axis=0, tile...  20.5 us
    all_to_all x1, blocking collectives, reduce_gradient(): lax.all_to_all(parts, 'dp', split_axis=0, concat_axis=0, tiled=True, axis...  20.2 us
    all_to_all x1, waiting for transfers between devices, on_device(): lax.all_to_all(held(attended), 'space', split_axis=0, concat_axis=0, tile...  17 us
    ppermute x5, starting transfers between devices, flip(): return lax.ppermute(value, 'dp', [(i, i ^ bit) for i in range(32)])  15.1 us
    pallas_call x1, Pallas kernels, token_part(): pl.pallas_call(token_kernel, in_specs=[SMEM, VMEM, VMEM, FAR_OFF, FAR_OFF...  10.3 us
    all_to_all x1, blocking collectives, reduce_gradient(): lax.all_to_all(parts, 'space', split_axis=0, concat_axis=0, tiled=True)  9.43 us
    ppermute x1, waiting for transfers between devices, reduce_gradient(): a_got = lax.ppermute(a_send, 'space', one)  7.73 us
  transfers between devices with their start and end apart: 13, of which 10 were waited for; matrix products, arithmetic and copies ran while one was open for 0% of the time, Pallas kernels for 6%

profile of v5, /device:TPU:32, one launch (start us, length us, event | category | flops | bytes accessed | tf_op | source)
XLA Modules:
  0.0 209.7 jit_solution(1739693143176329322)
XLA Ops:
  0.6 5.5 %all-to-all-start = ((bf16[8,2,32,4992]{3,2,1,0:T(8,128)(2,1)}), bf16[8,2,32,4992]{3,2,1,0:T(8,128)(2,1)}, u32[]{:S(2)}, u32[]{:S(2)}) async-start(bf16[8,2,32,4992]{3,2,1,0:T(8,128)(2,1)} %bitcast.23), calls=%async_computation | async-start | bytes 10223616 | tf_op jit(solution)/shard_map/all_to_all | solution.py:399
  6.8 3.0 %collective-permute-start = (bf16[1,80,512]{2,1,0:T(8,128)(2,1)S(1)}, bf16[1,80,512]{2,1,0:T(8,128)(2,1)S(1)}, u32[]{:S(2)}, u32[]{:S(2)}) collective-permute-start(bf16[1,80,512]{2,1,0:T(8,128)(2,1)S(1)} %concatenate.3.refs_0_), channel_id=1, source_target_pairs={{0,128},{8,136},{16,144},{24,152},{32,160},{40,168},{48,176},{56,1... | collective-permute-start | bytes 245768 | tf_op jit(solution)/shard_map/ppermute | solution.py:125
  9.8 43.5 %collective-permute-done.refs_1_ = bf16[1,80,512]{2,1,0:T(8,128)(2,1)S(1)} collective-permute-done((bf16[1,80,512]{2,1,0:T(8,128)(2,1)S(1)}, bf16[1,80,512]{2,1,0:T(8,128)(2,1)S(1)}, u32[]{:S(2)}, u32[]{:S(2)}) %collective-permute-start) | collective-permute-done | bytes 81952 | tf_op jit(solution)/shard_map/ppermute | solution.py:125
  53.3 6.4 %collective-permute-start.1 = (bf16[2,80,512]{2,1,0:T(8,128)(2,1)S(1)}, bf16[2,80,512]{2,1,0:T(8,128)(2,1)S(1)}, u32[]{:S(2)}, u32[]{:S(2)}) collective-permute-start(bf16[2,80,512]{2,1,0:T(8,128)(2,1)S(1)} %bitcast.21), channel_id=1, source_target_pairs={{0,64},{8,72},{16,80},{24,88},{32,96},{40,104},{48,112},{56,120},{... | collective-permute-start | bytes 491528 | tf_op jit(solution)/shard_map/ppermute | solution.py:125
  59.7 5.1 %collective-permute-done.1.refs_1_ = bf16[2,80,512]{2,1,0:T(8,128)(2,1)S(1)} collective-permute-done((bf16[2,80,512]{2,1,0:T(8,128)(2,1)S(1)}, bf16[2,80,512]{2,1,0:T(8,128)(2,1)S(1)}, u32[]{:S(2)}, u32[]{:S(2)}) %collective-permute-start.1) | collective-permute-done | bytes 163872 | tf_op jit(solution)/shard_map/ppermute | solution.py:125
  64.8 2.8 %collective-permute-start.2 = (bf16[4,80,512]{2,1,0:T(8,128)(2,1)S(1)}, bf16[4,80,512]{2,1,0:T(8,128)(2,1)S(1)}, u32[]{:S(2)}, u32[]{:S(2)}) collective-permute-start(bf16[4,80,512]{2,1,0:T(8,128)(2,1)S(1)} %bitcast.17), channel_id=1, source_target_pairs={{0,32},{8,40},{16,48},{24,56},{32,0},{40,8},{48,16},{56,24},{64,96... | collective-permute-start | bytes 983048 | tf_op jit(solution)/shard_map/ppermute | solution.py:125
  67.6 11.5 %collective-permute-done.2.refs_1_ = bf16[4,80,512]{2,1,0:T(8,128)(2,1)S(1)} collective-permute-done((bf16[4,80,512]{2,1,0:T(8,128)(2,1)S(1)}, bf16[4,80,512]{2,1,0:T(8,128)(2,1)S(1)}, u32[]{:S(2)}, u32[]{:S(2)}) %collective-permute-start.2) | collective-permute-done | bytes 327712 | tf_op jit(solution)/shard_map/ppermute | solution.py:125
  79.1 2.6 %collective-permute-start.3 = (bf16[8,80,512]{2,1,0:T(8,128)(2,1)S(1)}, bf16[8,80,512]{2,1,0:T(8,128)(2,1)S(1)}, u32[]{:S(2)}, u32[]{:S(2)}) collective-permute-start(bf16[8,80,512]{2,1,0:T(8,128)(2,1)S(1)} %bitcast.15), channel_id=1, source_target_pairs={{0,16},{8,24},{16,0},{24,8},{32,48},{40,56},{48,32},{56,40},{64,80... | collective-permute-start | bytes 1966088 | tf_op jit(solution)/shard_map/ppermute | solution.py:125
  81.7 5.7 %spatial_attention.1 = bf16[8,2,32,1664]{3,2,1,0:T(8,128)(2,1)} custom-call(bf16[8,2,32,4992]{3,2,1,0:T(8,128)(2,1)} %all-to-all-done.qkv_ref), custom_call_target="tpu_custom_call" | custom-call | flops 872415232 | bytes 6815744 | tf_op jit(solution)/shard_map/spatial_attention/pallas_call | solution.py:59
  87.4 20.5 %all-to-all-start.1 = ((bf16[8,2,32,1664]{3,2,1,0:T(8,128)(2,1)}), bf16[8,2,32,1664]{3,2,1,0:T(8,128)(2,1)}, u32[]{:S(2)}, u32[]{:S(2)}) async-start(bf16[8,2,32,1664]{3,2,1,0:T(8,128)(2,1)} %spatial_attention.1), calls=%async_computation.1 | async-start | bytes 3407872 | tf_op jit(solution)/shard_map/all_to_all | solution.py:407
  108.0 0.3 collective-permute-start.4
  108.4 5.9 %time_weights.1.time_ref = bf16[13,2,256,256]{3,2,1,0:T(8,128)(2,1)} custom-call(bf16[16,32,3328]{2,1,0:T(8,128)(2,1)} %bitcast.24), custom_call_target="tpu_custom_call" | custom-call | flops 436207616 | bytes 7000000 | tf_op jit(solution)/shard_map/time_weights/pallas_call | solution.py:103
  114.3 17.0 %all-to-all-done.1.value = bf16[8,2,32,1664]{3,2,1,0:T(8,128)(2,1)} async-done(((bf16[8,2,32,1664]{3,2,1,0:T(8,128)(2,1)}), bf16[8,2,32,1664]{3,2,1,0:T(8,128)(2,1)}, u32[]{:S(2)}, u32[]{:S(2)}) %all-to-all-start.1) | async-done | bytes 1703968 | tf_op jit(solution)/shard_map/all_to_all | solution.py:407
  131.4 2.0 copy-done
  133.3 10.3 %token_part.1 = (bf16[16,32,512]{2,1,0:T(8,128)(2,1)}, f32[8,2,32,128]{3,2,1,0:T(8,128)}, bf16[32,80,512]{2,1,0:T(8,128)(2,1)}, f32[32,128]{1,0:T(8,128)S(1)}) custom-call(s32[5]{0:T(128)S(1)} %stack.23.place_ref, bf16[8,2,32,1664]{3,2,1,0:T(8,128)(2,1)} %all-to-all-done.1.value, bf16[13,2,256,256]{3,2,1,0:T(8,128)(2,1)S(1)} %copy-done, ...), custom_call_target="tpu_custom_call" | custom-call | flops 4499999744 | bytes 12000000 | tf_op jit(solution)/shard_map/token_part/pallas_call | solution.py:214
  143.6 3.4 %all-to-all-start.2 = ((f32[8,2,32,128]{3,2,1,0:T(8,128)}), f32[8,2,32,128]{3,2,1,0:T(8,128)S(1)}, u32[]{:S(2)}, u32[]{:S(2)}) async-start(f32[8,2,32,128]{3,2,1,0:T(8,128)} %get-tuple-element.19), calls=%async_computation.2 | async-start | bytes 524288 | tf_op jit(solution)/shard_map/all_to_all | solution.py:411
  147.7 6.2 %all-to-all-done.2.stats_ref = f32[8,2,32,128]{3,2,1,0:T(8,128)S(1)} async-done(((f32[8,2,32,128]{3,2,1,0:T(8,128)}), f32[8,2,32,128]{3,2,1,0:T(8,128)S(1)}, u32[]{:S(2)}, u32[]{:S(2)}) %all-to-all-start.2) | async-done | bytes 262176 | tf_op jit(solution)/shard_map/all_to_all | solution.py:411
  153.9 2.9 %coef_part.1 = (bf16[16,80,512]{2,1,0:T(8,128)(2,1)S(1)}, bf16[16,80,512]{2,1,0:T(8,128)(2,1)S(1)}, f32[1,1]{1,0:T(1,128)}) custom-call(s32[5]{0:T(128)S(1)} %stack.23.place_ref, s32[1]{0:T(128)S(6)} %copy.10.pos_ref, f32[8,2,32,128]{3,2,1,0:T(8,128)S(1)} %all-to-all-done.2.stats_ref, f32[32,128]{1,0:T(8,128)S(1)} %get-tuple-element.20.lens_ref, ...), custom_call_target="tpu_custom_call" | custom-call | flops 4000000 | bytes 6000000 | tf_op jit(solution)/shard_map/coef_part/pallas_call | solution.py:287
  156.8 0.1 collective-permute-start.5
  156.9 3.0 %collective-permute-done.5.got_ref = bf16[16,80,512]{2,1,0:T(8,128)(2,1)S(1)} collective-permute-done((bf16[16,80,512]{2,1,0:T(8,128)(2,1)S(1)}, bf16[16,80,512]{2,1,0:T(8,128)(2,1)S(1)}, u32[]{:S(2)}, u32[]{:S(2)}) %collective-permute-start.5) | collective-permute-done | bytes 1310752 | tf_op jit(solution)/shard_map/ppermute | solution.py:363
  160.0 0.9 first_sum.1
  160.9 0.4 collective-permute-start.6
  161.2 1.7 collective-permute-start.7
  163.0 7.7 %collective-permute-done.6.a_got = bf16[8,80,256]{2,1,0:T(8,128)(2,1)S(1)} collective-permute-done((bf16[8,80,256]{2,1,0:T(8,128)(2,1)S(1)}, bf16[8,80,256]{2,1,0:T(8,128)(2,1)S(1)}, u32[]{:S(2)}, u32[]{:S(2)}) %collective-permute-start.6) | collective-permute-done | bytes 327712 | tf_op jit(solution)/shard_map/ppermute | solution.py:368
  170.7 1.3 collective-permute-done.7.b_got
  172.0 0.2 second_sum.1
  172.2 1.7 collective-permute-start.8
  173.9 4.9 %collective-permute-done.8.a_got = bf16[8,80,128]{2,1,0:T(8,128)(2,1)S(1)} collective-permute-done((bf16[8,80,128]{2,1,0:T(8,128)(2,1)S(1)}, bf16[8,80,128]{2,1,0:T(8,128)(2,1)S(1)}, u32[]{:S(2)}, u32[]{:S(2)}) %collective-permute-start.8) | collective-permute-done | bytes 163872 | tf_op jit(solution)/shard_map/ppermute | solution.py:374
  178.8 0.4 collective-permute-done.9.b_got
  179.3 20.2 %all_to_all.25.parts = bf16[16,80,128]{2,1,0:T(8,128)(2,1)S(1)} all-to-all(bf16[16,80,128]{2,1,0:T(8,128)(2,1)S(1)} %third_sum.1), channel_id=1, replica_groups={{0,16,32,48,64,80,96,112,128,144,160,176,192,208,224,240},{8,24,40,56,7..., dimensions={0} | all-to-all | bytes 655360 | tf_op jit(solution)/shard_map/all_to_all | solution.py:379
  199.5 9.4 %all_to_all.26.parts = bf16[8,80,128]{2,1,0:T(8,128)(2,1)S(1)} all-to-all(bf16[8,80,128]{2,1,0:T(8,128)(2,1)S(1)} %owned_sum.1), channel_id=1, replica_groups=mesh['dp'=32,'space'=8] {'space'}, dimensions={0} | all-to-all | bytes 327680 | tf_op jit(solution)/shard_map/all_to_all | solution.py:384
  208.9 0.8 last_sum.1
  (17 shorter events, 0.4 us)
Async XLA Ops:
  0.6 6.1 %copy-start.2 = (bf16[1,77,512]{2,1,0:T(8,128)(2,1)S(1)}, bf16[1,77,512]{2,1,0:T(8,128)(2,1)}, u32[]{:S(2)}) copy-start(bf16[1,77,512]{2,1,0:T(8,128)(2,1)} %param.9) | copy-start | bytes 236548
  0.6 81.1 %all-to-all-start = ((bf16[8,2,32,4992]{3,2,1,0:T(8,128)(2,1)}), bf16[8,2,32,4992]{3,2,1,0:T(8,128)(2,1)}, u32[]{:S(2)}, u32[]{:S(2)}) async-start(bf16[8,2,32,4992]{3,2,1,0:T(8,128)(2,1)} %bitcast.23), calls=%async_computation | async-start | bytes 10223616 | tf_op jit(solution)/shard_map/all_to_all | solution.py:399
  6.8 46.5 %collective-permute-start = (bf16[1,80,512]{2,1,0:T(8,128)(2,1)S(1)}, bf16[1,80,512]{2,1,0:T(8,128)(2,1)S(1)}, u32[]{:S(2)}, u32[]{:S(2)}) collective-permute-start(bf16[1,80,512]{2,1,0:T(8,128)(2,1)S(1)} %concatenate.3.refs_0_), channel_id=1, source_target_pairs={{0,128},{8,136},{16,144},{24,152},{32,160},{40,168},{48,176},{56,1... | collective-permute-start | bytes 245768 | tf_op jit(solution)/shard_map/ppermute | solution.py:125
  53.3 11.4 %collective-permute-start.1 = (bf16[2,80,512]{2,1,0:T(8,128)(2,1)S(1)}, bf16[2,80,512]{2,1,0:T(8,128)(2,1)S(1)}, u32[]{:S(2)}, u32[]{:S(2)}) collective-permute-start(bf16[2,80,512]{2,1,0:T(8,128)(2,1)S(1)} %bitcast.21), channel_id=1, source_target_pairs={{0,64},{8,72},{16,80},{24,88},{32,96},{40,104},{48,112},{56,120},{... | collective-permute-start | bytes 491528 | tf_op jit(solution)/shard_map/ppermute | solution.py:125
  64.8 14.3 %collective-permute-start.2 = (bf16[4,80,512]{2,1,0:T(8,128)(2,1)S(1)}, bf16[4,80,512]{2,1,0:T(8,128)(2,1)S(1)}, u32[]{:S(2)}, u32[]{:S(2)}) collective-permute-start(bf16[4,80,512]{2,1,0:T(8,128)(2,1)S(1)} %bitcast.17), channel_id=1, source_target_pairs={{0,32},{8,40},{16,48},{24,56},{32,0},{40,8},{48,16},{56,24},{64,96... | collective-permute-start | bytes 983048 | tf_op jit(solution)/shard_map/ppermute | solution.py:125
  79.1 28.8 %collective-permute-start.3 = (bf16[8,80,512]{2,1,0:T(8,128)(2,1)S(1)}, bf16[8,80,512]{2,1,0:T(8,128)(2,1)S(1)}, u32[]{:S(2)}, u32[]{:S(2)}) collective-permute-start(bf16[8,80,512]{2,1,0:T(8,128)(2,1)S(1)} %bitcast.15), channel_id=1, source_target_pairs={{0,16},{8,24},{16,0},{24,8},{32,48},{40,56},{48,32},{56,40},{64,80... | collective-permute-start | bytes 1966088 | tf_op jit(solution)/shard_map/ppermute | solution.py:125
  87.4 43.9 %all-to-all-start.1 = ((bf16[8,2,32,1664]{3,2,1,0:T(8,128)(2,1)}), bf16[8,2,32,1664]{3,2,1,0:T(8,128)(2,1)}, u32[]{:S(2)}, u32[]{:S(2)}) async-start(bf16[8,2,32,1664]{3,2,1,0:T(8,128)(2,1)} %spatial_attention.1), calls=%async_computation.1 | async-start | bytes 3407872 | tf_op jit(solution)/shard_map/all_to_all | solution.py:407
  108.0 6.3 %copy-start.1 = (bf16[2,8,80,512]{3,2,1,0:T(8,128)(2,1)}, bf16[2,8,80,512]{3,2,1,0:T(8,128)(2,1)S(1)}, u32[]{:S(2)}) copy-start(bf16[2,8,80,512]{3,2,1,0:T(8,128)(2,1)S(1)} %join.7) | copy-start | bytes 3932164
  108.0 6.3 %collective-permute-start.4 = (bf16[16,80,512]{2,1,0:T(8,128)(2,1)S(1)}, bf16[16,80,512]{2,1,0:T(8,128)(2,1)S(1)}, u32[]{:S(2)}, u32[]{:S(2)}) collective-permute-start(bf16[16,80,512]{2,1,0:T(8,128)(2,1)S(1)} %bitcast.19), channel_id=1, source_target_pairs={{0,8},{8,0},{16,24},{24,16},{32,40},{40,32},{48,56},{56,48},{64,72... | collective-permute-start | bytes 3932168 | tf_op jit(solution)/shard_map/ppermute | solution.py:125
  131.4 2.0 copy-start
  143.6 10.3 %all-to-all-start.2 = ((f32[8,2,32,128]{3,2,1,0:T(8,128)}), f32[8,2,32,128]{3,2,1,0:T(8,128)S(1)}, u32[]{:S(2)}, u32[]{:S(2)}) async-start(f32[8,2,32,128]{3,2,1,0:T(8,128)} %get-tuple-element.19), calls=%async_computation.2 | async-start | bytes 524288 | tf_op jit(solution)/shard_map/all_to_all | solution.py:411
  156.8 3.1 %collective-permute-start.5 = (bf16[16,80,512]{2,1,0:T(8,128)(2,1)S(1)}, bf16[16,80,512]{2,1,0:T(8,128)(2,1)S(1)}, u32[]{:S(2)}, u32[]{:S(2)}) collective-permute-start(bf16[16,80,512]{2,1,0:T(8,128)(2,1)S(1)} %get-tuple-element.23), channel_id=1, source_target_pairs={{0,8},{8,0},{16,24},{24,16},{32,40},{40,32},{48,56},{56,48},{64,72... | collective-permute-start | bytes 3932168 | tf_op jit(solution)/shard_map/ppermute | solution.py:363
  160.9 9.8 %collective-permute-start.6 = (bf16[8,80,256]{2,1,0:T(8,128)(2,1)S(1)}, bf16[8,80,256]{2,1,0:T(8,128)(2,1)S(1)}, u32[]{:S(2)}, u32[]{:S(2)}) collective-permute-start(bf16[8,80,256]{2,1,0:T(8,128)(2,1)S(1)} %get-tuple-element.25), channel_id=1, source_target_pairs={{0,2},{1,3},{2,0},{3,1},{4,6},{5,7},{6,4},{7,5},{8,10},{9,11},{10,... | collective-permute-start | bytes 983048 | tf_op jit(solution)/shard_map/ppermute | solution.py:368
  161.2 10.8 %collective-permute-start.7 = (bf16[8,80,256]{2,1,0:T(8,128)(2,1)S(1)}, bf16[8,80,256]{2,1,0:T(8,128)(2,1)S(1)}, u32[]{:S(2)}, u32[]{:S(2)}) collective-permute-start(bf16[8,80,256]{2,1,0:T(8,128)(2,1)S(1)} %get-tuple-element.27), channel_id=1, source_target_pairs={{0,6},{1,7},{2,4},{3,5},{4,2},{5,3},{6,0},{7,1},{8,14},{9,15},{10,... | collective-permute-start | bytes 983048 | tf_op jit(solution)/shard_map/ppermute | solution.py:369
  172.2 6.6 %collective-permute-start.8 = (bf16[8,80,128]{2,1,0:T(8,128)(2,1)S(1)}, bf16[8,80,128]{2,1,0:T(8,128)(2,1)S(1)}, u32[]{:S(2)}, u32[]{:S(2)}) collective-permute-start(bf16[8,80,128]{2,1,0:T(8,128)(2,1)S(1)} %get-tuple-element.29), channel_id=1, source_target_pairs={{0,6},{1,7},{2,4},{3,5},{4,2},{5,3},{6,0},{7,1},{8,14},{9,15},{10,... | collective-permute-start | bytes 491528 | tf_op jit(solution)/shard_map/ppermute | solution.py:374
  173.9 5.3 %collective-permute-start.9 = (bf16[8,80,128]{2,1,0:T(8,128)(2,1)S(1)}, bf16[8,80,128]{2,1,0:T(8,128)(2,1)S(1)}, u32[]{:S(2)}, u32[]{:S(2)}) collective-permute-start(bf16[8,80,128]{2,1,0:T(8,128)(2,1)S(1)} %get-tuple-element.31), channel_id=1, source_target_pairs={{0,2},{1,3},{2,0},{3,1},{4,6},{5,7},{6,4},{7,5},{8,10},{9,11},{10,... | collective-permute-start | bytes 491528 | tf_op jit(solution)/shard_map/ppermute | solution.py:375

commit v6 on v5

--- a/solution.py
+++ b/solution.py
@@ -1,3 +1,4 @@
+import functools
 import math
 
 import jax
@@ -41,9 +42,13 @@
 SPLIT = 7
 
 
-def spatial_kernel(qkv_ref, out_ref):
+HALF = LOCAL // 2
+
+
+def spatial_kernel(half, qkv_ref, out_ref):
+    part = pl.ds(half * HALF, HALF)
     for h in range(HEADS):
-        q = qkv_ref[:, 0, :, pl.ds(h * HD, HD)].reshape(PATCHES, HD)
+        q = qkv_ref[:, 0, part, pl.ds(h * HD, HD)].reshape(PATCHES // 2, HD)
         k = qkv_ref[:, 0, :, pl.ds(FEATURES + h * HD, HD)].reshape(PATCHES, HD)
         v = qkv_ref[:, 0, :, pl.ds(2 * FEATURES + h * HD, HD)].reshape(PATCHES, HD)
         s = nt(q, k)
@@ -52,21 +57,21 @@
         total = jnp.sum(e, axis=-1, keepdims=True)
         o = jnp.dot(e.astype(jnp.bfloat16), v, preferred_element_type=jnp.float32)
         o = (o * (1.0 / total)).astype(jnp.bfloat16)
-        out_ref[:, 0, :, pl.ds(h * HD, HD)] = o.reshape(8, LOCAL, HD)
-
-
-def spatial_attention(blocks):
+        out_ref[:, 0, :, pl.ds(h * HD, HD)] = o.reshape(8, HALF, HD)
+
+
+def spatial_attention(blocks, half):
     return pl.pallas_call(
-        spatial_kernel,
+        functools.partial(spatial_kernel, half),
         grid=(2,),
         in_specs=[pl.BlockSpec((8, 1, LOCAL, 3 * FEATURES), lambda f: (0, f, 0, 0))],
-        out_specs=pl.BlockSpec((8, 1, LOCAL, FEATURES), lambda f: (0, f, 0, 0)),
-        out_shape=pltpu.HBM((8, 2, LOCAL, FEATURES), jnp.bfloat16),
+        out_specs=pl.BlockSpec((8, 1, HALF, FEATURES), lambda f: (0, f, 0, 0)),
+        out_shape=pltpu.HBM((8, 2, HALF, FEATURES), jnp.bfloat16),
         compiler_params=GRANT,
         cost_estimate=pl.CostEstimate(
-            flops=8 * HEADS * PATCHES * PATCHES * HD,
+            flops=4 * HEADS * PATCHES * PATCHES * HD,
             bytes_accessed=2 * PATCHES * 4 * FEATURES * 2,
-            transcendentals=2 * HEADS * PATCHES * PATCHES,
+            transcendentals=HEADS * PATCHES * PATCHES,
         ),
         name="spatial_attention",
     )(blocks)
@@ -75,7 +80,7 @@
 ROWS = FRAMES * 16
 
 
-def time_kernel(tqk_ref, out_ref, tqk, weights, load_sem, sems):
+def time_kernel(tqk_ref, low_ref, high_ref, tqk, weights, load_sem, sems):
     load = pltpu.make_async_copy(tqk_ref, tqk, load_sem)
     load.start()
     load.wait()
@@ -83,8 +88,8 @@
     c = lax.broadcasted_iota(jnp.int32, (ROWS, ROWS), 1)
     bias = jnp.where((r & 15) == (c & 15), 0.0, -1e30).astype(jnp.float32)
     stores = []
-    for h in range(HEADS):
-        for g in range(LOCAL // 16):
+    for g, out_ref in enumerate((low_ref, high_ref)):
+        for h in range(HEADS):
             part = pl.ds(g * 16, 16)
             q = tqk[:, part, pl.ds(h * HD, HD)].reshape(ROWS, HD)
             k = tqk[:, part, pl.ds(FEATURES + h * HD, HD)].reshape(ROWS, HD)
@@ -92,8 +97,8 @@
             m = jnp.max(s, axis=-1, keepdims=True)
             e = jnp.exp2((s - m) * SCORE_LOG2)
             total = jnp.sum(e, axis=-1, keepdims=True)
-            weights[h, g] = (e * (1.0 / total)).astype(jnp.bfloat16)
-        stores.append(pltpu.make_async_copy(weights.at[h], out_ref.at[h], sems.at[h]))
+            weights[g, h] = (e * (1.0 / total)).astype(jnp.bfloat16)
+        stores.append(pltpu.make_async_copy(weights.at[g], out_ref, sems.at[g]))
         stores[-1].start()
     for store in stores:
         store.wait()
@@ -103,13 +108,13 @@
     return pl.pallas_call(
         time_kernel,
         in_specs=[FAR_OFF],
-        out_specs=FAR_OFF,
-        out_shape=pltpu.HBM((HEADS, 2, ROWS, ROWS), jnp.bfloat16),
+        out_specs=[FAR_OFF] * 2,
+        out_shape=[pltpu.HBM((HEADS, ROWS, ROWS), jnp.bfloat16)] * 2,
         scratch_shapes=[
             pltpu.VMEM((FRAMES, LOCAL, 2 * FEATURES), jnp.bfloat16),
-            pltpu.VMEM((HEADS, 2, ROWS, ROWS), jnp.bfloat16),
+            pltpu.VMEM((2, HEADS, ROWS, ROWS), jnp.bfloat16),
             pltpu.SemaphoreType.DMA,
-            pltpu.SemaphoreType.DMA((HEADS,)),
+            pltpu.SemaphoreType.DMA((2,)),
         ],
         compiler_params=GRANT,
         cost_estimate=pl.CostEstimate(
@@ -130,112 +135,183 @@
     refs[-1][1] = refs[1][...]
 
 
-def doubled(value, bit, *behind):
+def flip_y(value):
+    pairs = [(i * 8 + s, (i ^ 16) * 8 + (s ^ 1)) for i in range(32) for s in range(8)]
+    return lax.ppermute(value, ("dp", "space"), pairs)
+
+
+def doubled(value, other):
     both = pl.pallas_call(
         join_kernel,
-        in_specs=[VMEM] * 2 + [ANY] * len(behind),
+        in_specs=[VMEM] * 2,
         out_specs=VMEM,
         out_shape=jax.ShapeDtypeStruct((2,) + value.shape, value.dtype),
         compiler_params=pltpu.CompilerParams(vmem_limit_bytes=8 * MIB),
         cost_estimate=pl.CostEstimate(flops=0, bytes_accessed=1_000_000, transcendentals=0),
         name="join",
-    )(value, flip(value, bit), *behind)
+    )(value, other)
     return both.reshape((-1,) + value.shape[1:])
 
 
+GROUP = 8
+
+
 def token_kernel(
-    place_ref, value, time_ref, proj_ref, mine_ref, other_ref,
-    emb_ref, stats_ref, grad_ref, lens_ref,
-    proj, mine, comb, video, grads, sems, grad_sems,
+    half, place_ref, value, time_ref, proj_ref, mine_ref, other_ref, *refs
 ):
+    if half == 0:
+        emb_ref, stats_ref, grad_ref, proj, caps, comb, video, grads, sems, grad_sems = refs
+    else:
+        (
+            _, old_stats, old_ref, emb_ref, all_stats_ref, grad_ref, lens_ref,
+            proj, caps, comb, video, grads, sems, grad_sems, olds, old_sems, stats_ref,
+        ) = refs
+        old_loads = [
+            pltpu.make_async_copy(
+                old_ref.at[pl.ds(i * GROUP, GROUP)], olds.at[pl.ds(i * GROUP, GROUP)], old_sems.at[i]
+            )
+            for i in range(CAPTIONS // GROUP)
+        ]
     proj_load = pltpu.make_async_copy(proj_ref, proj, sems.at[0])
-    mine_load = pltpu.make_async_copy(mine_ref, mine, sems.at[1])
-    proj_load.start()
-    mine_load.start()
+    cap_loads = [
+        pltpu.make_async_copy(ref, caps.at[i], sems.at[1 + i])
+        for i, ref in enumerate((mine_ref, other_ref))
+    ]
+    for load in (proj_load, *cap_loads):
+        load.start()
+    if half == 1:
+        for load in old_loads:
+            load.start()
     for h in range(HEADS):
         cols = pl.ds(h * HD, HD)
-        for g in range(LOCAL // 16):
-            part = pl.ds(g * 16, 16)
-            v = value[:, :, part, cols].reshape(ROWS, HD)
-            o = jnp.dot(time_ref[h, g], v, preferred_element_type=jnp.float32)
-            o = (v.astype(jnp.float32) + o).astype(jnp.bfloat16)
-            comb[:, part, cols] = o.reshape(FRAMES, 16, HD)
-    tokens = FRAMES * LOCAL
+        v = value[:, :, :, cols].reshape(ROWS, HD)
+        o = jnp.dot(time_ref[h], v, preferred_element_type=jnp.float32)
+        comb[:, cols] = (v.astype(jnp.float32) + o).astype(jnp.bfloat16)
     proj_load.wait()
-    projected = jnp.dot(
-        comb[...].reshape(tokens, FEATURES), proj[...], preferred_element_type=jnp.float32
-    )
+    projected = jnp.dot(comb[...], proj[...], preferred_element_type=jnp.float32)
     scale = lax.rsqrt(jnp.mean(projected * projected, axis=-1, keepdims=True) + 1e-06)
     emb = (projected * scale).astype(jnp.bfloat16)
-    video[...] = emb.reshape(FRAMES, LOCAL, EMB)
-    emb_store = pltpu.make_async_copy(video, emb_ref, sems.at[2])
+    video[...] = emb.reshape(FRAMES, HALF, EMB)
+    emb_store = pltpu.make_async_copy(
+        video, emb_ref.at[:, pl.ds(half * HALF, HALF)], sems.at[3]
+    )
     emb_store.start()
-    mine_load.wait()
 
     eye = lax.broadcasted_iota(jnp.int32, (PADDED, 128), 0) == lax.broadcasted_iota(
         jnp.int32, (PADDED, 128), 1
     )
+
+    def as_row(col):
+        return jnp.sum(jnp.where(eye, col, 0.0), axis=0, keepdims=True)
+
+    def as_col(row):
+        return jnp.sum(jnp.where(eye, row, 0.0), axis=-1, keepdims=True)
+
     y_hi, core, z = place_ref[0], place_ref[1], place_ref[4]
-    group = 8
     stores = []
-    for i, (ref, c) in enumerate(((mine, core), (other_ref, 1 - core))):
-        for m0 in range(0, CAPTIONS // 2, group):
-            sim = nt(ref[pl.ds(m0, group)].reshape(group * PADDED, EMB), emb)
+    for i in range(2):
+        cap_loads[i].wait()
+        for m0 in range(0, CAPTIONS // 2, GROUP):
+            slot = i * CAPTIONS // 2 + m0
+            block = pl.ds(slot, GROUP)
+            sim = nt(caps[i, pl.ds(m0, GROUP)].reshape(GROUP * PADDED, EMB), emb)
             top = jnp.max(sim, axis=-1, keepdims=True)
+            if half == 1:
+                old_top, old_total = (
+                    jnp.concatenate(
+                        [as_col(old_stats[k, slot + j : slot + j + 1, :]) for j in range(GROUP)], axis=0
+                    )
+                    for k in range(2)
+                )
+                top = jnp.maximum(top, old_top)
+                factor = jnp.exp2((old_top - top) * SHARP_LOG2)
             w = jnp.exp2((sim - top) * SHARP_LOG2)
             total = jnp.sum(w, axis=-1, keepdims=True)
             product = jnp.dot(w.astype(jnp.bfloat16), emb, preferred_element_type=jnp.float32)
-            slot = i * CAPTIONS // 2 + m0
-            grads[pl.ds(slot, group)] = product.astype(jnp.bfloat16).reshape(group, PADDED, EMB)
-            for j in range(group):
-                m = m0 + j
-                flips = (m >> 3 & 1) + (m >> 2 & 1) * 2 + (m >> 1 & 1) * 4
-                at = (y_hi ^ (m & 1)) * 16 + (z ^ flips) * 2 + c
+            if half == 1:
+                total = total + old_total * factor
+                old_loads[slot // GROUP].wait()
+                old = olds[block].reshape(GROUP * PADDED, EMB).astype(jnp.float32)
+                product = product + old * factor
+            grads[block] = product.astype(jnp.bfloat16).reshape(GROUP, PADDED, EMB)
+            if half == 0:
                 stores.append(
                     pltpu.make_async_copy(
-                        grads.at[slot + j], grad_ref.at[at], grad_sems.at[slot + j]
+                        grads.at[block], grad_ref.at[block], grad_sems.at[slot // GROUP]
                     )
                 )
                 stores[-1].start()
+            for j in range(GROUP):
+                m = m0 + j
                 rng = slice(j * PADDED, (j + 1) * PADDED)
-                top_row = jnp.sum(jnp.where(eye, top[rng], 0.0), axis=0, keepdims=True)
-                total_row = jnp.sum(jnp.where(eye, total[rng], 0.0), axis=0, keepdims=True)
-                for k in range(8):
-                    stats_ref[k, 0, pl.ds(at, 1), :] = top_row
-                    stats_ref[k, 1, pl.ds(at, 1), :] = total_row
-                lens_ref[pl.ds(at, 1), :] = ref[m, SLOTS : SLOTS + 1, :128].astype(jnp.float32)
+                if half == 0:
+                    at = slot + j
+                else:
+                    flips = (m >> 3 & 1) + (m >> 2 & 1) * 2 + (m >> 1 & 1) * 4
+                    side = core if i == 0 else 1 - core
+                    at = (y_hi ^ (m & 1)) * 16 + (z ^ flips) * 2 + side
+                    stores.append(
+                        pltpu.make_async_copy(
+                            grads.at[slot + j], grad_ref.at[at], grad_sems.at[slot + j]
+                        )
+                    )
+                    stores[-1].start()
+                    lens_ref[pl.ds(at, 1), :] = caps[i, m, SLOTS : SLOTS + 1, :128].astype(
+                        jnp.float32
+                    )
+                stats_ref[0, pl.ds(at, 1), :] = as_row(top[rng])
+                stats_ref[1, pl.ds(at, 1), :] = as_row(total[rng])
+    if half == 1:
+        for k in range(8):
+            all_stats_ref[k] = stats_ref[...]
     emb_store.wait()
     for store in stores:
         store.wait()
 
 
-def token_part(place, spatial, time, proj_weight, mine, other):
-    bf16 = jnp.bfloat16
+def token_part(half, place, value, time, proj_weight, mine, other, before=()):
+    bf16, f32 = jnp.bfloat16, jnp.float32
+    emb = pltpu.HBM((FRAMES, LOCAL, EMB), bf16)
+    grad = pltpu.HBM((CAPTIONS, PADDED, EMB), bf16)
+    one = jax.ShapeDtypeStruct((2, CAPTIONS, 128), f32)
+    scratch = [
+        pltpu.VMEM((FEATURES, EMB), bf16),
+        pltpu.VMEM((2, CAPTIONS // 2, PADDED, EMB), bf16),
+        pltpu.VMEM((ROWS, FEATURES), bf16),
+        pltpu.VMEM((FRAMES, HALF, EMB), bf16),
+        pltpu.VMEM((CAPTIONS, PADDED, EMB), bf16),
+        pltpu.SemaphoreType.DMA((4,)),
+        pltpu.SemaphoreType.DMA((CAPTIONS,)),
+    ]
+    if half == 0:
+        out_shape, out_specs, more_specs, aliases = [emb, one, grad], [FAR_OFF, VMEM, FAR_OFF], [], {}
+    else:
+        out_shape = [
+            emb,
+            jax.ShapeDtypeStruct((8, 2, CAPTIONS, 128), f32),
+            grad,
+            jax.ShapeDtypeStruct((CAPTIONS, 128), f32),
+        ]
+        out_specs = [FAR_OFF, VMEM, FAR_OFF, VMEM]
+        more_specs, aliases = [FAR_OFF, VMEM, FAR_OFF], {6: 0}
+        scratch += [
+            pltpu.VMEM((CAPTIONS, PADDED, EMB), bf16),
+            pltpu.SemaphoreType.DMA((CAPTIONS // GROUP,)),
+            pltpu.VMEM((2, CAPTIONS, 128), f32),
+        ]
     return pl.pallas_call(
-        token_kernel,
-        in_specs=[SMEM, VMEM, VMEM, FAR_OFF, FAR_OFF, VMEM],
-        out_specs=[FAR_OFF, VMEM, FAR_OFF, VMEM],
-        out_shape=[
-            pltpu.HBM((FRAMES, LOCAL, EMB), bf16),
-            jax.ShapeDtypeStruct((8, 2, CAPTIONS, 128), jnp.float32),
-            pltpu.HBM((CAPTIONS, PADDED, EMB), bf16),
-            jax.ShapeDtypeStruct((CAPTIONS, 128), jnp.float32),
-        ],
-        scratch_shapes=[
-            pltpu.VMEM((FEATURES, EMB), bf16),
-            pltpu.VMEM((CAPTIONS // 2, PADDED, EMB), bf16),
-            pltpu.VMEM((FRAMES, LOCAL, FEATURES), bf16),
-            pltpu.VMEM((FRAMES, LOCAL, EMB), bf16),
-            pltpu.VMEM((CAPTIONS, PADDED, EMB), bf16),
-            pltpu.SemaphoreType.DMA((3,)),
-            pltpu.SemaphoreType.DMA((CAPTIONS,)),
-        ],
-        compiler_params=GRANT,
+        functools.partial(token_kernel, half),
+        in_specs=[SMEM, VMEM, VMEM, FAR_OFF, FAR_OFF, FAR_OFF] + more_specs,
+        out_specs=out_specs,
+        out_shape=out_shape,
+        scratch_shapes=scratch,
+        input_output_aliases=aliases,
+        compiler_params=pltpu.CompilerParams(vmem_limit_bytes=28 * MIB),
         cost_estimate=pl.CostEstimate(
-            flops=4_500_000_000, bytes_accessed=12_000_000, transcendentals=1_300_000
+            flops=2_250_000_000, bytes_accessed=10_000_000, transcendentals=700_000
         ),
         name="token_part",
-    )(place, spatial, time, held(proj_weight), held(mine), other)
+    )(place, value, time, held(proj_weight), held(mine), held(other), *before)
 
 
 def coef_kernel(
@@ -398,15 +474,19 @@
     blocks = clip_qkv.reshape(8, 2, LOCAL, 3 * FEATURES)
     blocks = lax.all_to_all(blocks, "space", split_axis=0, concat_axis=0, tiled=True)
     time = time_weights(temporal_qk[0])
-    caps = doubled(caps, 16)
-    caps = doubled(caps, 8)
-    caps = doubled(caps, 4)
-    caps = doubled(caps, 2)
+    caps = doubled(caps, flip_y(caps))
+    for bit in (8, 4, 2):
+        caps = doubled(caps, flip(caps, bit))
     other = flip(caps, 1)
-    attended = spatial_attention(blocks)
-    spatial = lax.all_to_all(held(attended), "space", split_axis=0, concat_axis=0, tiled=True)
+    values = [
+        lax.all_to_all(
+            held(spatial_attention(blocks, half)), "space", split_axis=0, concat_axis=0, tiled=True
+        )
+        for half in range(2)
+    ]
+    before = token_part(0, place, values[0], time[0], proj_weight, caps, other)
     video, stats, grad, lens = token_part(
-        place, spatial, time, proj_weight, caps, other
+        1, place, values[1], time[1], proj_weight, caps, other, before
     )
     stats = lax.all_to_all(stats, "space", split_axis=0, concat_axis=0, tiled=True)
     send, keep, loss = coef_part(place, positive, stats, lens, grad)

time: 210 us -> 205 us (0.976)
  Pallas kernels: 26.9 us -> 41.2 us
  waiting for transfers between devices: 101 us -> 87.8 us
  starting transfers between devices: 48.4 us -> 37.5 us
  local copies, waits for them, and re-layouts: 2.06 us -> 4.35 us
    ppermute x5 -> x4, waiting for transfers between devices: 60.1 us -> 32.3 us  [flip(): return lax.ppermute(value, 'dp', [(i, i ^ bit) for i in range(32)])]
    all_to_all x1, waiting for transfers between devices: 0.01 us -> 21.6 us  [on_device(): lax.all_to_all(blocks, 'space', split_axis=0, concat_axis=0, tiled=True)]
    pallas_call x7 -> x9, Pallas kernels: 22.1 us -> 36.3 us  [the longest x2 20.8 us: token_part(): pl.pallas_call(functools.partial(token_kernel, half), in_specs=[SMEM, VME...]
    all_to_all x1 -> x2, starting transfers between devices: 20.5 us -> 7.76 us  [on_device(): lax.all_to_all(held(spatial_attention(blocks, half)), 'space', split_axis...]
    all_to_all x1 -> x2, waiting for transfers between devices: 17 us -> 7.83 us  [on_device(): lax.all_to_all(held(spatial_attention(blocks, half)), 'space', split_axis...]
    ppermute x5 -> x4, starting transfers between devices: 15.1 us -> 11.2 us  [flip(): return lax.ppermute(value, 'dp', [(i, i ^ bit) for i in range(32)])]
    ppermute x0 -> x1, starting transfers between devices: none -> 3.55 us  [flip_y(): return lax.ppermute(value, ('dp', 'space'), pairs)]
    ppermute x0 -> x1, waiting for transfers between devices: none -> 2.42 us  [flip_y(): return lax.ppermute(value, ('dp', 'space'), pairs)]
  transfers between devices with their start and end apart: 13 -> 14, of which waited for: 10 -> 12; matrix products, arithmetic and copies ran while one was open for 0% -> 0% of each run, Pallas kernels for 6% -> 11%
where the time goes in v6:
time: 205 us; the launch traced here: 204 us
  waiting for transfers between devices  87.8 us (43%)
  Pallas kernels  41.2 us (20%)
  starting transfers between devices  37.5 us (18%)
  blocking collectives  31.2 us (15%)
  local copies, waits for them, and re-layouts  4.35 us (2%)
  between operations  2.14 us (1%)
    ppermute x4, waiting for transfers between devices, flip(): return lax.ppermute(value, 'dp', [(i, i ^ bit) for i in range(32)])  32.3 us
    all_to_all x1, blocking collectives, reduce_gradient(): lax.all_to_all(parts, 'dp', split_axis=0, concat_axis=0, tiled=True, axis...  21.8 us
    all_to_all x1, waiting for transfers between devices, on_device(): lax.all_to_all(blocks, 'space', split_axis=0, concat_axis=0, tiled=True)  21.6 us
    pallas_call x2, Pallas kernels, token_part(): pl.pallas_call(functools.partial(token_kernel, half), in_specs=[SMEM, VME...  20.8 us
    ppermute x4, starting transfers between devices, flip(): return lax.ppermute(value, 'dp', [(i, i ^ bit) for i in range(32)])  11.2 us
    all_to_all x1, blocking collectives, reduce_gradient(): lax.all_to_all(parts, 'space', split_axis=0, concat_axis=0, tiled=True)  9.43 us
    pallas_call x2, Pallas kernels, spatial_attention(): pl.pallas_call(functools.partial(spatial_kernel, half), grid=(2,), in_spe...  9.13 us
    all_to_all x2, waiting for transfers between devices, on_device(): lax.all_to_all(held(spatial_attention(blocks, half)), 'space', split_axis...  7.83 us
  transfers between devices with their start and end apart: 14, of which 12 were waited for; matrix products, arithmetic and copies ran while one was open for 0% of the time, Pallas kernels for 11%

profile of v6, /device:TPU:32, one launch (start us, length us, event | category | flops | bytes accessed | tf_op | source)
XLA Modules:
  0.0 204.1 jit_solution(9978622575698044188)
XLA Ops:
  0.6 5.5 %all-to-all-start = ((bf16[8,2,32,4992]{3,2,1,0:T(8,128)(2,1)}), bf16[8,2,32,4992]{3,2,1,0:T(8,128)(2,1)}, u32[]{:S(2)}, u32[]{:S(2)}) async-start(bf16[8,2,32,4992]{3,2,1,0:T(8,128)(2,1)} %bitcast.24), calls=%async_computation | async-start | bytes 10223616 | tf_op jit(solution)/shard_map/all_to_all | solution.py:475
  6.8 3.5 %collective-permute-start = (bf16[1,80,512]{2,1,0:T(8,128)(2,1)S(1)}, bf16[1,80,512]{2,1,0:T(8,128)(2,1)S(1)}, u32[]{:S(2)}, u32[]{:S(2)}) collective-permute-start(bf16[1,80,512]{2,1,0:T(8,128)(2,1)S(1)} %concatenate.3.refs_0_), channel_id=1, source_target_pairs={{0,129},{1,128},{2,131},{3,130},{4,133},{5,132},{6,135},{7,134},{8... | collective-permute-start | bytes 245768 | tf_op jit(solution)/shard_map/ppermute | solution.py:140
  10.3 2.4 %collective-permute-done.refs_1_ = bf16[1,80,512]{2,1,0:T(8,128)(2,1)S(1)} collective-permute-done((bf16[1,80,512]{2,1,0:T(8,128)(2,1)S(1)}, bf16[1,80,512]{2,1,0:T(8,128)(2,1)S(1)}, u32[]{:S(2)}, u32[]{:S(2)}) %collective-permute-start) | collective-permute-done | bytes 81952 | tf_op jit(solution)/shard_map/ppermute | solution.py:140
  12.8 6.4 %collective-permute-start.1 = (bf16[2,80,512]{2,1,0:T(8,128)(2,1)S(1)}, bf16[2,80,512]{2,1,0:T(8,128)(2,1)S(1)}, u32[]{:S(2)}, u32[]{:S(2)}) collective-permute-start(bf16[2,80,512]{2,1,0:T(8,128)(2,1)S(1)} %bitcast.22), channel_id=1, source_target_pairs={{0,64},{8,72},{16,80},{24,88},{32,96},{40,104},{48,112},{56,120},{... | collective-permute-start | bytes 491528 | tf_op jit(solution)/shard_map/ppermute | solution.py:130
  19.1 5.5 %collective-permute-done.1.refs_1_ = bf16[2,80,512]{2,1,0:T(8,128)(2,1)S(1)} collective-permute-done((bf16[2,80,512]{2,1,0:T(8,128)(2,1)S(1)}, bf16[2,80,512]{2,1,0:T(8,128)(2,1)S(1)}, u32[]{:S(2)}, u32[]{:S(2)}) %collective-permute-start.1) | collective-permute-done | bytes 163872 | tf_op jit(solution)/shard_map/ppermute | solution.py:130
  24.7 2.4 %collective-permute-start.2 = (bf16[4,80,512]{2,1,0:T(8,128)(2,1)S(1)}, bf16[4,80,512]{2,1,0:T(8,128)(2,1)S(1)}, u32[]{:S(2)}, u32[]{:S(2)}) collective-permute-start(bf16[4,80,512]{2,1,0:T(8,128)(2,1)S(1)} %bitcast.20), channel_id=1, source_target_pairs={{0,32},{8,40},{16,48},{24,56},{32,0},{40,8},{48,16},{56,24},{64,96... | collective-permute-start | bytes 983048 | tf_op jit(solution)/shard_map/ppermute | solution.py:130
  27.0 11.8 %collective-permute-done.2.refs_1_ = bf16[4,80,512]{2,1,0:T(8,128)(2,1)S(1)} collective-permute-done((bf16[4,80,512]{2,1,0:T(8,128)(2,1)S(1)}, bf16[4,80,512]{2,1,0:T(8,128)(2,1)S(1)}, u32[]{:S(2)}, u32[]{:S(2)}) %collective-permute-start.2) | collective-permute-done | bytes 327712 | tf_op jit(solution)/shard_map/ppermute | solution.py:130
  38.9 2.3 %collective-permute-start.3 = (bf16[8,80,512]{2,1,0:T(8,128)(2,1)S(1)}, bf16[8,80,512]{2,1,0:T(8,128)(2,1)S(1)}, u32[]{:S(2)}, u32[]{:S(2)}) collective-permute-start(bf16[8,80,512]{2,1,0:T(8,128)(2,1)S(1)} %bitcast.18), channel_id=1, source_target_pairs={{0,16},{8,24},{16,0},{24,8},{32,48},{40,56},{48,32},{56,40},{64,80... | collective-permute-start | bytes 1966088 | tf_op jit(solution)/shard_map/ppermute | solution.py:130
  41.2 15.0 %collective-permute-done.3.refs_1_ = bf16[8,80,512]{2,1,0:T(8,128)(2,1)S(1)} collective-permute-done((bf16[8,80,512]{2,1,0:T(8,128)(2,1)S(1)}, bf16[8,80,512]{2,1,0:T(8,128)(2,1)S(1)}, u32[]{:S(2)}, u32[]{:S(2)}) %collective-permute-start.3) | collective-permute-done | bytes 655392 | tf_op jit(solution)/shard_map/ppermute | solution.py:130
  56.4 21.6 %all-to-all-done.qkv_ref = bf16[8,2,32,4992]{3,2,1,0:T(8,128)(2,1)} async-done(((bf16[8,2,32,4992]{3,2,1,0:T(8,128)(2,1)}), bf16[8,2,32,4992]{3,2,1,0:T(8,128)(2,1)}, u32[]{:S(2)}, u32[]{:S(2)}) %all-to-all-start) | async-done | bytes 5111840 | tf_op jit(solution)/shard_map/all_to_all | solution.py:475
  78.0 4.5 %spatial_attention.3 = bf16[8,2,16,1664]{3,2,1,0:T(8,128)(2,1)} custom-call(bf16[8,2,32,4992]{3,2,1,0:T(8,128)(2,1)} %all-to-all-done.qkv_ref), custom_call_target="tpu_custom_call" | custom-call | flops 436207616 | bytes 6815744 | tf_op jit(solution)/shard_map/spatial_attention/pallas_call | solution.py:64
  82.5 3.5 %all-to-all-start.2 = ((bf16[8,2,16,1664]{3,2,1,0:T(8,128)(2,1)}), bf16[8,2,16,1664]{3,2,1,0:T(8,128)(2,1)S(1)}, u32[]{:S(2)}, u32[]{:S(2)}) async-start(bf16[8,2,16,1664]{3,2,1,0:T(8,128)(2,1)} %spatial_attention.3), calls=%async_computation.2 | async-start | bytes 1703936 | tf_op jit(solution)/shard_map/all_to_all | solution.py:482
  86.1 4.6 %spatial_attention.2 = bf16[8,2,16,1664]{3,2,1,0:T(8,128)(2,1)} custom-call(bf16[8,2,32,4992]{3,2,1,0:T(8,128)(2,1)} %all-to-all-done.qkv_ref), custom_call_target="tpu_custom_call" | custom-call | flops 436207616 | bytes 6815744 | tf_op jit(solution)/shard_map/spatial_attention/pallas_call | solution.py:64
  90.7 7.8 %all-to-all-done.2.value = bf16[8,2,16,1664]{3,2,1,0:T(8,128)(2,1)S(1)} async-done(((bf16[8,2,16,1664]{3,2,1,0:T(8,128)(2,1)}), bf16[8,2,16,1664]{3,2,1,0:T(8,128)(2,1)S(1)}, u32[]{:S(2)}, u32[]{:S(2)}) %all-to-all-start.2) | async-done | bytes 852000 | tf_op jit(solution)/shard_map/all_to_all | solution.py:482
  98.5 4.2 %all-to-all-start.1 = ((bf16[8,2,16,1664]{3,2,1,0:T(8,128)(2,1)}), bf16[8,2,16,1664]{3,2,1,0:T(8,128)(2,1)}, u32[]{:S(2)}, u32[]{:S(2)}) async-start(bf16[8,2,16,1664]{3,2,1,0:T(8,128)(2,1)} %spatial_attention.2), calls=%async_computation.1 | async-start | bytes 1703936 | tf_op jit(solution)/shard_map/all_to_all | solution.py:482
  102.8 6.3 %time_weights.1 = (bf16[13,256,256]{2,1,0:T(8,128)(2,1)}, bf16[13,256,256]{2,1,0:T(8,128)(2,1)}) custom-call(bf16[16,32,3328]{2,1,0:T(8,128)(2,1)} %bitcast.25), custom_call_target="tpu_custom_call" | custom-call | flops 436207616 | bytes 7000000 | tf_op jit(solution)/shard_map/time_weights/pallas_call | solution.py:108
  109.2 1.1 copy-done.4
  110.2 1.5 copy-done.3
  111.7 7.6 %token_part.2 = (bf16[16,32,512]{2,1,0:T(8,128)(2,1)}, f32[2,32,128]{2,1,0:T(8,128)S(1)}, bf16[32,80,512]{2,1,0:T(8,128)(2,1)}) custom-call(s32[5]{0:T(128)S(1)} %stack.23.place_ref, bf16[8,2,16,1664]{3,2,1,0:T(8,128)(2,1)} %copy-done.5, bf16[13,256,256]{2,1,0:T(8,128)(2,1)S(1)} %copy-done.3, bf16[1664,512]{1,0:T(8,128)(2,1)} %proj_ref.3, ...), custom_call_target="tpu_custom_call" | custom-call | flops 2249999872 | bytes 10000000 | tf_op jit(solution)/shard_map/token_part/pallas_call | solution.py:302
  119.3 1.7 copy-done.1
  121.0 13.2 %token_part.3 = (bf16[16,32,512]{2,1,0:T(8,128)(2,1)}, f32[8,2,32,128]{3,2,1,0:T(8,128)}, bf16[32,80,512]{2,1,0:T(8,128)(2,1)}, f32[32,128]{1,0:T(8,128)S(1)}) custom-call(s32[5]{0:T(128)S(1)} %stack.23.place_ref, bf16[8,2,16,1664]{3,2,1,0:T(8,128)(2,1)} %all-to-all-done.1.value, ...), custom_call_target="tpu_custom_call", output_to_operand_aliasing={{0}: (6, {})} | custom-call | flops 2249999872 | bytes 10000000 | tf_op jit(solution)/shard_map/token_part/pallas_call | solution.py:302
  134.2 5.6 %all-to-all-start.3 = ((f32[8,2,32,128]{3,2,1,0:T(8,128)}), f32[8,2,32,128]{3,2,1,0:T(8,128)S(1)}, u32[]{:S(2)}, u32[]{:S(2)}) async-start(f32[8,2,32,128]{3,2,1,0:T(8,128)} %get-tuple-element.29), calls=%async_computation.3 | async-start | bytes 524288 | tf_op jit(solution)/shard_map/all_to_all | solution.py:491
  140.5 6.3 %all-to-all-done.3.stats_ref = f32[8,2,32,128]{3,2,1,0:T(8,128)S(1)} async-done(((f32[8,2,32,128]{3,2,1,0:T(8,128)}), f32[8,2,32,128]{3,2,1,0:T(8,128)S(1)}, u32[]{:S(2)}, u32[]{:S(2)}) %all-to-all-start.3) | async-done | bytes 262176 | tf_op jit(solution)/shard_map/all_to_all | solution.py:491
  146.7 2.9 %coef_part.1 = (bf16[16,80,512]{2,1,0:T(8,128)(2,1)S(1)}, bf16[16,80,512]{2,1,0:T(8,128)(2,1)S(1)}, f32[1,1]{1,0:T(1,128)}) custom-call(s32[5]{0:T(128)S(1)} %stack.23.place_ref, s32[1]{0:T(128)S(6)} %copy.12.pos_ref, f32[8,2,32,128]{3,2,1,0:T(8,128)S(1)} %all-to-all-done.3.stats_ref, f32[32,128]{1,0:T(8,128)S(1)} %get-tuple-element.30.lens_ref, ...), custom_call_target="tpu_custom_call" | custom-call | flops 4000000 | bytes 6000000 | tf_op jit(solution)/shard_map/coef_part/pallas_call | solution.py:363
  149.8 3.0 %collective-permute-done.5.got_ref = bf16[16,80,512]{2,1,0:T(8,128)(2,1)S(1)} collective-permute-done((bf16[16,80,512]{2,1,0:T(8,128)(2,1)S(1)}, bf16[16,80,512]{2,1,0:T(8,128)(2,1)S(1)}, u32[]{:S(2)}, u32[]{:S(2)}) %collective-permute-start.5) | collective-permute-done | bytes 1310752 | tf_op jit(solution)/shard_map/ppermute | solution.py:439
  154.1 1.7 collective-permute-start.7
  155.8 7.7 %collective-permute-done.6.a_got = bf16[8,80,256]{2,1,0:T(8,128)(2,1)S(1)} collective-permute-done((bf16[8,80,256]{2,1,0:T(8,128)(2,1)S(1)}, bf16[8,80,256]{2,1,0:T(8,128)(2,1)S(1)}, u32[]{:S(2)}, u32[]{:S(2)}) %collective-permute-start.6) | collective-permute-done | bytes 327712 | tf_op jit(solution)/shard_map/ppermute | solution.py:444
  163.5 1.3 collective-permute-done.7.b_got
  165.0 1.7 collective-permute-start.8
  166.7 4.9 %collective-permute-done.8.a_got = bf16[8,80,128]{2,1,0:T(8,128)(2,1)S(1)} collective-permute-done((bf16[8,80,128]{2,1,0:T(8,128)(2,1)S(1)}, bf16[8,80,128]{2,1,0:T(8,128)(2,1)S(1)}, u32[]{:S(2)}, u32[]{:S(2)}) %collective-permute-start.8) | collective-permute-done | bytes 163872 | tf_op jit(solution)/shard_map/ppermute | solution.py:450
  172.1 21.8 %all_to_all.30.parts = bf16[16,80,128]{2,1,0:T(8,128)(2,1)S(1)} all-to-all(bf16[16,80,128]{2,1,0:T(8,128)(2,1)S(1)} %third_sum.1), channel_id=1, replica_groups={{0,16,32,48,64,80,96,112,128,144,160,176,192,208,224,240},{8,24,40,56,7..., dimensions={0} | all-to-all | bytes 655360 | tf_op jit(solution)/shard_map/all_to_all | solution.py:455
  193.9 9.4 %all_to_all.31.parts = bf16[8,80,128]{2,1,0:T(8,128)(2,1)S(1)} all-to-all(bf16[8,80,128]{2,1,0:T(8,128)(2,1)S(1)} %owned_sum.1), channel_id=1, replica_groups=mesh['dp'=32,'space'=8] {'space'}, dimensions={0} | all-to-all | bytes 327680 | tf_op jit(solution)/shard_map/all_to_all | solution.py:460
  (29 shorter events, 3.2 us)
Async XLA Ops:
  0.6 6.1 %copy-start.6 = (bf16[1,77,512]{2,1,0:T(8,128)(2,1)S(1)}, bf16[1,77,512]{2,1,0:T(8,128)(2,1)}, u32[]{:S(2)}) copy-start(bf16[1,77,512]{2,1,0:T(8,128)(2,1)} %param.9) | copy-start | bytes 236548
  0.6 77.4 %all-to-all-start = ((bf16[8,2,32,4992]{3,2,1,0:T(8,128)(2,1)}), bf16[8,2,32,4992]{3,2,1,0:T(8,128)(2,1)}, u32[]{:S(2)}, u32[]{:S(2)}) async-start(bf16[8,2,32,4992]{3,2,1,0:T(8,128)(2,1)} %bitcast.24), calls=%async_computation | async-start | bytes 10223616 | tf_op jit(solution)/shard_map/all_to_all | solution.py:475
  6.8 6.0 %collective-permute-start = (bf16[1,80,512]{2,1,0:T(8,128)(2,1)S(1)}, bf16[1,80,512]{2,1,0:T(8,128)(2,1)S(1)}, u32[]{:S(2)}, u32[]{:S(2)}) collective-permute-start(bf16[1,80,512]{2,1,0:T(8,128)(2,1)S(1)} %concatenate.3.refs_0_), channel_id=1, source_target_pairs={{0,129},{1,128},{2,131},{3,130},{4,133},{5,132},{6,135},{7,134},{8... | collective-permute-start | bytes 245768 | tf_op jit(solution)/shard_map/ppermute | solution.py:140
  12.8 11.9 %collective-permute-start.1 = (bf16[2,80,512]{2,1,0:T(8,128)(2,1)S(1)}, bf16[2,80,512]{2,1,0:T(8,128)(2,1)S(1)}, u32[]{:S(2)}, u32[]{:S(2)}) collective-permute-start(bf16[2,80,512]{2,1,0:T(8,128)(2,1)S(1)} %bitcast.22), channel_id=1, source_target_pairs={{0,64},{8,72},{16,80},{24,88},{32,96},{40,104},{48,112},{56,120},{... | collective-permute-start | bytes 491528 | tf_op jit(solution)/shard_map/ppermute | solution.py:130
  24.7 14.2 %collective-permute-start.2 = (bf16[4,80,512]{2,1,0:T(8,128)(2,1)S(1)}, bf16[4,80,512]{2,1,0:T(8,128)(2,1)S(1)}, u32[]{:S(2)}, u32[]{:S(2)}) collective-permute-start(bf16[4,80,512]{2,1,0:T(8,128)(2,1)S(1)} %bitcast.20), channel_id=1, source_target_pairs={{0,32},{8,40},{16,48},{24,56},{32,0},{40,8},{48,16},{56,24},{64,96... | collective-permute-start | bytes 983048 | tf_op jit(solution)/shard_map/ppermute | solution.py:130
  38.9 17.4 %collective-permute-start.3 = (bf16[8,80,512]{2,1,0:T(8,128)(2,1)S(1)}, bf16[8,80,512]{2,1,0:T(8,128)(2,1)S(1)}, u32[]{:S(2)}, u32[]{:S(2)}) collective-permute-start(bf16[8,80,512]{2,1,0:T(8,128)(2,1)S(1)} %bitcast.18), channel_id=1, source_target_pairs={{0,16},{8,24},{16,0},{24,8},{32,48},{40,56},{48,32},{56,40},{64,80... | collective-permute-start | bytes 1966088 | tf_op jit(solution)/shard_map/ppermute | solution.py:130
  56.3 26.2 %copy-start = (bf16[2,8,80,512]{3,2,1,0:T(8,128)(2,1)}, bf16[2,8,80,512]{3,2,1,0:T(8,128)(2,1)S(1)}, u32[]{:S(2)}) copy-start(bf16[2,8,80,512]{3,2,1,0:T(8,128)(2,1)S(1)} %join.7) | copy-start | bytes 3932164
  56.3 52.8 %collective-permute-start.4 = (bf16[16,80,512]{2,1,0:T(8,128)(2,1)S(1)}, bf16[16,80,512]{2,1,0:T(8,128)(2,1)S(1)}, u32[]{:S(2)}, u32[]{:S(2)}) collective-permute-start(bf16[16,80,512]{2,1,0:T(8,128)(2,1)S(1)} %bitcast.15), channel_id=1, source_target_pairs={{0,8},{8,0},{16,24},{24,16},{32,40},{40,32},{48,56},{56,48},{64,72... | collective-permute-start | bytes 3932168 | tf_op jit(solution)/shard_map/ppermute | solution.py:130
  82.5 16.0 %all-to-all-start.2 = ((bf16[8,2,16,1664]{3,2,1,0:T(8,128)(2,1)}), bf16[8,2,16,1664]{3,2,1,0:T(8,128)(2,1)S(1)}, u32[]{:S(2)}, u32[]{:S(2)}) async-start(bf16[8,2,16,1664]{3,2,1,0:T(8,128)(2,1)} %spatial_attention.3), calls=%async_computation.2 | async-start | bytes 1703936 | tf_op jit(solution)/shard_map/all_to_all | solution.py:482
  98.5 10.6 %copy-start.5 = (bf16[8,2,16,1664]{3,2,1,0:T(8,128)(2,1)}, bf16[8,2,16,1664]{3,2,1,0:T(8,128)(2,1)S(1)}, u32[]{:S(2)}) copy-start(bf16[8,2,16,1664]{3,2,1,0:T(8,128)(2,1)S(1)} %all-to-all-done.2.value) | copy-start | bytes 2555908
  98.5 20.7 %all-to-all-start.1 = ((bf16[8,2,16,1664]{3,2,1,0:T(8,128)(2,1)}), bf16[8,2,16,1664]{3,2,1,0:T(8,128)(2,1)}, u32[]{:S(2)}, u32[]{:S(2)}) async-start(bf16[8,2,16,1664]{3,2,1,0:T(8,128)(2,1)} %spatial_attention.2), calls=%async_computation.1 | async-start | bytes 1703936 | tf_op jit(solution)/shard_map/all_to_all | solution.py:482
  109.1 1.1 copy-start.4
  110.2 1.5 copy-start.3
  111.7 7.6 %copy-start.2 = (bf16[13,256,256]{2,1,0:T(8,128)(2,1)S(1)}, bf16[13,256,256]{2,1,0:T(8,128)(2,1)}, u32[]{:S(2)}) copy-start(bf16[13,256,256]{2,1,0:T(8,128)(2,1)} %get-tuple-element.23.time_ref) | copy-start | bytes 5111812
  119.3 1.7 copy-start.1
  134.2 12.5 %all-to-all-start.3 = ((f32[8,2,32,128]{3,2,1,0:T(8,128)}), f32[8,2,32,128]{3,2,1,0:T(8,128)S(1)}, u32[]{:S(2)}, u32[]{:S(2)}) async-start(f32[8,2,32,128]{3,2,1,0:T(8,128)} %get-tuple-element.29), calls=%async_computation.3 | async-start | bytes 524288 | tf_op jit(solution)/shard_map/all_to_all | solution.py:491
  149.7 3.1 %collective-permute-start.5 = (bf16[16,80,512]{2,1,0:T(8,128)(2,1)S(1)}, bf16[16,80,512]{2,1,0:T(8,128)(2,1)S(1)}, u32[]{:S(2)}, u32[]{:S(2)}) collective-permute-start(bf16[16,80,512]{2,1,0:T(8,128)(2,1)S(1)} %get-tuple-element.33), channel_id=1, source_target_pairs={{0,8},{8,0},{16,24},{24,16},{32,40},{40,32},{48,56},{56,48},{64,72... | collective-permute-start | bytes 3932168 | tf_op jit(solution)/shard_map/ppermute | solution.py:439
  153.7 9.8 %collective-permute-start.6 = (bf16[8,80,256]{2,1,0:T(8,128)(2,1)S(1)}, bf16[8,80,256]{2,1,0:T(8,128)(2,1)S(1)}, u32[]{:S(2)}, u32[]{:S(2)}) collective-permute-start(bf16[8,80,256]{2,1,0:T(8,128)(2,1)S(1)} %get-tuple-element.35), channel_id=1, source_target_pairs={{0,2},{1,3},{2,0},{3,1},{4,6},{5,7},{6,4},{7,5},{8,10},{9,11},{10,... | collective-permute-start | bytes 983048 | tf_op jit(solution)/shard_map/ppermute | solution.py:444
  154.1 10.8 %collective-permute-start.7 = (bf16[8,80,256]{2,1,0:T(8,128)(2,1)S(1)}, bf16[8,80,256]{2,1,0:T(8,128)(2,1)S(1)}, u32[]{:S(2)}, u32[]{:S(2)}) collective-permute-start(bf16[8,80,256]{2,1,0:T(8,128)(2,1)S(1)} %get-tuple-element.37), channel_id=1, source_target_pairs={{0,6},{1,7},{2,4},{3,5},{4,2},{5,3},{6,0},{7,1},{8,14},{9,15},{10,... | collective-permute-start | bytes 983048 | tf_op jit(solution)/shard_map/ppermute | solution.py:445
  165.0 6.6 %collective-permute-start.8 = (bf16[8,80,128]{2,1,0:T(8,128)(2,1)S(1)}, bf16[8,80,128]{2,1,0:T(8,128)(2,1)S(1)}, u32[]{:S(2)}, u32[]{:S(2)}) collective-permute-start(bf16[8,80,128]{2,1,0:T(8,128)(2,1)S(1)} %get-tuple-element.39), channel_id=1, source_target_pairs={{0,6},{1,7},{2,4},{3,5},{4,2},{5,3},{6,0},{7,1},{8,14},{9,15},{10,... | collective-permute-start | bytes 491528 | tf_op jit(solution)/shard_map/ppermute | solution.py:450
  166.7 5.3 %collective-permute-start.9 = (bf16[8,80,128]{2,1,0:T(8,128)(2,1)S(1)}, bf16[8,80,128]{2,1,0:T(8,128)(2,1)S(1)}, u32[]{:S(2)}, u32[]{:S(2)}) collective-permute-start(bf16[8,80,128]{2,1,0:T(8,128)(2,1)S(1)} %get-tuple-element.41), channel_id=1, source_target_pairs={{0,2},{1,3},{2,0},{3,1},{4,6},{5,7},{6,4},{7,5},{8,10},{9,11},{10,... | collective-permute-start | bytes 491528 | tf_op jit(solution)/shard_map/ppermute | solution.py:451

commit v7 on v5

--- a/solution.py
+++ b/solution.py
@@ -30,6 +30,16 @@
 FAR_OFF = pl.BlockSpec(memory_space=pltpu.HBM)
 ANY = pl.BlockSpec(memory_space=pl.ANY)
 
+
+def owner(g1, a):
+    return (g1 * 2 + ((a >> 1) ^ g1)) * 2 + (a & 1)
+
+
+def quad_place(place_ref):
+    x, y = place_ref[2], place_ref[3]
+    return x >> 1, ((x >> 1) ^ (x & 1)) * 2 + y
+
+
 def held(value):
     return pltpu.with_memory_space_constraint(value, pltpu.HBM)
 
@@ -41,27 +51,148 @@
 SPLIT = 7
 
 
-def spatial_kernel(qkv_ref, out_ref):
-    for h in range(HEADS):
-        q = qkv_ref[:, 0, :, pl.ds(h * HD, HD)].reshape(PATCHES, HD)
-        k = qkv_ref[:, 0, :, pl.ds(FEATURES + h * HD, HD)].reshape(PATCHES, HD)
-        v = qkv_ref[:, 0, :, pl.ds(2 * FEATURES + h * HD, HD)].reshape(PATCHES, HD)
-        s = nt(q, k)
-        m = jnp.max(s, axis=-1, keepdims=True)
-        e = jnp.exp2((s - m) * SCORE_LOG2)
-        total = jnp.sum(e, axis=-1, keepdims=True)
-        o = jnp.dot(e.astype(jnp.bfloat16), v, preferred_element_type=jnp.float32)
-        o = (o * (1.0 / total)).astype(jnp.bfloat16)
-        out_ref[:, 0, :, pl.ds(h * HD, HD)] = o.reshape(8, LOCAL, HD)
-
-
-def spatial_attention(blocks):
+ROW = (LOCAL, 3 * FEATURES)
+FULL = pltpu.CompilerParams(vmem_limit_bytes=60 * MIB)
+
+
+def copied(pairs, buf, sems):
+    loads = [
+        pltpu.make_async_copy(src, buf.at[i], sems.at[0, i]) for i, (src, _) in enumerate(pairs)
+    ]
+    stores = [
+        pltpu.make_async_copy(buf.at[i], dst, sems.at[1, i]) for i, (_, dst) in enumerate(pairs)
+    ]
+    for load in loads:
+        load.start()
+    for load, store in zip(loads, stores):
+        load.wait()
+        store.start()
+    for store in stores:
+        store.wait()
+
+
+def copying(kernel, name, operands, shapes, count, params=FULL):
+    return pl.pallas_call(
+        kernel,
+        in_specs=[SMEM] + [ANY] * (len(operands) - 1),
+        out_specs=[ANY] * len(shapes),
+        out_shape=[jax.ShapeDtypeStruct((n,) + ROW, jnp.bfloat16) for n in shapes],
+        scratch_shapes=[
+            pltpu.VMEM((count,) + ROW, jnp.bfloat16),
+            pltpu.SemaphoreType.DMA((2, count)),
+        ],
+        compiler_params=params,
+        cost_estimate=pl.CostEstimate(flops=0, bytes_accessed=6_000_000, transcendentals=0),
+        name=name,
+    )(*operands)
+
+
+def across_kernel(place_ref, clip_ref, out_ref, buf, sems):
+    g1, _ = quad_place(place_ref)
+    copied([(clip_ref.at[2 * owner(1 - g1, a) + 1], out_ref.at[a]) for a in range(4)], buf, sems)
+
+
+def quads_kernel(place_ref, clip_ref, one, two, three, buf, sems):
+    _, a = quad_place(place_ref)
+    pairs = [
+        (clip_ref.at[2 * owner(g, a ^ k)], ref.at[g])
+        for k, ref in ((1, one), (2, two), (3, three))
+        for g in range(2)
+    ]
+    copied(pairs, buf, sems)
+
+
+def own_kernel(place_ref, clip_ref, first, seconds, kept, buf, sems):
+    g1, a = quad_place(place_ref)
+    pairs = [(clip_ref.at[2 * owner(1 - g1, a)], first.at[0])]
+    pairs += [(clip_ref.at[2 * owner(g1, a ^ k) + 1], seconds.at[k - 1]) for k in (1, 2, 3)]
+    pairs += [(clip_ref.at[2 * owner(g1, a) + f], kept.at[f]) for f in range(2)]
+    copied(pairs, buf, sems)
+
+
+def turn_kernel(place_ref, first_ref, one, two, three, behind_ref, out_ref, buf, sems):
+    g1, _ = quad_place(place_ref)
+    pairs = [(first_ref.at[0], out_ref.at[0])]
+    pairs += [(ref.at[1 - g1], out_ref.at[k]) for k, ref in ((1, one), (2, two), (3, three))]
+    copied(pairs, buf, sems)
+
+
+def spread_kernel(place_ref, seconds_ref, across_ref, one, two, three, buf, sems):
+    _, a = quad_place(place_ref)
+    pairs = []
+    for k, ref in ((1, one), (2, two), (3, three)):
+        pairs += [(seconds_ref.at[k - 1], ref.at[0]), (across_ref.at[a ^ k], ref.at[1])]
+    copied(pairs, buf, sems)
+
+
+def swap(value, bits):
+    return lax.ppermute(value, "space", [(s, s ^ bits) for s in range(8)])
+
+
+def bring_frames(clip, place, behind):
+    (across,) = copying(across_kernel, "across", (place, clip), (4,), 4)
+    across = swap(across, 6)
+    quads = copying(quads_kernel, "quads", (place, clip), (2, 2, 2), 6)
+    quads = [swap(quad, k) for k, quad in zip((1, 2, 3), quads)]
+    first, seconds, kept = copying(own_kernel, "own", (place, clip), (1, 3, 2), 6)
+    few = pltpu.CompilerParams(vmem_limit_bytes=8 * MIB)
+    (turned,) = copying(turn_kernel, "turn", (place, first, *quads, behind), (4,), 4, few)
+    turned = swap(turned, 6)
+    pairs = copying(spread_kernel, "spread", (place, seconds, across), (2, 2, 2), 6, few)
+    started = pairs[0]
+    pairs = [swap(pair, k) for k, pair in zip((1, 2, 3), pairs)]
+    return (kept, across, turned, *quads, *pairs), started
+
+
+def spatial_kernel(place_ref, kept_ref, across_ref, turned_ref, *refs):
+    quads, pairs, (_, out_ref, buf, res, sems, store_sems) = refs[:3], refs[3:6], refs[6:]
+    g1, a = quad_place(place_ref)
+    first = [kept_ref.at[0]] + [ref.at[g1] for ref in quads] + [turned_ref.at[k] for k in range(4)]
+    second = [kept_ref.at[1]] + [ref.at[0] for ref in pairs]
+    second += [across_ref.at[a]] + [ref.at[1] for ref in pairs]
+    loads = [
+        [pltpu.make_async_copy(src, buf.at[f, i], sems.at[f, i]) for i, src in enumerate(sources)]
+        for f, sources in enumerate((first, second))
+    ]
+    for f in range(2):
+        for load in loads[f]:
+            load.start()
+    stores = [
+        pltpu.make_async_copy(res.at[f], out_ref.at[:, f], store_sems.at[f]) for f in range(2)
+    ]
+    for f in range(2):
+        for load in loads[f]:
+            load.wait()
+        for h in range(HEADS):
+            q = buf[f, :, :, pl.ds(h * HD, HD)].reshape(PATCHES, HD)
+            k = buf[f, :, :, pl.ds(FEATURES + h * HD, HD)].reshape(PATCHES, HD)
+            v = buf[f, :, :, pl.ds(2 * FEATURES + h * HD, HD)].reshape(PATCHES, HD)
+            s = nt(q, k)
+            m = jnp.max(s, axis=-1, keepdims=True)
+            e = jnp.exp2((s - m) * SCORE_LOG2)
+            total = jnp.sum(e, axis=-1, keepdims=True)
+            o = jnp.dot(e.astype(jnp.bfloat16), v, preferred_element_type=jnp.float32)
+            o = (o * (1.0 / total)).astype(jnp.bfloat16)
+            for i in range(8):
+                at = owner(g1 if i < 4 else 1 - g1, a ^ (i & 3))
+                res[f, at, :, pl.ds(h * HD, HD)] = o[i * LOCAL : (i + 1) * LOCAL]
+        stores[f].start()
+    for store in stores:
+        store.wait()
+
+
+def spatial_attention(place, pieces, behind):
     return pl.pallas_call(
         spatial_kernel,
-        grid=(2,),
-        in_specs=[pl.BlockSpec((8, 1, LOCAL, 3 * FEATURES), lambda f: (0, f, 0, 0))],
-        out_specs=pl.BlockSpec((8, 1, LOCAL, FEATURES), lambda f: (0, f, 0, 0)),
-        out_shape=pltpu.HBM((8, 2, LOCAL, FEATURES), jnp.bfloat16),
+        in_specs=[SMEM] + [ANY] * (len(pieces) + 1),
+        out_specs=ANY,
+        out_shape=jax.ShapeDtypeStruct((8, 2, LOCAL, FEATURES), jnp.bfloat16),
+        scratch_shapes=[
+            pltpu.VMEM((2, 8) + ROW, jnp.bfloat16),
+            pltpu.VMEM((2, 8, LOCAL, FEATURES), jnp.bfloat16),
+            pltpu.SemaphoreType.DMA((2, 8)),
+            pltpu.SemaphoreType.DMA((2,)),
+        ],
         compiler_params=GRANT,
         cost_estimate=pl.CostEstimate(
             flops=8 * HEADS * PATCHES * PATCHES * HD,
@@ -69,16 +200,17 @@
             transcendentals=2 * HEADS * PATCHES * PATCHES,
         ),
         name="spatial_attention",
-    )(blocks)
+    )(place, *pieces, behind)
 
 
 ROWS = FRAMES * 16
 
 
-def time_kernel(tqk_ref, out_ref, tqk, weights, load_sem, sems):
+def time_kernel(tqk_ref, behind_ref, out_ref, mark_ref, tqk, weights, load_sem, sems):
     load = pltpu.make_async_copy(tqk_ref, tqk, load_sem)
     load.start()
     load.wait()
+    mark_ref[...] = jnp.zeros_like(mark_ref)
     r = lax.broadcasted_iota(jnp.int32, (ROWS, ROWS), 0)
     c = lax.broadcasted_iota(jnp.int32, (ROWS, ROWS), 1)
     bias = jnp.where((r & 15) == (c & 15), 0.0, -1e30).astype(jnp.float32)
@@ -99,12 +231,15 @@
         store.wait()
 
 
-def time_weights(temporal_qk):
+def time_weights(temporal_qk, behind):
     return pl.pallas_call(
         time_kernel,
-        in_specs=[FAR_OFF],
-        out_specs=FAR_OFF,
-        out_shape=pltpu.HBM((HEADS, 2, ROWS, ROWS), jnp.bfloat16),
+        in_specs=[ANY] * 2,
+        out_specs=[ANY, VMEM],
+        out_shape=[
+            jax.ShapeDtypeStruct((HEADS, 2, ROWS, ROWS), jnp.bfloat16),
+            jax.ShapeDtypeStruct((8, 128), jnp.float32),
+        ],
         scratch_shapes=[
             pltpu.VMEM((FRAMES, LOCAL, 2 * FEATURES), jnp.bfloat16),
             pltpu.VMEM((HEADS, 2, ROWS, ROWS), jnp.bfloat16),
@@ -118,7 +253,7 @@
             transcendentals=2 * HEADS * ROWS * ROWS,
         ),
         name="time_weights",
-    )(held(temporal_qk))
+    )(temporal_qk, behind)
 
 
 def flip(value, bit):
@@ -130,7 +265,12 @@
     refs[-1][1] = refs[1][...]
 
 
-def doubled(value, bit, *behind):
+def flip_y(value):
+    pairs = [(i * 8 + s, (i ^ 16) * 8 + (s ^ 1)) for i in range(32) for s in range(8)]
+    return lax.ppermute(value, ("dp", "space"), pairs)
+
+
+def doubled(value, other, *behind):
     both = pl.pallas_call(
         join_kernel,
         in_specs=[VMEM] * 2 + [ANY] * len(behind),
@@ -139,14 +279,14 @@
         compiler_params=pltpu.CompilerParams(vmem_limit_bytes=8 * MIB),
         cost_estimate=pl.CostEstimate(flops=0, bytes_accessed=1_000_000, transcendentals=0),
         name="join",
-    )(value, flip(value, bit), *behind)
+    )(value, other, *behind)
     return both.reshape((-1,) + value.shape[1:])
 
 
 def token_kernel(
     place_ref, value, time_ref, proj_ref, mine_ref, other_ref,
-    emb_ref, stats_ref, grad_ref, lens_ref,
-    proj, mine, comb, video, grads, sems, grad_sems,
+    emb_ref, all_stats_ref, grad_ref, lens_ref,
+    proj, mine, comb, video, grads, stats_ref, sems, grad_sems,
 ):
     proj_load = pltpu.make_async_copy(proj_ref, proj, sems.at[0])
     mine_load = pltpu.make_async_copy(mine_ref, mine, sems.at[1])
@@ -200,10 +340,11 @@
                 rng = slice(j * PADDED, (j + 1) * PADDED)
                 top_row = jnp.sum(jnp.where(eye, top[rng], 0.0), axis=0, keepdims=True)
                 total_row = jnp.sum(jnp.where(eye, total[rng], 0.0), axis=0, keepdims=True)
-                for k in range(8):
-                    stats_ref[k, 0, pl.ds(at, 1), :] = top_row
-                    stats_ref[k, 1, pl.ds(at, 1), :] = total_row
+                stats_ref[0, pl.ds(at, 1), :] = top_row
+                stats_ref[1, pl.ds(at, 1), :] = total_row
                 lens_ref[pl.ds(at, 1), :] = ref[m, SLOTS : SLOTS + 1, :128].astype(jnp.float32)
+    for k in range(8):
+        all_stats_ref[k] = stats_ref[...]
     emb_store.wait()
     for store in stores:
         store.wait()
@@ -227,6 +368,7 @@
             pltpu.VMEM((FRAMES, LOCAL, FEATURES), bf16),
             pltpu.VMEM((FRAMES, LOCAL, EMB), bf16),
             pltpu.VMEM((CAPTIONS, PADDED, EMB), bf16),
+            pltpu.VMEM((2, CAPTIONS, 128), jnp.float32),
             pltpu.SemaphoreType.DMA((3,)),
             pltpu.SemaphoreType.DMA((CAPTIONS,)),
         ],
@@ -395,16 +537,15 @@
         caption_lens.astype(jnp.bfloat16)[:, None, None], (1, PADDED - SLOTS, EMB)
     )
     caps = jnp.concatenate([caption_tokens, lens_row], axis=1)
-    blocks = clip_qkv.reshape(8, 2, LOCAL, 3 * FEATURES)
-    blocks = lax.all_to_all(blocks, "space", split_axis=0, concat_axis=0, tiled=True)
-    time = time_weights(temporal_qk[0])
-    caps = doubled(caps, 16)
-    caps = doubled(caps, 8)
-    caps = doubled(caps, 4)
-    caps = doubled(caps, 2)
+    caps = doubled(caps, flip_y(caps))
+    caps = doubled(caps, flip(caps, 8))
+    pieces, started = bring_frames(clip_qkv[0], place, caps)
+    time, done = time_weights(temporal_qk[0], started)
+    attended = spatial_attention(place, pieces, done)
+    caps = doubled(caps, flip(caps, 4), attended)
+    caps = doubled(caps, flip(caps, 2))
     other = flip(caps, 1)
-    attended = spatial_attention(blocks)
-    spatial = lax.all_to_all(held(attended), "space", split_axis=0, concat_axis=0, tiled=True)
+    spatial = lax.all_to_all(attended, "space", split_axis=0, concat_axis=0, tiled=True)
     video, stats, grad, lens = token_part(
         place, spatial, time, proj_weight, caps, other
     )

time: 210 us -> 184 us (0.88)
  waiting for transfers between devices: 101 us -> 68.5 us
  starting transfers between devices: 48.4 us -> 36.1 us
  Pallas kernels: 26.9 us -> 39 us
  local copies, waits for them, and re-layouts: 2.06 us -> 5.32 us
  blocking collectives: 29.6 us -> 32.4 us
    ppermute x5 -> x4, waiting for transfers between devices: 60.1 us -> 11.1 us  [flip(): return lax.ppermute(value, 'dp', [(i, i ^ bit) for i in range(32)])]
    ppermute x0 -> x9, waiting for transfers between devices: none -> 23.5 us  [the longest x8 20.8 us: swap(): return lax.ppermute(value, 'space', [(s, s ^ bits) for s in range(8)])]
    all_to_all x2 -> x1, starting transfers between devices: 25.9 us -> 3.59 us  [on_device(): lax.all_to_all(attended, 'space', split_axis=0, concat_axis=0, tiled=True)]
    ppermute x0 -> x9, starting transfers between devices: none -> 15.3 us  [the longest x8 12.2 us: swap(): return lax.ppermute(value, 'space', [(s, s ^ bits) for s in range(8)])]
    pallas_call x2 -> x7, Pallas kernels: 11.6 us -> 23.7 us  [the longest x5 12 us: copying(): pl.pallas_call(kernel, in_specs=[SMEM] + [ANY] * (len(operands) - 1), out...]
    all_to_all x2 -> x1, waiting for transfers between devices: 17 us -> 10.3 us  [on_device(): lax.all_to_all(attended, 'space', split_axis=0, concat_axis=0, tiled=True)]
    ppermute x5 -> x4, starting transfers between devices: 15.1 us -> 9.85 us  [flip(): return lax.ppermute(value, 'dp', [(i, i ^ bit) for i in range(32)])]
    all_to_all x1, blocking collectives: 20.2 us -> 23 us  [reduce_gradient(): lax.all_to_all(parts, 'dp', split_axis=0, concat_axis=0, tiled=True, axis...]
  transfers between devices with their start and end apart: 13 -> 20, of which waited for: 10 -> 14; matrix products, arithmetic and copies ran while one was open for 0% -> 0% of each run, Pallas kernels for 6% -> 12%
where the time goes in v7:
time: 184 us; the launch traced here: 183 us
  waiting for transfers between devices  68.5 us (37%)
  Pallas kernels  39 us (21%)
  starting transfers between devices  36.1 us (20%)
  blocking collectives  32.4 us (18%)
  local copies, waits for them, and re-layouts  5.32 us (3%)
  between operations  2.15 us (1%)
    all_to_all x1, blocking collectives, reduce_gradient(): lax.all_to_all(parts, 'dp', split_axis=0, concat_axis=0, tiled=True, axis...  23 us
    ppermute x8, waiting for transfers between devices, swap(): return lax.ppermute(value, 'space', [(s, s ^ bits) for s in range(8)])  20.8 us
    ppermute x8, starting transfers between devices, swap(): return lax.ppermute(value, 'space', [(s, s ^ bits) for s in range(8)])  12.2 us
    pallas_call x5, Pallas kernels, copying(): pl.pallas_call(kernel, in_specs=[SMEM] + [ANY] * (len(operands) - 1), out...  12 us
    ppermute x4, waiting for transfers between devices, flip(): return lax.ppermute(value, 'dp', [(i, i ^ bit) for i in range(32)])  11.1 us
    all_to_all x1, waiting for transfers between devices, on_device(): lax.all_to_all(attended, 'space', split_axis=0, concat_axis=0, tiled=True)  10.3 us
    ppermute x4, starting transfers between devices, flip(): return lax.ppermute(value, 'dp', [(i, i ^ bit) for i in range(32)])  9.85 us
    all_to_all x1, blocking collectives, reduce_gradient(): lax.all_to_all(parts, 'space', split_axis=0, concat_axis=0, tiled=True)  9.43 us
  transfers between devices with their start and end apart: 20, of which 14 were waited for; matrix products, arithmetic and copies ran while one was open for 0% of the time, Pallas kernels for 12%

profile of v7, /device:TPU:32, one launch (start us, length us, event | category | flops | bytes accessed | tf_op | source)
XLA Modules:
  0.0 183.5 jit_solution(13831527570994290420)
XLA Ops:
  1.3 3.1 %quads.1 = (bf16[2,32,4992]{2,1,0:T(8,128)(2,1)}, bf16[2,32,4992]{2,1,0:T(8,128)(2,1)}, bf16[2,32,4992]{2,1,0:T(8,128)(2,1)}) custom-call(s32[5]{0:T(128)} %stack.23.place_ref, bf16[16,32,4992]{2,1,0:T(8,128)(2,1)} %bitcast.23), custom_call_target="tpu_custom_call" | custom-call | bytes 6000000 | tf_op jit(solution)/shard_map/quads/pallas_call | solution.py:75
  7.5 2.8 %across.1 = bf16[4,32,4992]{2,1,0:T(8,128)(2,1)} custom-call(s32[5]{0:T(128)} %stack.23.place_ref, bf16[16,32,4992]{2,1,0:T(8,128)(2,1)} %bitcast.24), custom_call_target="tpu_custom_call" | custom-call | bytes 6000000 | tf_op jit(solution)/shard_map/across/pallas_call | solution.py:75
  10.3 2.2 %collective-permute-start = (bf16[4,32,4992]{2,1,0:T(8,128)(2,1)}, bf16[4,32,4992]{2,1,0:T(8,128)(2,1)S(1)}, u32[]{:S(2)}, u32[]{:S(2)}) collective-permute-start(bf16[4,32,4992]{2,1,0:T(8,128)(2,1)} %across.1), channel_id=1, source_target_pairs={{0,6},{1,7},{2,4},{3,5},{4,2},{5,3},{6,0},{7,1},{8,14},{9,15},{10,... | collective-permute-start | bytes 3833864 | tf_op jit(solution)/shard_map/ppermute | solution.py:129
  13.7 3.1 %collective-permute-start.4 = (bf16[1,80,512]{2,1,0:T(8,128)(2,1)S(1)}, bf16[1,80,512]{2,1,0:T(8,128)(2,1)S(1)}, u32[]{:S(2)}, u32[]{:S(2)}) collective-permute-start(bf16[1,80,512]{2,1,0:T(8,128)(2,1)S(1)} %concatenate.3.refs_0_), channel_id=1, source_target_pairs={{0,129},{1,128},{2,131},{3,130},{4,133},{5,132},{6,135},{7,134},{8... | collective-permute-start | bytes 245768 | tf_op jit(solution)/shard_map/ppermute | solution.py:270
  16.8 2.6 %collective-permute-done.4.refs_1_ = bf16[1,80,512]{2,1,0:T(8,128)(2,1)S(1)} collective-permute-done((bf16[1,80,512]{2,1,0:T(8,128)(2,1)S(1)}, bf16[1,80,512]{2,1,0:T(8,128)(2,1)S(1)}, u32[]{:S(2)}, u32[]{:S(2)}) %collective-permute-start.4) | collective-permute-done | bytes 81952 | tf_op jit(solution)/shard_map/ppermute | solution.py:270
  19.4 6.4 %collective-permute-start.5 = (bf16[2,80,512]{2,1,0:T(8,128)(2,1)S(1)}, bf16[2,80,512]{2,1,0:T(8,128)(2,1)S(1)}, u32[]{:S(2)}, u32[]{:S(2)}) collective-permute-start(bf16[2,80,512]{2,1,0:T(8,128)(2,1)S(1)} %bitcast.21), channel_id=1, source_target_pairs={{0,64},{8,72},{16,80},{24,88},{32,96},{40,104},{48,112},{56,120},{... | collective-permute-start | bytes 491528 | tf_op jit(solution)/shard_map/ppermute | solution.py:260
  25.8 3.0 %own.1 = (bf16[1,32,4992]{2,1,0:T(8,128)(2,1)}, bf16[3,32,4992]{2,1,0:T(8,128)(2,1)}, bf16[2,32,4992]{2,1,0:T(8,128)(2,1)}) custom-call(s32[5]{0:T(128)} %stack.23.place_ref, bf16[16,32,4992]{2,1,0:T(8,128)(2,1)} %bitcast.25), custom_call_target="tpu_custom_call" | custom-call | bytes 6000000 | tf_op jit(solution)/shard_map/own/pallas_call | solution.py:75
  30.3 5.4 %collective-permute-done.3.three.refs_2_ = bf16[2,32,4992]{2,1,0:T(8,128)(2,1)S(1)} collective-permute-done((bf16[2,32,4992]{2,1,0:T(8,128)(2,1)}, bf16[2,32,4992]{2,1,0:T(8,128)(2,1)S(1)}, u32[]{:S(2)}, u32[]{:S(2)}) %collective-permute-start.3) | collective-permute-done | bytes 639008 | tf_op jit(solution)/shard_map/ppermute | solution.py:129
  38.0 2.8 %collective-permute-start.6 = (bf16[4,32,4992]{2,1,0:T(8,128)(2,1)S(1)}, bf16[4,32,4992]{2,1,0:T(8,128)(2,1)S(1)}, u32[]{:S(2)}, u32[]{:S(2)}) collective-permute-start(bf16[4,32,4992]{2,1,0:T(8,128)(2,1)S(1)} %turn.1), channel_id=1, source_target_pairs={{0,6},{1,7},{2,4},{3,5},{4,2},{5,3},{6,0},{7,1},{8,14},{9,15},{10,... | collective-permute-start | bytes 3833864 | tf_op jit(solution)/shard_map/ppermute | solution.py:129
  41.5 1.8 spread.1
  44.5 2.4 %collective-permute-start.9 = (bf16[2,32,4992]{2,1,0:T(8,128)(2,1)S(1)}, bf16[2,32,4992]{2,1,0:T(8,128)(2,1)S(1)}, u32[]{:S(2)}, u32[]{:S(2)}) collective-permute-start(bf16[2,32,4992]{2,1,0:T(8,128)(2,1)S(1)} %get-tuple-element.37), channel_id=1, source_target_pairs={{0,3},{1,2},{2,1},{3,0},{4,7},{5,6},{6,5},{7,4},{8,11},{9,10},{10,... | collective-permute-start | bytes 1916936 | tf_op jit(solution)/shard_map/ppermute | solution.py:129
  46.9 3.3 %collective-permute-start.10 = (bf16[4,80,512]{2,1,0:T(8,128)(2,1)S(1)}, bf16[4,80,512]{2,1,0:T(8,128)(2,1)S(1)}, u32[]{:S(2)}, u32[]{:S(2)}) collective-permute-start(bf16[4,80,512]{2,1,0:T(8,128)(2,1)S(1)} %bitcast.17), channel_id=1, source_target_pairs={{0,32},{8,40},{16,48},{24,56},{32,0},{40,8},{48,16},{56,24},{64,96... | collective-permute-start | bytes 983048 | tf_op jit(solution)/shard_map/ppermute | solution.py:260
  50.2 5.8 %time_weights.1 = (bf16[13,2,256,256]{3,2,1,0:T(8,128)(2,1)S(1)}, f32[8,128]{1,0:T(8,128)S(1)}) custom-call(bf16[16,32,3328]{2,1,0:T(8,128)(2,1)S(1)} %bitcast.15, bf16[2,32,4992]{2,1,0:T(8,128)(2,1)S(1)} %get-tuple-element.35.behind_ref), custom_call_target="tpu_custom_call" | custom-call | flops 436207616 | bytes 7000000 | tf_op jit(solution)/shard_map/time_weights/pallas_call | solution.py:235
  56.0 1.7 copy-done.5
  57.7 10.8 %collective-permute-done.6.turned_ref = bf16[4,32,4992]{2,1,0:T(8,128)(2,1)S(1)} collective-permute-done((bf16[4,32,4992]{2,1,0:T(8,128)(2,1)S(1)}, bf16[4,32,4992]{2,1,0:T(8,128)(2,1)S(1)}, u32[]{:S(2)}, u32[]{:S(2)}) %collective-permute-start.6) | collective-permute-done | bytes 1277984 | tf_op jit(solution)/shard_map/ppermute | solution.py:129
  68.5 4.0 %collective-permute-done.9.refs_5_ = bf16[2,32,4992]{2,1,0:T(8,128)(2,1)S(1)} collective-permute-done((bf16[2,32,4992]{2,1,0:T(8,128)(2,1)S(1)}, bf16[2,32,4992]{2,1,0:T(8,128)(2,1)S(1)}, u32[]{:S(2)}, u32[]{:S(2)}) %collective-permute-start.9) | collective-permute-done | bytes 639008 | tf_op jit(solution)/shard_map/ppermute | solution.py:129
  72.5 6.0 %spatial_attention.1.refs_2_ = bf16[8,2,32,1664]{3,2,1,0:T(8,128)(2,1)} custom-call(s32[5]{0:T(128)S(1)} %copy-done.4, bf16[2,32,4992]{2,1,0:T(8,128)(2,1)S(1)} %copy-done.2, bf16[4,32,4992]{2,1,0:T(8,128)(2,1)S(1)} %collective-permute-done.across_ref, bf16[4,32,4992]{2,1,0:T(8,128)(2,1)S(1)} %collective-permute-done.6.turned_ref, ...), custom_call_target="tpu_custom_call" | custom-call | flops 872415232 | bytes 6815744 | tf_op jit(solution)/shard_map/spatial_attention/pallas_call | solution.py:185
  78.7 3.6 %all-to-all-start = ((bf16[8,2,32,1664]{3,2,1,0:T(8,128)(2,1)}), bf16[8,2,32,1664]{3,2,1,0:T(8,128)(2,1)S(1)}, u32[]{:S(2)}, u32[]{:S(2)}) async-start(bf16[8,2,32,1664]{3,2,1,0:T(8,128)(2,1)} %spatial_attention.1.refs_2_), calls=%async_computation | async-start | bytes 3407872 | tf_op jit(solution)/shard_map/all_to_all | solution.py:548
  82.3 9.6 %collective-permute-done.11.refs_1_ = bf16[8,80,512]{2,1,0:T(8,128)(2,1)S(1)} collective-permute-done((bf16[8,80,512]{2,1,0:T(8,128)(2,1)S(1)}, bf16[8,80,512]{2,1,0:T(8,128)(2,1)S(1)}, u32[]{:S(2)}, u32[]{:S(2)}) %collective-permute-start.11) | collective-permute-done | bytes 655392 | tf_op jit(solution)/shard_map/ppermute | solution.py:260
  93.1 10.3 %all-to-all-done.value = bf16[8,2,32,1664]{3,2,1,0:T(8,128)(2,1)S(1)} async-done(((bf16[8,2,32,1664]{3,2,1,0:T(8,128)(2,1)}), bf16[8,2,32,1664]{3,2,1,0:T(8,128)(2,1)S(1)}, u32[]{:S(2)}, u32[]{:S(2)}) %all-to-all-start) | async-done | bytes 1703968 | tf_op jit(solution)/shard_map/all_to_all | solution.py:548
  103.4 2.0 %copy-done.6 = bf16[13,2,256,256]{3,2,1,0:T(8,128)(2,1)S(1)} copy-done((bf16[13,2,256,256]{3,2,1,0:T(8,128)(2,1)S(1)}, bf16[13,2,256,256]{3,2,1,0:T(8,128)(2,1)}, u32[]{:S(2)}) %copy-start.6) | copy-done | bytes 3407896
  105.4 9.2 %token_part.1 = (bf16[16,32,512]{2,1,0:T(8,128)(2,1)}, f32[8,2,32,128]{3,2,1,0:T(8,128)}, bf16[32,80,512]{2,1,0:T(8,128)(2,1)}, f32[32,128]{1,0:T(8,128)S(1)}) custom-call(s32[5]{0:T(128)S(1)} %copy-done.4, bf16[8,2,32,1664]{3,2,1,0:T(8,128)(2,1)S(1)} %all-to-all-done.value, bf16[13,2,256,256]{3,2,1,0:T(8,128)(2,1)S(1)} %copy-done.6, ...), custom_call_target="tpu_custom_call" | custom-call | flops 4499999744 | bytes 12000000 | tf_op jit(solution)/shard_map/token_part/pallas_call | solution.py:355
  114.5 3.4 %all-to-all-start.1 = ((f32[8,2,32,128]{3,2,1,0:T(8,128)}), f32[8,2,32,128]{3,2,1,0:T(8,128)S(1)}, u32[]{:S(2)}, u32[]{:S(2)}) async-start(f32[8,2,32,128]{3,2,1,0:T(8,128)} %get-tuple-element.41), calls=%async_computation.1 | async-start | bytes 524288 | tf_op jit(solution)/shard_map/all_to_all | solution.py:552
  118.6 6.2 %all-to-all-done.1.stats_ref = f32[8,2,32,128]{3,2,1,0:T(8,128)S(1)} async-done(((f32[8,2,32,128]{3,2,1,0:T(8,128)}), f32[8,2,32,128]{3,2,1,0:T(8,128)S(1)}, u32[]{:S(2)}, u32[]{:S(2)}) %all-to-all-start.1) | async-done | bytes 262176 | tf_op jit(solution)/shard_map/all_to_all | solution.py:552
  124.8 2.9 %coef_part.1 = (bf16[16,80,512]{2,1,0:T(8,128)(2,1)S(1)}, bf16[16,80,512]{2,1,0:T(8,128)(2,1)S(1)}, f32[1,1]{1,0:T(1,128)}) custom-call(s32[5]{0:T(128)S(1)} %copy-done.4, s32[1]{0:T(128)S(6)} %copy.10.pos_ref, f32[8,2,32,128]{3,2,1,0:T(8,128)S(1)} %all-to-all-done.1.stats_ref, f32[32,128]{1,0:T(8,128)S(1)} %get-tuple-element.42.lens_ref, ...), custom_call_target="tpu_custom_call" | custom-call | flops 4000000 | bytes 6000000 | tf_op jit(solution)/shard_map/coef_part/pallas_call | solution.py:429
  127.9 3.0 %collective-permute-done.13.got_ref = bf16[16,80,512]{2,1,0:T(8,128)(2,1)S(1)} collective-permute-done((bf16[16,80,512]{2,1,0:T(8,128)(2,1)S(1)}, bf16[16,80,512]{2,1,0:T(8,128)(2,1)S(1)}, u32[]{:S(2)}, u32[]{:S(2)}) %collective-permute-start.13) | collective-permute-done | bytes 1310752 | tf_op jit(solution)/shard_map/ppermute | solution.py:505
  132.2 1.7 collective-permute-start.15
  133.9 7.7 %collective-permute-done.14.a_got = bf16[8,80,256]{2,1,0:T(8,128)(2,1)S(1)} collective-permute-done((bf16[8,80,256]{2,1,0:T(8,128)(2,1)S(1)}, bf16[8,80,256]{2,1,0:T(8,128)(2,1)S(1)}, u32[]{:S(2)}, u32[]{:S(2)}) %collective-permute-start.14) | collective-permute-done | bytes 327712 | tf_op jit(solution)/shard_map/ppermute | solution.py:510
  143.1 1.7 collective-permute-start.16
  144.8 4.9 %collective-permute-done.16.a_got = bf16[8,80,128]{2,1,0:T(8,128)(2,1)S(1)} collective-permute-done((bf16[8,80,128]{2,1,0:T(8,128)(2,1)S(1)}, bf16[8,80,128]{2,1,0:T(8,128)(2,1)S(1)}, u32[]{:S(2)}, u32[]{:S(2)}) %collective-permute-start.16) | collective-permute-done | bytes 163872 | tf_op jit(solution)/shard_map/ppermute | solution.py:516
  150.2 23.0 %all_to_all.20.parts = bf16[16,80,128]{2,1,0:T(8,128)(2,1)S(1)} all-to-all(bf16[16,80,128]{2,1,0:T(8,128)(2,1)S(1)} %third_sum.1), channel_id=1, replica_groups={{0,16,32,48,64,80,96,112,128,144,160,176,192,208,224,240},{8,24,40,56,7..., dimensions={0} | all-to-all | bytes 655360 | tf_op jit(solution)/shard_map/all_to_all | solution.py:521
  173.3 9.4 %all_to_all.21.parts = bf16[8,80,128]{2,1,0:T(8,128)(2,1)S(1)} all-to-all(bf16[8,80,128]{2,1,0:T(8,128)(2,1)S(1)} %owned_sum.1), channel_id=1, replica_groups=mesh['dp'=32,'space'=8] {'space'}, dimensions={0} | all-to-all | bytes 327680 | tf_op jit(solution)/shard_map/all_to_all | solution.py:526
  (46 shorter events, 15.6 us)
Async XLA Ops:
  4.4 25.9 %collective-permute-start.1 = (bf16[2,32,4992]{2,1,0:T(8,128)(2,1)}, bf16[2,32,4992]{2,1,0:T(8,128)(2,1)S(1)}, u32[]{:S(2)}, u32[]{:S(2)}) collective-permute-start(bf16[2,32,4992]{2,1,0:T(8,128)(2,1)} %get-tuple-element.31), channel_id=1, source_target_pairs={{0,1},{1,0},{2,3},{3,2},{4,5},{5,4},{6,7},{7,6},{8,9},{9,8},{10,11... | collective-permute-start | bytes 1916936 | tf_op jit(solution)/shard_map/ppermute | solution.py:129
  6.0 7.6 %copy-start.7 = (bf16[1,77,512]{2,1,0:T(8,128)(2,1)S(1)}, bf16[1,77,512]{2,1,0:T(8,128)(2,1)}, u32[]{:S(2)}) copy-start(bf16[1,77,512]{2,1,0:T(8,128)(2,1)} %param.9) | copy-start | bytes 236548
  6.0 24.2 %collective-permute-start.2 = (bf16[2,32,4992]{2,1,0:T(8,128)(2,1)}, bf16[2,32,4992]{2,1,0:T(8,128)(2,1)S(1)}, u32[]{:S(2)}, u32[]{:S(2)}) collective-permute-start(bf16[2,32,4992]{2,1,0:T(8,128)(2,1)} %get-tuple-element.32), channel_id=1, source_target_pairs={{0,2},{1,3},{2,0},{3,1},{4,6},{5,7},{6,4},{7,5},{8,10},{9,11},{10,... | collective-permute-start | bytes 1916936 | tf_op jit(solution)/shard_map/ppermute | solution.py:129
  10.3 31.2 %collective-permute-start = (bf16[4,32,4992]{2,1,0:T(8,128)(2,1)}, bf16[4,32,4992]{2,1,0:T(8,128)(2,1)S(1)}, u32[]{:S(2)}, u32[]{:S(2)}) collective-permute-start(bf16[4,32,4992]{2,1,0:T(8,128)(2,1)} %across.1), channel_id=1, source_target_pairs={{0,6},{1,7},{2,4},{3,5},{4,2},{5,3},{6,0},{7,1},{8,14},{9,15},{10,... | collective-permute-start | bytes 3833864 | tf_op jit(solution)/shard_map/ppermute | solution.py:129
  12.5 23.2 %collective-permute-start.3 = (bf16[2,32,4992]{2,1,0:T(8,128)(2,1)}, bf16[2,32,4992]{2,1,0:T(8,128)(2,1)S(1)}, u32[]{:S(2)}, u32[]{:S(2)}) collective-permute-start(bf16[2,32,4992]{2,1,0:T(8,128)(2,1)} %get-tuple-element.33), channel_id=1, source_target_pairs={{0,3},{1,2},{2,1},{3,0},{4,7},{5,6},{6,5},{7,4},{8,11},{9,10},{10,... | collective-permute-start | bytes 1916936 | tf_op jit(solution)/shard_map/ppermute | solution.py:129
  13.7 5.7 %collective-permute-start.4 = (bf16[1,80,512]{2,1,0:T(8,128)(2,1)S(1)}, bf16[1,80,512]{2,1,0:T(8,128)(2,1)S(1)}, u32[]{:S(2)}, u32[]{:S(2)}) collective-permute-start(bf16[1,80,512]{2,1,0:T(8,128)(2,1)S(1)} %concatenate.3.refs_0_), channel_id=1, source_target_pairs={{0,129},{1,128},{2,131},{3,130},{4,133},{5,132},{6,135},{7,134},{8... | collective-permute-start | bytes 245768 | tf_op jit(solution)/shard_map/ppermute | solution.py:270
  19.4 16.3 %copy-start.4 = (s32[5]{0:T(128)S(1)}, s32[5]{0:T(128)}, u32[]{:S(2)}) copy-start(s32[5]{0:T(128)} %stack.23.place_ref) | copy-start | bytes 64
  19.4 10.8 %collective-permute-start.5 = (bf16[2,80,512]{2,1,0:T(8,128)(2,1)S(1)}, bf16[2,80,512]{2,1,0:T(8,128)(2,1)S(1)}, u32[]{:S(2)}, u32[]{:S(2)}) collective-permute-start(bf16[2,80,512]{2,1,0:T(8,128)(2,1)S(1)} %bitcast.21), channel_id=1, source_target_pairs={{0,64},{8,72},{16,80},{24,88},{32,96},{40,104},{48,112},{56,120},{... | collective-permute-start | bytes 491528 | tf_op jit(solution)/shard_map/ppermute | solution.py:260
  30.3 11.3 %copy-start.1 = (bf16[3,32,4992]{2,1,0:T(8,128)(2,1)S(1)}, bf16[3,32,4992]{2,1,0:T(8,128)(2,1)}, u32[]{:S(2)}) copy-start(bf16[3,32,4992]{2,1,0:T(8,128)(2,1)} %get-tuple-element.34.seconds_ref) | copy-start | bytes 2875396
  35.7 1.0 copy-start.3
  36.7 13.5 %copy-start = (bf16[1,16,32,3328]{3,2,1,0:T(8,128)(2,1)S(1)}, bf16[1,16,32,3328]{3,2,1,0:T(8,128)(2,1)}, u32[]{:S(2)}) copy-start(bf16[1,16,32,3328]{3,2,1,0:T(8,128)(2,1)} %param.7) | copy-start | bytes 10223620
  38.0 30.4 %collective-permute-start.6 = (bf16[4,32,4992]{2,1,0:T(8,128)(2,1)S(1)}, bf16[4,32,4992]{2,1,0:T(8,128)(2,1)S(1)}, u32[]{:S(2)}, u32[]{:S(2)}) collective-permute-start(bf16[4,32,4992]{2,1,0:T(8,128)(2,1)S(1)} %turn.1), channel_id=1, source_target_pairs={{0,6},{1,7},{2,4},{3,5},{4,2},{5,3},{6,0},{7,1},{8,14},{9,15},{10,... | collective-permute-start | bytes 3833864 | tf_op jit(solution)/shard_map/ppermute | solution.py:129
  43.3 25.2 %collective-permute-start.7 = (bf16[2,32,4992]{2,1,0:T(8,128)(2,1)S(1)}, bf16[2,32,4992]{2,1,0:T(8,128)(2,1)S(1)}, u32[]{:S(2)}, u32[]{:S(2)}) collective-permute-start(bf16[2,32,4992]{2,1,0:T(8,128)(2,1)S(1)} %get-tuple-element.35.behind_ref), channel_id=1, source_target_pairs={{0,1},{1,0},{2,3},{3,2},{4,5},{5,4},{6,7},{7,6},{8,9},{9,8},{10,11... | collective-permute-start | bytes 1916936 | tf_op jit(solution)/shard_map/ppermute | solution.py:129
  44.3 24.2 %collective-permute-start.8 = (bf16[2,32,4992]{2,1,0:T(8,128)(2,1)S(1)}, bf16[2,32,4992]{2,1,0:T(8,128)(2,1)S(1)}, u32[]{:S(2)}, u32[]{:S(2)}) collective-permute-start(bf16[2,32,4992]{2,1,0:T(8,128)(2,1)S(1)} %get-tuple-element.36), channel_id=1, source_target_pairs={{0,2},{1,3},{2,0},{3,1},{4,6},{5,7},{6,4},{7,5},{8,10},{9,11},{10,... | collective-permute-start | bytes 1916936 | tf_op jit(solution)/shard_map/ppermute | solution.py:129
  44.5 27.9 %collective-permute-start.9 = (bf16[2,32,4992]{2,1,0:T(8,128)(2,1)S(1)}, bf16[2,32,4992]{2,1,0:T(8,128)(2,1)S(1)}, u32[]{:S(2)}, u32[]{:S(2)}) collective-permute-start(bf16[2,32,4992]{2,1,0:T(8,128)(2,1)S(1)} %get-tuple-element.37), channel_id=1, source_target_pairs={{0,3},{1,2},{2,1},{3,0},{4,7},{5,6},{6,5},{7,4},{8,11},{9,10},{10,... | collective-permute-start | bytes 1916936 | tf_op jit(solution)/shard_map/ppermute | solution.py:129
  46.9 31.5 %collective-permute-start.10 = (bf16[4,80,512]{2,1,0:T(8,128)(2,1)S(1)}, bf16[4,80,512]{2,1,0:T(8,128)(2,1)S(1)}, u32[]{:S(2)}, u32[]{:S(2)}) collective-permute-start(bf16[4,80,512]{2,1,0:T(8,128)(2,1)S(1)} %bitcast.17), channel_id=1, source_target_pairs={{0,32},{8,40},{16,48},{24,56},{32,0},{40,8},{48,16},{56,24},{64,96... | collective-permute-start | bytes 983048 | tf_op jit(solution)/shard_map/ppermute | solution.py:260
  50.2 22.3 %copy-start.2 = (bf16[2,32,4992]{2,1,0:T(8,128)(2,1)S(1)}, bf16[2,32,4992]{2,1,0:T(8,128)(2,1)}, u32[]{:S(2)}) copy-start(bf16[2,32,4992]{2,1,0:T(8,128)(2,1)} %get-tuple-element.29.kept_ref) | copy-start | bytes 1916932
  56.0 1.7 copy-start.5
  78.5 13.4 %collective-permute-start.11 = (bf16[8,80,512]{2,1,0:T(8,128)(2,1)S(1)}, bf16[8,80,512]{2,1,0:T(8,128)(2,1)S(1)}, u32[]{:S(2)}, u32[]{:S(2)}) collective-permute-start(bf16[8,80,512]{2,1,0:T(8,128)(2,1)S(1)} %bitcast.19), channel_id=1, source_target_pairs={{0,16},{8,24},{16,0},{24,8},{32,48},{40,56},{48,32},{56,40},{64,80... | collective-permute-start | bytes 1966088 | tf_op jit(solution)/shard_map/ppermute | solution.py:260
  78.7 24.7 %all-to-all-start = ((bf16[8,2,32,1664]{3,2,1,0:T(8,128)(2,1)}), bf16[8,2,32,1664]{3,2,1,0:T(8,128)(2,1)S(1)}, u32[]{:S(2)}, u32[]{:S(2)}) async-start(bf16[8,2,32,1664]{3,2,1,0:T(8,128)(2,1)} %spatial_attention.1.refs_2_), calls=%async_computation | async-start | bytes 3407872 | tf_op jit(solution)/shard_map/all_to_all | solution.py:548
  93.1 10.3 %collective-permute-start.12 = (bf16[16,80,512]{2,1,0:T(8,128)(2,1)}, bf16[16,80,512]{2,1,0:T(8,128)(2,1)}, u32[]{:S(2)}, u32[]{:S(2)}) collective-permute-start(bf16[16,80,512]{2,1,0:T(8,128)(2,1)} %bitcast.11.mine_ref), channel_id=1, source_target_pairs={{0,8},{8,0},{16,24},{24,16},{32,40},{40,32},{48,56},{56,48},{64,72... | collective-permute-start | bytes 3932168 | tf_op jit(solution)/shard_map/ppermute | solution.py:260
  103.4 2.0 %copy-start.6 = (bf16[13,2,256,256]{3,2,1,0:T(8,128)(2,1)S(1)}, bf16[13,2,256,256]{3,2,1,0:T(8,128)(2,1)}, u32[]{:S(2)}) copy-start(bf16[13,2,256,256]{3,2,1,0:T(8,128)(2,1)} %copy-done.5) | copy-start | bytes 10223620
  114.5 10.3 %all-to-all-start.1 = ((f32[8,2,32,128]{3,2,1,0:T(8,128)}), f32[8,2,32,128]{3,2,1,0:T(8,128)S(1)}, u32[]{:S(2)}, u32[]{:S(2)}) async-start(f32[8,2,32,128]{3,2,1,0:T(8,128)} %get-tuple-element.41), calls=%async_computation.1 | async-start | bytes 524288 | tf_op jit(solution)/shard_map/all_to_all | solution.py:552
  127.8 3.1 %collective-permute-start.13 = (bf16[16,80,512]{2,1,0:T(8,128)(2,1)S(1)}, bf16[16,80,512]{2,1,0:T(8,128)(2,1)S(1)}, u32[]{:S(2)}, u32[]{:S(2)}) collective-permute-start(bf16[16,80,512]{2,1,0:T(8,128)(2,1)S(1)} %get-tuple-element.45), channel_id=1, source_target_pairs={{0,8},{8,0},{16,24},{24,16},{32,40},{40,32},{48,56},{56,48},{64,72... | collective-permute-start | bytes 3932168 | tf_op jit(solution)/shard_map/ppermute | solution.py:505
  131.8 9.8 %collective-permute-start.14 = (bf16[8,80,256]{2,1,0:T(8,128)(2,1)S(1)}, bf16[8,80,256]{2,1,0:T(8,128)(2,1)S(1)}, u32[]{:S(2)}, u32[]{:S(2)}) collective-permute-start(bf16[8,80,256]{2,1,0:T(8,128)(2,1)S(1)} %get-tuple-element.47), channel_id=1, source_target_pairs={{0,2},{1,3},{2,0},{3,1},{4,6},{5,7},{6,4},{7,5},{8,10},{9,11},{10,... | collective-permute-start | bytes 983048 | tf_op jit(solution)/shard_map/ppermute | solution.py:510
  132.2 10.8 %collective-permute-start.15 = (bf16[8,80,256]{2,1,0:T(8,128)(2,1)S(1)}, bf16[8,80,256]{2,1,0:T(8,128)(2,1)S(1)}, u32[]{:S(2)}, u32[]{:S(2)}) collective-permute-start(bf16[8,80,256]{2,1,0:T(8,128)(2,1)S(1)} %get-tuple-element.49), channel_id=1, source_target_pairs={{0,6},{1,7},{2,4},{3,5},{4,2},{5,3},{6,0},{7,1},{8,14},{9,15},{10,... | collective-permute-start | bytes 983048 | tf_op jit(solution)/shard_map/ppermute | solution.py:511
  143.1 6.6 %collective-permute-start.16 = (bf16[8,80,128]{2,1,0:T(8,128)(2,1)S(1)}, bf16[8,80,128]{2,1,0:T(8,128)(2,1)S(1)}, u32[]{:S(2)}, u32[]{:S(2)}) collective-permute-start(bf16[8,80,128]{2,1,0:T(8,128)(2,1)S(1)} %get-tuple-element.51), channel_id=1, source_target_pairs={{0,6},{1,7},{2,4},{3,5},{4,2},{5,3},{6,0},{7,1},{8,14},{9,15},{10,... | collective-permute-start | bytes 491528 | tf_op jit(solution)/shard_map/ppermute | solution.py:516
  144.8 5.3 %collective-permute-start.17 = (bf16[8,80,128]{2,1,0:T(8,128)(2,1)S(1)}, bf16[8,80,128]{2,1,0:T(8,128)(2,1)S(1)}, u32[]{:S(2)}, u32[]{:S(2)}) collective-permute-start(bf16[8,80,128]{2,1,0:T(8,128)(2,1)S(1)} %get-tuple-element.53), channel_id=1, source_target_pairs={{0,2},{1,3},{2,0},{3,1},{4,6},{5,7},{6,4},{7,5},{8,10},{9,11},{10,... | collective-permute-start | bytes 491528 | tf_op jit(solution)/shard_map/ppermute | solution.py:517

commit v8 on v7

--- a/solution.py
+++ b/solution.py
@@ -35,8 +35,13 @@
     return (g1 * 2 + ((a >> 1) ^ g1)) * 2 + (a & 1)
 
 
-def quad_place(place_ref):
-    x, y = place_ref[2], place_ref[3]
+def place():
+    dp, space = lax.axis_index("dp"), lax.axis_index("space")
+    return dp >> 4, dp & 1, space >> 1, space & 1, (dp >> 1) & 7
+
+
+def quad_place():
+    _, _, x, y, _ = place()
     return x >> 1, ((x >> 1) ^ (x & 1)) * 2 + y
 
 
@@ -74,7 +79,7 @@
 def copying(kernel, name, operands, shapes, count, params=FULL):
     return pl.pallas_call(
         kernel,
-        in_specs=[SMEM] + [ANY] * (len(operands) - 1),
+        in_specs=[ANY] * len(operands),
         out_specs=[ANY] * len(shapes),
         out_shape=[jax.ShapeDtypeStruct((n,) + ROW, jnp.bfloat16) for n in shapes],
         scratch_shapes=[
@@ -87,69 +92,74 @@
     )(*operands)
 
 
-def across_kernel(place_ref, clip_ref, out_ref, buf, sems):
-    g1, _ = quad_place(place_ref)
+def relay_kernel(clip_ref, one, two, three, buf, sems):
+    g1, a = quad_place()
+    refs = ((1, one), (2, two), (3, three))
+    copied([(clip_ref.at[2 * owner(1 - g1, a ^ k)], ref.at[0]) for k, ref in refs], buf, sems)
+
+
+def across_kernel(clip_ref, out_ref, buf, sems):
+    g1, _ = quad_place()
     copied([(clip_ref.at[2 * owner(1 - g1, a) + 1], out_ref.at[a]) for a in range(4)], buf, sems)
 
 
-def quads_kernel(place_ref, clip_ref, one, two, three, buf, sems):
-    _, a = quad_place(place_ref)
+def quads_kernel(clip_ref, one, two, three, buf, sems):
+    g1, a = quad_place()
     pairs = [
-        (clip_ref.at[2 * owner(g, a ^ k)], ref.at[g])
+        (clip_ref.at[2 * owner(g1, a ^ k) + f], ref.at[f])
         for k, ref in ((1, one), (2, two), (3, three))
-        for g in range(2)
+        for f in range(2)
     ]
     copied(pairs, buf, sems)
 
 
-def own_kernel(place_ref, clip_ref, first, seconds, kept, buf, sems):
-    g1, a = quad_place(place_ref)
+def own_kernel(clip_ref, first, kept, buf, sems):
+    g1, a = quad_place()
     pairs = [(clip_ref.at[2 * owner(1 - g1, a)], first.at[0])]
-    pairs += [(clip_ref.at[2 * owner(g1, a ^ k) + 1], seconds.at[k - 1]) for k in (1, 2, 3)]
     pairs += [(clip_ref.at[2 * owner(g1, a) + f], kept.at[f]) for f in range(2)]
     copied(pairs, buf, sems)
 
 
-def turn_kernel(place_ref, first_ref, one, two, three, behind_ref, out_ref, buf, sems):
-    g1, _ = quad_place(place_ref)
-    pairs = [(first_ref.at[0], out_ref.at[0])]
-    pairs += [(ref.at[1 - g1], out_ref.at[k]) for k, ref in ((1, one), (2, two), (3, three))]
-    copied(pairs, buf, sems)
-
-
-def spread_kernel(place_ref, seconds_ref, across_ref, one, two, three, buf, sems):
-    _, a = quad_place(place_ref)
-    pairs = []
-    for k, ref in ((1, one), (2, two), (3, three)):
-        pairs += [(seconds_ref.at[k - 1], ref.at[0]), (across_ref.at[a ^ k], ref.at[1])]
-    copied(pairs, buf, sems)
+def turn_kernel(first_ref, one, two, three, behind_ref, out_ref, buf, sems):
+    refs = (first_ref, one, two, three)
+    copied([(ref.at[0], out_ref.at[k]) for k, ref in enumerate(refs)], buf, sems)
+
+
+def spread_kernel(across_ref, behind_ref, one, two, three, buf, sems):
+    _, a = quad_place()
+    refs = ((1, one), (2, two), (3, three))
+    copied([(across_ref.at[a ^ k], ref.at[0]) for k, ref in refs], buf, sems)
 
 
 def swap(value, bits):
     return lax.ppermute(value, "space", [(s, s ^ bits) for s in range(8)])
 
 
-def bring_frames(clip, place, behind):
-    (across,) = copying(across_kernel, "across", (place, clip), (4,), 4)
+def swap_quad(values):
+    return [swap(value, k) for k, value in zip((1, 2, 3), values)]
+
+
+def bring_frames(clip, behind):
+    relays = swap_quad(copying(relay_kernel, "relay", (clip,), (1, 1, 1), 3))
+    (across,) = copying(across_kernel, "across", (clip,), (4,), 4)
     across = swap(across, 6)
-    quads = copying(quads_kernel, "quads", (place, clip), (2, 2, 2), 6)
-    quads = [swap(quad, k) for k, quad in zip((1, 2, 3), quads)]
-    first, seconds, kept = copying(own_kernel, "own", (place, clip), (1, 3, 2), 6)
+    quads = copying(quads_kernel, "quads", (clip,), (2, 2, 2), 6)
+    prepared = quads[0]
+    quads = swap_quad(quads)
+    first, kept = copying(own_kernel, "own", (clip,), (1, 2), 3)
     few = pltpu.CompilerParams(vmem_limit_bytes=8 * MIB)
-    (turned,) = copying(turn_kernel, "turn", (place, first, *quads, behind), (4,), 4, few)
+    (turned,) = copying(turn_kernel, "turn", (first, *relays, prepared), (4,), 4, few)
     turned = swap(turned, 6)
-    pairs = copying(spread_kernel, "spread", (place, seconds, across), (2, 2, 2), 6, few)
-    started = pairs[0]
-    pairs = [swap(pair, k) for k, pair in zip((1, 2, 3), pairs)]
-    return (kept, across, turned, *quads, *pairs), started
-
-
-def spatial_kernel(place_ref, kept_ref, across_ref, turned_ref, *refs):
-    quads, pairs, (_, out_ref, buf, res, sems, store_sems) = refs[:3], refs[3:6], refs[6:]
-    g1, a = quad_place(place_ref)
-    first = [kept_ref.at[0]] + [ref.at[g1] for ref in quads] + [turned_ref.at[k] for k in range(4)]
-    second = [kept_ref.at[1]] + [ref.at[0] for ref in pairs]
-    second += [across_ref.at[a]] + [ref.at[1] for ref in pairs]
+    spread = copying(spread_kernel, "spread", (across, behind), (1, 1, 1), 3, few)
+    return (kept, across, turned, *quads, *swap_quad(spread)), spread[0]
+
+
+def spatial_kernel(kept_ref, across_ref, turned_ref, *refs):
+    quads, spread, (_, out_ref, buf, res, sems, store_sems) = refs[:3], refs[3:6], refs[6:]
+    g1, a = quad_place()
+    first = [ref.at[0] for ref in (kept_ref, *quads)] + [turned_ref.at[k] for k in range(4)]
+    second = [ref.at[1] for ref in (kept_ref, *quads)]
+    second += [across_ref.at[a]] + [ref.at[0] for ref in spread]
     loads = [
         [pltpu.make_async_copy(src, buf.at[f, i], sems.at[f, i]) for i, src in enumerate(sources)]
         for f, sources in enumerate((first, second))
@@ -181,10 +191,10 @@
         store.wait()
 
 
-def spatial_attention(place, pieces, behind):
+def spatial_attention(pieces, behind):
     return pl.pallas_call(
         spatial_kernel,
-        in_specs=[SMEM] + [ANY] * (len(pieces) + 1),
+        in_specs=[ANY] * (len(pieces) + 1),
         out_specs=ANY,
         out_shape=jax.ShapeDtypeStruct((8, 2, LOCAL, FEATURES), jnp.bfloat16),
         scratch_shapes=[
@@ -200,7 +210,7 @@
             transcendentals=2 * HEADS * PATCHES * PATCHES,
         ),
         name="spatial_attention",
-    )(place, *pieces, behind)
+    )(*pieces, behind)
 
 
 ROWS = FRAMES * 16
@@ -284,20 +294,29 @@
 
 
 def token_kernel(
-    place_ref, value, time_ref, proj_ref, mine_ref, other_ref,
+    value_ref, time_ref, proj_ref, mine_ref, other_ref,
     emb_ref, all_stats_ref, grad_ref, lens_ref,
-    proj, mine, comb, video, grads, stats_ref, sems, grad_sems,
+    value, time, proj, mine, comb, video, grads, stats_ref, sems, time_sems, grad_sems,
 ):
+    value_load = pltpu.make_async_copy(value_ref, value, sems.at[3])
+    value_load.start()
+    time_loads = [
+        pltpu.make_async_copy(time_ref.at[h], time.at[h], time_sems.at[h]) for h in range(HEADS)
+    ]
+    for load in time_loads:
+        load.start()
     proj_load = pltpu.make_async_copy(proj_ref, proj, sems.at[0])
     mine_load = pltpu.make_async_copy(mine_ref, mine, sems.at[1])
     proj_load.start()
     mine_load.start()
+    value_load.wait()
     for h in range(HEADS):
+        time_loads[h].wait()
         cols = pl.ds(h * HD, HD)
         for g in range(LOCAL // 16):
             part = pl.ds(g * 16, 16)
             v = value[:, :, part, cols].reshape(ROWS, HD)
-            o = jnp.dot(time_ref[h, g], v, preferred_element_type=jnp.float32)
+            o = jnp.dot(time[h, g], v, preferred_element_type=jnp.float32)
             o = (v.astype(jnp.float32) + o).astype(jnp.bfloat16)
             comb[:, part, cols] = o.reshape(FRAMES, 16, HD)
     tokens = FRAMES * LOCAL
@@ -315,7 +334,7 @@
     eye = lax.broadcasted_iota(jnp.int32, (PADDED, 128), 0) == lax.broadcasted_iota(
         jnp.int32, (PADDED, 128), 1
     )
-    y_hi, core, z = place_ref[0], place_ref[1], place_ref[4]
+    y_hi, core, _, _, z = place()
     group = 8
     stores = []
     for i, (ref, c) in enumerate(((mine, core), (other_ref, 1 - core))):
@@ -350,38 +369,41 @@
         store.wait()
 
 
-def token_part(place, spatial, time, proj_weight, mine, other):
+def token_part(spatial, time, proj_weight, mine, other):
     bf16 = jnp.bfloat16
     return pl.pallas_call(
         token_kernel,
-        in_specs=[SMEM, VMEM, VMEM, FAR_OFF, FAR_OFF, VMEM],
-        out_specs=[FAR_OFF, VMEM, FAR_OFF, VMEM],
+        in_specs=[ANY, ANY, ANY, ANY, VMEM],
+        out_specs=[ANY, VMEM, ANY, VMEM],
         out_shape=[
-            pltpu.HBM((FRAMES, LOCAL, EMB), bf16),
+            jax.ShapeDtypeStruct((FRAMES, LOCAL, EMB), bf16),
             jax.ShapeDtypeStruct((8, 2, CAPTIONS, 128), jnp.float32),
-            pltpu.HBM((CAPTIONS, PADDED, EMB), bf16),
+            jax.ShapeDtypeStruct((CAPTIONS, PADDED, EMB), bf16),
             jax.ShapeDtypeStruct((CAPTIONS, 128), jnp.float32),
         ],
         scratch_shapes=[
+            pltpu.VMEM((8, 2, LOCAL, FEATURES), bf16),
+            pltpu.VMEM((HEADS, 2, ROWS, ROWS), bf16),
             pltpu.VMEM((FEATURES, EMB), bf16),
             pltpu.VMEM((CAPTIONS // 2, PADDED, EMB), bf16),
             pltpu.VMEM((FRAMES, LOCAL, FEATURES), bf16),
             pltpu.VMEM((FRAMES, LOCAL, EMB), bf16),
             pltpu.VMEM((CAPTIONS, PADDED, EMB), bf16),
             pltpu.VMEM((2, CAPTIONS, 128), jnp.float32),
-            pltpu.SemaphoreType.DMA((3,)),
+            pltpu.SemaphoreType.DMA((4,)),
+            pltpu.SemaphoreType.DMA((HEADS,)),
             pltpu.SemaphoreType.DMA((CAPTIONS,)),
         ],
-        compiler_params=GRANT,
+        compiler_params=pltpu.CompilerParams(vmem_limit_bytes=48 * MIB),
         cost_estimate=pl.CostEstimate(
             flops=4_500_000_000, bytes_accessed=12_000_000, transcendentals=1_300_000
         ),
         name="token_part",
-    )(place, spatial, time, held(proj_weight), held(mine), other)
+    )(spatial, time, proj_weight, mine, other)
 
 
 def coef_kernel(
-    place_ref, pos_ref, stats_ref, lens_ref, grad_ref, send_ref, keep_ref, loss_ref, hold, grad, sems
+    pos_ref, stats_ref, lens_ref, grad_ref, send_ref, keep_ref, loss_ref, hold, grad, sems
 ):
     group = 8
     loads = [
@@ -409,13 +431,13 @@
     loss_ref[...] = log_total - jnp.sum(jnp.where(onehot, logits, 0.0), axis=0, keepdims=True)
     grad_logit = LOGIT_SCALE * (jnp.exp(logits - log_total) - onehot.astype(jnp.float32))
     coef = jnp.where(live, grad_logit / lens_col, 0.0)
-    mine = stats_ref[place_ref[2] * 2 + place_ref[3], 0]
+    mine = stats_ref[lax.axis_index("space"), 0]
     hold[...] = coef * jnp.exp2((mine - soft) * SHARP_LOG2)
 
     eye = lax.broadcasted_iota(jnp.int32, (PADDED, 128), 0) == lax.broadcasted_iota(
         jnp.int32, (PADDED, 128), 1
     )
-    core = place_ref[1]
+    core = lax.axis_index("dp") & 1
     for m in range(CAPTIONS // 2):
         if 2 * m % group == 0:
             loads[2 * m // group].wait()
@@ -424,11 +446,11 @@
             ref[m] = (grad[j].astype(jnp.float32) * col).astype(jnp.bfloat16)
 
 
-def coef_part(place, pos, stats, lens, grad):
+def coef_part(pos, stats, lens, grad):
     half = jax.ShapeDtypeStruct((CAPTIONS // 2, PADDED, EMB), jnp.bfloat16)
     return pl.pallas_call(
         coef_kernel,
-        in_specs=[SMEM, SMEM, VMEM, VMEM, FAR_OFF],
+        in_specs=[SMEM, VMEM, VMEM, ANY],
         out_specs=[VMEM] * 3,
         out_shape=[half, half, jax.ShapeDtypeStruct((1, 1), jnp.float32)],
         scratch_shapes=[
@@ -441,7 +463,7 @@
             flops=4_000_000, bytes_accessed=6_000_000, transcendentals=100_000
         ),
         name="coef_part",
-    )(place, pos, stats, lens, held(grad))
+    )(pos, stats, lens, grad)
 
 
 def small_call(kernel, name, operands, out_shapes, specs=None):
@@ -460,8 +482,8 @@
     return (a.astype(jnp.float32) + b.astype(jnp.float32)).astype(jnp.bfloat16)
 
 
-def first_sum_kernel(place_ref, keep_ref, got_ref, a_keep, a_send, b_keep, b_send):
-    x = place_ref[2]
+def first_sum_kernel(keep_ref, got_ref, a_keep, a_send, b_keep, b_send):
+    x = lax.axis_index("space") >> 1
     plan = (
         (0, ((a_keep, 0, 0), (a_send, 0, 1), (a_send, 1, 2), (a_keep, 1, 3))),
         (8, ((b_keep, 0, 0), (b_keep, 1, 1), (b_send, 1, 2), (b_send, 0, 3))),
@@ -498,14 +520,13 @@
         out[:, 0, pl.ds(x * 128, 128)] = total[:SLOTS]
 
 
-def reduce_gradient(place, send, keep):
+def reduce_gradient(send, keep):
     bf16 = jnp.bfloat16
     one = [(s, s ^ 2) for s in range(8)]
     three = [(s, s ^ 6) for s in range(8)]
     got = lax.ppermute(send, "dp", [(i, i ^ 1) for i in range(32)])
     a_keep, a_send, b_keep, b_send = small_call(
-        first_sum_kernel, "first_sum", (place, keep, got), [((8, PADDED, 256), bf16)] * 4,
-        [SMEM, VMEM, VMEM],
+        first_sum_kernel, "first_sum", (keep, got), [((8, PADDED, 256), bf16)] * 4
     )
     a_got = lax.ppermute(a_send, "space", one)
     b_got = lax.ppermute(b_send, "space", three)
@@ -529,29 +550,23 @@
 
 
 def on_device(clip_qkv, temporal_qk, proj_weight, caption_tokens, caption_lens, positive):
-    dp = lax.axis_index("dp")
-    space = lax.axis_index("space")
-    x, y = space >> 1, space & 1
-    place = jnp.stack([dp >> 4, dp & 1, x, y, (dp >> 1) & 7]).astype(jnp.int32)
     lens_row = jnp.broadcast_to(
         caption_lens.astype(jnp.bfloat16)[:, None, None], (1, PADDED - SLOTS, EMB)
     )
     caps = jnp.concatenate([caption_tokens, lens_row], axis=1)
     caps = doubled(caps, flip_y(caps))
     caps = doubled(caps, flip(caps, 8))
-    pieces, started = bring_frames(clip_qkv[0], place, caps)
+    pieces, started = bring_frames(clip_qkv[0], caps)
     time, done = time_weights(temporal_qk[0], started)
-    attended = spatial_attention(place, pieces, done)
-    caps = doubled(caps, flip(caps, 4), attended)
+    caps = doubled(caps, flip(caps, 4), done)
     caps = doubled(caps, flip(caps, 2))
     other = flip(caps, 1)
+    attended = spatial_attention(pieces, done)
     spatial = lax.all_to_all(attended, "space", split_axis=0, concat_axis=0, tiled=True)
-    video, stats, grad, lens = token_part(
-        place, spatial, time, proj_weight, caps, other
-    )
+    video, stats, grad, lens = token_part(spatial, time, proj_weight, caps, other)
     stats = lax.all_to_all(stats, "space", split_axis=0, concat_axis=0, tiled=True)
-    send, keep, loss = coef_part(place, positive, stats, lens, grad)
-    caption_grad = reduce_gradient(place, send, keep)
+    send, keep, loss = coef_part(positive, stats, lens, grad)
+    caption_grad = reduce_gradient(send, keep)
     return video[None], caption_grad, loss.reshape(1)
 
 

time: 184 us -> 191 us (1.038)
  waiting for transfers between devices: 68.5 us -> 80.3 us
  blocking collectives: 32.4 us -> 27.8 us
    all_to_all x1, waiting for transfers between devices: 10.3 us -> 18.6 us  [on_device(): lax.all_to_all(attended, 'space', split_axis=0, concat_axis=0, tiled=True)]
    ppermute x8 -> x11, waiting for transfers between devices: 20.8 us -> 29.1 us  [swap(): return lax.ppermute(value, 'space', [(s, s ^ bits) for s in range(8)])]
    ppermute x4, waiting for transfers between devices: 11.1 us -> 6.3 us  [flip(): return lax.ppermute(value, 'dp', [(i, i ^ bit) for i in range(32)])]
    all_to_all x1, blocking collectives: 23 us -> 18.4 us  [reduce_gradient(): lax.all_to_all(parts, 'dp', split_axis=0, concat_axis=0, tiled=True, axis...]
    ppermute x8 -> x11, starting transfers between devices: 12.2 us -> 8.78 us  [swap(): return lax.ppermute(value, 'space', [(s, s ^ bits) for s in range(8)])]
    ppermute x4, starting transfers between devices: 9.85 us -> 12.2 us  [flip(): return lax.ppermute(value, 'dp', [(i, i ^ bit) for i in range(32)])]
    unnamed x16 -> x20, local copies, waits for them, and re-layouts: 4.65 us -> 6.8 us
    pallas_call x8 -> x9, Pallas kernels: 30 us -> 28.2 us  [the longest x1 10.5 us: token_part(): pl.pallas_call(token_kernel, in_specs=[ANY, ANY, ANY, ANY, VMEM], out_spe...]
  transfers between devices with their start and end apart: 20 -> 23, of which waited for: 14 -> 16; matrix products, arithmetic and copies ran while one was open for 0% -> 0% of each run, Pallas kernels for 12% -> 11%
where the time goes in v8:
time: 191 us; the launch traced here: 190 us
  waiting for transfers between devices  80.3 us (42%)
  Pallas kernels  37.7 us (20%)
  starting transfers between devices  35.5 us (19%)
  blocking collectives  27.8 us (15%)
  local copies, waits for them, and re-layouts  6.81 us (4%)
  between operations  2.15 us (1%)
    ppermute x11, waiting for transfers between devices, swap(): return lax.ppermute(value, 'space', [(s, s ^ bits) for s in range(8)])  29.1 us
    all_to_all x1, waiting for transfers between devices, on_device(): lax.all_to_all(attended, 'space', split_axis=0, concat_axis=0, tiled=True)  18.6 us
    all_to_all x1, blocking collectives, reduce_gradient(): lax.all_to_all(parts, 'dp', split_axis=0, concat_axis=0, tiled=True, axis...  18.4 us
    ppermute x4, starting transfers between devices, flip(): return lax.ppermute(value, 'dp', [(i, i ^ bit) for i in range(32)])  12.2 us
    pallas_call x1, Pallas kernels, token_part(): pl.pallas_call(token_kernel, in_specs=[ANY, ANY, ANY, ANY, VMEM], out_spe...  10.5 us
    pallas_call x6, Pallas kernels, copying(): pl.pallas_call(kernel, in_specs=[ANY] * len(operands), out_specs=[ANY] *...  9.98 us
    all_to_all x1, blocking collectives, reduce_gradient(): lax.all_to_all(parts, 'space', split_axis=0, concat_axis=0, tiled=True)  9.43 us
    ppermute x11, starting transfers between devices, swap(): return lax.ppermute(value, 'space', [(s, s ^ bits) for s in range(8)])  8.78 us
  transfers between devices with their start and end apart: 23, of which 16 were waited for; matrix products, arithmetic and copies ran while one was open for 0% of the time, Pallas kernels for 11%

profile of v8, /device:TPU:32, one launch (start us, length us, event | category | flops | bytes accessed | tf_op | source)
XLA Modules:
  0.0 190.3 jit_solution(16784588019328957658)
XLA Ops:
  0.6 2.1 %across.1 = bf16[4,32,4992]{2,1,0:T(8,128)(2,1)} custom-call(bf16[16,32,4992]{2,1,0:T(8,128)(2,1)} %bitcast.18), custom_call_target="tpu_custom_call" | custom-call | bytes 6000000 | tf_op jit(solution)/shard_map/across/pallas_call | solution.py:80
  2.8 2.8 %collective-permute-start = (bf16[4,32,4992]{2,1,0:T(8,128)(2,1)}, bf16[4,32,4992]{2,1,0:T(8,128)(2,1)S(1)}, u32[]{:S(2)}, u32[]{:S(2)}) collective-permute-start(bf16[4,32,4992]{2,1,0:T(8,128)(2,1)} %across.1), channel_id=1, source_target_pairs={{0,6},{1,7},{2,4},{3,5},{4,2},{5,3},{6,0},{7,1},{8,14},{9,15},{10,... | collective-permute-start | bytes 3833864 | tf_op jit(solution)/shard_map/ppermute | solution.py:135
  5.6 2.0 %relay.1 = (bf16[1,32,4992]{2,1,0:T(8,128)(2,1)}, bf16[1,32,4992]{2,1,0:T(8,128)(2,1)}, bf16[1,32,4992]{2,1,0:T(8,128)(2,1)}) custom-call(bf16[16,32,4992]{2,1,0:T(8,128)(2,1)} %bitcast.19), custom_call_target="tpu_custom_call" | custom-call | bytes 6000000 | tf_op jit(solution)/shard_map/relay/pallas_call | solution.py:80
  11.2 2.4 %quads.1 = (bf16[2,32,4992]{2,1,0:T(8,128)(2,1)}, bf16[2,32,4992]{2,1,0:T(8,128)(2,1)}, bf16[2,32,4992]{2,1,0:T(8,128)(2,1)}) custom-call(bf16[16,32,4992]{2,1,0:T(8,128)(2,1)} %bitcast.20), custom_call_target="tpu_custom_call" | custom-call | bytes 6000000 | tf_op jit(solution)/shard_map/quads/pallas_call | solution.py:80
  13.6 2.1 %own.1 = (bf16[1,32,4992]{2,1,0:T(8,128)(2,1)}, bf16[2,32,4992]{2,1,0:T(8,128)(2,1)}) custom-call(bf16[16,32,4992]{2,1,0:T(8,128)(2,1)} %bitcast.21), custom_call_target="tpu_custom_call" | custom-call | bytes 6000000 | tf_op jit(solution)/shard_map/own/pallas_call | solution.py:80
  15.7 1.8 collective-permute-done.1.one
  17.5 2.5 %collective-permute-done.2.two = bf16[1,32,4992]{2,1,0:T(8,128)(2,1)S(1)} collective-permute-done((bf16[1,32,4992]{2,1,0:T(8,128)(2,1)}, bf16[1,32,4992]{2,1,0:T(8,128)(2,1)S(1)}, u32[]{:S(2)}, u32[]{:S(2)}) %collective-permute-start.2) | collective-permute-done | bytes 319520 | tf_op jit(solution)/shard_map/ppermute | solution.py:135
  20.0 5.0 %collective-permute-done.3.three = bf16[1,32,4992]{2,1,0:T(8,128)(2,1)S(1)} collective-permute-done((bf16[1,32,4992]{2,1,0:T(8,128)(2,1)}, bf16[1,32,4992]{2,1,0:T(8,128)(2,1)S(1)}, u32[]{:S(2)}, u32[]{:S(2)}) %collective-permute-start.3) | collective-permute-done | bytes 319520 | tf_op jit(solution)/shard_map/ppermute | solution.py:135
  28.0 3.1 %collective-permute-start.8 = (bf16[1,80,512]{2,1,0:T(8,128)(2,1)S(1)}, bf16[1,80,512]{2,1,0:T(8,128)(2,1)S(1)}, u32[]{:S(2)}, u32[]{:S(2)}) collective-permute-start(bf16[1,80,512]{2,1,0:T(8,128)(2,1)S(1)} %concatenate.3.refs_0_), channel_id=1, source_target_pairs={{0,129},{1,128},{2,131},{3,130},{4,133},{5,132},{6,135},{7,134},{8... | collective-permute-start | bytes 245768 | tf_op jit(solution)/shard_map/ppermute | solution.py:280
  31.1 2.6 %collective-permute-done.8.refs_1_ = bf16[1,80,512]{2,1,0:T(8,128)(2,1)S(1)} collective-permute-done((bf16[1,80,512]{2,1,0:T(8,128)(2,1)S(1)}, bf16[1,80,512]{2,1,0:T(8,128)(2,1)S(1)}, u32[]{:S(2)}, u32[]{:S(2)}) %collective-permute-start.8) | collective-permute-done | bytes 81952 | tf_op jit(solution)/shard_map/ppermute | solution.py:280
  33.7 6.4 %collective-permute-start.9 = (bf16[2,80,512]{2,1,0:T(8,128)(2,1)S(1)}, bf16[2,80,512]{2,1,0:T(8,128)(2,1)S(1)}, u32[]{:S(2)}, u32[]{:S(2)}) collective-permute-start(bf16[2,80,512]{2,1,0:T(8,128)(2,1)S(1)} %bitcast.16), channel_id=1, source_target_pairs={{0,64},{8,72},{16,80},{24,88},{32,96},{40,104},{48,112},{56,120},{... | collective-permute-start | bytes 491528 | tf_op jit(solution)/shard_map/ppermute | solution.py:270
  40.8 3.1 %collective-permute-done.9.refs_1_ = bf16[2,80,512]{2,1,0:T(8,128)(2,1)S(1)} collective-permute-done((bf16[2,80,512]{2,1,0:T(8,128)(2,1)S(1)}, bf16[2,80,512]{2,1,0:T(8,128)(2,1)S(1)}, u32[]{:S(2)}, u32[]{:S(2)}) %collective-permute-start.9) | collective-permute-done | bytes 163872 | tf_op jit(solution)/shard_map/ppermute | solution.py:270
  44.0 3.4 %collective-permute-start.13 = (bf16[4,80,512]{2,1,0:T(8,128)(2,1)S(1)}, bf16[4,80,512]{2,1,0:T(8,128)(2,1)S(1)}, u32[]{:S(2)}, u32[]{:S(2)}) collective-permute-start(bf16[4,80,512]{2,1,0:T(8,128)(2,1)S(1)} %bitcast.11), channel_id=1, source_target_pairs={{0,32},{8,40},{16,48},{24,56},{32,0},{40,8},{48,16},{56,24},{64,96... | collective-permute-start | bytes 983048 | tf_op jit(solution)/shard_map/ppermute | solution.py:270
  48.0 5.9 %time_weights.1 = (bf16[13,2,256,256]{3,2,1,0:T(8,128)(2,1)S(1)}, f32[8,128]{1,0:T(8,128)S(1)}) custom-call(bf16[16,32,3328]{2,1,0:T(8,128)(2,1)S(1)} %bitcast.10, bf16[1,32,4992]{2,1,0:T(8,128)(2,1)S(1)} %get-tuple-element.39.behind_ref), custom_call_target="tpu_custom_call" | custom-call | flops 436207616 | bytes 7000000 | tf_op jit(solution)/shard_map/time_weights/pallas_call | solution.py:245
  55.6 3.2 %collective-permute-done.13.refs_1_ = bf16[4,80,512]{2,1,0:T(8,128)(2,1)S(1)} collective-permute-done((bf16[4,80,512]{2,1,0:T(8,128)(2,1)S(1)}, bf16[4,80,512]{2,1,0:T(8,128)(2,1)S(1)}, u32[]{:S(2)}, u32[]{:S(2)}) %collective-permute-start.13) | collective-permute-done | bytes 327712 | tf_op jit(solution)/shard_map/ppermute | solution.py:270
  58.8 2.4 %collective-permute-start.14 = (bf16[8,80,512]{2,1,0:T(8,128)(2,1)S(1)}, bf16[8,80,512]{2,1,0:T(8,128)(2,1)}, u32[]{:S(2)}, u32[]{:S(2)}) collective-permute-start(bf16[8,80,512]{2,1,0:T(8,128)(2,1)S(1)} %bitcast.14), channel_id=1, source_target_pairs={{0,16},{8,24},{16,0},{24,8},{32,48},{40,56},{48,32},{56,40},{64,80... | collective-permute-start | bytes 1966088 | tf_op jit(solution)/shard_map/ppermute | solution.py:270
  62.4 9.9 %collective-permute-done.7.refs_2_ = bf16[2,32,4992]{2,1,0:T(8,128)(2,1)S(1)} collective-permute-done((bf16[2,32,4992]{2,1,0:T(8,128)(2,1)S(1)}, bf16[2,32,4992]{2,1,0:T(8,128)(2,1)S(1)}, u32[]{:S(2)}, u32[]{:S(2)}) %collective-permute-start.7) | collective-permute-done | bytes 639008 | tf_op jit(solution)/shard_map/ppermute | solution.py:135
  72.2 6.5 %collective-permute-done.10.refs_3_ = bf16[1,32,4992]{2,1,0:T(8,128)(2,1)S(1)} collective-permute-done((bf16[1,32,4992]{2,1,0:T(8,128)(2,1)S(1)}, bf16[1,32,4992]{2,1,0:T(8,128)(2,1)S(1)}, u32[]{:S(2)}, u32[]{:S(2)}) %collective-permute-start.10) | collective-permute-done | bytes 319520 | tf_op jit(solution)/shard_map/ppermute | solution.py:135
  78.8 3.4 %collective-permute-done.12.refs_5_ = bf16[1,32,4992]{2,1,0:T(8,128)(2,1)S(1)} collective-permute-done((bf16[1,32,4992]{2,1,0:T(8,128)(2,1)S(1)}, bf16[1,32,4992]{2,1,0:T(8,128)(2,1)S(1)}, u32[]{:S(2)}, u32[]{:S(2)}) %collective-permute-start.12) | collective-permute-done | bytes 319520 | tf_op jit(solution)/shard_map/ppermute | solution.py:135
  82.2 5.4 %spatial_attention.1 = bf16[8,2,32,1664]{3,2,1,0:T(8,128)(2,1)} custom-call(bf16[2,32,4992]{2,1,0:T(8,128)(2,1)S(1)} %copy-done.2, bf16[4,32,4992]{2,1,0:T(8,128)(2,1)S(1)} %collective-permute-done.across_ref, bf16[4,32,4992]{2,1,0:T(8,128)(2,1)S(1)} %collective-permute-done.4.turned_ref, bf16[2,32,4992]{2,1,0:T(8,128)(2,1)S(1)} %collective-permute-done.5.refs_0_, ...), custom_call_target="tpu_custom_call" | custom-call | flops 872415232 | bytes 6815744 | tf_op jit(solution)/shard_map/spatial_attention/pallas_call | solution.py:195
  87.6 4.0 %all-to-all-start = ((bf16[8,2,32,1664]{3,2,1,0:T(8,128)(2,1)}), bf16[8,2,32,1664]{3,2,1,0:T(8,128)(2,1)S(1)}, u32[]{:S(2)}, u32[]{:S(2)}) async-start(bf16[8,2,32,1664]{3,2,1,0:T(8,128)(2,1)} %spatial_attention.1), calls=%async_computation | async-start | bytes 3407872 | tf_op jit(solution)/shard_map/all_to_all | solution.py:565
  91.6 2.2 %join.7 = bf16[2,8,80,512]{3,2,1,0:T(8,128)(2,1)} custom-call(bf16[8,80,512]{2,1,0:T(8,128)(2,1)S(1)} %bitcast.15, bf16[8,80,512]{2,1,0:T(8,128)(2,1)} %collective-permute-done.14.refs_1_), custom_call_target="tpu_custom_call" | custom-call | bytes 1000000 | tf_op jit(solution)/shard_map/join/pallas_call | solution.py:284
  93.9 18.6 %all-to-all-done.value_ref = bf16[8,2,32,1664]{3,2,1,0:T(8,128)(2,1)S(1)} async-done(((bf16[8,2,32,1664]{3,2,1,0:T(8,128)(2,1)}), bf16[8,2,32,1664]{3,2,1,0:T(8,128)(2,1)S(1)}, u32[]{:S(2)}, u32[]{:S(2)}) %all-to-all-start) | async-done | bytes 1703968 | tf_op jit(solution)/shard_map/all_to_all | solution.py:565
  114.9 10.5 %token_part.1 = (bf16[16,32,512]{2,1,0:T(8,128)(2,1)}, f32[8,2,32,128]{3,2,1,0:T(8,128)}, bf16[32,80,512]{2,1,0:T(8,128)(2,1)}, f32[32,128]{1,0:T(8,128)S(1)}) custom-call(bf16[8,2,32,1664]{3,2,1,0:T(8,128)(2,1)S(1)} %all-to-all-done.value_ref, bf16[13,2,256,256]{3,2,1,0:T(8,128)(2,1)} %copy-done.5, bf16[1664,512]{1,0:T(8,128)(2,1)} %proj_ref.1, ...), custom_call_target="tpu_custom_call" | custom-call | flops 4499999744 | bytes 12000000 | tf_op jit(solution)/shard_map/token_part/pallas_call | solution.py:374
  125.4 3.4 %all-to-all-start.1 = ((f32[8,2,32,128]{3,2,1,0:T(8,128)}), f32[8,2,32,128]{3,2,1,0:T(8,128)S(1)}, u32[]{:S(2)}, u32[]{:S(2)}) async-start(f32[8,2,32,128]{3,2,1,0:T(8,128)} %get-tuple-element.45), calls=%async_computation.1 | async-start | bytes 524288 | tf_op jit(solution)/shard_map/all_to_all | solution.py:567
  129.5 6.2 %all-to-all-done.1.stats_ref = f32[8,2,32,128]{3,2,1,0:T(8,128)S(1)} async-done(((f32[8,2,32,128]{3,2,1,0:T(8,128)}), f32[8,2,32,128]{3,2,1,0:T(8,128)S(1)}, u32[]{:S(2)}, u32[]{:S(2)}) %all-to-all-start.1) | async-done | bytes 262176 | tf_op jit(solution)/shard_map/all_to_all | solution.py:567
  137.4 2.3 %coef_part.1 = (bf16[16,80,512]{2,1,0:T(8,128)(2,1)S(1)}, bf16[16,80,512]{2,1,0:T(8,128)(2,1)S(1)}, f32[1,1]{1,0:T(1,128)}) custom-call(s32[1]{0:T(128)S(6)} %copy.10.pos_ref, f32[8,2,32,128]{3,2,1,0:T(8,128)S(1)} %all-to-all-done.1.stats_ref, f32[32,128]{1,0:T(8,128)S(1)} %get-tuple-element.46.lens_ref, bf16[32,80,512]{2,1,0:T(8,128)(2,1)S(1)} %copy-done.1), custom_call_target="tpu_custom_call" | custom-call | flops 4000000 | bytes 6000000 | tf_op jit(solution)/shard_map/coef_part/pallas_call | solution.py:451
  139.9 3.0 %collective-permute-done.16.got_ref = bf16[16,80,512]{2,1,0:T(8,128)(2,1)S(1)} collective-permute-done((bf16[16,80,512]{2,1,0:T(8,128)(2,1)S(1)}, bf16[16,80,512]{2,1,0:T(8,128)(2,1)S(1)}, u32[]{:S(2)}, u32[]{:S(2)}) %collective-permute-start.16) | collective-permute-done | bytes 1310752 | tf_op jit(solution)/shard_map/ppermute | solution.py:527
  145.3 7.7 %collective-permute-done.17.a_got = bf16[8,80,256]{2,1,0:T(8,128)(2,1)S(1)} collective-permute-done((bf16[8,80,256]{2,1,0:T(8,128)(2,1)S(1)}, bf16[8,80,256]{2,1,0:T(8,128)(2,1)S(1)}, u32[]{:S(2)}, u32[]{:S(2)}) %collective-permute-start.17) | collective-permute-done | bytes 327712 | tf_op jit(solution)/shard_map/ppermute | solution.py:531
  156.3 4.9 %collective-permute-done.19.a_got = bf16[8,80,128]{2,1,0:T(8,128)(2,1)S(1)} collective-permute-done((bf16[8,80,128]{2,1,0:T(8,128)(2,1)S(1)}, bf16[8,80,128]{2,1,0:T(8,128)(2,1)S(1)}, u32[]{:S(2)}, u32[]{:S(2)}) %collective-permute-start.19) | collective-permute-done | bytes 163872 | tf_op jit(solution)/shard_map/ppermute | solution.py:537
  161.7 18.4 %all_to_all.20.parts = bf16[16,80,128]{2,1,0:T(8,128)(2,1)S(1)} all-to-all(bf16[16,80,128]{2,1,0:T(8,128)(2,1)S(1)} %third_sum.1), channel_id=1, replica_groups={{0,16,32,48,64,80,96,112,128,144,160,176,192,208,224,240},{8,24,40,56,7..., dimensions={0} | all-to-all | bytes 655360 | tf_op jit(solution)/shard_map/all_to_all | solution.py:542
  180.1 9.4 %all_to_all.21.parts = bf16[8,80,128]{2,1,0:T(8,128)(2,1)S(1)} all-to-all(bf16[8,80,128]{2,1,0:T(8,128)(2,1)S(1)} %owned_sum.1), channel_id=1, replica_groups=mesh['dp'=32,'space'=8] {'space'}, dimensions={0} | all-to-all | bytes 327680 | tf_op jit(solution)/shard_map/all_to_all | solution.py:547
  (56 shorter events, 21.3 us)
Async XLA Ops:
  2.8 41.2 %collective-permute-start = (bf16[4,32,4992]{2,1,0:T(8,128)(2,1)}, bf16[4,32,4992]{2,1,0:T(8,128)(2,1)S(1)}, u32[]{:S(2)}, u32[]{:S(2)}) collective-permute-start(bf16[4,32,4992]{2,1,0:T(8,128)(2,1)} %across.1), channel_id=1, source_target_pairs={{0,6},{1,7},{2,4},{3,5},{4,2},{5,3},{6,0},{7,1},{8,14},{9,15},{10,... | collective-permute-start | bytes 3833864 | tf_op jit(solution)/shard_map/ppermute | solution.py:135
  7.6 9.9 %collective-permute-start.1 = (bf16[1,32,4992]{2,1,0:T(8,128)(2,1)}, bf16[1,32,4992]{2,1,0:T(8,128)(2,1)S(1)}, u32[]{:S(2)}, u32[]{:S(2)}) collective-permute-start(bf16[1,32,4992]{2,1,0:T(8,128)(2,1)} %get-tuple-element.33), channel_id=1, source_target_pairs={{0,1},{1,0},{2,3},{3,2},{4,5},{5,4},{6,7},{7,6},{8,9},{9,8},{10,11... | collective-permute-start | bytes 958472 | tf_op jit(solution)/shard_map/ppermute | solution.py:135
  9.3 10.7 %collective-permute-start.2 = (bf16[1,32,4992]{2,1,0:T(8,128)(2,1)}, bf16[1,32,4992]{2,1,0:T(8,128)(2,1)S(1)}, u32[]{:S(2)}, u32[]{:S(2)}) collective-permute-start(bf16[1,32,4992]{2,1,0:T(8,128)(2,1)} %get-tuple-element.34), channel_id=1, source_target_pairs={{0,2},{1,3},{2,0},{3,1},{4,6},{5,7},{6,4},{7,5},{8,10},{9,11},{10,... | collective-permute-start | bytes 958472 | tf_op jit(solution)/shard_map/ppermute | solution.py:135
  9.5 15.4 %collective-permute-start.3 = (bf16[1,32,4992]{2,1,0:T(8,128)(2,1)}, bf16[1,32,4992]{2,1,0:T(8,128)(2,1)S(1)}, u32[]{:S(2)}, u32[]{:S(2)}) collective-permute-start(bf16[1,32,4992]{2,1,0:T(8,128)(2,1)} %get-tuple-element.35), channel_id=1, source_target_pairs={{0,3},{1,2},{2,1},{3,0},{4,7},{5,6},{6,5},{7,4},{8,11},{9,10},{10,... | collective-permute-start | bytes 958472 | tf_op jit(solution)/shard_map/ppermute | solution.py:135
  13.6 11.4 %copy-start.3 = (bf16[2,32,4992]{2,1,0:T(8,128)(2,1)S(1)}, bf16[2,32,4992]{2,1,0:T(8,128)(2,1)}, u32[]{:S(2)}) copy-start(bf16[2,32,4992]{2,1,0:T(8,128)(2,1)} %get-tuple-element.36.behind_ref) | copy-start | bytes 1916932
  13.6 14.4 %copy-start.8 = (bf16[1,77,512]{2,1,0:T(8,128)(2,1)S(1)}, bf16[1,77,512]{2,1,0:T(8,128)(2,1)}, u32[]{:S(2)}) copy-start(bf16[1,77,512]{2,1,0:T(8,128)(2,1)} %param.9) | copy-start | bytes 236548
  13.6 30.3 %copy-start.9 = (bf16[2,32,4992]{2,1,0:T(8,128)(2,1)S(1)}, bf16[2,32,4992]{2,1,0:T(8,128)(2,1)}, u32[]{:S(2)}) copy-start(bf16[2,32,4992]{2,1,0:T(8,128)(2,1)} %get-tuple-element.38) | copy-start | bytes 1916932
  25.9 22.1 %copy-start = (bf16[1,16,32,3328]{3,2,1,0:T(8,128)(2,1)S(1)}, bf16[1,16,32,3328]{3,2,1,0:T(8,128)(2,1)}, u32[]{:S(2)}) copy-start(bf16[1,16,32,3328]{3,2,1,0:T(8,128)(2,1)} %param.7) | copy-start | bytes 10223620
  26.7 45.5 %collective-permute-start.4 = (bf16[4,32,4992]{2,1,0:T(8,128)(2,1)S(1)}, bf16[4,32,4992]{2,1,0:T(8,128)(2,1)S(1)}, u32[]{:S(2)}, u32[]{:S(2)}) collective-permute-start(bf16[4,32,4992]{2,1,0:T(8,128)(2,1)S(1)} %turn.1), channel_id=1, source_target_pairs={{0,6},{1,7},{2,4},{3,5},{4,2},{5,3},{6,0},{7,1},{8,14},{9,15},{10,... | collective-permute-start | bytes 3833864 | tf_op jit(solution)/shard_map/ppermute | solution.py:135
  28.0 5.7 %collective-permute-start.8 = (bf16[1,80,512]{2,1,0:T(8,128)(2,1)S(1)}, bf16[1,80,512]{2,1,0:T(8,128)(2,1)S(1)}, u32[]{:S(2)}, u32[]{:S(2)}) collective-permute-start(bf16[1,80,512]{2,1,0:T(8,128)(2,1)S(1)} %concatenate.3.refs_0_), channel_id=1, source_target_pairs={{0,129},{1,128},{2,131},{3,130},{4,133},{5,132},{6,135},{7,134},{8... | collective-permute-start | bytes 245768 | tf_op jit(solution)/shard_map/ppermute | solution.py:280
  33.7 10.2 %collective-permute-start.9 = (bf16[2,80,512]{2,1,0:T(8,128)(2,1)S(1)}, bf16[2,80,512]{2,1,0:T(8,128)(2,1)S(1)}, u32[]{:S(2)}, u32[]{:S(2)}) collective-permute-start(bf16[2,80,512]{2,1,0:T(8,128)(2,1)S(1)} %bitcast.16), channel_id=1, source_target_pairs={{0,64},{8,72},{16,80},{24,88},{32,96},{40,104},{48,112},{56,120},{... | collective-permute-start | bytes 491528 | tf_op jit(solution)/shard_map/ppermute | solution.py:270
  40.1 21.1 %collective-permute-start.5 = (bf16[2,32,4992]{2,1,0:T(8,128)(2,1)S(1)}, bf16[2,32,4992]{2,1,0:T(8,128)(2,1)S(1)}, u32[]{:S(2)}, u32[]{:S(2)}) collective-permute-start(bf16[2,32,4992]{2,1,0:T(8,128)(2,1)S(1)} %copy-done.3), channel_id=1, source_target_pairs={{0,1},{1,0},{2,3},{3,2},{4,5},{5,4},{6,7},{7,6},{8,9},{9,8},{10,11... | collective-permute-start | bytes 1916936 | tf_op jit(solution)/shard_map/ppermute | solution.py:135
  40.5 21.0 %collective-permute-start.6 = (bf16[2,32,4992]{2,1,0:T(8,128)(2,1)}, bf16[2,32,4992]{2,1,0:T(8,128)(2,1)S(1)}, u32[]{:S(2)}, u32[]{:S(2)}) collective-permute-start(bf16[2,32,4992]{2,1,0:T(8,128)(2,1)} %get-tuple-element.37), channel_id=1, source_target_pairs={{0,2},{1,3},{2,0},{3,1},{4,6},{5,7},{6,4},{7,5},{8,10},{9,11},{10,... | collective-permute-start | bytes 1916936 | tf_op jit(solution)/shard_map/ppermute | solution.py:135
  43.9 28.3 %collective-permute-start.7 = (bf16[2,32,4992]{2,1,0:T(8,128)(2,1)S(1)}, bf16[2,32,4992]{2,1,0:T(8,128)(2,1)S(1)}, u32[]{:S(2)}, u32[]{:S(2)}) collective-permute-start(bf16[2,32,4992]{2,1,0:T(8,128)(2,1)S(1)} %copy-done.9), channel_id=1, source_target_pairs={{0,3},{1,2},{2,1},{3,0},{4,7},{5,6},{6,5},{7,4},{8,11},{9,10},{10,... | collective-permute-start | bytes 1916936 | tf_op jit(solution)/shard_map/ppermute | solution.py:135
  44.0 14.8 %collective-permute-start.13 = (bf16[4,80,512]{2,1,0:T(8,128)(2,1)S(1)}, bf16[4,80,512]{2,1,0:T(8,128)(2,1)S(1)}, u32[]{:S(2)}, u32[]{:S(2)}) collective-permute-start(bf16[4,80,512]{2,1,0:T(8,128)(2,1)S(1)} %bitcast.11), channel_id=1, source_target_pairs={{0,32},{8,40},{16,48},{24,56},{32,0},{40,8},{48,16},{56,24},{64,96... | collective-permute-start | bytes 983048 | tf_op jit(solution)/shard_map/ppermute | solution.py:270
  53.9 1.7 copy-start.5
  55.6 26.6 %copy-start.2 = (bf16[2,32,4992]{2,1,0:T(8,128)(2,1)S(1)}, bf16[2,32,4992]{2,1,0:T(8,128)(2,1)}, u32[]{:S(2)}) copy-start(bf16[2,32,4992]{2,1,0:T(8,128)(2,1)} %get-tuple-element.31.kept_ref) | copy-start | bytes 1916932
  58.8 32.8 %collective-permute-start.14 = (bf16[8,80,512]{2,1,0:T(8,128)(2,1)S(1)}, bf16[8,80,512]{2,1,0:T(8,128)(2,1)}, u32[]{:S(2)}, u32[]{:S(2)}) collective-permute-start(bf16[8,80,512]{2,1,0:T(8,128)(2,1)S(1)} %bitcast.14), channel_id=1, source_target_pairs={{0,16},{8,24},{16,0},{24,8},{32,48},{40,56},{48,32},{56,40},{64,80... | collective-permute-start | bytes 1966088 | tf_op jit(solution)/shard_map/ppermute | solution.py:270
  61.2 17.5 %collective-permute-start.10 = (bf16[1,32,4992]{2,1,0:T(8,128)(2,1)S(1)}, bf16[1,32,4992]{2,1,0:T(8,128)(2,1)S(1)}, u32[]{:S(2)}, u32[]{:S(2)}) collective-permute-start(bf16[1,32,4992]{2,1,0:T(8,128)(2,1)S(1)} %get-tuple-element.39.behind_ref), channel_id=1, source_target_pairs={{0,1},{1,0},{2,3},{3,2},{4,5},{5,4},{6,7},{7,6},{8,9},{9,8},{10,11... | collective-permute-start | bytes 958472 | tf_op jit(solution)/shard_map/ppermute | solution.py:135
  61.5 17.2 %collective-permute-start.11 = (bf16[1,32,4992]{2,1,0:T(8,128)(2,1)S(1)}, bf16[1,32,4992]{2,1,0:T(8,128)(2,1)S(1)}, u32[]{:S(2)}, u32[]{:S(2)}) collective-permute-start(bf16[1,32,4992]{2,1,0:T(8,128)(2,1)S(1)} %get-tuple-element.40), channel_id=1, source_target_pairs={{0,2},{1,3},{2,0},{3,1},{4,6},{5,7},{6,4},{7,5},{8,10},{9,11},{10,... | collective-permute-start | bytes 958472 | tf_op jit(solution)/shard_map/ppermute | solution.py:135
  72.2 10.0 %collective-permute-start.12 = (bf16[1,32,4992]{2,1,0:T(8,128)(2,1)S(1)}, bf16[1,32,4992]{2,1,0:T(8,128)(2,1)S(1)}, u32[]{:S(2)}, u32[]{:S(2)}) collective-permute-start(bf16[1,32,4992]{2,1,0:T(8,128)(2,1)S(1)} %get-tuple-element.41), channel_id=1, source_target_pairs={{0,3},{1,2},{2,1},{3,0},{4,7},{5,6},{6,5},{7,4},{8,11},{9,10},{10,... | collective-permute-start | bytes 958472 | tf_op jit(solution)/shard_map/ppermute | solution.py:135
  87.6 24.9 %all-to-all-start = ((bf16[8,2,32,1664]{3,2,1,0:T(8,128)(2,1)}), bf16[8,2,32,1664]{3,2,1,0:T(8,128)(2,1)S(1)}, u32[]{:S(2)}, u32[]{:S(2)}) async-start(bf16[8,2,32,1664]{3,2,1,0:T(8,128)(2,1)} %spatial_attention.1), calls=%async_computation | async-start | bytes 3407872 | tf_op jit(solution)/shard_map/all_to_all | solution.py:565
  93.9 18.6 %collective-permute-start.15 = (bf16[16,80,512]{2,1,0:T(8,128)(2,1)}, bf16[16,80,512]{2,1,0:T(8,128)(2,1)S(1)}, u32[]{:S(2)}, u32[]{:S(2)}) collective-permute-start(bf16[16,80,512]{2,1,0:T(8,128)(2,1)} %bitcast.6.mine_ref), channel_id=1, source_target_pairs={{0,8},{8,0},{16,24},{24,16},{32,40},{40,32},{48,56},{56,48},{64,72... | collective-permute-start | bytes 3932168 | tf_op jit(solution)/shard_map/ppermute | solution.py:270
  112.5 1.0 copy-start.6
  113.6 1.3 copy-start.7
  125.4 10.3 %all-to-all-start.1 = ((f32[8,2,32,128]{3,2,1,0:T(8,128)}), f32[8,2,32,128]{3,2,1,0:T(8,128)S(1)}, u32[]{:S(2)}, u32[]{:S(2)}) async-start(f32[8,2,32,128]{3,2,1,0:T(8,128)} %get-tuple-element.45), calls=%async_computation.1 | async-start | bytes 524288 | tf_op jit(solution)/shard_map/all_to_all | solution.py:567
  135.7 1.7 copy-start.1
  139.8 3.1 %collective-permute-start.16 = (bf16[16,80,512]{2,1,0:T(8,128)(2,1)S(1)}, bf16[16,80,512]{2,1,0:T(8,128)(2,1)S(1)}, u32[]{:S(2)}, u32[]{:S(2)}) collective-permute-start(bf16[16,80,512]{2,1,0:T(8,128)(2,1)S(1)} %get-tuple-element.49), channel_id=1, source_target_pairs={{0,8},{8,0},{16,24},{24,16},{32,40},{40,32},{48,56},{56,48},{64,72... | collective-permute-start | bytes 3932168 | tf_op jit(solution)/shard_map/ppermute | solution.py:527
  143.2 9.8 %collective-permute-start.17 = (bf16[8,80,256]{2,1,0:T(8,128)(2,1)S(1)}, bf16[8,80,256]{2,1,0:T(8,128)(2,1)S(1)}, u32[]{:S(2)}, u32[]{:S(2)}) collective-permute-start(bf16[8,80,256]{2,1,0:T(8,128)(2,1)S(1)} %get-tuple-element.51), channel_id=1, source_target_pairs={{0,2},{1,3},{2,0},{3,1},{4,6},{5,7},{6,4},{7,5},{8,10},{9,11},{10,... | collective-permute-start | bytes 983048 | tf_op jit(solution)/shard_map/ppermute | solution.py:531
  143.6 10.8 %collective-permute-start.18 = (bf16[8,80,256]{2,1,0:T(8,128)(2,1)S(1)}, bf16[8,80,256]{2,1,0:T(8,128)(2,1)S(1)}, u32[]{:S(2)}, u32[]{:S(2)}) collective-permute-start(bf16[8,80,256]{2,1,0:T(8,128)(2,1)S(1)} %get-tuple-element.53), channel_id=1, source_target_pairs={{0,6},{1,7},{2,4},{3,5},{4,2},{5,3},{6,0},{7,1},{8,14},{9,15},{10,... | collective-permute-start | bytes 983048 | tf_op jit(solution)/shard_map/ppermute | solution.py:532
  154.5 6.6 %collective-permute-start.19 = (bf16[8,80,128]{2,1,0:T(8,128)(2,1)S(1)}, bf16[8,80,128]{2,1,0:T(8,128)(2,1)S(1)}, u32[]{:S(2)}, u32[]{:S(2)}) collective-permute-start(bf16[8,80,128]{2,1,0:T(8,128)(2,1)S(1)} %get-tuple-element.55), channel_id=1, source_target_pairs={{0,6},{1,7},{2,4},{3,5},{4,2},{5,3},{6,0},{7,1},{8,14},{9,15},{10,... | collective-permute-start | bytes 491528 | tf_op jit(solution)/shard_map/ppermute | solution.py:537
  156.3 5.3 %collective-permute-start.20 = (bf16[8,80,128]{2,1,0:T(8,128)(2,1)S(1)}, bf16[8,80,128]{2,1,0:T(8,128)(2,1)S(1)}, u32[]{:S(2)}, u32[]{:S(2)}) collective-permute-start(bf16[8,80,128]{2,1,0:T(8,128)(2,1)S(1)} %get-tuple-element.57), channel_id=1, source_target_pairs={{0,2},{1,3},{2,0},{3,1},{4,6},{5,7},{6,4},{7,5},{8,10},{9,11},{10,... | collective-permute-start | bytes 491528 | tf_op jit(solution)/shard_map/ppermute | solution.py:538
  (1 other events, 1.0 us)

commit v9 on v8

--- a/solution.py
+++ b/solution.py
@@ -1,3 +1,4 @@
+import functools
 import math
 
 import jax
@@ -92,74 +93,64 @@
     )(*operands)
 
 
-def relay_kernel(clip_ref, one, two, three, buf, sems):
-    g1, a = quad_place()
-    refs = ((1, one), (2, two), (3, three))
-    copied([(clip_ref.at[2 * owner(1 - g1, a ^ k)], ref.at[0]) for k, ref in refs], buf, sems)
-
-
-def across_kernel(clip_ref, out_ref, buf, sems):
-    g1, _ = quad_place()
-    copied([(clip_ref.at[2 * owner(1 - g1, a) + 1], out_ref.at[a]) for a in range(4)], buf, sems)
-
-
-def quads_kernel(clip_ref, one, two, three, buf, sems):
+def depart_kernel(clip_ref, one, two, three, across_ref, buf, sems):
     g1, a = quad_place()
     pairs = [
-        (clip_ref.at[2 * owner(g1, a ^ k) + f], ref.at[f])
+        (clip_ref.at[2 * owner(g, a ^ k)], ref.at[g])
         for k, ref in ((1, one), (2, two), (3, three))
-        for f in range(2)
+        for g in range(2)
     ]
+    pairs += [(clip_ref.at[2 * owner(1 - g1, b) + 1], across_ref.at[b]) for b in range(4)]
     copied(pairs, buf, sems)
 
 
-def own_kernel(clip_ref, first, kept, buf, sems):
+def own_kernel(clip_ref, first, seconds, kept, buf, sems):
     g1, a = quad_place()
     pairs = [(clip_ref.at[2 * owner(1 - g1, a)], first.at[0])]
+    pairs += [(clip_ref.at[2 * owner(g1, a ^ k) + 1], seconds.at[k - 1]) for k in (1, 2, 3)]
     pairs += [(clip_ref.at[2 * owner(g1, a) + f], kept.at[f]) for f in range(2)]
     copied(pairs, buf, sems)
 
 
 def turn_kernel(first_ref, one, two, three, behind_ref, out_ref, buf, sems):
-    refs = (first_ref, one, two, three)
-    copied([(ref.at[0], out_ref.at[k]) for k, ref in enumerate(refs)], buf, sems)
-
-
-def spread_kernel(across_ref, behind_ref, one, two, three, buf, sems):
+    g1, _ = quad_place()
+    pairs = [(first_ref.at[0], out_ref.at[0])]
+    pairs += [(ref.at[1 - g1], out_ref.at[k]) for k, ref in ((1, one), (2, two), (3, three))]
+    copied(pairs, buf, sems)
+
+
+def spread_kernel(seconds_ref, across_ref, one, two, three, buf, sems):
     _, a = quad_place()
-    refs = ((1, one), (2, two), (3, three))
-    copied([(across_ref.at[a ^ k], ref.at[0]) for k, ref in refs], buf, sems)
+    pairs = []
+    for k, ref in ((1, one), (2, two), (3, three)):
+        pairs += [(seconds_ref.at[k - 1], ref.at[0]), (across_ref.at[a ^ k], ref.at[1])]
+    copied(pairs, buf, sems)
 
 
 def swap(value, bits):
     return lax.ppermute(value, "space", [(s, s ^ bits) for s in range(8)])
 
 
-def swap_quad(values):
-    return [swap(value, k) for k, value in zip((1, 2, 3), values)]
-
-
 def bring_frames(clip, behind):
-    relays = swap_quad(copying(relay_kernel, "relay", (clip,), (1, 1, 1), 3))
-    (across,) = copying(across_kernel, "across", (clip,), (4,), 4)
+    *quads, across = copying(depart_kernel, "depart", (clip,), (2, 2, 2, 4), 10)
     across = swap(across, 6)
-    quads = copying(quads_kernel, "quads", (clip,), (2, 2, 2), 6)
-    prepared = quads[0]
-    quads = swap_quad(quads)
-    first, kept = copying(own_kernel, "own", (clip,), (1, 2), 3)
+    quads = [swap(quad, k) for k, quad in zip((1, 2, 3), quads)]
+    first, seconds, kept = copying(own_kernel, "own", (clip,), (1, 3, 2), 6)
     few = pltpu.CompilerParams(vmem_limit_bytes=8 * MIB)
-    (turned,) = copying(turn_kernel, "turn", (first, *relays, prepared), (4,), 4, few)
+    (turned,) = copying(turn_kernel, "turn", (first, *quads, behind), (4,), 4, few)
     turned = swap(turned, 6)
-    spread = copying(spread_kernel, "spread", (across, behind), (1, 1, 1), 3, few)
-    return (kept, across, turned, *quads, *swap_quad(spread)), spread[0]
+    pairs = copying(spread_kernel, "spread", (seconds, across), (2, 2, 2), 6, few)
+    started = pairs[0]
+    pairs = [swap(pair, k) for k, pair in zip((1, 2, 3), pairs)]
+    return (kept, across, turned, *quads, *pairs), started
 
 
 def spatial_kernel(kept_ref, across_ref, turned_ref, *refs):
-    quads, spread, (_, out_ref, buf, res, sems, store_sems) = refs[:3], refs[3:6], refs[6:]
+    quads, pairs, (_, out_ref, buf, res, sems, store_sems) = refs[:3], refs[3:6], refs[6:]
     g1, a = quad_place()
-    first = [ref.at[0] for ref in (kept_ref, *quads)] + [turned_ref.at[k] for k in range(4)]
-    second = [ref.at[1] for ref in (kept_ref, *quads)]
-    second += [across_ref.at[a]] + [ref.at[0] for ref in spread]
+    first = [kept_ref.at[0]] + [ref.at[g1] for ref in quads] + [turned_ref.at[k] for k in range(4)]
+    second = [kept_ref.at[1]] + [ref.at[0] for ref in pairs]
+    second += [across_ref.at[a]] + [ref.at[1] for ref in pairs]
     loads = [
         [pltpu.make_async_copy(src, buf.at[f, i], sems.at[f, i]) for i, src in enumerate(sources)]
         for f, sources in enumerate((first, second))
@@ -294,29 +285,20 @@
 
 
 def token_kernel(
-    value_ref, time_ref, proj_ref, mine_ref, other_ref,
+    value, time_ref, proj_ref, mine_ref, other_ref,
     emb_ref, all_stats_ref, grad_ref, lens_ref,
-    value, time, proj, mine, comb, video, grads, stats_ref, sems, time_sems, grad_sems,
+    proj, mine, comb, video, grads, stats_ref, sems, grad_sems,
 ):
-    value_load = pltpu.make_async_copy(value_ref, value, sems.at[3])
-    value_load.start()
-    time_loads = [
-        pltpu.make_async_copy(time_ref.at[h], time.at[h], time_sems.at[h]) for h in range(HEADS)
-    ]
-    for load in time_loads:
-        load.start()
     proj_load = pltpu.make_async_copy(proj_ref, proj, sems.at[0])
     mine_load = pltpu.make_async_copy(mine_ref, mine, sems.at[1])
     proj_load.start()
     mine_load.start()
-    value_load.wait()
     for h in range(HEADS):
-        time_loads[h].wait()
         cols = pl.ds(h * HD, HD)
         for g in range(LOCAL // 16):
             part = pl.ds(g * 16, 16)
             v = value[:, :, part, cols].reshape(ROWS, HD)
-            o = jnp.dot(time[h, g], v, preferred_element_type=jnp.float32)
+            o = jnp.dot(time_ref[h, g], v, preferred_element_type=jnp.float32)
             o = (v.astype(jnp.float32) + o).astype(jnp.bfloat16)
             comb[:, part, cols] = o.reshape(FRAMES, 16, HD)
     tokens = FRAMES * LOCAL
@@ -373,33 +355,30 @@
     bf16 = jnp.bfloat16
     return pl.pallas_call(
         token_kernel,
-        in_specs=[ANY, ANY, ANY, ANY, VMEM],
-        out_specs=[ANY, VMEM, ANY, VMEM],
+        in_specs=[VMEM, VMEM, FAR_OFF, FAR_OFF, VMEM],
+        out_specs=[FAR_OFF, VMEM, FAR_OFF, VMEM],
         out_shape=[
-            jax.ShapeDtypeStruct((FRAMES, LOCAL, EMB), bf16),
+            pltpu.HBM((FRAMES, LOCAL, EMB), bf16),
             jax.ShapeDtypeStruct((8, 2, CAPTIONS, 128), jnp.float32),
-            jax.ShapeDtypeStruct((CAPTIONS, PADDED, EMB), bf16),
+            pltpu.HBM((CAPTIONS, PADDED, EMB), bf16),
             jax.ShapeDtypeStruct((CAPTIONS, 128), jnp.float32),
         ],
         scratch_shapes=[
-            pltpu.VMEM((8, 2, LOCAL, FEATURES), bf16),
-            pltpu.VMEM((HEADS, 2, ROWS, ROWS), bf16),
             pltpu.VMEM((FEATURES, EMB), bf16),
             pltpu.VMEM((CAPTIONS // 2, PADDED, EMB), bf16),
             pltpu.VMEM((FRAMES, LOCAL, FEATURES), bf16),
             pltpu.VMEM((FRAMES, LOCAL, EMB), bf16),
             pltpu.VMEM((CAPTIONS, PADDED, EMB), bf16),
             pltpu.VMEM((2, CAPTIONS, 128), jnp.float32),
-            pltpu.SemaphoreType.DMA((4,)),
-            pltpu.SemaphoreType.DMA((HEADS,)),
+            pltpu.SemaphoreType.DMA((3,)),
             pltpu.SemaphoreType.DMA((CAPTIONS,)),
         ],
-        compiler_params=pltpu.CompilerParams(vmem_limit_bytes=48 * MIB),
+        compiler_params=GRANT,
         cost_estimate=pl.CostEstimate(
             flops=4_500_000_000, bytes_accessed=12_000_000, transcendentals=1_300_000
         ),
         name="token_part",
-    )(spatial, time, proj_weight, mine, other)
+    )(spatial, time, held(proj_weight), held(mine), other)
 
 
 def coef_kernel(
@@ -450,7 +429,7 @@
     half = jax.ShapeDtypeStruct((CAPTIONS // 2, PADDED, EMB), jnp.bfloat16)
     return pl.pallas_call(
         coef_kernel,
-        in_specs=[SMEM, VMEM, VMEM, ANY],
+        in_specs=[SMEM, VMEM, VMEM, FAR_OFF],
         out_specs=[VMEM] * 3,
         out_shape=[half, half, jax.ShapeDtypeStruct((1, 1), jnp.float32)],
         scratch_shapes=[
@@ -463,7 +442,7 @@
             flops=4_000_000, bytes_accessed=6_000_000, transcendentals=100_000
         ),
         name="coef_part",
-    )(pos, stats, lens, grad)
+    )(pos, stats, lens, held(grad))
 
 
 def small_call(kernel, name, operands, out_shapes, specs=None):
@@ -486,26 +465,39 @@
     x = lax.axis_index("space") >> 1
     plan = (
         (0, ((a_keep, 0, 0), (a_send, 0, 1), (a_send, 1, 2), (a_keep, 1, 3))),
-        (8, ((b_keep, 0, 0), (b_keep, 1, 1), (b_send, 1, 2), (b_send, 0, 3))),
+        (4, ((b_keep, 0, 0), (b_keep, 1, 1), (b_send, 1, 2), (b_send, 0, 3))),
     )
     for start, parts in plan:
-        for ref, at, flip in parts:
-            cols = pl.ds(pl.multiple_of((x ^ flip) * 128, 128), 128)
+        for ref, at, flipped in parts:
+            cols = pl.ds(pl.multiple_of((x ^ flipped) * 128, 128), 128)
             for m in range(8):
+                source = m // 4 * 8 + start + m % 4
                 ref[m, :, pl.ds(at * 128, 128)] = added(
-                    keep_ref[start + m, :, cols], got_ref[start + m, :, cols]
+                    keep_ref[source, :, cols], got_ref[source, :, cols]
                 )
 
 
 def second_sum_kernel(a_keep, a_got, b_keep, b_got, a_mine, a_send, b_mine, b_send):
-    for keep, got, mine, send in ((a_keep, a_got, a_mine, a_send), (b_keep, b_got, b_mine, b_send)):
-        mine[...] = added(keep[:, :, :128], got[:, :, :128])
-        send[...] = added(keep[:, :, 128:], got[:, :, 128:])
-
-
-def third_sum_kernel(a_mine, a_got, b_mine, b_got, out):
-    out[pl.ds(0, 8)] = added(a_mine[...], a_got[...])
-    out[pl.ds(8, 8)] = added(b_mine[...], b_got[...])
+    a_mine[...] = added(a_keep[:, :, :128], a_got[:, :, :128])
+    a_send[...] = added(a_keep[:, :, 128:], a_got[:, :, 128:])
+    y_hi = lax.axis_index("dp") >> 4
+    for ref, side in ((b_mine, y_hi), (b_send, 1 - y_hi)):
+        some = pl.ds(side * 4, 4)
+        ref[...] = added(b_keep[some], b_got[some])
+
+
+def third_sum_kernel(a_keep, a_got, b_keep, b_got, a_mine, a_send, b_mine, b_send):
+    y_hi = lax.axis_index("dp") >> 4
+    for ref, side in ((a_mine, y_hi), (a_send, 1 - y_hi)):
+        some = pl.ds(side * 4, 4)
+        ref[...] = added(a_keep[some], a_got[some])
+    b_mine[...] = added(b_keep[:, :, :128], b_got[:, :, :128])
+    b_send[...] = added(b_keep[:, :, 128:], b_got[:, :, 128:])
+
+
+def fourth_sum_kernel(a_mine, a_got, b_mine, b_got, out):
+    out[pl.ds(0, 4)] = added(a_mine[...], a_got[...])
+    out[pl.ds(4, 4)] = added(b_mine[...], b_got[...])
 
 
 def owned_sum_kernel(parts, out):
@@ -522,26 +514,25 @@
 
 def reduce_gradient(send, keep):
     bf16 = jnp.bfloat16
-    one = [(s, s ^ 2) for s in range(8)]
-    three = [(s, s ^ 6) for s in range(8)]
     got = lax.ppermute(send, "dp", [(i, i ^ 1) for i in range(32)])
     a_keep, a_send, b_keep, b_send = small_call(
         first_sum_kernel, "first_sum", (keep, got), [((8, PADDED, 256), bf16)] * 4
     )
-    a_got = lax.ppermute(a_send, "space", one)
-    b_got = lax.ppermute(b_send, "space", three)
-    a_mine, a_send, b_mine, b_send = small_call(
-        second_sum_kernel, "second_sum", (a_keep, a_got, b_keep, b_got),
-        [((8, PADDED, 128), bf16)] * 4,
-    )
-    a_got = lax.ppermute(a_send, "space", three)
-    b_got = lax.ppermute(b_send, "space", one)
+    a_keep, a_send, b_keep, b_send = small_call(
+        second_sum_kernel, "second_sum", (a_keep, swap(a_send, 2), b_keep, swap(b_send, 6)),
+        [((8, PADDED, 128), bf16)] * 2 + [((4, PADDED, 256), bf16)] * 2,
+    )
+    a_keep, a_send, b_keep, b_send = small_call(
+        third_sum_kernel, "third_sum", (a_keep, swap(a_send, 6), b_keep, flip_y(b_send)),
+        [((4, PADDED, 128), bf16)] * 4,
+    )
     (parts,) = small_call(
-        third_sum_kernel, "third_sum", (a_mine, a_got, b_mine, b_got), [((16, PADDED, 128), bf16)]
+        fourth_sum_kernel, "fourth_sum", (a_keep, flip_y(a_send), b_keep, swap(b_send, 2)),
+        [((8, PADDED, 128), bf16)],
     )
     parts = lax.all_to_all(
         parts, "dp", split_axis=0, concat_axis=0, tiled=True,
-        axis_index_groups=[[2 * m + c for m in range(16)] for c in range(2)],
+        axis_index_groups=[[y * 16 + z * 2 + c for z in range(8)] for y in range(2) for c in range(2)],
     )
     (parts,) = small_call(owned_sum_kernel, "owned_sum", (parts,), [((8, PADDED, 128), bf16)])
     parts = lax.all_to_all(parts, "space", split_axis=0, concat_axis=0, tiled=True)
@@ -555,8 +546,9 @@
     )
     caps = jnp.concatenate([caption_tokens, lens_row], axis=1)
     caps = doubled(caps, flip_y(caps))
-    caps = doubled(caps, flip(caps, 8))
-    pieces, started = bring_frames(clip_qkv[0], caps)
+    far = flip(caps, 8)
+    pieces, started = bring_frames(clip_qkv[0], far)
+    caps = doubled(caps, far, started)
     time, done = time_weights(temporal_qk[0], started)
     caps = doubled(caps, flip(caps, 4), done)
     caps = doubled(caps, flip(caps, 2))

time: 191 us -> 185 us (0.969)
  starting transfers between devices: 35.5 us -> 40.8 us
  Pallas kernels: 37.7 us -> 32.6 us
  blocking collectives: 27.8 us -> 24.4 us
  waiting for transfers between devices: 80.3 us -> 77.1 us
    ppermute x4 -> x0, waiting for transfers between devices: 14.4 us -> none  [the longest x1 7.73 us: reduce_gradient(): a_got = lax.ppermute(a_send, 'space', one)]
    ppermute x11 -> x12, waiting for transfers between devices: 29.1 us -> 39.7 us  [swap(): return lax.ppermute(value, 'space', [(s, s ^ bits) for s in range(8)])]
    ppermute x11 -> x12, starting transfers between devices: 8.78 us -> 14.2 us  [swap(): return lax.ppermute(value, 'space', [(s, s ^ bits) for s in range(8)])]
    ppermute x1 -> x3, waiting for transfers between devices: 2.64 us -> 7.62 us  [flip_y(): return lax.ppermute(value, ('dp', 'space'), pairs)]
    ppermute x1 -> x3, starting transfers between devices: 3.1 us -> 7.8 us  [flip_y(): return lax.ppermute(value, ('dp', 'space'), pairs)]
    all_to_all x1, blocking collectives: 18.4 us -> 14.5 us  [reduce_gradient(): lax.all_to_all(parts, 'dp', split_axis=0, concat_axis=0, tiled=True, axis...]
    ppermute x4 -> x0, starting transfers between devices: 3.85 us -> none  [the longest x1 1.73 us: reduce_gradient(): a_got = lax.ppermute(a_send, 'space', three)]
    ppermute x4, waiting for transfers between devices: 6.3 us -> 2.97 us  [flip(): return lax.ppermute(value, 'dp', [(i, i ^ bit) for i in range(32)])]
  transfers between devices with their start and end apart: 23 -> 22, of which waited for: 16 -> 16; matrix products, arithmetic and copies ran while one was open for 0% -> 0% of each run, Pallas kernels for 11% -> 10%
where the time goes in v9:
time: 185 us; the launch traced here: 184 us
  waiting for transfers between devices  77.1 us (42%)
  starting transfers between devices  40.8 us (22%)
  Pallas kernels  32.6 us (18%)
  blocking collectives  24.4 us (13%)
  local copies, waits for them, and re-layouts  7.01 us (4%)
  between operations  2.11 us (1%)
    ppermute x12, waiting for transfers between devices, swap(): return lax.ppermute(value, 'space', [(s, s ^ bits) for s in range(8)])  39.7 us
    all_to_all x1, waiting for transfers between devices, on_device(): lax.all_to_all(attended, 'space', split_axis=0, concat_axis=0, tiled=True)  17.5 us
    all_to_all x1, blocking collectives, reduce_gradient(): lax.all_to_all(parts, 'dp', split_axis=0, concat_axis=0, tiled=True, axis...  14.5 us
    ppermute x12, starting transfers between devices, swap(): return lax.ppermute(value, 'space', [(s, s ^ bits) for s in range(8)])  14.2 us
    ppermute x4, starting transfers between devices, flip(): return lax.ppermute(value, 'dp', [(i, i ^ bit) for i in range(32)])  11.3 us
    all_to_all x1, blocking collectives, reduce_gradient(): lax.all_to_all(parts, 'space', split_axis=0, concat_axis=0, tiled=True)  9.89 us
    pallas_call x1, Pallas kernels, token_part(): pl.pallas_call(token_kernel, in_specs=[VMEM, VMEM, FAR_OFF, FAR_OFF, VMEM...  8.08 us
    ppermute x3, starting transfers between devices, flip_y(): return lax.ppermute(value, ('dp', 'space'), pairs)  7.8 us
  transfers between devices with their start and end apart: 22, of which 16 were waited for; matrix products, arithmetic and copies ran while one was open for 0% of the time, Pallas kernels for 10%

profile of v9, /device:TPU:32, one launch (start us, length us, event | category | flops | bytes accessed | tf_op | source)
XLA Modules:
  0.0 184.0 jit_solution(7932887271172286149)
XLA Ops:
  0.6 2.8 %depart.1 = (bf16[2,32,4992]{2,1,0:T(8,128)(2,1)}, bf16[2,32,4992]{2,1,0:T(8,128)(2,1)}, bf16[2,32,4992]{2,1,0:T(8,128)(2,1)}, bf16[4,32,4992]{2,1,0:T(8,128)(2,1)}) custom-call(bf16[16,32,4992]{2,1,0:T(8,128)(2,1)} %bitcast.17), custom_call_target="tpu_custom_call" | custom-call | bytes 6000000 | tf_op jit(solution)/shard_map/depart/pallas_call | solution.py:81
  3.5 2.8 %collective-permute-start = (bf16[4,32,4992]{2,1,0:T(8,128)(2,1)}, bf16[4,32,4992]{2,1,0:T(8,128)(2,1)S(1)}, u32[]{:S(2)}, u32[]{:S(2)}) collective-permute-start(bf16[4,32,4992]{2,1,0:T(8,128)(2,1)} %get-tuple-element.35), channel_id=1, source_target_pairs={{0,6},{1,7},{2,4},{3,5},{4,2},{5,3},{6,0},{7,1},{8,14},{9,15},{10,... | collective-permute-start | bytes 3833864 | tf_op jit(solution)/shard_map/ppermute | solution.py:131
  10.5 3.1 %collective-permute-start.4 = (bf16[1,80,512]{2,1,0:T(8,128)(2,1)S(1)}, bf16[1,80,512]{2,1,0:T(8,128)(2,1)S(1)}, u32[]{:S(2)}, u32[]{:S(2)}) collective-permute-start(bf16[1,80,512]{2,1,0:T(8,128)(2,1)S(1)} %concatenate.3.refs_0_), channel_id=1, source_target_pairs={{0,129},{1,128},{2,131},{3,130},{4,133},{5,132},{6,135},{7,134},{8... | collective-permute-start | bytes 245768 | tf_op jit(solution)/shard_map/ppermute | solution.py:271
  13.6 2.6 %collective-permute-done.4.refs_1_ = bf16[1,80,512]{2,1,0:T(8,128)(2,1)S(1)} collective-permute-done((bf16[1,80,512]{2,1,0:T(8,128)(2,1)S(1)}, bf16[1,80,512]{2,1,0:T(8,128)(2,1)S(1)}, u32[]{:S(2)}, u32[]{:S(2)}) %collective-permute-start.4) | collective-permute-done | bytes 81952 | tf_op jit(solution)/shard_map/ppermute | solution.py:271
  16.3 6.4 %collective-permute-start.5 = (bf16[2,80,512]{2,1,0:T(8,128)(2,1)S(1)}, bf16[2,80,512]{2,1,0:T(8,128)(2,1)S(1)}, u32[]{:S(2)}, u32[]{:S(2)}) collective-permute-start(bf16[2,80,512]{2,1,0:T(8,128)(2,1)S(1)} %bitcast.15), channel_id=1, source_target_pairs={{0,64},{8,72},{16,80},{24,88},{32,96},{40,104},{48,112},{56,120},{... | collective-permute-start | bytes 491528 | tf_op jit(solution)/shard_map/ppermute | solution.py:261
  22.6 2.3 %own.1 = (bf16[1,32,4992]{2,1,0:T(8,128)(2,1)}, bf16[3,32,4992]{2,1,0:T(8,128)(2,1)}, bf16[2,32,4992]{2,1,0:T(8,128)(2,1)}) custom-call(bf16[16,32,4992]{2,1,0:T(8,128)(2,1)} %bitcast.18), custom_call_target="tpu_custom_call" | custom-call | bytes 6000000 | tf_op jit(solution)/shard_map/own/pallas_call | solution.py:81
  25.0 2.1 %collective-permute-done.5.behind_ref.refs_1_ = bf16[2,80,512]{2,1,0:T(8,128)(2,1)S(1)} collective-permute-done((bf16[2,80,512]{2,1,0:T(8,128)(2,1)S(1)}, bf16[2,80,512]{2,1,0:T(8,128)(2,1)S(1)}, u32[]{:S(2)}, u32[]{:S(2)}) %collective-permute-start.5) | collective-permute-done | bytes 163872 | tf_op jit(solution)/shard_map/ppermute | solution.py:261
  27.1 10.2 %collective-permute-done.3.three.refs_2_ = bf16[2,32,4992]{2,1,0:T(8,128)(2,1)S(1)} collective-permute-done((bf16[2,32,4992]{2,1,0:T(8,128)(2,1)}, bf16[2,32,4992]{2,1,0:T(8,128)(2,1)S(1)}, u32[]{:S(2)}, u32[]{:S(2)}) %collective-permute-start.3) | collective-permute-done | bytes 639008 | tf_op jit(solution)/shard_map/ppermute | solution.py:131
  40.9 3.4 %collective-permute-start.10 = (bf16[4,80,512]{2,1,0:T(8,128)(2,1)S(1)}, bf16[4,80,512]{2,1,0:T(8,128)(2,1)S(1)}, u32[]{:S(2)}, u32[]{:S(2)}) collective-permute-start(bf16[4,80,512]{2,1,0:T(8,128)(2,1)S(1)} %bitcast.13), channel_id=1, source_target_pairs={{0,32},{8,40},{16,48},{24,56},{32,0},{40,8},{48,16},{56,24},{64,96... | collective-permute-start | bytes 983048 | tf_op jit(solution)/shard_map/ppermute | solution.py:261
  44.5 2.8 %collective-permute-start.9 = (bf16[2,32,4992]{2,1,0:T(8,128)(2,1)S(1)}, bf16[2,32,4992]{2,1,0:T(8,128)(2,1)S(1)}, u32[]{:S(2)}, u32[]{:S(2)}) collective-permute-start(bf16[2,32,4992]{2,1,0:T(8,128)(2,1)S(1)} %get-tuple-element.43), channel_id=1, source_target_pairs={{0,3},{1,2},{2,1},{3,0},{4,7},{5,6},{6,5},{7,4},{8,11},{9,10},{10,... | collective-permute-start | bytes 1916936 | tf_op jit(solution)/shard_map/ppermute | solution.py:131
  47.7 5.8 %time_weights.1 = (bf16[13,2,256,256]{3,2,1,0:T(8,128)(2,1)S(1)}, f32[8,128]{1,0:T(8,128)S(1)}) custom-call(bf16[16,32,3328]{2,1,0:T(8,128)(2,1)S(1)} %bitcast.10, bf16[2,32,4992]{2,1,0:T(8,128)(2,1)S(1)} %get-tuple-element.41.behind_ref.refs_2_), custom_call_target="tpu_custom_call" | custom-call | flops 436207616 | bytes 7000000 | tf_op jit(solution)/shard_map/time_weights/pallas_call | solution.py:236
  57.7 11.0 %collective-permute-done.6.turned_ref = bf16[4,32,4992]{2,1,0:T(8,128)(2,1)S(1)} collective-permute-done((bf16[4,32,4992]{2,1,0:T(8,128)(2,1)S(1)}, bf16[4,32,4992]{2,1,0:T(8,128)(2,1)S(1)}, u32[]{:S(2)}, u32[]{:S(2)}) %collective-permute-start.6) | collective-permute-done | bytes 1277984 | tf_op jit(solution)/shard_map/ppermute | solution.py:131
  68.7 4.5 %collective-permute-done.9.refs_5_ = bf16[2,32,4992]{2,1,0:T(8,128)(2,1)S(1)} collective-permute-done((bf16[2,32,4992]{2,1,0:T(8,128)(2,1)S(1)}, bf16[2,32,4992]{2,1,0:T(8,128)(2,1)S(1)}, u32[]{:S(2)}, u32[]{:S(2)}) %collective-permute-start.9) | collective-permute-done | bytes 639008 | tf_op jit(solution)/shard_map/ppermute | solution.py:131
  74.6 5.4 %spatial_attention.1 = bf16[8,2,32,1664]{3,2,1,0:T(8,128)(2,1)} custom-call(bf16[2,32,4992]{2,1,0:T(8,128)(2,1)S(1)} %copy-done.2, bf16[4,32,4992]{2,1,0:T(8,128)(2,1)S(1)} %collective-permute-done.across_ref, bf16[4,32,4992]{2,1,0:T(8,128)(2,1)S(1)} %collective-permute-done.6.turned_ref, bf16[2,32,4992]{2,1,0:T(8,128)(2,1)S(1)} %collective-permute-done.1.one.refs_0_, ...), custom_call_target="tpu_custom_call" | custom-call | flops 872415232 | bytes 6815744 | tf_op jit(solution)/shard_map/spatial_attention/pallas_call | solution.py:186
  80.0 4.0 %all-to-all-start = ((bf16[8,2,32,1664]{3,2,1,0:T(8,128)(2,1)}), bf16[8,2,32,1664]{3,2,1,0:T(8,128)(2,1)S(1)}, u32[]{:S(2)}, u32[]{:S(2)}) async-start(bf16[8,2,32,1664]{3,2,1,0:T(8,128)(2,1)} %spatial_attention.1), calls=%async_computation | async-start | bytes 3407872 | tf_op jit(solution)/shard_map/all_to_all | solution.py:557
  84.0 2.2 %join.7 = bf16[2,8,80,512]{3,2,1,0:T(8,128)(2,1)} custom-call(bf16[8,80,512]{2,1,0:T(8,128)(2,1)S(1)} %bitcast.12, bf16[8,80,512]{2,1,0:T(8,128)(2,1)} %collective-permute-done.11.refs_1_), custom_call_target="tpu_custom_call" | custom-call | bytes 1000000 | tf_op jit(solution)/shard_map/join/pallas_call | solution.py:275
  86.2 17.5 %all-to-all-done.value = bf16[8,2,32,1664]{3,2,1,0:T(8,128)(2,1)S(1)} async-done(((bf16[8,2,32,1664]{3,2,1,0:T(8,128)(2,1)}), bf16[8,2,32,1664]{3,2,1,0:T(8,128)(2,1)S(1)}, u32[]{:S(2)}, u32[]{:S(2)}) %all-to-all-start) | async-done | bytes 1703968 | tf_op jit(solution)/shard_map/all_to_all | solution.py:557
  104.7 2.0 %copy-done.5 = bf16[13,2,256,256]{3,2,1,0:T(8,128)(2,1)S(1)} copy-done((bf16[13,2,256,256]{3,2,1,0:T(8,128)(2,1)S(1)}, bf16[13,2,256,256]{3,2,1,0:T(8,128)(2,1)}, u32[]{:S(2)}) %copy-start.5) | copy-done | bytes 3407896
  108.0 8.1 %token_part.1 = (bf16[16,32,512]{2,1,0:T(8,128)(2,1)}, f32[8,2,32,128]{3,2,1,0:T(8,128)}, bf16[32,80,512]{2,1,0:T(8,128)(2,1)}, f32[32,128]{1,0:T(8,128)S(1)}) custom-call(bf16[8,2,32,1664]{3,2,1,0:T(8,128)(2,1)S(1)} %all-to-all-done.value, bf16[13,2,256,256]{3,2,1,0:T(8,128)(2,1)S(1)} %copy-done.5, bf16[1664,512]{1,0:T(8,128)(2,1)} %proj_ref.1, ...), custom_call_target="tpu_custom_call" | custom-call | flops 4499999744 | bytes 12000000 | tf_op jit(solution)/shard_map/token_part/pallas_call | solution.py:356
  116.1 3.4 %all-to-all-start.1 = ((f32[8,2,32,128]{3,2,1,0:T(8,128)}), f32[8,2,32,128]{3,2,1,0:T(8,128)S(1)}, u32[]{:S(2)}, u32[]{:S(2)}) async-start(f32[8,2,32,128]{3,2,1,0:T(8,128)} %get-tuple-element.47), calls=%async_computation.1 | async-start | bytes 524288 | tf_op jit(solution)/shard_map/all_to_all | solution.py:559
  120.2 6.2 %all-to-all-done.1.stats_ref = f32[8,2,32,128]{3,2,1,0:T(8,128)S(1)} async-done(((f32[8,2,32,128]{3,2,1,0:T(8,128)}), f32[8,2,32,128]{3,2,1,0:T(8,128)S(1)}, u32[]{:S(2)}, u32[]{:S(2)}) %all-to-all-start.1) | async-done | bytes 262176 | tf_op jit(solution)/shard_map/all_to_all | solution.py:559
  126.4 2.4 %coef_part.1 = (bf16[16,80,512]{2,1,0:T(8,128)(2,1)S(1)}, bf16[16,80,512]{2,1,0:T(8,128)(2,1)S(1)}, f32[1,1]{1,0:T(1,128)}) custom-call(s32[1]{0:T(128)S(6)} %copy.10.pos_ref, f32[8,2,32,128]{3,2,1,0:T(8,128)S(1)} %all-to-all-done.1.stats_ref, f32[32,128]{1,0:T(8,128)S(1)} %get-tuple-element.48.lens_ref, bf16[32,80,512]{2,1,0:T(8,128)(2,1)} %get-tuple-element.49.grad_ref), custom_call_target="tpu_custom_call" | custom-call | flops 4000000 | bytes 6000000 | tf_op jit(solution)/shard_map/coef_part/pallas_call | solution.py:430
  128.9 3.0 %collective-permute-done.13.got_ref = bf16[16,80,512]{2,1,0:T(8,128)(2,1)S(1)} collective-permute-done((bf16[16,80,512]{2,1,0:T(8,128)(2,1)S(1)}, bf16[16,80,512]{2,1,0:T(8,128)(2,1)S(1)}, u32[]{:S(2)}, u32[]{:S(2)}) %collective-permute-start.13) | collective-permute-done | bytes 1310752 | tf_op jit(solution)/shard_map/ppermute | solution.py:517
  132.6 1.7 collective-permute-start.15
  134.4 7.7 %collective-permute-done.14.a_got = bf16[8,80,256]{2,1,0:T(8,128)(2,1)S(1)} collective-permute-done((bf16[8,80,256]{2,1,0:T(8,128)(2,1)S(1)}, bf16[8,80,256]{2,1,0:T(8,128)(2,1)S(1)}, u32[]{:S(2)}, u32[]{:S(2)}) %collective-permute-start.14) | collective-permute-done | bytes 327712 | tf_op jit(solution)/shard_map/ppermute | solution.py:131
  143.6 1.7 collective-permute-start.16
  145.3 2.3 %collective-permute-start.17 = (bf16[4,80,256]{2,1,0:T(8,128)(2,1)S(1)}, bf16[4,80,256]{2,1,0:T(8,128)(2,1)S(1)}, u32[]{:S(2)}, u32[]{:S(2)}) collective-permute-start(bf16[4,80,256]{2,1,0:T(8,128)(2,1)S(1)} %get-tuple-element.59), channel_id=1, source_target_pairs={{0,129},{1,128},{2,131},{3,130},{4,133},{5,132},{6,135},{7,134},{8... | collective-permute-start | bytes 491528 | tf_op jit(solution)/shard_map/ppermute | solution.py:271
  147.6 2.6 %collective-permute-done.16.a_got = bf16[8,80,128]{2,1,0:T(8,128)(2,1)S(1)} collective-permute-done((bf16[8,80,128]{2,1,0:T(8,128)(2,1)S(1)}, bf16[8,80,128]{2,1,0:T(8,128)(2,1)S(1)}, u32[]{:S(2)}, u32[]{:S(2)}) %collective-permute-start.16) | collective-permute-done | bytes 163872 | tf_op jit(solution)/shard_map/ppermute | solution.py:131
  151.9 2.4 %collective-permute-start.18 = (bf16[4,80,128]{2,1,0:T(8,128)(2,1)S(1)}, bf16[4,80,128]{2,1,0:T(8,128)(2,1)S(1)}, u32[]{:S(2)}, u32[]{:S(2)}) collective-permute-start(bf16[4,80,128]{2,1,0:T(8,128)(2,1)S(1)} %get-tuple-element.61), channel_id=1, source_target_pairs={{0,129},{1,128},{2,131},{3,130},{4,133},{5,132},{6,135},{7,134},{8... | collective-permute-start | bytes 245768 | tf_op jit(solution)/shard_map/ppermute | solution.py:271
  154.3 3.3 %collective-permute-done.18.a_got = bf16[4,80,128]{2,1,0:T(8,128)(2,1)S(1)} collective-permute-done((bf16[4,80,128]{2,1,0:T(8,128)(2,1)S(1)}, bf16[4,80,128]{2,1,0:T(8,128)(2,1)S(1)}, u32[]{:S(2)}, u32[]{:S(2)}) %collective-permute-start.18) | collective-permute-done | bytes 81952 | tf_op jit(solution)/shard_map/ppermute | solution.py:271
  158.8 14.5 %all_to_all.20.parts = bf16[8,80,128]{2,1,0:T(8,128)(2,1)S(1)} all-to-all(bf16[8,80,128]{2,1,0:T(8,128)(2,1)S(1)} %fourth_sum.1), channel_id=1, replica_groups={{0,16,32,48,64,80,96,112},{8,24,40,56,72,88,104,120},{128,144,160,176,1..., dimensions={0} | all-to-all | bytes 327680 | tf_op jit(solution)/shard_map/all_to_all | solution.py:533
  173.4 9.9 %all_to_all.21.parts = bf16[8,80,128]{2,1,0:T(8,128)(2,1)S(1)} all-to-all(bf16[8,80,128]{2,1,0:T(8,128)(2,1)S(1)} %owned_sum.1), channel_id=1, replica_groups=mesh['dp'=32,'space'=8] {'space'}, dimensions={0} | all-to-all | bytes 327680 | tf_op jit(solution)/shard_map/all_to_all | solution.py:538
  (51 shorter events, 21.7 us)
Async XLA Ops:
  0.6 9.9 %copy-start.8 = (bf16[1,77,512]{2,1,0:T(8,128)(2,1)S(1)}, bf16[1,77,512]{2,1,0:T(8,128)(2,1)}, u32[]{:S(2)}) copy-start(bf16[1,77,512]{2,1,0:T(8,128)(2,1)} %param.9) | copy-start | bytes 236548
  3.5 36.1 %collective-permute-start = (bf16[4,32,4992]{2,1,0:T(8,128)(2,1)}, bf16[4,32,4992]{2,1,0:T(8,128)(2,1)S(1)}, u32[]{:S(2)}, u32[]{:S(2)}) collective-permute-start(bf16[4,32,4992]{2,1,0:T(8,128)(2,1)} %get-tuple-element.35), channel_id=1, source_target_pairs={{0,6},{1,7},{2,4},{3,5},{4,2},{5,3},{6,0},{7,1},{8,14},{9,15},{10,... | collective-permute-start | bytes 3833864 | tf_op jit(solution)/shard_map/ppermute | solution.py:131
  6.3 20.8 %collective-permute-start.1 = (bf16[2,32,4992]{2,1,0:T(8,128)(2,1)}, bf16[2,32,4992]{2,1,0:T(8,128)(2,1)S(1)}, u32[]{:S(2)}, u32[]{:S(2)}) collective-permute-start(bf16[2,32,4992]{2,1,0:T(8,128)(2,1)} %get-tuple-element.37), channel_id=1, source_target_pairs={{0,1},{1,0},{2,3},{3,2},{4,5},{5,4},{6,7},{7,6},{8,9},{9,8},{10,11... | collective-permute-start | bytes 1916936 | tf_op jit(solution)/shard_map/ppermute | solution.py:131
  7.9 19.2 %collective-permute-start.2 = (bf16[2,32,4992]{2,1,0:T(8,128)(2,1)}, bf16[2,32,4992]{2,1,0:T(8,128)(2,1)S(1)}, u32[]{:S(2)}, u32[]{:S(2)}) collective-permute-start(bf16[2,32,4992]{2,1,0:T(8,128)(2,1)} %get-tuple-element.38), channel_id=1, source_target_pairs={{0,2},{1,3},{2,0},{3,1},{4,6},{5,7},{6,4},{7,5},{8,10},{9,11},{10,... | collective-permute-start | bytes 1916936 | tf_op jit(solution)/shard_map/ppermute | solution.py:131
  8.1 29.1 %collective-permute-start.3 = (bf16[2,32,4992]{2,1,0:T(8,128)(2,1)}, bf16[2,32,4992]{2,1,0:T(8,128)(2,1)S(1)}, u32[]{:S(2)}, u32[]{:S(2)}) collective-permute-start(bf16[2,32,4992]{2,1,0:T(8,128)(2,1)} %get-tuple-element.39), channel_id=1, source_target_pairs={{0,3},{1,2},{2,1},{3,0},{4,7},{5,6},{6,5},{7,4},{8,11},{9,10},{10,... | collective-permute-start | bytes 1916936 | tf_op jit(solution)/shard_map/ppermute | solution.py:131
  10.5 5.7 %collective-permute-start.4 = (bf16[1,80,512]{2,1,0:T(8,128)(2,1)S(1)}, bf16[1,80,512]{2,1,0:T(8,128)(2,1)S(1)}, u32[]{:S(2)}, u32[]{:S(2)}) collective-permute-start(bf16[1,80,512]{2,1,0:T(8,128)(2,1)S(1)} %concatenate.3.refs_0_), channel_id=1, source_target_pairs={{0,129},{1,128},{2,131},{3,130},{4,133},{5,132},{6,135},{7,134},{8... | collective-permute-start | bytes 245768 | tf_op jit(solution)/shard_map/ppermute | solution.py:271
  16.3 10.8 %collective-permute-start.5 = (bf16[2,80,512]{2,1,0:T(8,128)(2,1)S(1)}, bf16[2,80,512]{2,1,0:T(8,128)(2,1)S(1)}, u32[]{:S(2)}, u32[]{:S(2)}) collective-permute-start(bf16[2,80,512]{2,1,0:T(8,128)(2,1)S(1)} %bitcast.15), channel_id=1, source_target_pairs={{0,64},{8,72},{16,80},{24,88},{32,96},{40,104},{48,112},{56,120},{... | collective-permute-start | bytes 491528 | tf_op jit(solution)/shard_map/ppermute | solution.py:261
  37.3 1.0 copy-start.3
  38.2 1.4 copy-start.1
  39.1 29.6 %collective-permute-start.6 = (bf16[4,32,4992]{2,1,0:T(8,128)(2,1)S(1)}, bf16[4,32,4992]{2,1,0:T(8,128)(2,1)S(1)}, u32[]{:S(2)}, u32[]{:S(2)}) collective-permute-start(bf16[4,32,4992]{2,1,0:T(8,128)(2,1)S(1)} %turn.1), channel_id=1, source_target_pairs={{0,6},{1,7},{2,4},{3,5},{4,2},{5,3},{6,0},{7,1},{8,14},{9,15},{10,... | collective-permute-start | bytes 3833864 | tf_op jit(solution)/shard_map/ppermute | solution.py:131
  39.6 8.1 %copy-start = (bf16[1,16,32,3328]{3,2,1,0:T(8,128)(2,1)S(1)}, bf16[1,16,32,3328]{3,2,1,0:T(8,128)(2,1)}, u32[]{:S(2)}) copy-start(bf16[1,16,32,3328]{3,2,1,0:T(8,128)(2,1)} %param.7) | copy-start | bytes 10223620
  40.9 15.2 %collective-permute-start.10 = (bf16[4,80,512]{2,1,0:T(8,128)(2,1)S(1)}, bf16[4,80,512]{2,1,0:T(8,128)(2,1)S(1)}, u32[]{:S(2)}, u32[]{:S(2)}) collective-permute-start(bf16[4,80,512]{2,1,0:T(8,128)(2,1)S(1)} %bitcast.13), channel_id=1, source_target_pairs={{0,32},{8,40},{16,48},{24,56},{32,0},{40,8},{48,16},{56,24},{64,96... | collective-permute-start | bytes 983048 | tf_op jit(solution)/shard_map/ppermute | solution.py:261
  44.3 24.4 %collective-permute-start.8 = (bf16[2,32,4992]{2,1,0:T(8,128)(2,1)S(1)}, bf16[2,32,4992]{2,1,0:T(8,128)(2,1)S(1)}, u32[]{:S(2)}, u32[]{:S(2)}) collective-permute-start(bf16[2,32,4992]{2,1,0:T(8,128)(2,1)S(1)} %get-tuple-element.42), channel_id=1, source_target_pairs={{0,2},{1,3},{2,0},{3,1},{4,6},{5,7},{6,4},{7,5},{8,10},{9,11},{10,... | collective-permute-start | bytes 1916936 | tf_op jit(solution)/shard_map/ppermute | solution.py:131
  44.5 28.7 %collective-permute-start.9 = (bf16[2,32,4992]{2,1,0:T(8,128)(2,1)S(1)}, bf16[2,32,4992]{2,1,0:T(8,128)(2,1)S(1)}, u32[]{:S(2)}, u32[]{:S(2)}) collective-permute-start(bf16[2,32,4992]{2,1,0:T(8,128)(2,1)S(1)} %get-tuple-element.43), channel_id=1, source_target_pairs={{0,3},{1,2},{2,1},{3,0},{4,7},{5,6},{6,5},{7,4},{8,11},{9,10},{10,... | collective-permute-start | bytes 1916936 | tf_op jit(solution)/shard_map/ppermute | solution.py:131
  47.3 27.3 %collective-permute-start.7 = (bf16[2,32,4992]{2,1,0:T(8,128)(2,1)S(1)}, bf16[2,32,4992]{2,1,0:T(8,128)(2,1)S(1)}, u32[]{:S(2)}, u32[]{:S(2)}) collective-permute-start(bf16[2,32,4992]{2,1,0:T(8,128)(2,1)S(1)} %get-tuple-element.41.behind_ref.refs_2_), channel_id=1, source_target_pairs={{0,1},{1,0},{2,3},{3,2},{4,5},{5,4},{6,7},{7,6},{8,9},{9,8},{10,11... | collective-permute-start | bytes 1916936 | tf_op jit(solution)/shard_map/ppermute | solution.py:131
  53.6 1.7 copy-start.4
  55.3 19.3 %copy-start.2 = (bf16[2,32,4992]{2,1,0:T(8,128)(2,1)S(1)}, bf16[2,32,4992]{2,1,0:T(8,128)(2,1)}, u32[]{:S(2)}) copy-start(bf16[2,32,4992]{2,1,0:T(8,128)(2,1)} %get-tuple-element.34.kept_ref) | copy-start | bytes 1916932
  56.1 27.8 %collective-permute-start.11 = (bf16[8,80,512]{2,1,0:T(8,128)(2,1)S(1)}, bf16[8,80,512]{2,1,0:T(8,128)(2,1)}, u32[]{:S(2)}, u32[]{:S(2)}) collective-permute-start(bf16[8,80,512]{2,1,0:T(8,128)(2,1)S(1)} %bitcast.11), channel_id=1, source_target_pairs={{0,16},{8,24},{16,0},{24,8},{32,48},{40,56},{48,32},{56,40},{64,80... | collective-permute-start | bytes 1966088 | tf_op jit(solution)/shard_map/ppermute | solution.py:261
  80.0 23.7 %all-to-all-start = ((bf16[8,2,32,1664]{3,2,1,0:T(8,128)(2,1)}), bf16[8,2,32,1664]{3,2,1,0:T(8,128)(2,1)S(1)}, u32[]{:S(2)}, u32[]{:S(2)}) async-start(bf16[8,2,32,1664]{3,2,1,0:T(8,128)(2,1)} %spatial_attention.1), calls=%async_computation | async-start | bytes 3407872 | tf_op jit(solution)/shard_map/all_to_all | solution.py:557
  86.2 17.5 %collective-permute-start.12 = (bf16[16,80,512]{2,1,0:T(8,128)(2,1)}, bf16[16,80,512]{2,1,0:T(8,128)(2,1)S(1)}, u32[]{:S(2)}, u32[]{:S(2)}) collective-permute-start(bf16[16,80,512]{2,1,0:T(8,128)(2,1)} %bitcast.6.mine_ref), channel_id=1, source_target_pairs={{0,8},{8,0},{16,24},{24,16},{32,40},{40,32},{48,56},{56,48},{64,72... | collective-permute-start | bytes 3932168 | tf_op jit(solution)/shard_map/ppermute | solution.py:261
  103.7 1.0 copy-start.6
  104.7 2.0 %copy-start.5 = (bf16[13,2,256,256]{3,2,1,0:T(8,128)(2,1)S(1)}, bf16[13,2,256,256]{3,2,1,0:T(8,128)(2,1)}, u32[]{:S(2)}) copy-start(bf16[13,2,256,256]{3,2,1,0:T(8,128)(2,1)} %copy-done.4) | copy-start | bytes 10223620
  106.7 1.3 copy-start.7
  116.1 10.3 %all-to-all-start.1 = ((f32[8,2,32,128]{3,2,1,0:T(8,128)}), f32[8,2,32,128]{3,2,1,0:T(8,128)S(1)}, u32[]{:S(2)}, u32[]{:S(2)}) async-start(f32[8,2,32,128]{3,2,1,0:T(8,128)} %get-tuple-element.47), calls=%async_computation.1 | async-start | bytes 524288 | tf_op jit(solution)/shard_map/all_to_all | solution.py:559
  128.8 3.1 %collective-permute-start.13 = (bf16[16,80,512]{2,1,0:T(8,128)(2,1)S(1)}, bf16[16,80,512]{2,1,0:T(8,128)(2,1)S(1)}, u32[]{:S(2)}, u32[]{:S(2)}) collective-permute-start(bf16[16,80,512]{2,1,0:T(8,128)(2,1)S(1)} %get-tuple-element.51), channel_id=1, source_target_pairs={{0,8},{8,0},{16,24},{24,16},{32,40},{40,32},{48,56},{56,48},{64,72... | collective-permute-start | bytes 3932168 | tf_op jit(solution)/shard_map/ppermute | solution.py:517
  132.3 9.8 %collective-permute-start.14 = (bf16[8,80,256]{2,1,0:T(8,128)(2,1)S(1)}, bf16[8,80,256]{2,1,0:T(8,128)(2,1)S(1)}, u32[]{:S(2)}, u32[]{:S(2)}) collective-permute-start(bf16[8,80,256]{2,1,0:T(8,128)(2,1)S(1)} %get-tuple-element.53), channel_id=1, source_target_pairs={{0,2},{1,3},{2,0},{3,1},{4,6},{5,7},{6,4},{7,5},{8,10},{9,11},{10,... | collective-permute-start | bytes 983048 | tf_op jit(solution)/shard_map/ppermute | solution.py:131
  132.6 10.8 %collective-permute-start.15 = (bf16[8,80,256]{2,1,0:T(8,128)(2,1)S(1)}, bf16[8,80,256]{2,1,0:T(8,128)(2,1)S(1)}, u32[]{:S(2)}, u32[]{:S(2)}) collective-permute-start(bf16[8,80,256]{2,1,0:T(8,128)(2,1)S(1)} %get-tuple-element.55), channel_id=1, source_target_pairs={{0,6},{1,7},{2,4},{3,5},{4,2},{5,3},{6,0},{7,1},{8,14},{9,15},{10,... | collective-permute-start | bytes 983048 | tf_op jit(solution)/shard_map/ppermute | solution.py:131
  143.6 6.6 %collective-permute-start.16 = (bf16[8,80,128]{2,1,0:T(8,128)(2,1)S(1)}, bf16[8,80,128]{2,1,0:T(8,128)(2,1)S(1)}, u32[]{:S(2)}, u32[]{:S(2)}) collective-permute-start(bf16[8,80,128]{2,1,0:T(8,128)(2,1)S(1)} %get-tuple-element.57), channel_id=1, source_target_pairs={{0,6},{1,7},{2,4},{3,5},{4,2},{5,3},{6,0},{7,1},{8,14},{9,15},{10,... | collective-permute-start | bytes 491528 | tf_op jit(solution)/shard_map/ppermute | solution.py:131
  145.3 6.5 %collective-permute-start.17 = (bf16[4,80,256]{2,1,0:T(8,128)(2,1)S(1)}, bf16[4,80,256]{2,1,0:T(8,128)(2,1)S(1)}, u32[]{:S(2)}, u32[]{:S(2)}) collective-permute-start(bf16[4,80,256]{2,1,0:T(8,128)(2,1)S(1)} %get-tuple-element.59), channel_id=1, source_target_pairs={{0,129},{1,128},{2,131},{3,130},{4,133},{5,132},{6,135},{7,134},{8... | collective-permute-start | bytes 491528 | tf_op jit(solution)/shard_map/ppermute | solution.py:271
  151.9 5.7 %collective-permute-start.18 = (bf16[4,80,128]{2,1,0:T(8,128)(2,1)S(1)}, bf16[4,80,128]{2,1,0:T(8,128)(2,1)S(1)}, u32[]{:S(2)}, u32[]{:S(2)}) collective-permute-start(bf16[4,80,128]{2,1,0:T(8,128)(2,1)S(1)} %get-tuple-element.61), channel_id=1, source_target_pairs={{0,129},{1,128},{2,131},{3,130},{4,133},{5,132},{6,135},{7,134},{8... | collective-permute-start | bytes 245768 | tf_op jit(solution)/shard_map/ppermute | solution.py:271
  154.3 4.4 %collective-permute-start.19 = (bf16[4,80,128]{2,1,0:T(8,128)(2,1)S(1)}, bf16[4,80,128]{2,1,0:T(8,128)(2,1)S(1)}, u32[]{:S(2)}, u32[]{:S(2)}) collective-permute-start(bf16[4,80,128]{2,1,0:T(8,128)(2,1)S(1)} %get-tuple-element.63), channel_id=1, source_target_pairs={{0,2},{1,3},{2,0},{3,1},{4,6},{5,7},{6,4},{7,5},{8,10},{9,11},{10,... | collective-permute-start | bytes 245768 | tf_op jit(solution)/shard_map/ppermute | solution.py:131

commit v10 on v9

--- a/solution.py
+++ b/solution.py
@@ -465,39 +465,26 @@
     x = lax.axis_index("space") >> 1
     plan = (
         (0, ((a_keep, 0, 0), (a_send, 0, 1), (a_send, 1, 2), (a_keep, 1, 3))),
-        (4, ((b_keep, 0, 0), (b_keep, 1, 1), (b_send, 1, 2), (b_send, 0, 3))),
+        (8, ((b_keep, 0, 0), (b_keep, 1, 1), (b_send, 1, 2), (b_send, 0, 3))),
     )
     for start, parts in plan:
-        for ref, at, flipped in parts:
-            cols = pl.ds(pl.multiple_of((x ^ flipped) * 128, 128), 128)
+        for ref, at, flip in parts:
+            cols = pl.ds(pl.multiple_of((x ^ flip) * 128, 128), 128)
             for m in range(8):
-                source = m // 4 * 8 + start + m % 4
                 ref[m, :, pl.ds(at * 128, 128)] = added(
-                    keep_ref[source, :, cols], got_ref[source, :, cols]
+                    keep_ref[start + m, :, cols], got_ref[start + m, :, cols]
                 )
 
 
 def second_sum_kernel(a_keep, a_got, b_keep, b_got, a_mine, a_send, b_mine, b_send):
-    a_mine[...] = added(a_keep[:, :, :128], a_got[:, :, :128])
-    a_send[...] = added(a_keep[:, :, 128:], a_got[:, :, 128:])
-    y_hi = lax.axis_index("dp") >> 4
-    for ref, side in ((b_mine, y_hi), (b_send, 1 - y_hi)):
-        some = pl.ds(side * 4, 4)
-        ref[...] = added(b_keep[some], b_got[some])
-
-
-def third_sum_kernel(a_keep, a_got, b_keep, b_got, a_mine, a_send, b_mine, b_send):
-    y_hi = lax.axis_index("dp") >> 4
-    for ref, side in ((a_mine, y_hi), (a_send, 1 - y_hi)):
-        some = pl.ds(side * 4, 4)
-        ref[...] = added(a_keep[some], a_got[some])
-    b_mine[...] = added(b_keep[:, :, :128], b_got[:, :, :128])
-    b_send[...] = added(b_keep[:, :, 128:], b_got[:, :, 128:])
-
-
-def fourth_sum_kernel(a_mine, a_got, b_mine, b_got, out):
-    out[pl.ds(0, 4)] = added(a_mine[...], a_got[...])
-    out[pl.ds(4, 4)] = added(b_mine[...], b_got[...])
+    for keep, got, mine, send in ((a_keep, a_got, a_mine, a_send), (b_keep, b_got, b_mine, b_send)):
+        mine[...] = added(keep[:, :, :128], got[:, :, :128])
+        send[...] = added(keep[:, :, 128:], got[:, :, 128:])
+
+
+def third_sum_kernel(a_mine, a_got, b_mine, b_got, out):
+    out[pl.ds(0, 8)] = added(a_mine[...], a_got[...])
+    out[pl.ds(8, 8)] = added(b_mine[...], b_got[...])
 
 
 def owned_sum_kernel(parts, out):
@@ -514,25 +501,26 @@
 
 def reduce_gradient(send, keep):
     bf16 = jnp.bfloat16
+    one = [(s, s ^ 2) for s in range(8)]
+    three = [(s, s ^ 6) for s in range(8)]
     got = lax.ppermute(send, "dp", [(i, i ^ 1) for i in range(32)])
     a_keep, a_send, b_keep, b_send = small_call(
         first_sum_kernel, "first_sum", (keep, got), [((8, PADDED, 256), bf16)] * 4
     )
-    a_keep, a_send, b_keep, b_send = small_call(
-        second_sum_kernel, "second_sum", (a_keep, swap(a_send, 2), b_keep, swap(b_send, 6)),
-        [((8, PADDED, 128), bf16)] * 2 + [((4, PADDED, 256), bf16)] * 2,
-    )
-    a_keep, a_send, b_keep, b_send = small_call(
-        third_sum_kernel, "third_sum", (a_keep, swap(a_send, 6), b_keep, flip_y(b_send)),
-        [((4, PADDED, 128), bf16)] * 4,
-    )
+    a_got = lax.ppermute(a_send, "space", one)
+    b_got = lax.ppermute(b_send, "space", three)
+    a_mine, a_send, b_mine, b_send = small_call(
+        second_sum_kernel, "second_sum", (a_keep, a_got, b_keep, b_got),
+        [((8, PADDED, 128), bf16)] * 4,
+    )
+    a_got = lax.ppermute(a_send, "space", three)
+    b_got = lax.ppermute(b_send, "space", one)
     (parts,) = small_call(
-        fourth_sum_kernel, "fourth_sum", (a_keep, flip_y(a_send), b_keep, swap(b_send, 2)),
-        [((8, PADDED, 128), bf16)],
+        third_sum_kernel, "third_sum", (a_mine, a_got, b_mine, b_got), [((16, PADDED, 128), bf16)]
     )
     parts = lax.all_to_all(
         parts, "dp", split_axis=0, concat_axis=0, tiled=True,
-        axis_index_groups=[[y * 16 + z * 2 + c for z in range(8)] for y in range(2) for c in range(2)],
+        axis_index_groups=[[2 * m + c for m in range(16)] for c in range(2)],
     )
     (parts,) = small_call(owned_sum_kernel, "owned_sum", (parts,), [((8, PADDED, 128), bf16)])
     parts = lax.all_to_all(parts, "space", split_axis=0, concat_axis=0, tiled=True)
@@ -548,9 +536,9 @@
     caps = doubled(caps, flip_y(caps))
     far = flip(caps, 8)
     pieces, started = bring_frames(clip_qkv[0], far)
-    caps = doubled(caps, far, started)
     time, done = time_weights(temporal_qk[0], started)
-    caps = doubled(caps, flip(caps, 4), done)
+    caps = doubled(caps, far, done)
+    caps = doubled(caps, flip(caps, 4))
     caps = doubled(caps, flip(caps, 2))
     other = flip(caps, 1)
     attended = spatial_attention(pieces, done)

time: 185 us -> 191 us (1.032)
  blocking collectives: 24.4 us -> 29.4 us
  waiting for transfers between devices: 77.1 us -> 81 us
  starting transfers between devices: 40.8 us -> 37.2 us
    ppermute x0 -> x4, waiting for transfers between devices: none -> 14.4 us  [the longest x1 7.73 us: reduce_gradient(): a_got = lax.ppermute(a_send, 'space', one)]
    ppermute x12 -> x8, waiting for transfers between devices: 39.7 us -> 25.7 us  [swap(): return lax.ppermute(value, 'space', [(s, s ^ bits) for s in range(8)])]
    ppermute x4, waiting for transfers between devices: 2.97 us -> 10.5 us  [flip(): return lax.ppermute(value, 'dp', [(i, i ^ bit) for i in range(32)])]
    all_to_all x1, blocking collectives: 14.5 us -> 19.9 us  [reduce_gradient(): lax.all_to_all(parts, 'dp', split_axis=0, concat_axis=0, tiled=True, axis...]
    ppermute x3 -> x1, waiting for transfers between devices: 7.62 us -> 2.64 us  [flip_y(): return lax.ppermute(value, ('dp', 'space'), pairs)]
    ppermute x3 -> x1, starting transfers between devices: 7.8 us -> 3.1 us  [flip_y(): return lax.ppermute(value, ('dp', 'space'), pairs)]
    ppermute x12 -> x8, starting transfers between devices: 14.2 us -> 10.4 us  [swap(): return lax.ppermute(value, 'space', [(s, s ^ bits) for s in range(8)])]
    ppermute x0 -> x4, starting transfers between devices: none -> 3.85 us  [the longest x1 1.73 us: reduce_gradient(): a_got = lax.ppermute(a_send, 'space', three)]
  transfers between devices with their start and end apart: 22 -> 20, of which waited for: 16 -> 15; matrix products, arithmetic and copies ran while one was open for 0% -> 0% of each run, Pallas kernels for 10% -> 9%
where the time goes in v10:
time: 191 us; the launch traced here: 190 us
  waiting for transfers between devices  81 us (42%)
  starting transfers between devices  37.2 us (19%)
  Pallas kernels  32.5 us (17%)
  blocking collectives  29.4 us (15%)
  local copies, waits for them, and re-layouts  8.22 us (4%)
  between operations  2.1 us (1%)
    ppermute x8, waiting for transfers between devices, swap(): return lax.ppermute(value, 'space', [(s, s ^ bits) for s in range(8)])  25.7 us
    all_to_all x1, blocking collectives, reduce_gradient(): lax.all_to_all(parts, 'dp', split_axis=0, concat_axis=0, tiled=True, axis...  19.9 us
    all_to_all x1, waiting for transfers between devices, on_device(): lax.all_to_all(attended, 'space', split_axis=0, concat_axis=0, tiled=True)  18.6 us
    ppermute x4, starting transfers between devices, flip(): return lax.ppermute(value, 'dp', [(i, i ^ bit) for i in range(32)])  11.3 us
    ppermute x4, waiting for transfers between devices, flip(): return lax.ppermute(value, 'dp', [(i, i ^ bit) for i in range(32)])  10.5 us
    ppermute x8, starting transfers between devices, swap(): return lax.ppermute(value, 'space', [(s, s ^ bits) for s in range(8)])  10.4 us
    all_to_all x1, blocking collectives, reduce_gradient(): lax.all_to_all(parts, 'space', split_axis=0, concat_axis=0, tiled=True)  9.43 us
    unnamed x18, local copies, waits for them, and re-layouts  8.21 us
  transfers between devices with their start and end apart: 20, of which 15 were waited for; matrix products, arithmetic and copies ran while one was open for 0% of the time, Pallas kernels for 9%

profile of v10, /device:TPU:32, one launch (start us, length us, event | category | flops | bytes accessed | tf_op | source)
XLA Modules:
  0.0 190.4 jit_solution(8112459663543776237)
XLA Ops:
  0.6 2.8 %depart.1 = (bf16[2,32,4992]{2,1,0:T(8,128)(2,1)}, bf16[2,32,4992]{2,1,0:T(8,128)(2,1)}, bf16[2,32,4992]{2,1,0:T(8,128)(2,1)}, bf16[4,32,4992]{2,1,0:T(8,128)(2,1)}) custom-call(bf16[16,32,4992]{2,1,0:T(8,128)(2,1)} %bitcast.17), custom_call_target="tpu_custom_call" | custom-call | bytes 6000000 | tf_op jit(solution)/shard_map/depart/pallas_call | solution.py:81
  3.5 2.8 %collective-permute-start = (bf16[4,32,4992]{2,1,0:T(8,128)(2,1)}, bf16[4,32,4992]{2,1,0:T(8,128)(2,1)S(1)}, u32[]{:S(2)}, u32[]{:S(2)}) collective-permute-start(bf16[4,32,4992]{2,1,0:T(8,128)(2,1)} %get-tuple-element.31), channel_id=1, source_target_pairs={{0,6},{1,7},{2,4},{3,5},{4,2},{5,3},{6,0},{7,1},{8,14},{9,15},{10,... | collective-permute-start | bytes 3833864 | tf_op jit(solution)/shard_map/ppermute | solution.py:131
  8.1 1.7 collective-permute-start.3
  10.5 3.1 %collective-permute-start.4 = (bf16[1,80,512]{2,1,0:T(8,128)(2,1)S(1)}, bf16[1,80,512]{2,1,0:T(8,128)(2,1)S(1)}, u32[]{:S(2)}, u32[]{:S(2)}) collective-permute-start(bf16[1,80,512]{2,1,0:T(8,128)(2,1)S(1)} %concatenate.3.refs_0_), channel_id=1, source_target_pairs={{0,129},{1,128},{2,131},{3,130},{4,133},{5,132},{6,135},{7,134},{8... | collective-permute-start | bytes 245768 | tf_op jit(solution)/shard_map/ppermute | solution.py:271
  13.6 2.6 %collective-permute-done.4.refs_1_ = bf16[1,80,512]{2,1,0:T(8,128)(2,1)S(1)} collective-permute-done((bf16[1,80,512]{2,1,0:T(8,128)(2,1)S(1)}, bf16[1,80,512]{2,1,0:T(8,128)(2,1)S(1)}, u32[]{:S(2)}, u32[]{:S(2)}) %collective-permute-start.4) | collective-permute-done | bytes 81952 | tf_op jit(solution)/shard_map/ppermute | solution.py:271
  16.3 6.4 %collective-permute-start.5 = (bf16[2,80,512]{2,1,0:T(8,128)(2,1)S(1)}, bf16[2,80,512]{2,1,0:T(8,128)(2,1)S(1)}, u32[]{:S(2)}, u32[]{:S(2)}) collective-permute-start(bf16[2,80,512]{2,1,0:T(8,128)(2,1)S(1)} %bitcast.15), channel_id=1, source_target_pairs={{0,64},{8,72},{16,80},{24,88},{32,96},{40,104},{48,112},{56,120},{... | collective-permute-start | bytes 491528 | tf_op jit(solution)/shard_map/ppermute | solution.py:261
  22.6 2.3 %own.1 = (bf16[1,32,4992]{2,1,0:T(8,128)(2,1)}, bf16[3,32,4992]{2,1,0:T(8,128)(2,1)}, bf16[2,32,4992]{2,1,0:T(8,128)(2,1)}) custom-call(bf16[16,32,4992]{2,1,0:T(8,128)(2,1)} %bitcast.18), custom_call_target="tpu_custom_call" | custom-call | bytes 6000000 | tf_op jit(solution)/shard_map/own/pallas_call | solution.py:81
  25.0 2.1 %collective-permute-done.5.behind_ref.refs_1_ = bf16[2,80,512]{2,1,0:T(8,128)(2,1)S(1)} collective-permute-done((bf16[2,80,512]{2,1,0:T(8,128)(2,1)S(1)}, bf16[2,80,512]{2,1,0:T(8,128)(2,1)S(1)}, u32[]{:S(2)}, u32[]{:S(2)}) %collective-permute-start.5) | collective-permute-done | bytes 163872 | tf_op jit(solution)/shard_map/ppermute | solution.py:261
  27.1 10.2 %collective-permute-done.3.three.refs_2_ = bf16[2,32,4992]{2,1,0:T(8,128)(2,1)S(1)} collective-permute-done((bf16[2,32,4992]{2,1,0:T(8,128)(2,1)}, bf16[2,32,4992]{2,1,0:T(8,128)(2,1)S(1)}, u32[]{:S(2)}, u32[]{:S(2)}) %collective-permute-start.3) | collective-permute-done | bytes 639008 | tf_op jit(solution)/shard_map/ppermute | solution.py:131
  42.1 5.8 %time_weights.1 = (bf16[13,2,256,256]{3,2,1,0:T(8,128)(2,1)S(1)}, f32[8,128]{1,0:T(8,128)S(1)}) custom-call(bf16[16,32,3328]{2,1,0:T(8,128)(2,1)S(1)} %bitcast.10, bf16[2,32,4992]{2,1,0:T(8,128)(2,1)S(1)} %get-tuple-element.37.behind_ref), custom_call_target="tpu_custom_call" | custom-call | flops 436207616 | bytes 7000000 | tf_op jit(solution)/shard_map/time_weights/pallas_call | solution.py:236
  47.9 1.7 copy-done.4
  49.6 3.4 %collective-permute-start.10 = (bf16[4,80,512]{2,1,0:T(8,128)(2,1)S(1)}, bf16[4,80,512]{2,1,0:T(8,128)(2,1)S(1)}, u32[]{:S(2)}, u32[]{:S(2)}) collective-permute-start(bf16[4,80,512]{2,1,0:T(8,128)(2,1)S(1)} %bitcast.13), channel_id=1, source_target_pairs={{0,32},{8,40},{16,48},{24,56},{32,0},{40,8},{48,16},{56,24},{64,96... | collective-permute-start | bytes 983048 | tf_op jit(solution)/shard_map/ppermute | solution.py:261
  56.5 8.3 %collective-permute-done.10.refs_1_ = bf16[4,80,512]{2,1,0:T(8,128)(2,1)S(1)} collective-permute-done((bf16[4,80,512]{2,1,0:T(8,128)(2,1)S(1)}, bf16[4,80,512]{2,1,0:T(8,128)(2,1)S(1)}, u32[]{:S(2)}, u32[]{:S(2)}) %collective-permute-start.10) | collective-permute-done | bytes 327712 | tf_op jit(solution)/shard_map/ppermute | solution.py:261
  66.4 2.3 %collective-permute-done.6.turned_ref = bf16[4,32,4992]{2,1,0:T(8,128)(2,1)S(1)} collective-permute-done((bf16[4,32,4992]{2,1,0:T(8,128)(2,1)S(1)}, bf16[4,32,4992]{2,1,0:T(8,128)(2,1)S(1)}, u32[]{:S(2)}, u32[]{:S(2)}) %collective-permute-start.6) | collective-permute-done | bytes 1277984 | tf_op jit(solution)/shard_map/ppermute | solution.py:131
  69.4 2.5 %collective-permute-done.8.refs_4_ = bf16[2,32,4992]{2,1,0:T(8,128)(2,1)S(1)} collective-permute-done((bf16[2,32,4992]{2,1,0:T(8,128)(2,1)S(1)}, bf16[2,32,4992]{2,1,0:T(8,128)(2,1)S(1)}, u32[]{:S(2)}, u32[]{:S(2)}) %collective-permute-start.8) | collective-permute-done | bytes 639008 | tf_op jit(solution)/shard_map/ppermute | solution.py:131
  71.9 10.0 %collective-permute-done.9.refs_5_ = bf16[2,32,4992]{2,1,0:T(8,128)(2,1)S(1)} collective-permute-done((bf16[2,32,4992]{2,1,0:T(8,128)(2,1)S(1)}, bf16[2,32,4992]{2,1,0:T(8,128)(2,1)S(1)}, u32[]{:S(2)}, u32[]{:S(2)}) %collective-permute-start.9) | collective-permute-done | bytes 639008 | tf_op jit(solution)/shard_map/ppermute | solution.py:131
  81.9 5.4 %spatial_attention.1 = bf16[8,2,32,1664]{3,2,1,0:T(8,128)(2,1)} custom-call(bf16[2,32,4992]{2,1,0:T(8,128)(2,1)S(1)} %copy-done.2, bf16[4,32,4992]{2,1,0:T(8,128)(2,1)S(1)} %collective-permute-done.across_ref, bf16[4,32,4992]{2,1,0:T(8,128)(2,1)S(1)} %collective-permute-done.6.turned_ref, bf16[2,32,4992]{2,1,0:T(8,128)(2,1)S(1)} %collective-permute-done.1.one.refs_0_, ...), custom_call_target="tpu_custom_call" | custom-call | flops 872415232 | bytes 6815744 | tf_op jit(solution)/shard_map/spatial_attention/pallas_call | solution.py:186
  87.3 5.1 %all-to-all-start = ((bf16[8,2,32,1664]{3,2,1,0:T(8,128)(2,1)}), bf16[8,2,32,1664]{3,2,1,0:T(8,128)(2,1)S(1)}, u32[]{:S(2)}, u32[]{:S(2)}) async-start(bf16[8,2,32,1664]{3,2,1,0:T(8,128)(2,1)} %spatial_attention.1), calls=%async_computation | async-start | bytes 3407872 | tf_op jit(solution)/shard_map/all_to_all | solution.py:545
  92.4 2.2 %join.7 = bf16[2,8,80,512]{3,2,1,0:T(8,128)(2,1)} custom-call(bf16[8,80,512]{2,1,0:T(8,128)(2,1)S(1)} %bitcast.12, bf16[8,80,512]{2,1,0:T(8,128)(2,1)} %collective-permute-done.11.refs_1_), custom_call_target="tpu_custom_call" | custom-call | bytes 1000000 | tf_op jit(solution)/shard_map/join/pallas_call | solution.py:275
  94.6 18.6 %all-to-all-done.value = bf16[8,2,32,1664]{3,2,1,0:T(8,128)(2,1)S(1)} async-done(((bf16[8,2,32,1664]{3,2,1,0:T(8,128)(2,1)}), bf16[8,2,32,1664]{3,2,1,0:T(8,128)(2,1)S(1)}, u32[]{:S(2)}, u32[]{:S(2)}) %all-to-all-start) | async-done | bytes 1703968 | tf_op jit(solution)/shard_map/all_to_all | solution.py:545
  114.3 2.0 %copy-done.5 = bf16[13,2,256,256]{3,2,1,0:T(8,128)(2,1)S(1)} copy-done((bf16[13,2,256,256]{3,2,1,0:T(8,128)(2,1)S(1)}, bf16[13,2,256,256]{3,2,1,0:T(8,128)(2,1)}, u32[]{:S(2)}) %copy-start.5) | copy-done | bytes 3407896
  117.6 8.1 %token_part.1 = (bf16[16,32,512]{2,1,0:T(8,128)(2,1)}, f32[8,2,32,128]{3,2,1,0:T(8,128)}, bf16[32,80,512]{2,1,0:T(8,128)(2,1)}, f32[32,128]{1,0:T(8,128)S(1)}) custom-call(bf16[8,2,32,1664]{3,2,1,0:T(8,128)(2,1)S(1)} %all-to-all-done.value, bf16[13,2,256,256]{3,2,1,0:T(8,128)(2,1)S(1)} %copy-done.5, bf16[1664,512]{1,0:T(8,128)(2,1)} %proj_ref.1, ...), custom_call_target="tpu_custom_call" | custom-call | flops 4499999744 | bytes 12000000 | tf_op jit(solution)/shard_map/token_part/pallas_call | solution.py:356
  125.6 3.4 %all-to-all-start.1 = ((f32[8,2,32,128]{3,2,1,0:T(8,128)}), f32[8,2,32,128]{3,2,1,0:T(8,128)S(1)}, u32[]{:S(2)}, u32[]{:S(2)}) async-start(f32[8,2,32,128]{3,2,1,0:T(8,128)} %get-tuple-element.43), calls=%async_computation.1 | async-start | bytes 524288 | tf_op jit(solution)/shard_map/all_to_all | solution.py:547
  129.7 6.2 %all-to-all-done.1.stats_ref = f32[8,2,32,128]{3,2,1,0:T(8,128)S(1)} async-done(((f32[8,2,32,128]{3,2,1,0:T(8,128)}), f32[8,2,32,128]{3,2,1,0:T(8,128)S(1)}, u32[]{:S(2)}, u32[]{:S(2)}) %all-to-all-start.1) | async-done | bytes 262176 | tf_op jit(solution)/shard_map/all_to_all | solution.py:547
  135.9 2.4 %coef_part.1 = (bf16[16,80,512]{2,1,0:T(8,128)(2,1)S(1)}, bf16[16,80,512]{2,1,0:T(8,128)(2,1)S(1)}, f32[1,1]{1,0:T(1,128)}) custom-call(s32[1]{0:T(128)S(6)} %copy.10.pos_ref, f32[8,2,32,128]{3,2,1,0:T(8,128)S(1)} %all-to-all-done.1.stats_ref, f32[32,128]{1,0:T(8,128)S(1)} %get-tuple-element.44.lens_ref, bf16[32,80,512]{2,1,0:T(8,128)(2,1)} %get-tuple-element.45.grad_ref), custom_call_target="tpu_custom_call" | custom-call | flops 4000000 | bytes 6000000 | tf_op jit(solution)/shard_map/coef_part/pallas_call | solution.py:430
  138.4 3.0 %collective-permute-done.13.got_ref = bf16[16,80,512]{2,1,0:T(8,128)(2,1)S(1)} collective-permute-done((bf16[16,80,512]{2,1,0:T(8,128)(2,1)S(1)}, bf16[16,80,512]{2,1,0:T(8,128)(2,1)S(1)}, u32[]{:S(2)}, u32[]{:S(2)}) %collective-permute-start.13) | collective-permute-done | bytes 1310752 | tf_op jit(solution)/shard_map/ppermute | solution.py:506
  142.2 1.7 collective-permute-start.15
  143.9 7.7 %collective-permute-done.14.a_got = bf16[8,80,256]{2,1,0:T(8,128)(2,1)S(1)} collective-permute-done((bf16[8,80,256]{2,1,0:T(8,128)(2,1)S(1)}, bf16[8,80,256]{2,1,0:T(8,128)(2,1)S(1)}, u32[]{:S(2)}, u32[]{:S(2)}) %collective-permute-start.14) | collective-permute-done | bytes 327712 | tf_op jit(solution)/shard_map/ppermute | solution.py:510
  153.1 1.7 collective-permute-start.16
  154.8 4.9 %collective-permute-done.16.a_got = bf16[8,80,128]{2,1,0:T(8,128)(2,1)S(1)} collective-permute-done((bf16[8,80,128]{2,1,0:T(8,128)(2,1)S(1)}, bf16[8,80,128]{2,1,0:T(8,128)(2,1)S(1)}, u32[]{:S(2)}, u32[]{:S(2)}) %collective-permute-start.16) | collective-permute-done | bytes 163872 | tf_op jit(solution)/shard_map/ppermute | solution.py:516
  160.2 19.9 %all_to_all.20.parts = bf16[16,80,128]{2,1,0:T(8,128)(2,1)S(1)} all-to-all(bf16[16,80,128]{2,1,0:T(8,128)(2,1)S(1)} %third_sum.1), channel_id=1, replica_groups={{0,16,32,48,64,80,96,112,128,144,160,176,192,208,224,240},{8,24,40,56,7..., dimensions={0} | all-to-all | bytes 655360 | tf_op jit(solution)/shard_map/all_to_all | solution.py:521
  180.2 9.4 %all_to_all.21.parts = bf16[8,80,128]{2,1,0:T(8,128)(2,1)S(1)} all-to-all(bf16[8,80,128]{2,1,0:T(8,128)(2,1)S(1)} %owned_sum.1), channel_id=1, replica_groups=mesh['dp'=32,'space'=8] {'space'}, dimensions={0} | all-to-all | bytes 327680 | tf_op jit(solution)/shard_map/all_to_all | solution.py:526
  (46 shorter events, 18.4 us)
Async XLA Ops:
  0.6 9.8 %copy-start.8 = (bf16[1,77,512]{2,1,0:T(8,128)(2,1)S(1)}, bf16[1,77,512]{2,1,0:T(8,128)(2,1)}, u32[]{:S(2)}) copy-start(bf16[1,77,512]{2,1,0:T(8,128)(2,1)} %param.9) | copy-start | bytes 236548
  3.5 36.1 %collective-permute-start = (bf16[4,32,4992]{2,1,0:T(8,128)(2,1)}, bf16[4,32,4992]{2,1,0:T(8,128)(2,1)S(1)}, u32[]{:S(2)}, u32[]{:S(2)}) collective-permute-start(bf16[4,32,4992]{2,1,0:T(8,128)(2,1)} %get-tuple-element.31), channel_id=1, source_target_pairs={{0,6},{1,7},{2,4},{3,5},{4,2},{5,3},{6,0},{7,1},{8,14},{9,15},{10,... | collective-permute-start | bytes 3833864 | tf_op jit(solution)/shard_map/ppermute | solution.py:131
  6.3 20.8 %collective-permute-start.1 = (bf16[2,32,4992]{2,1,0:T(8,128)(2,1)}, bf16[2,32,4992]{2,1,0:T(8,128)(2,1)S(1)}, u32[]{:S(2)}, u32[]{:S(2)}) collective-permute-start(bf16[2,32,4992]{2,1,0:T(8,128)(2,1)} %get-tuple-element.33), channel_id=1, source_target_pairs={{0,1},{1,0},{2,3},{3,2},{4,5},{5,4},{6,7},{7,6},{8,9},{9,8},{10,11... | collective-permute-start | bytes 1916936 | tf_op jit(solution)/shard_map/ppermute | solution.py:131
  7.9 19.2 %collective-permute-start.2 = (bf16[2,32,4992]{2,1,0:T(8,128)(2,1)}, bf16[2,32,4992]{2,1,0:T(8,128)(2,1)S(1)}, u32[]{:S(2)}, u32[]{:S(2)}) collective-permute-start(bf16[2,32,4992]{2,1,0:T(8,128)(2,1)} %get-tuple-element.34), channel_id=1, source_target_pairs={{0,2},{1,3},{2,0},{3,1},{4,6},{5,7},{6,4},{7,5},{8,10},{9,11},{10,... | collective-permute-start | bytes 1916936 | tf_op jit(solution)/shard_map/ppermute | solution.py:131
  8.1 29.1 %collective-permute-start.3 = (bf16[2,32,4992]{2,1,0:T(8,128)(2,1)}, bf16[2,32,4992]{2,1,0:T(8,128)(2,1)S(1)}, u32[]{:S(2)}, u32[]{:S(2)}) collective-permute-start(bf16[2,32,4992]{2,1,0:T(8,128)(2,1)} %get-tuple-element.35), channel_id=1, source_target_pairs={{0,3},{1,2},{2,1},{3,0},{4,7},{5,6},{6,5},{7,4},{8,11},{9,10},{10,... | collective-permute-start | bytes 1916936 | tf_op jit(solution)/shard_map/ppermute | solution.py:131
  10.5 5.7 %collective-permute-start.4 = (bf16[1,80,512]{2,1,0:T(8,128)(2,1)S(1)}, bf16[1,80,512]{2,1,0:T(8,128)(2,1)S(1)}, u32[]{:S(2)}, u32[]{:S(2)}) collective-permute-start(bf16[1,80,512]{2,1,0:T(8,128)(2,1)S(1)} %concatenate.3.refs_0_), channel_id=1, source_target_pairs={{0,129},{1,128},{2,131},{3,130},{4,133},{5,132},{6,135},{7,134},{8... | collective-permute-start | bytes 245768 | tf_op jit(solution)/shard_map/ppermute | solution.py:271
  16.3 10.8 %collective-permute-start.5 = (bf16[2,80,512]{2,1,0:T(8,128)(2,1)S(1)}, bf16[2,80,512]{2,1,0:T(8,128)(2,1)S(1)}, u32[]{:S(2)}, u32[]{:S(2)}) collective-permute-start(bf16[2,80,512]{2,1,0:T(8,128)(2,1)S(1)} %bitcast.15), channel_id=1, source_target_pairs={{0,64},{8,72},{16,80},{24,88},{32,96},{40,104},{48,112},{56,120},{... | collective-permute-start | bytes 491528 | tf_op jit(solution)/shard_map/ppermute | solution.py:261
  37.3 1.0 copy-start.3
  38.2 3.8 %copy-start = (bf16[1,16,32,3328]{3,2,1,0:T(8,128)(2,1)S(1)}, bf16[1,16,32,3328]{3,2,1,0:T(8,128)(2,1)}, u32[]{:S(2)}) copy-start(bf16[1,16,32,3328]{3,2,1,0:T(8,128)(2,1)} %param.7) | copy-start | bytes 10223620
  39.0 29.6 %collective-permute-start.6 = (bf16[4,32,4992]{2,1,0:T(8,128)(2,1)S(1)}, bf16[4,32,4992]{2,1,0:T(8,128)(2,1)S(1)}, u32[]{:S(2)}, u32[]{:S(2)}) collective-permute-start(bf16[4,32,4992]{2,1,0:T(8,128)(2,1)S(1)} %turn.1), channel_id=1, source_target_pairs={{0,6},{1,7},{2,4},{3,5},{4,2},{5,3},{6,0},{7,1},{8,14},{9,15},{10,... | collective-permute-start | bytes 3833864 | tf_op jit(solution)/shard_map/ppermute | solution.py:131
  39.6 1.2 copy-start.1
  47.9 1.7 copy-start.4
  49.6 32.3 %copy-start.2 = (bf16[2,32,4992]{2,1,0:T(8,128)(2,1)S(1)}, bf16[2,32,4992]{2,1,0:T(8,128)(2,1)}, u32[]{:S(2)}) copy-start(bf16[2,32,4992]{2,1,0:T(8,128)(2,1)} %get-tuple-element.30.kept_ref) | copy-start | bytes 1916932
  49.6 15.2 %collective-permute-start.10 = (bf16[4,80,512]{2,1,0:T(8,128)(2,1)S(1)}, bf16[4,80,512]{2,1,0:T(8,128)(2,1)S(1)}, u32[]{:S(2)}, u32[]{:S(2)}) collective-permute-start(bf16[4,80,512]{2,1,0:T(8,128)(2,1)S(1)} %bitcast.13), channel_id=1, source_target_pairs={{0,32},{8,40},{16,48},{24,56},{32,0},{40,8},{48,16},{56,24},{64,96... | collective-permute-start | bytes 983048 | tf_op jit(solution)/shard_map/ppermute | solution.py:261
  53.0 16.4 %collective-permute-start.7 = (bf16[2,32,4992]{2,1,0:T(8,128)(2,1)S(1)}, bf16[2,32,4992]{2,1,0:T(8,128)(2,1)S(1)}, u32[]{:S(2)}, u32[]{:S(2)}) collective-permute-start(bf16[2,32,4992]{2,1,0:T(8,128)(2,1)S(1)} %get-tuple-element.37.behind_ref), channel_id=1, source_target_pairs={{0,1},{1,0},{2,3},{3,2},{4,5},{5,4},{6,7},{7,6},{8,9},{9,8},{10,11... | collective-permute-start | bytes 1916936 | tf_op jit(solution)/shard_map/ppermute | solution.py:131
  54.6 17.3 %collective-permute-start.8 = (bf16[2,32,4992]{2,1,0:T(8,128)(2,1)S(1)}, bf16[2,32,4992]{2,1,0:T(8,128)(2,1)S(1)}, u32[]{:S(2)}, u32[]{:S(2)}) collective-permute-start(bf16[2,32,4992]{2,1,0:T(8,128)(2,1)S(1)} %get-tuple-element.38), channel_id=1, source_target_pairs={{0,2},{1,3},{2,0},{3,1},{4,6},{5,7},{6,4},{7,5},{8,10},{9,11},{10,... | collective-permute-start | bytes 1916936 | tf_op jit(solution)/shard_map/ppermute | solution.py:131
  54.8 27.1 %collective-permute-start.9 = (bf16[2,32,4992]{2,1,0:T(8,128)(2,1)S(1)}, bf16[2,32,4992]{2,1,0:T(8,128)(2,1)S(1)}, u32[]{:S(2)}, u32[]{:S(2)}) collective-permute-start(bf16[2,32,4992]{2,1,0:T(8,128)(2,1)S(1)} %get-tuple-element.39), channel_id=1, source_target_pairs={{0,3},{1,2},{2,1},{3,0},{4,7},{5,6},{6,5},{7,4},{8,11},{9,10},{10,... | collective-permute-start | bytes 1916936 | tf_op jit(solution)/shard_map/ppermute | solution.py:131
  64.8 27.6 %collective-permute-start.11 = (bf16[8,80,512]{2,1,0:T(8,128)(2,1)S(1)}, bf16[8,80,512]{2,1,0:T(8,128)(2,1)}, u32[]{:S(2)}, u32[]{:S(2)}) collective-permute-start(bf16[8,80,512]{2,1,0:T(8,128)(2,1)S(1)} %bitcast.11), channel_id=1, source_target_pairs={{0,16},{8,24},{16,0},{24,8},{32,48},{40,56},{48,32},{56,40},{64,80... | collective-permute-start | bytes 1966088 | tf_op jit(solution)/shard_map/ppermute | solution.py:261
  87.3 25.9 %all-to-all-start = ((bf16[8,2,32,1664]{3,2,1,0:T(8,128)(2,1)}), bf16[8,2,32,1664]{3,2,1,0:T(8,128)(2,1)S(1)}, u32[]{:S(2)}, u32[]{:S(2)}) async-start(bf16[8,2,32,1664]{3,2,1,0:T(8,128)(2,1)} %spatial_attention.1), calls=%async_computation | async-start | bytes 3407872 | tf_op jit(solution)/shard_map/all_to_all | solution.py:545
  94.6 18.6 %collective-permute-start.12 = (bf16[16,80,512]{2,1,0:T(8,128)(2,1)}, bf16[16,80,512]{2,1,0:T(8,128)(2,1)S(1)}, u32[]{:S(2)}, u32[]{:S(2)}) collective-permute-start(bf16[16,80,512]{2,1,0:T(8,128)(2,1)} %bitcast.6.mine_ref), channel_id=1, source_target_pairs={{0,8},{8,0},{16,24},{24,16},{32,40},{40,32},{48,56},{56,48},{64,72... | collective-permute-start | bytes 3932168 | tf_op jit(solution)/shard_map/ppermute | solution.py:261
  113.2 1.1 copy-start.6
  114.3 2.0 %copy-start.5 = (bf16[13,2,256,256]{3,2,1,0:T(8,128)(2,1)S(1)}, bf16[13,2,256,256]{3,2,1,0:T(8,128)(2,1)}, u32[]{:S(2)}) copy-start(bf16[13,2,256,256]{3,2,1,0:T(8,128)(2,1)} %copy-done.4) | copy-start | bytes 10223620
  116.2 1.3 copy-start.7
  125.6 10.3 %all-to-all-start.1 = ((f32[8,2,32,128]{3,2,1,0:T(8,128)}), f32[8,2,32,128]{3,2,1,0:T(8,128)S(1)}, u32[]{:S(2)}, u32[]{:S(2)}) async-start(f32[8,2,32,128]{3,2,1,0:T(8,128)} %get-tuple-element.43), calls=%async_computation.1 | async-start | bytes 524288 | tf_op jit(solution)/shard_map/all_to_all | solution.py:547
  138.3 3.1 %collective-permute-start.13 = (bf16[16,80,512]{2,1,0:T(8,128)(2,1)S(1)}, bf16[16,80,512]{2,1,0:T(8,128)(2,1)S(1)}, u32[]{:S(2)}, u32[]{:S(2)}) collective-permute-start(bf16[16,80,512]{2,1,0:T(8,128)(2,1)S(1)} %get-tuple-element.47), channel_id=1, source_target_pairs={{0,8},{8,0},{16,24},{24,16},{32,40},{40,32},{48,56},{56,48},{64,72... | collective-permute-start | bytes 3932168 | tf_op jit(solution)/shard_map/ppermute | solution.py:506
  141.8 9.8 %collective-permute-start.14 = (bf16[8,80,256]{2,1,0:T(8,128)(2,1)S(1)}, bf16[8,80,256]{2,1,0:T(8,128)(2,1)S(1)}, u32[]{:S(2)}, u32[]{:S(2)}) collective-permute-start(bf16[8,80,256]{2,1,0:T(8,128)(2,1)S(1)} %get-tuple-element.49), channel_id=1, source_target_pairs={{0,2},{1,3},{2,0},{3,1},{4,6},{5,7},{6,4},{7,5},{8,10},{9,11},{10,... | collective-permute-start | bytes 983048 | tf_op jit(solution)/shard_map/ppermute | solution.py:510
  142.2 10.8 %collective-permute-start.15 = (bf16[8,80,256]{2,1,0:T(8,128)(2,1)S(1)}, bf16[8,80,256]{2,1,0:T(8,128)(2,1)S(1)}, u32[]{:S(2)}, u32[]{:S(2)}) collective-permute-start(bf16[8,80,256]{2,1,0:T(8,128)(2,1)S(1)} %get-tuple-element.51), channel_id=1, source_target_pairs={{0,6},{1,7},{2,4},{3,5},{4,2},{5,3},{6,0},{7,1},{8,14},{9,15},{10,... | collective-permute-start | bytes 983048 | tf_op jit(solution)/shard_map/ppermute | solution.py:511
  153.1 6.6 %collective-permute-start.16 = (bf16[8,80,128]{2,1,0:T(8,128)(2,1)S(1)}, bf16[8,80,128]{2,1,0:T(8,128)(2,1)S(1)}, u32[]{:S(2)}, u32[]{:S(2)}) collective-permute-start(bf16[8,80,128]{2,1,0:T(8,128)(2,1)S(1)} %get-tuple-element.53), channel_id=1, source_target_pairs={{0,6},{1,7},{2,4},{3,5},{4,2},{5,3},{6,0},{7,1},{8,14},{9,15},{10,... | collective-permute-start | bytes 491528 | tf_op jit(solution)/shard_map/ppermute | solution.py:516
  154.8 5.3 %collective-permute-start.17 = (bf16[8,80,128]{2,1,0:T(8,128)(2,1)S(1)}, bf16[8,80,128]{2,1,0:T(8,128)(2,1)S(1)}, u32[]{:S(2)}, u32[]{:S(2)}) collective-permute-start(bf16[8,80,128]{2,1,0:T(8,128)(2,1)S(1)} %get-tuple-element.55), channel_id=1, source_target_pairs={{0,2},{1,3},{2,0},{3,1},{4,6},{5,7},{6,4},{7,5},{8,10},{9,11},{10,... | collective-permute-start | bytes 491528 | tf_op jit(solution)/shard_map/ppermute | solution.py:517

commit v11 on v10

--- a/solution.py
+++ b/solution.py
@@ -112,7 +112,7 @@
     copied(pairs, buf, sems)
 
 
-def turn_kernel(first_ref, one, two, three, behind_ref, out_ref, buf, sems):
+def turn_kernel(first_ref, one, two, three, behind_ref, started_ref, out_ref, buf, sems):
     g1, _ = quad_place()
     pairs = [(first_ref.at[0], out_ref.at[0])]
     pairs += [(ref.at[1 - g1], out_ref.at[k]) for k, ref in ((1, one), (2, two), (3, three))]
@@ -137,11 +137,11 @@
     quads = [swap(quad, k) for k, quad in zip((1, 2, 3), quads)]
     first, seconds, kept = copying(own_kernel, "own", (clip,), (1, 3, 2), 6)
     few = pltpu.CompilerParams(vmem_limit_bytes=8 * MIB)
-    (turned,) = copying(turn_kernel, "turn", (first, *quads, behind), (4,), 4, few)
-    turned = swap(turned, 6)
     pairs = copying(spread_kernel, "spread", (seconds, across), (2, 2, 2), 6, few)
     started = pairs[0]
     pairs = [swap(pair, k) for k, pair in zip((1, 2, 3), pairs)]
+    (turned,) = copying(turn_kernel, "turn", (first, *quads, behind, started), (4,), 4, few)
+    turned = swap(turned, 6)
     return (kept, across, turned, *quads, *pairs), started
 
 
@@ -537,11 +537,11 @@
     far = flip(caps, 8)
     pieces, started = bring_frames(clip_qkv[0], far)
     time, done = time_weights(temporal_qk[0], started)
-    caps = doubled(caps, far, done)
-    caps = doubled(caps, flip(caps, 4))
+    caps = doubled(caps, far)
+    attended = spatial_attention(pieces, done)
+    caps = doubled(caps, flip(caps, 4), attended)
     caps = doubled(caps, flip(caps, 2))
     other = flip(caps, 1)
-    attended = spatial_attention(pieces, done)
     spatial = lax.all_to_all(attended, "space", split_axis=0, concat_axis=0, tiled=True)
     video, stats, grad, lens = token_part(spatial, time, proj_weight, caps, other)
     stats = lax.all_to_all(stats, "space", split_axis=0, concat_axis=0, tiled=True)

time: 191 us -> 181 us (0.948)
  waiting for transfers between devices: 81 us -> 72.1 us
  local copies, waits for them, and re-layouts: 8.22 us -> 4.87 us
  blocking collectives: 29.4 us -> 32.2 us
    all_to_all x1, waiting for transfers between devices: 18.6 us -> 10.3 us  [on_device(): lax.all_to_all(attended, 'space', split_axis=0, concat_axis=0, tiled=True)]
    unnamed x18 -> x14, local copies, waits for them, and re-layouts: 8.21 us -> 4.86 us
    all_to_all x1, blocking collectives: 19.9 us -> 22.8 us  [reduce_gradient(): lax.all_to_all(parts, 'dp', split_axis=0, concat_axis=0, tiled=True, axis...]
    ppermute x8, starting transfers between devices: 10.4 us -> 12.7 us  [swap(): return lax.ppermute(value, 'space', [(s, s ^ bits) for s in range(8)])]
  transfers between devices with their start and end apart: 20 -> 20, of which waited for: 15 -> 13; matrix products, arithmetic and copies ran while one was open for 0% -> 0% of each run, Pallas kernels for 9% -> 9%
where the time goes in v11:
time: 181 us
  waiting for transfers between devices  72.1 us (40%)
  starting transfers between devices  36.8 us (20%)
  Pallas kernels  32.6 us (18%)
  blocking collectives  32.2 us (18%)
  local copies, waits for them, and re-layouts  4.87 us (3%)
  between operations  2.16 us (1%)
    ppermute x8, waiting for transfers between devices, swap(): return lax.ppermute(value, 'space', [(s, s ^ bits) for s in range(8)])  25.1 us
    all_to_all x1, blocking collectives, reduce_gradient(): lax.all_to_all(parts, 'dp', split_axis=0, concat_axis=0, tiled=True, axis...  22.8 us
    ppermute x8, starting transfers between devices, swap(): return lax.ppermute(value, 'space', [(s, s ^ bits) for s in range(8)])  12.7 us
    ppermute x4, waiting for transfers between devices, flip(): return lax.ppermute(value, 'dp', [(i, i ^ bit) for i in range(32)])  10.4 us
    all_to_all x1, waiting for transfers between devices, on_device(): lax.all_to_all(attended, 'space', split_axis=0, concat_axis=0, tiled=True)  10.3 us
    ppermute x4, starting transfers between devices, flip(): return lax.ppermute(value, 'dp', [(i, i ^ bit) for i in range(32)])  10.1 us
    all_to_all x1, blocking collectives, reduce_gradient(): lax.all_to_all(parts, 'space', split_axis=0, concat_axis=0, tiled=True)  9.43 us
    pallas_call x1, Pallas kernels, token_part(): pl.pallas_call(token_kernel, in_specs=[VMEM, VMEM, FAR_OFF, FAR_OFF, VMEM...  9.18 us
  transfers between devices with their start and end apart: 20, of which 13 were waited for; matrix products, arithmetic and copies ran while one was open for 0% of the time, Pallas kernels for 9%

profile of v11, /device:TPU:32, one launch (start us, length us, event | category | flops | bytes accessed | tf_op | source)
XLA Modules:
  0.0 180.8 jit_solution(9575505430364926043)
XLA Ops:
  0.6 2.8 %depart.1 = (bf16[2,32,4992]{2,1,0:T(8,128)(2,1)}, bf16[2,32,4992]{2,1,0:T(8,128)(2,1)}, bf16[2,32,4992]{2,1,0:T(8,128)(2,1)}, bf16[4,32,4992]{2,1,0:T(8,128)(2,1)}) custom-call(bf16[16,32,4992]{2,1,0:T(8,128)(2,1)} %bitcast.17), custom_call_target="tpu_custom_call" | custom-call | bytes 6000000 | tf_op jit(solution)/shard_map/depart/pallas_call | solution.py:81
  3.5 2.8 %collective-permute-start = (bf16[4,32,4992]{2,1,0:T(8,128)(2,1)}, bf16[4,32,4992]{2,1,0:T(8,128)(2,1)S(1)}, u32[]{:S(2)}, u32[]{:S(2)}) collective-permute-start(bf16[4,32,4992]{2,1,0:T(8,128)(2,1)} %get-tuple-element.31), channel_id=1, source_target_pairs={{0,6},{1,7},{2,4},{3,5},{4,2},{5,3},{6,0},{7,1},{8,14},{9,15},{10,... | collective-permute-start | bytes 3833864 | tf_op jit(solution)/shard_map/ppermute | solution.py:131
  8.1 1.7 collective-permute-start.3
  10.5 3.1 %collective-permute-start.4 = (bf16[1,80,512]{2,1,0:T(8,128)(2,1)S(1)}, bf16[1,80,512]{2,1,0:T(8,128)(2,1)S(1)}, u32[]{:S(2)}, u32[]{:S(2)}) collective-permute-start(bf16[1,80,512]{2,1,0:T(8,128)(2,1)S(1)} %concatenate.3.refs_0_), channel_id=1, source_target_pairs={{0,129},{1,128},{2,131},{3,130},{4,133},{5,132},{6,135},{7,134},{8... | collective-permute-start | bytes 245768 | tf_op jit(solution)/shard_map/ppermute | solution.py:271
  13.6 2.6 %collective-permute-done.4.refs_1_ = bf16[1,80,512]{2,1,0:T(8,128)(2,1)S(1)} collective-permute-done((bf16[1,80,512]{2,1,0:T(8,128)(2,1)S(1)}, bf16[1,80,512]{2,1,0:T(8,128)(2,1)S(1)}, u32[]{:S(2)}, u32[]{:S(2)}) %collective-permute-start.4) | collective-permute-done | bytes 81952 | tf_op jit(solution)/shard_map/ppermute | solution.py:271
  16.3 6.4 %collective-permute-start.5 = (bf16[2,80,512]{2,1,0:T(8,128)(2,1)S(1)}, bf16[2,80,512]{2,1,0:T(8,128)(2,1)S(1)}, u32[]{:S(2)}, u32[]{:S(2)}) collective-permute-start(bf16[2,80,512]{2,1,0:T(8,128)(2,1)S(1)} %bitcast.15), channel_id=1, source_target_pairs={{0,64},{8,72},{16,80},{24,88},{32,96},{40,104},{48,112},{56,120},{... | collective-permute-start | bytes 491528 | tf_op jit(solution)/shard_map/ppermute | solution.py:261
  22.6 2.3 %own.1 = (bf16[1,32,4992]{2,1,0:T(8,128)(2,1)}, bf16[3,32,4992]{2,1,0:T(8,128)(2,1)}, bf16[2,32,4992]{2,1,0:T(8,128)(2,1)}) custom-call(bf16[16,32,4992]{2,1,0:T(8,128)(2,1)} %bitcast.18), custom_call_target="tpu_custom_call" | custom-call | bytes 6000000 | tf_op jit(solution)/shard_map/own/pallas_call | solution.py:81
  25.0 9.8 %collective-permute-done.across_ref = bf16[4,32,4992]{2,1,0:T(8,128)(2,1)S(1)} collective-permute-done((bf16[4,32,4992]{2,1,0:T(8,128)(2,1)}, bf16[4,32,4992]{2,1,0:T(8,128)(2,1)S(1)}, u32[]{:S(2)}, u32[]{:S(2)}) %collective-permute-start) | collective-permute-done | bytes 1277984 | tf_op jit(solution)/shard_map/ppermute | solution.py:131
  38.1 2.8 %collective-permute-start.6 = (bf16[4,32,4992]{2,1,0:T(8,128)(2,1)S(1)}, bf16[4,32,4992]{2,1,0:T(8,128)(2,1)S(1)}, u32[]{:S(2)}, u32[]{:S(2)}) collective-permute-start(bf16[4,32,4992]{2,1,0:T(8,128)(2,1)S(1)} %turn.1), channel_id=1, source_target_pairs={{0,6},{1,7},{2,4},{3,5},{4,2},{5,3},{6,0},{7,1},{8,14},{9,15},{10,... | collective-permute-start | bytes 3833864 | tf_op jit(solution)/shard_map/ppermute | solution.py:131
  42.6 1.9 %collective-permute-start.9 = (bf16[2,32,4992]{2,1,0:T(8,128)(2,1)S(1)}, bf16[2,32,4992]{2,1,0:T(8,128)(2,1)S(1)}, u32[]{:S(2)}, u32[]{:S(2)}) collective-permute-start(bf16[2,32,4992]{2,1,0:T(8,128)(2,1)S(1)} %get-tuple-element.39), channel_id=1, source_target_pairs={{0,3},{1,2},{2,1},{3,0},{4,7},{5,6},{6,5},{7,4},{8,11},{9,10},{10,... | collective-permute-start | bytes 1916936 | tf_op jit(solution)/shard_map/ppermute | solution.py:131
  44.5 3.5 %collective-permute-start.10 = (bf16[4,80,512]{2,1,0:T(8,128)(2,1)S(1)}, bf16[4,80,512]{2,1,0:T(8,128)(2,1)S(1)}, u32[]{:S(2)}, u32[]{:S(2)}) collective-permute-start(bf16[4,80,512]{2,1,0:T(8,128)(2,1)S(1)} %bitcast.13), channel_id=1, source_target_pairs={{0,32},{8,40},{16,48},{24,56},{32,0},{40,8},{48,16},{56,24},{64,96... | collective-permute-start | bytes 983048 | tf_op jit(solution)/shard_map/ppermute | solution.py:261
  48.0 5.8 %time_weights.1 = (bf16[13,2,256,256]{3,2,1,0:T(8,128)(2,1)S(1)}, f32[8,128]{1,0:T(8,128)S(1)}) custom-call(bf16[16,32,3328]{2,1,0:T(8,128)(2,1)S(1)} %bitcast.10, bf16[2,32,4992]{2,1,0:T(8,128)(2,1)S(1)} %get-tuple-element.37.started_ref.behind_ref), custom_call_target="tpu_custom_call" | custom-call | flops 436207616 | bytes 7000000 | tf_op jit(solution)/shard_map/time_weights/pallas_call | solution.py:236
  53.9 1.7 copy-done.4
  55.6 1.8 %collective-permute-done.7.refs_3_ = bf16[2,32,4992]{2,1,0:T(8,128)(2,1)S(1)} collective-permute-done((bf16[2,32,4992]{2,1,0:T(8,128)(2,1)S(1)}, bf16[2,32,4992]{2,1,0:T(8,128)(2,1)S(1)}, u32[]{:S(2)}, u32[]{:S(2)}) %collective-permute-start.7) | collective-permute-done | bytes 639008 | tf_op jit(solution)/shard_map/ppermute | solution.py:131
  57.4 2.5 %collective-permute-done.8.refs_4_ = bf16[2,32,4992]{2,1,0:T(8,128)(2,1)S(1)} collective-permute-done((bf16[2,32,4992]{2,1,0:T(8,128)(2,1)S(1)}, bf16[2,32,4992]{2,1,0:T(8,128)(2,1)S(1)}, u32[]{:S(2)}, u32[]{:S(2)}) %collective-permute-start.8) | collective-permute-done | bytes 639008 | tf_op jit(solution)/shard_map/ppermute | solution.py:131
  59.9 11.0 %collective-permute-done.9.refs_5_ = bf16[2,32,4992]{2,1,0:T(8,128)(2,1)S(1)} collective-permute-done((bf16[2,32,4992]{2,1,0:T(8,128)(2,1)S(1)}, bf16[2,32,4992]{2,1,0:T(8,128)(2,1)S(1)}, u32[]{:S(2)}, u32[]{:S(2)}) %collective-permute-start.9) | collective-permute-done | bytes 639008 | tf_op jit(solution)/shard_map/ppermute | solution.py:131
  70.8 5.4 %spatial_attention.1.refs_2_ = bf16[8,2,32,1664]{3,2,1,0:T(8,128)(2,1)} custom-call(bf16[2,32,4992]{2,1,0:T(8,128)(2,1)S(1)} %copy-done.2, bf16[4,32,4992]{2,1,0:T(8,128)(2,1)S(1)} %collective-permute-done.across_ref, bf16[4,32,4992]{2,1,0:T(8,128)(2,1)S(1)} %collective-permute-done.6.turned_ref, ...), custom_call_target="tpu_custom_call" | custom-call | flops 872415232 | bytes 6815744 | tf_op jit(solution)/shard_map/spatial_attention/pallas_call | solution.py:186
  76.5 3.6 %all-to-all-start = ((bf16[8,2,32,1664]{3,2,1,0:T(8,128)(2,1)}), bf16[8,2,32,1664]{3,2,1,0:T(8,128)(2,1)S(1)}, u32[]{:S(2)}, u32[]{:S(2)}) async-start(bf16[8,2,32,1664]{3,2,1,0:T(8,128)(2,1)} %spatial_attention.1.refs_2_), calls=%async_computation | async-start | bytes 3407872 | tf_op jit(solution)/shard_map/all_to_all | solution.py:545
  80.1 10.4 %collective-permute-done.11.refs_1_ = bf16[8,80,512]{2,1,0:T(8,128)(2,1)S(1)} collective-permute-done((bf16[8,80,512]{2,1,0:T(8,128)(2,1)S(1)}, bf16[8,80,512]{2,1,0:T(8,128)(2,1)S(1)}, u32[]{:S(2)}, u32[]{:S(2)}) %collective-permute-start.11) | collective-permute-done | bytes 655392 | tf_op jit(solution)/shard_map/ppermute | solution.py:261
  91.7 10.3 %all-to-all-done.value = bf16[8,2,32,1664]{3,2,1,0:T(8,128)(2,1)S(1)} async-done(((bf16[8,2,32,1664]{3,2,1,0:T(8,128)(2,1)}), bf16[8,2,32,1664]{3,2,1,0:T(8,128)(2,1)S(1)}, u32[]{:S(2)}, u32[]{:S(2)}) %all-to-all-start) | async-done | bytes 1703968 | tf_op jit(solution)/shard_map/all_to_all | solution.py:545
  102.0 2.0 %copy-done.5 = bf16[13,2,256,256]{3,2,1,0:T(8,128)(2,1)S(1)} copy-done((bf16[13,2,256,256]{3,2,1,0:T(8,128)(2,1)S(1)}, bf16[13,2,256,256]{3,2,1,0:T(8,128)(2,1)}, u32[]{:S(2)}) %copy-start.5) | copy-done | bytes 3407896
  104.0 9.2 %token_part.1 = (bf16[16,32,512]{2,1,0:T(8,128)(2,1)}, f32[8,2,32,128]{3,2,1,0:T(8,128)}, bf16[32,80,512]{2,1,0:T(8,128)(2,1)}, f32[32,128]{1,0:T(8,128)S(1)}) custom-call(bf16[8,2,32,1664]{3,2,1,0:T(8,128)(2,1)S(1)} %all-to-all-done.value, bf16[13,2,256,256]{3,2,1,0:T(8,128)(2,1)S(1)} %copy-done.5, bf16[1664,512]{1,0:T(8,128)(2,1)} %proj_ref.1, ...), custom_call_target="tpu_custom_call" | custom-call | flops 4499999744 | bytes 12000000 | tf_op jit(solution)/shard_map/token_part/pallas_call | solution.py:356
  113.2 3.4 %all-to-all-start.1 = ((f32[8,2,32,128]{3,2,1,0:T(8,128)}), f32[8,2,32,128]{3,2,1,0:T(8,128)S(1)}, u32[]{:S(2)}, u32[]{:S(2)}) async-start(f32[8,2,32,128]{3,2,1,0:T(8,128)} %get-tuple-element.43), calls=%async_computation.1 | async-start | bytes 524288 | tf_op jit(solution)/shard_map/all_to_all | solution.py:547
  117.3 6.2 %all-to-all-done.1.stats_ref = f32[8,2,32,128]{3,2,1,0:T(8,128)S(1)} async-done(((f32[8,2,32,128]{3,2,1,0:T(8,128)}), f32[8,2,32,128]{3,2,1,0:T(8,128)S(1)}, u32[]{:S(2)}, u32[]{:S(2)}) %all-to-all-start.1) | async-done | bytes 262176 | tf_op jit(solution)/shard_map/all_to_all | solution.py:547
  123.5 2.4 %coef_part.1 = (bf16[16,80,512]{2,1,0:T(8,128)(2,1)S(1)}, bf16[16,80,512]{2,1,0:T(8,128)(2,1)S(1)}, f32[1,1]{1,0:T(1,128)}) custom-call(s32[1]{0:T(128)S(6)} %copy.10.pos_ref, f32[8,2,32,128]{3,2,1,0:T(8,128)S(1)} %all-to-all-done.1.stats_ref, f32[32,128]{1,0:T(8,128)S(1)} %get-tuple-element.44.lens_ref, bf16[32,80,512]{2,1,0:T(8,128)(2,1)} %get-tuple-element.45.grad_ref), custom_call_target="tpu_custom_call" | custom-call | flops 4000000 | bytes 6000000 | tf_op jit(solution)/shard_map/coef_part/pallas_call | solution.py:430
  126.0 3.0 %collective-permute-done.13.got_ref = bf16[16,80,512]{2,1,0:T(8,128)(2,1)S(1)} collective-permute-done((bf16[16,80,512]{2,1,0:T(8,128)(2,1)S(1)}, bf16[16,80,512]{2,1,0:T(8,128)(2,1)S(1)}, u32[]{:S(2)}, u32[]{:S(2)}) %collective-permute-start.13) | collective-permute-done | bytes 1310752 | tf_op jit(solution)/shard_map/ppermute | solution.py:506
  129.7 1.7 collective-permute-start.15
  131.4 7.7 %collective-permute-done.14.a_got = bf16[8,80,256]{2,1,0:T(8,128)(2,1)S(1)} collective-permute-done((bf16[8,80,256]{2,1,0:T(8,128)(2,1)S(1)}, bf16[8,80,256]{2,1,0:T(8,128)(2,1)S(1)}, u32[]{:S(2)}, u32[]{:S(2)}) %collective-permute-start.14) | collective-permute-done | bytes 327712 | tf_op jit(solution)/shard_map/ppermute | solution.py:510
  140.6 1.7 collective-permute-start.16
  142.4 4.9 %collective-permute-done.16.a_got = bf16[8,80,128]{2,1,0:T(8,128)(2,1)S(1)} collective-permute-done((bf16[8,80,128]{2,1,0:T(8,128)(2,1)S(1)}, bf16[8,80,128]{2,1,0:T(8,128)(2,1)S(1)}, u32[]{:S(2)}, u32[]{:S(2)}) %collective-permute-start.16) | collective-permute-done | bytes 163872 | tf_op jit(solution)/shard_map/ppermute | solution.py:516
  147.8 22.8 %all_to_all.20.parts = bf16[16,80,128]{2,1,0:T(8,128)(2,1)S(1)} all-to-all(bf16[16,80,128]{2,1,0:T(8,128)(2,1)S(1)} %third_sum.1), channel_id=1, replica_groups={{0,16,32,48,64,80,96,112,128,144,160,176,192,208,224,240},{8,24,40,56,7..., dimensions={0} | all-to-all | bytes 655360 | tf_op jit(solution)/shard_map/all_to_all | solution.py:521
  170.6 9.4 %all_to_all.21.parts = bf16[8,80,128]{2,1,0:T(8,128)(2,1)S(1)} all-to-all(bf16[8,80,128]{2,1,0:T(8,128)(2,1)S(1)} %owned_sum.1), channel_id=1, replica_groups=mesh['dp'=32,'space'=8] {'space'}, dimensions={0} | all-to-all | bytes 327680 | tf_op jit(solution)/shard_map/all_to_all | solution.py:526
  (42 shorter events, 11.7 us)
Async XLA Ops:
  0.6 9.9 %copy-start.6 = (bf16[1,77,512]{2,1,0:T(8,128)(2,1)S(1)}, bf16[1,77,512]{2,1,0:T(8,128)(2,1)}, u32[]{:S(2)}) copy-start(bf16[1,77,512]{2,1,0:T(8,128)(2,1)} %param.9) | copy-start | bytes 236548
  3.5 31.3 %collective-permute-start = (bf16[4,32,4992]{2,1,0:T(8,128)(2,1)}, bf16[4,32,4992]{2,1,0:T(8,128)(2,1)S(1)}, u32[]{:S(2)}, u32[]{:S(2)}) collective-permute-start(bf16[4,32,4992]{2,1,0:T(8,128)(2,1)} %get-tuple-element.31), channel_id=1, source_target_pairs={{0,6},{1,7},{2,4},{3,5},{4,2},{5,3},{6,0},{7,1},{8,14},{9,15},{10,... | collective-permute-start | bytes 3833864 | tf_op jit(solution)/shard_map/ppermute | solution.py:131
  6.3 30.9 %collective-permute-start.1 = (bf16[2,32,4992]{2,1,0:T(8,128)(2,1)}, bf16[2,32,4992]{2,1,0:T(8,128)(2,1)S(1)}, u32[]{:S(2)}, u32[]{:S(2)}) collective-permute-start(bf16[2,32,4992]{2,1,0:T(8,128)(2,1)} %get-tuple-element.33), channel_id=1, source_target_pairs={{0,1},{1,0},{2,3},{3,2},{4,5},{5,4},{6,7},{7,6},{8,9},{9,8},{10,11... | collective-permute-start | bytes 1916936 | tf_op jit(solution)/shard_map/ppermute | solution.py:131
  7.9 29.3 %collective-permute-start.2 = (bf16[2,32,4992]{2,1,0:T(8,128)(2,1)}, bf16[2,32,4992]{2,1,0:T(8,128)(2,1)S(1)}, u32[]{:S(2)}, u32[]{:S(2)}) collective-permute-start(bf16[2,32,4992]{2,1,0:T(8,128)(2,1)} %get-tuple-element.34), channel_id=1, source_target_pairs={{0,2},{1,3},{2,0},{3,1},{4,6},{5,7},{6,4},{7,5},{8,10},{9,11},{10,... | collective-permute-start | bytes 1916936 | tf_op jit(solution)/shard_map/ppermute | solution.py:131
  8.1 29.1 %collective-permute-start.3 = (bf16[2,32,4992]{2,1,0:T(8,128)(2,1)}, bf16[2,32,4992]{2,1,0:T(8,128)(2,1)S(1)}, u32[]{:S(2)}, u32[]{:S(2)}) collective-permute-start(bf16[2,32,4992]{2,1,0:T(8,128)(2,1)} %get-tuple-element.35), channel_id=1, source_target_pairs={{0,3},{1,2},{2,1},{3,0},{4,7},{5,6},{6,5},{7,4},{8,11},{9,10},{10,... | collective-permute-start | bytes 1916936 | tf_op jit(solution)/shard_map/ppermute | solution.py:131
  10.5 5.7 %collective-permute-start.4 = (bf16[1,80,512]{2,1,0:T(8,128)(2,1)S(1)}, bf16[1,80,512]{2,1,0:T(8,128)(2,1)S(1)}, u32[]{:S(2)}, u32[]{:S(2)}) collective-permute-start(bf16[1,80,512]{2,1,0:T(8,128)(2,1)S(1)} %concatenate.3.refs_0_), channel_id=1, source_target_pairs={{0,129},{1,128},{2,131},{3,130},{4,133},{5,132},{6,135},{7,134},{8... | collective-permute-start | bytes 245768 | tf_op jit(solution)/shard_map/ppermute | solution.py:271
  16.3 21.0 %collective-permute-start.5 = (bf16[2,80,512]{2,1,0:T(8,128)(2,1)S(1)}, bf16[2,80,512]{2,1,0:T(8,128)(2,1)S(1)}, u32[]{:S(2)}, u32[]{:S(2)}) collective-permute-start(bf16[2,80,512]{2,1,0:T(8,128)(2,1)S(1)} %bitcast.15), channel_id=1, source_target_pairs={{0,64},{8,72},{16,80},{24,88},{32,96},{40,104},{48,112},{56,120},{... | collective-permute-start | bytes 491528 | tf_op jit(solution)/shard_map/ppermute | solution.py:261
  34.8 1.2 copy-start.1
  36.0 1.3 copy-start.3
  37.3 10.7 %copy-start = (bf16[1,16,32,3328]{3,2,1,0:T(8,128)(2,1)S(1)}, bf16[1,16,32,3328]{3,2,1,0:T(8,128)(2,1)}, u32[]{:S(2)}) copy-start(bf16[1,16,32,3328]{3,2,1,0:T(8,128)(2,1)} %param.7) | copy-start | bytes 10223620
  38.1 32.7 %collective-permute-start.6 = (bf16[4,32,4992]{2,1,0:T(8,128)(2,1)S(1)}, bf16[4,32,4992]{2,1,0:T(8,128)(2,1)S(1)}, u32[]{:S(2)}, u32[]{:S(2)}) collective-permute-start(bf16[4,32,4992]{2,1,0:T(8,128)(2,1)S(1)} %turn.1), channel_id=1, source_target_pairs={{0,6},{1,7},{2,4},{3,5},{4,2},{5,3},{6,0},{7,1},{8,14},{9,15},{10,... | collective-permute-start | bytes 3833864 | tf_op jit(solution)/shard_map/ppermute | solution.py:131
  41.0 16.4 %collective-permute-start.7 = (bf16[2,32,4992]{2,1,0:T(8,128)(2,1)S(1)}, bf16[2,32,4992]{2,1,0:T(8,128)(2,1)S(1)}, u32[]{:S(2)}, u32[]{:S(2)}) collective-permute-start(bf16[2,32,4992]{2,1,0:T(8,128)(2,1)S(1)} %get-tuple-element.37.started_ref.behind_ref), channel_id=1, source_target_pairs={{0,1},{1,0},{2,3},{3,2},{4,5},{5,4},{6,7},{7,6},{8,9},{9,8},{10,11... | collective-permute-start | bytes 1916936 | tf_op jit(solution)/shard_map/ppermute | solution.py:131
  42.6 17.3 %collective-permute-start.8 = (bf16[2,32,4992]{2,1,0:T(8,128)(2,1)S(1)}, bf16[2,32,4992]{2,1,0:T(8,128)(2,1)S(1)}, u32[]{:S(2)}, u32[]{:S(2)}) collective-permute-start(bf16[2,32,4992]{2,1,0:T(8,128)(2,1)S(1)} %get-tuple-element.38), channel_id=1, source_target_pairs={{0,2},{1,3},{2,0},{3,1},{4,6},{5,7},{6,4},{7,5},{8,10},{9,11},{10,... | collective-permute-start | bytes 1916936 | tf_op jit(solution)/shard_map/ppermute | solution.py:131
  42.6 28.3 %collective-permute-start.9 = (bf16[2,32,4992]{2,1,0:T(8,128)(2,1)S(1)}, bf16[2,32,4992]{2,1,0:T(8,128)(2,1)S(1)}, u32[]{:S(2)}, u32[]{:S(2)}) collective-permute-start(bf16[2,32,4992]{2,1,0:T(8,128)(2,1)S(1)} %get-tuple-element.39), channel_id=1, source_target_pairs={{0,3},{1,2},{2,1},{3,0},{4,7},{5,6},{6,5},{7,4},{8,11},{9,10},{10,... | collective-permute-start | bytes 1916936 | tf_op jit(solution)/shard_map/ppermute | solution.py:131
  44.5 31.8 %collective-permute-start.10 = (bf16[4,80,512]{2,1,0:T(8,128)(2,1)S(1)}, bf16[4,80,512]{2,1,0:T(8,128)(2,1)S(1)}, u32[]{:S(2)}, u32[]{:S(2)}) collective-permute-start(bf16[4,80,512]{2,1,0:T(8,128)(2,1)S(1)} %bitcast.13), channel_id=1, source_target_pairs={{0,32},{8,40},{16,48},{24,56},{32,0},{40,8},{48,16},{56,24},{64,96... | collective-permute-start | bytes 983048 | tf_op jit(solution)/shard_map/ppermute | solution.py:261
  48.0 22.8 %copy-start.2 = (bf16[2,32,4992]{2,1,0:T(8,128)(2,1)S(1)}, bf16[2,32,4992]{2,1,0:T(8,128)(2,1)}, u32[]{:S(2)}) copy-start(bf16[2,32,4992]{2,1,0:T(8,128)(2,1)} %get-tuple-element.30.kept_ref) | copy-start | bytes 1916932
  53.9 1.7 copy-start.4
  76.3 14.2 %collective-permute-start.11 = (bf16[8,80,512]{2,1,0:T(8,128)(2,1)S(1)}, bf16[8,80,512]{2,1,0:T(8,128)(2,1)S(1)}, u32[]{:S(2)}, u32[]{:S(2)}) collective-permute-start(bf16[8,80,512]{2,1,0:T(8,128)(2,1)S(1)} %bitcast.11), channel_id=1, source_target_pairs={{0,16},{8,24},{16,0},{24,8},{32,48},{40,56},{48,32},{56,40},{64,80... | collective-permute-start | bytes 1966088 | tf_op jit(solution)/shard_map/ppermute | solution.py:261
  76.5 25.5 %all-to-all-start = ((bf16[8,2,32,1664]{3,2,1,0:T(8,128)(2,1)}), bf16[8,2,32,1664]{3,2,1,0:T(8,128)(2,1)S(1)}, u32[]{:S(2)}, u32[]{:S(2)}) async-start(bf16[8,2,32,1664]{3,2,1,0:T(8,128)(2,1)} %spatial_attention.1.refs_2_), calls=%async_computation | async-start | bytes 3407872 | tf_op jit(solution)/shard_map/all_to_all | solution.py:545
  91.7 10.3 %collective-permute-start.12 = (bf16[16,80,512]{2,1,0:T(8,128)(2,1)}, bf16[16,80,512]{2,1,0:T(8,128)(2,1)}, u32[]{:S(2)}, u32[]{:S(2)}) collective-permute-start(bf16[16,80,512]{2,1,0:T(8,128)(2,1)} %bitcast.6.mine_ref), channel_id=1, source_target_pairs={{0,8},{8,0},{16,24},{24,16},{32,40},{40,32},{48,56},{56,48},{64,72... | collective-permute-start | bytes 3932168 | tf_op jit(solution)/shard_map/ppermute | solution.py:261
  102.0 2.0 %copy-start.5 = (bf16[13,2,256,256]{3,2,1,0:T(8,128)(2,1)S(1)}, bf16[13,2,256,256]{3,2,1,0:T(8,128)(2,1)}, u32[]{:S(2)}) copy-start(bf16[13,2,256,256]{3,2,1,0:T(8,128)(2,1)} %copy-done.4) | copy-start | bytes 10223620
  113.2 10.3 %all-to-all-start.1 = ((f32[8,2,32,128]{3,2,1,0:T(8,128)}), f32[8,2,32,128]{3,2,1,0:T(8,128)S(1)}, u32[]{:S(2)}, u32[]{:S(2)}) async-start(f32[8,2,32,128]{3,2,1,0:T(8,128)} %get-tuple-element.43), calls=%async_computation.1 | async-start | bytes 524288 | tf_op jit(solution)/shard_map/all_to_all | solution.py:547
  125.9 3.1 %collective-permute-start.13 = (bf16[16,80,512]{2,1,0:T(8,128)(2,1)S(1)}, bf16[16,80,512]{2,1,0:T(8,128)(2,1)S(1)}, u32[]{:S(2)}, u32[]{:S(2)}) collective-permute-start(bf16[16,80,512]{2,1,0:T(8,128)(2,1)S(1)} %get-tuple-element.47), channel_id=1, source_target_pairs={{0,8},{8,0},{16,24},{24,16},{32,40},{40,32},{48,56},{56,48},{64,72... | collective-permute-start | bytes 3932168 | tf_op jit(solution)/shard_map/ppermute | solution.py:506
  129.3 9.8 %collective-permute-start.14 = (bf16[8,80,256]{2,1,0:T(8,128)(2,1)S(1)}, bf16[8,80,256]{2,1,0:T(8,128)(2,1)S(1)}, u32[]{:S(2)}, u32[]{:S(2)}) collective-permute-start(bf16[8,80,256]{2,1,0:T(8,128)(2,1)S(1)} %get-tuple-element.49), channel_id=1, source_target_pairs={{0,2},{1,3},{2,0},{3,1},{4,6},{5,7},{6,4},{7,5},{8,10},{9,11},{10,... | collective-permute-start | bytes 983048 | tf_op jit(solution)/shard_map/ppermute | solution.py:510
  129.7 10.8 %collective-permute-start.15 = (bf16[8,80,256]{2,1,0:T(8,128)(2,1)S(1)}, bf16[8,80,256]{2,1,0:T(8,128)(2,1)S(1)}, u32[]{:S(2)}, u32[]{:S(2)}) collective-permute-start(bf16[8,80,256]{2,1,0:T(8,128)(2,1)S(1)} %get-tuple-element.51), channel_id=1, source_target_pairs={{0,6},{1,7},{2,4},{3,5},{4,2},{5,3},{6,0},{7,1},{8,14},{9,15},{10,... | collective-permute-start | bytes 983048 | tf_op jit(solution)/shard_map/ppermute | solution.py:511
  140.6 6.6 %collective-permute-start.16 = (bf16[8,80,128]{2,1,0:T(8,128)(2,1)S(1)}, bf16[8,80,128]{2,1,0:T(8,128)(2,1)S(1)}, u32[]{:S(2)}, u32[]{:S(2)}) collective-permute-start(bf16[8,80,128]{2,1,0:T(8,128)(2,1)S(1)} %get-tuple-element.53), channel_id=1, source_target_pairs={{0,6},{1,7},{2,4},{3,5},{4,2},{5,3},{6,0},{7,1},{8,14},{9,15},{10,... | collective-permute-start | bytes 491528 | tf_op jit(solution)/shard_map/ppermute | solution.py:516
  142.4 5.3 %collective-permute-start.17 = (bf16[8,80,128]{2,1,0:T(8,128)(2,1)S(1)}, bf16[8,80,128]{2,1,0:T(8,128)(2,1)S(1)}, u32[]{:S(2)}, u32[]{:S(2)}) collective-permute-start(bf16[8,80,128]{2,1,0:T(8,128)(2,1)S(1)} %get-tuple-element.55), channel_id=1, source_target_pairs={{0,2},{1,3},{2,0},{3,1},{4,6},{5,7},{6,4},{7,5},{8,10},{9,11},{10,... | collective-permute-start | bytes 491528 | tf_op jit(solution)/shard_map/ppermute | solution.py:517

commit v12 on v11

--- a/solution.py
+++ b/solution.py
@@ -538,10 +538,10 @@
     pieces, started = bring_frames(clip_qkv[0], far)
     time, done = time_weights(temporal_qk[0], started)
     caps = doubled(caps, far)
-    attended = spatial_attention(pieces, done)
-    caps = doubled(caps, flip(caps, 4), attended)
+    caps = doubled(caps, flip(caps, 4), pieces[2])
     caps = doubled(caps, flip(caps, 2))
     other = flip(caps, 1)
+    attended = spatial_attention(pieces, done)
     spatial = lax.all_to_all(attended, "space", split_axis=0, concat_axis=0, tiled=True)
     video, stats, grad, lens = token_part(spatial, time, proj_weight, caps, other)
     stats = lax.all_to_all(stats, "space", split_axis=0, concat_axis=0, tiled=True)

time: 181 us -> 189 us (1.044)
  waiting for transfers between devices: 72.1 us -> 76.7 us
  local copies, waits for them, and re-layouts: 4.87 us -> 7.26 us
    all_to_all x1, waiting for transfers between devices: 10.3 us -> 20 us  [on_device(): lax.all_to_all(attended, 'space', split_axis=0, concat_axis=0, tiled=True)]
    ppermute x8, waiting for transfers between devices: 25.1 us -> 21.5 us  [swap(): return lax.ppermute(value, 'space', [(s, s ^ bits) for s in range(8)])]
    unnamed x14 -> x18, local copies, waits for them, and re-layouts: 4.86 us -> 7.25 us
  transfers between devices with their start and end apart: 20 -> 20, of which waited for: 13 -> 11; matrix products, arithmetic and copies ran while one was open for 0% -> 0% of each run, Pallas kernels for 9% -> 9%
where the time goes in v12:
time: 189 us
  waiting for transfers between devices  76.7 us (41%)
  starting transfers between devices  38.3 us (20%)
  Pallas kernels  32.6 us (17%)
  blocking collectives  31.8 us (17%)
  local copies, waits for them, and re-layouts  7.26 us (4%)
  between operations  2.17 us (1%)
    all_to_all x1, blocking collectives, reduce_gradient(): lax.all_to_all(parts, 'dp', split_axis=0, concat_axis=0, tiled=True, axis...  22.4 us
    ppermute x8, waiting for transfers between devices, swap(): return lax.ppermute(value, 'space', [(s, s ^ bits) for s in range(8)])  21.5 us
    all_to_all x1, waiting for transfers between devices, on_device(): lax.all_to_all(attended, 'space', split_axis=0, concat_axis=0, tiled=True)  20 us
    ppermute x8, starting transfers between devices, swap(): return lax.ppermute(value, 'space', [(s, s ^ bits) for s in range(8)])  12.7 us
    ppermute x4, starting transfers between devices, flip(): return lax.ppermute(value, 'dp', [(i, i ^ bit) for i in range(32)])  10 us
    all_to_all x1, blocking collectives, reduce_gradient(): lax.all_to_all(parts, 'space', split_axis=0, concat_axis=0, tiled=True)  9.43 us
    ppermute x4, waiting for transfers between devices, flip(): return lax.ppermute(value, 'dp', [(i, i ^ bit) for i in range(32)])  8.9 us
    pallas_call x1, Pallas kernels, token_part(): pl.pallas_call(token_kernel, in_specs=[VMEM, VMEM, FAR_OFF, FAR_OFF, VMEM...  8.06 us
  transfers between devices with their start and end apart: 20, of which 11 were waited for; matrix products, arithmetic and copies ran while one was open for 0% of the time, Pallas kernels for 9%

profile of v12, /device:TPU:32, one launch (start us, length us, event | category | flops | bytes accessed | tf_op | source)
XLA Modules:
  0.0 188.8 jit_solution(17351828741674797758)
XLA Ops:
  0.6 2.8 %depart.1 = (bf16[2,32,4992]{2,1,0:T(8,128)(2,1)}, bf16[2,32,4992]{2,1,0:T(8,128)(2,1)}, bf16[2,32,4992]{2,1,0:T(8,128)(2,1)}, bf16[4,32,4992]{2,1,0:T(8,128)(2,1)}) custom-call(bf16[16,32,4992]{2,1,0:T(8,128)(2,1)} %bitcast.17), custom_call_target="tpu_custom_call" | custom-call | bytes 6000000 | tf_op jit(solution)/shard_map/depart/pallas_call | solution.py:81
  3.5 2.8 %collective-permute-start = (bf16[4,32,4992]{2,1,0:T(8,128)(2,1)}, bf16[4,32,4992]{2,1,0:T(8,128)(2,1)S(1)}, u32[]{:S(2)}, u32[]{:S(2)}) collective-permute-start(bf16[4,32,4992]{2,1,0:T(8,128)(2,1)} %get-tuple-element.31), channel_id=1, source_target_pairs={{0,6},{1,7},{2,4},{3,5},{4,2},{5,3},{6,0},{7,1},{8,14},{9,15},{10,... | collective-permute-start | bytes 3833864 | tf_op jit(solution)/shard_map/ppermute | solution.py:131
  6.3 1.6 collective-permute-start.1
  8.1 1.7 collective-permute-start.3
  10.5 3.1 %collective-permute-start.4 = (bf16[1,80,512]{2,1,0:T(8,128)(2,1)S(1)}, bf16[1,80,512]{2,1,0:T(8,128)(2,1)S(1)}, u32[]{:S(2)}, u32[]{:S(2)}) collective-permute-start(bf16[1,80,512]{2,1,0:T(8,128)(2,1)S(1)} %concatenate.3.refs_0_), channel_id=1, source_target_pairs={{0,129},{1,128},{2,131},{3,130},{4,133},{5,132},{6,135},{7,134},{8... | collective-permute-start | bytes 245768 | tf_op jit(solution)/shard_map/ppermute | solution.py:271
  13.6 2.6 %collective-permute-done.4.refs_1_ = bf16[1,80,512]{2,1,0:T(8,128)(2,1)S(1)} collective-permute-done((bf16[1,80,512]{2,1,0:T(8,128)(2,1)S(1)}, bf16[1,80,512]{2,1,0:T(8,128)(2,1)S(1)}, u32[]{:S(2)}, u32[]{:S(2)}) %collective-permute-start.4) | collective-permute-done | bytes 81952 | tf_op jit(solution)/shard_map/ppermute | solution.py:271
  16.3 6.4 %collective-permute-start.5 = (bf16[2,80,512]{2,1,0:T(8,128)(2,1)S(1)}, bf16[2,80,512]{2,1,0:T(8,128)(2,1)S(1)}, u32[]{:S(2)}, u32[]{:S(2)}) collective-permute-start(bf16[2,80,512]{2,1,0:T(8,128)(2,1)S(1)} %bitcast.15), channel_id=1, source_target_pairs={{0,64},{8,72},{16,80},{24,88},{32,96},{40,104},{48,112},{56,120},{... | collective-permute-start | bytes 491528 | tf_op jit(solution)/shard_map/ppermute | solution.py:261
  22.6 2.3 %own.1 = (bf16[1,32,4992]{2,1,0:T(8,128)(2,1)}, bf16[3,32,4992]{2,1,0:T(8,128)(2,1)}, bf16[2,32,4992]{2,1,0:T(8,128)(2,1)}) custom-call(bf16[16,32,4992]{2,1,0:T(8,128)(2,1)} %bitcast.18), custom_call_target="tpu_custom_call" | custom-call | bytes 6000000 | tf_op jit(solution)/shard_map/own/pallas_call | solution.py:81
  25.0 9.9 %collective-permute-done.across_ref = bf16[4,32,4992]{2,1,0:T(8,128)(2,1)S(1)} collective-permute-done((bf16[4,32,4992]{2,1,0:T(8,128)(2,1)}, bf16[4,32,4992]{2,1,0:T(8,128)(2,1)S(1)}, u32[]{:S(2)}, u32[]{:S(2)}) %collective-permute-start) | collective-permute-done | bytes 1277984 | tf_op jit(solution)/shard_map/ppermute | solution.py:131
  38.1 2.8 %collective-permute-start.6 = (bf16[4,32,4992]{2,1,0:T(8,128)(2,1)S(1)}, bf16[4,32,4992]{2,1,0:T(8,128)(2,1)S(1)}, u32[]{:S(2)}, u32[]{:S(2)}) collective-permute-start(bf16[4,32,4992]{2,1,0:T(8,128)(2,1)S(1)} %turn.1), channel_id=1, source_target_pairs={{0,6},{1,7},{2,4},{3,5},{4,2},{5,3},{6,0},{7,1},{8,14},{9,15},{10,... | collective-permute-start | bytes 3833864 | tf_op jit(solution)/shard_map/ppermute | solution.py:131
  41.0 3.4 %collective-permute-start.10 = (bf16[4,80,512]{2,1,0:T(8,128)(2,1)S(1)}, bf16[4,80,512]{2,1,0:T(8,128)(2,1)S(1)}, u32[]{:S(2)}, u32[]{:S(2)}) collective-permute-start(bf16[4,80,512]{2,1,0:T(8,128)(2,1)S(1)} %bitcast.13), channel_id=1, source_target_pairs={{0,32},{8,40},{16,48},{24,56},{32,0},{40,8},{48,16},{56,24},{64,96... | collective-permute-start | bytes 983048 | tf_op jit(solution)/shard_map/ppermute | solution.py:261
  45.9 1.9 %collective-permute-start.9 = (bf16[2,32,4992]{2,1,0:T(8,128)(2,1)S(1)}, bf16[2,32,4992]{2,1,0:T(8,128)(2,1)S(1)}, u32[]{:S(2)}, u32[]{:S(2)}) collective-permute-start(bf16[2,32,4992]{2,1,0:T(8,128)(2,1)S(1)} %get-tuple-element.39), channel_id=1, source_target_pairs={{0,3},{1,2},{2,1},{3,0},{4,7},{5,6},{6,5},{7,4},{8,11},{9,10},{10,... | collective-permute-start | bytes 1916936 | tf_op jit(solution)/shard_map/ppermute | solution.py:131
  47.8 8.9 %collective-permute-done.10.refs_1_ = bf16[4,80,512]{2,1,0:T(8,128)(2,1)S(1)} collective-permute-done((bf16[4,80,512]{2,1,0:T(8,128)(2,1)S(1)}, bf16[4,80,512]{2,1,0:T(8,128)(2,1)S(1)}, u32[]{:S(2)}, u32[]{:S(2)}) %collective-permute-start.10) | collective-permute-done | bytes 327712 | tf_op jit(solution)/shard_map/ppermute | solution.py:261
  56.7 11.6 %collective-permute-done.6.turned_ref.refs_2_ = bf16[4,32,4992]{2,1,0:T(8,128)(2,1)S(1)} collective-permute-done((bf16[4,32,4992]{2,1,0:T(8,128)(2,1)S(1)}, bf16[4,32,4992]{2,1,0:T(8,128)(2,1)S(1)}, u32[]{:S(2)}, u32[]{:S(2)}) %collective-permute-start.6) | collective-permute-done | bytes 1277984 | tf_op jit(solution)/shard_map/ppermute | solution.py:131
  68.7 5.8 %time_weights.1 = (bf16[13,2,256,256]{3,2,1,0:T(8,128)(2,1)S(1)}, f32[8,128]{1,0:T(8,128)S(1)}) custom-call(bf16[16,32,3328]{2,1,0:T(8,128)(2,1)S(1)} %bitcast.10, bf16[2,32,4992]{2,1,0:T(8,128)(2,1)S(1)} %get-tuple-element.37.started_ref.behind_ref), custom_call_target="tpu_custom_call" | custom-call | flops 436207616 | bytes 7000000 | tf_op jit(solution)/shard_map/time_weights/pallas_call | solution.py:236
  74.5 1.7 copy-done.4
  76.3 5.4 %spatial_attention.1 = bf16[8,2,32,1664]{3,2,1,0:T(8,128)(2,1)} custom-call(bf16[2,32,4992]{2,1,0:T(8,128)(2,1)S(1)} %copy-done.2, bf16[4,32,4992]{2,1,0:T(8,128)(2,1)S(1)} %collective-permute-done.across_ref, bf16[4,32,4992]{2,1,0:T(8,128)(2,1)S(1)} %collective-permute-done.6.turned_ref.refs_2_, ...), custom_call_target="tpu_custom_call" | custom-call | flops 872415232 | bytes 6815744 | tf_op jit(solution)/shard_map/spatial_attention/pallas_call | solution.py:186
  81.7 5.1 %all-to-all-start = ((bf16[8,2,32,1664]{3,2,1,0:T(8,128)(2,1)}), bf16[8,2,32,1664]{3,2,1,0:T(8,128)(2,1)S(1)}, u32[]{:S(2)}, u32[]{:S(2)}) async-start(bf16[8,2,32,1664]{3,2,1,0:T(8,128)(2,1)} %spatial_attention.1), calls=%async_computation | async-start | bytes 3407872 | tf_op jit(solution)/shard_map/all_to_all | solution.py:545
  86.8 2.2 %join.7 = bf16[2,8,80,512]{3,2,1,0:T(8,128)(2,1)} custom-call(bf16[8,80,512]{2,1,0:T(8,128)(2,1)S(1)} %bitcast.12, bf16[8,80,512]{2,1,0:T(8,128)(2,1)} %collective-permute-done.11.refs_1_), custom_call_target="tpu_custom_call" | custom-call | bytes 1000000 | tf_op jit(solution)/shard_map/join/pallas_call | solution.py:275
  89.1 20.0 %all-to-all-done.value = bf16[8,2,32,1664]{3,2,1,0:T(8,128)(2,1)S(1)} async-done(((bf16[8,2,32,1664]{3,2,1,0:T(8,128)(2,1)}), bf16[8,2,32,1664]{3,2,1,0:T(8,128)(2,1)S(1)}, u32[]{:S(2)}, u32[]{:S(2)}) %all-to-all-start) | async-done | bytes 1703968 | tf_op jit(solution)/shard_map/all_to_all | solution.py:545
  110.2 2.0 %copy-done.5 = bf16[13,2,256,256]{3,2,1,0:T(8,128)(2,1)S(1)} copy-done((bf16[13,2,256,256]{3,2,1,0:T(8,128)(2,1)S(1)}, bf16[13,2,256,256]{3,2,1,0:T(8,128)(2,1)}, u32[]{:S(2)}) %copy-start.5) | copy-done | bytes 3407896
  113.5 8.1 %token_part.1 = (bf16[16,32,512]{2,1,0:T(8,128)(2,1)}, f32[8,2,32,128]{3,2,1,0:T(8,128)}, bf16[32,80,512]{2,1,0:T(8,128)(2,1)}, f32[32,128]{1,0:T(8,128)S(1)}) custom-call(bf16[8,2,32,1664]{3,2,1,0:T(8,128)(2,1)S(1)} %all-to-all-done.value, bf16[13,2,256,256]{3,2,1,0:T(8,128)(2,1)S(1)} %copy-done.5, bf16[1664,512]{1,0:T(8,128)(2,1)} %proj_ref.1, ...), custom_call_target="tpu_custom_call" | custom-call | flops 4499999744 | bytes 12000000 | tf_op jit(solution)/shard_map/token_part/pallas_call | solution.py:356
  121.5 3.4 %all-to-all-start.1 = ((f32[8,2,32,128]{3,2,1,0:T(8,128)}), f32[8,2,32,128]{3,2,1,0:T(8,128)S(1)}, u32[]{:S(2)}, u32[]{:S(2)}) async-start(f32[8,2,32,128]{3,2,1,0:T(8,128)} %get-tuple-element.43), calls=%async_computation.1 | async-start | bytes 524288 | tf_op jit(solution)/shard_map/all_to_all | solution.py:547
  125.6 6.2 %all-to-all-done.1.stats_ref = f32[8,2,32,128]{3,2,1,0:T(8,128)S(1)} async-done(((f32[8,2,32,128]{3,2,1,0:T(8,128)}), f32[8,2,32,128]{3,2,1,0:T(8,128)S(1)}, u32[]{:S(2)}, u32[]{:S(2)}) %all-to-all-start.1) | async-done | bytes 262176 | tf_op jit(solution)/shard_map/all_to_all | solution.py:547
  131.8 2.4 %coef_part.1 = (bf16[16,80,512]{2,1,0:T(8,128)(2,1)S(1)}, bf16[16,80,512]{2,1,0:T(8,128)(2,1)S(1)}, f32[1,1]{1,0:T(1,128)}) custom-call(s32[1]{0:T(128)S(6)} %copy.10.pos_ref, f32[8,2,32,128]{3,2,1,0:T(8,128)S(1)} %all-to-all-done.1.stats_ref, f32[32,128]{1,0:T(8,128)S(1)} %get-tuple-element.44.lens_ref, bf16[32,80,512]{2,1,0:T(8,128)(2,1)} %get-tuple-element.45.grad_ref), custom_call_target="tpu_custom_call" | custom-call | flops 4000000 | bytes 6000000 | tf_op jit(solution)/shard_map/coef_part/pallas_call | solution.py:430
  134.3 3.0 %collective-permute-done.13.got_ref = bf16[16,80,512]{2,1,0:T(8,128)(2,1)S(1)} collective-permute-done((bf16[16,80,512]{2,1,0:T(8,128)(2,1)S(1)}, bf16[16,80,512]{2,1,0:T(8,128)(2,1)S(1)}, u32[]{:S(2)}, u32[]{:S(2)}) %collective-permute-start.13) | collective-permute-done | bytes 1310752 | tf_op jit(solution)/shard_map/ppermute | solution.py:506
  138.1 1.7 collective-permute-start.15
  139.8 7.7 %collective-permute-done.14.a_got = bf16[8,80,256]{2,1,0:T(8,128)(2,1)S(1)} collective-permute-done((bf16[8,80,256]{2,1,0:T(8,128)(2,1)S(1)}, bf16[8,80,256]{2,1,0:T(8,128)(2,1)S(1)}, u32[]{:S(2)}, u32[]{:S(2)}) %collective-permute-start.14) | collective-permute-done | bytes 327712 | tf_op jit(solution)/shard_map/ppermute | solution.py:510
  149.0 1.7 collective-permute-start.16
  150.7 4.9 %collective-permute-done.16.a_got = bf16[8,80,128]{2,1,0:T(8,128)(2,1)S(1)} collective-permute-done((bf16[8,80,128]{2,1,0:T(8,128)(2,1)S(1)}, bf16[8,80,128]{2,1,0:T(8,128)(2,1)S(1)}, u32[]{:S(2)}, u32[]{:S(2)}) %collective-permute-start.16) | collective-permute-done | bytes 163872 | tf_op jit(solution)/shard_map/ppermute | solution.py:516
  156.1 22.4 %all_to_all.20.parts = bf16[16,80,128]{2,1,0:T(8,128)(2,1)S(1)} all-to-all(bf16[16,80,128]{2,1,0:T(8,128)(2,1)S(1)} %third_sum.1), channel_id=1, replica_groups={{0,16,32,48,64,80,96,112,128,144,160,176,192,208,224,240},{8,24,40,56,7..., dimensions={0} | all-to-all | bytes 655360 | tf_op jit(solution)/shard_map/all_to_all | solution.py:521
  178.6 9.4 %all_to_all.21.parts = bf16[8,80,128]{2,1,0:T(8,128)(2,1)S(1)} all-to-all(bf16[8,80,128]{2,1,0:T(8,128)(2,1)S(1)} %owned_sum.1), channel_id=1, replica_groups=mesh['dp'=32,'space'=8] {'space'}, dimensions={0} | all-to-all | bytes 327680 | tf_op jit(solution)/shard_map/all_to_all | solution.py:526
  (46 shorter events, 11.4 us)
Async XLA Ops:
  0.6 9.8 %copy-start.8 = (bf16[1,77,512]{2,1,0:T(8,128)(2,1)S(1)}, bf16[1,77,512]{2,1,0:T(8,128)(2,1)}, u32[]{:S(2)}) copy-start(bf16[1,77,512]{2,1,0:T(8,128)(2,1)} %param.9) | copy-start | bytes 236548
  3.5 31.3 %collective-permute-start = (bf16[4,32,4992]{2,1,0:T(8,128)(2,1)}, bf16[4,32,4992]{2,1,0:T(8,128)(2,1)S(1)}, u32[]{:S(2)}, u32[]{:S(2)}) collective-permute-start(bf16[4,32,4992]{2,1,0:T(8,128)(2,1)} %get-tuple-element.31), channel_id=1, source_target_pairs={{0,6},{1,7},{2,4},{3,5},{4,2},{5,3},{6,0},{7,1},{8,14},{9,15},{10,... | collective-permute-start | bytes 3833864 | tf_op jit(solution)/shard_map/ppermute | solution.py:131
  6.3 30.9 %collective-permute-start.1 = (bf16[2,32,4992]{2,1,0:T(8,128)(2,1)}, bf16[2,32,4992]{2,1,0:T(8,128)(2,1)S(1)}, u32[]{:S(2)}, u32[]{:S(2)}) collective-permute-start(bf16[2,32,4992]{2,1,0:T(8,128)(2,1)} %get-tuple-element.33), channel_id=1, source_target_pairs={{0,1},{1,0},{2,3},{3,2},{4,5},{5,4},{6,7},{7,6},{8,9},{9,8},{10,11... | collective-permute-start | bytes 1916936 | tf_op jit(solution)/shard_map/ppermute | solution.py:131
  7.9 29.3 %collective-permute-start.2 = (bf16[2,32,4992]{2,1,0:T(8,128)(2,1)}, bf16[2,32,4992]{2,1,0:T(8,128)(2,1)S(1)}, u32[]{:S(2)}, u32[]{:S(2)}) collective-permute-start(bf16[2,32,4992]{2,1,0:T(8,128)(2,1)} %get-tuple-element.34), channel_id=1, source_target_pairs={{0,2},{1,3},{2,0},{3,1},{4,6},{5,7},{6,4},{7,5},{8,10},{9,11},{10,... | collective-permute-start | bytes 1916936 | tf_op jit(solution)/shard_map/ppermute | solution.py:131
  8.1 29.1 %collective-permute-start.3 = (bf16[2,32,4992]{2,1,0:T(8,128)(2,1)}, bf16[2,32,4992]{2,1,0:T(8,128)(2,1)S(1)}, u32[]{:S(2)}, u32[]{:S(2)}) collective-permute-start(bf16[2,32,4992]{2,1,0:T(8,128)(2,1)} %get-tuple-element.35), channel_id=1, source_target_pairs={{0,3},{1,2},{2,1},{3,0},{4,7},{5,6},{6,5},{7,4},{8,11},{9,10},{10,... | collective-permute-start | bytes 1916936 | tf_op jit(solution)/shard_map/ppermute | solution.py:131
  10.5 5.7 %collective-permute-start.4 = (bf16[1,80,512]{2,1,0:T(8,128)(2,1)S(1)}, bf16[1,80,512]{2,1,0:T(8,128)(2,1)S(1)}, u32[]{:S(2)}, u32[]{:S(2)}) collective-permute-start(bf16[1,80,512]{2,1,0:T(8,128)(2,1)S(1)} %concatenate.3.refs_0_), channel_id=1, source_target_pairs={{0,129},{1,128},{2,131},{3,130},{4,133},{5,132},{6,135},{7,134},{8... | collective-permute-start | bytes 245768 | tf_op jit(solution)/shard_map/ppermute | solution.py:271
  16.3 21.0 %collective-permute-start.5 = (bf16[2,80,512]{2,1,0:T(8,128)(2,1)S(1)}, bf16[2,80,512]{2,1,0:T(8,128)(2,1)S(1)}, u32[]{:S(2)}, u32[]{:S(2)}) collective-permute-start(bf16[2,80,512]{2,1,0:T(8,128)(2,1)S(1)} %bitcast.15), channel_id=1, source_target_pairs={{0,64},{8,72},{16,80},{24,88},{32,96},{40,104},{48,112},{56,120},{... | collective-permute-start | bytes 491528 | tf_op jit(solution)/shard_map/ppermute | solution.py:261
  34.8 1.2 copy-start.1
  36.0 1.3 copy-start.3
  37.3 31.4 %copy-start = (bf16[1,16,32,3328]{3,2,1,0:T(8,128)(2,1)S(1)}, bf16[1,16,32,3328]{3,2,1,0:T(8,128)(2,1)}, u32[]{:S(2)}) copy-start(bf16[1,16,32,3328]{3,2,1,0:T(8,128)(2,1)} %param.7) | copy-start | bytes 10223620
  38.1 30.2 %collective-permute-start.6 = (bf16[4,32,4992]{2,1,0:T(8,128)(2,1)S(1)}, bf16[4,32,4992]{2,1,0:T(8,128)(2,1)S(1)}, u32[]{:S(2)}, u32[]{:S(2)}) collective-permute-start(bf16[4,32,4992]{2,1,0:T(8,128)(2,1)S(1)} %turn.1), channel_id=1, source_target_pairs={{0,6},{1,7},{2,4},{3,5},{4,2},{5,3},{6,0},{7,1},{8,14},{9,15},{10,... | collective-permute-start | bytes 3833864 | tf_op jit(solution)/shard_map/ppermute | solution.py:131
  41.0 15.7 %collective-permute-start.10 = (bf16[4,80,512]{2,1,0:T(8,128)(2,1)S(1)}, bf16[4,80,512]{2,1,0:T(8,128)(2,1)S(1)}, u32[]{:S(2)}, u32[]{:S(2)}) collective-permute-start(bf16[4,80,512]{2,1,0:T(8,128)(2,1)S(1)} %bitcast.13), channel_id=1, source_target_pairs={{0,32},{8,40},{16,48},{24,56},{32,0},{40,8},{48,16},{56,24},{64,96... | collective-permute-start | bytes 983048 | tf_op jit(solution)/shard_map/ppermute | solution.py:261
  44.4 31.9 %collective-permute-start.7 = (bf16[2,32,4992]{2,1,0:T(8,128)(2,1)S(1)}, bf16[2,32,4992]{2,1,0:T(8,128)(2,1)S(1)}, u32[]{:S(2)}, u32[]{:S(2)}) collective-permute-start(bf16[2,32,4992]{2,1,0:T(8,128)(2,1)S(1)} %get-tuple-element.37.started_ref.behind_ref), channel_id=1, source_target_pairs={{0,1},{1,0},{2,3},{3,2},{4,5},{5,4},{6,7},{7,6},{8,9},{9,8},{10,11... | collective-permute-start | bytes 1916936 | tf_op jit(solution)/shard_map/ppermute | solution.py:131
  45.9 30.3 %collective-permute-start.8 = (bf16[2,32,4992]{2,1,0:T(8,128)(2,1)S(1)}, bf16[2,32,4992]{2,1,0:T(8,128)(2,1)S(1)}, u32[]{:S(2)}, u32[]{:S(2)}) collective-permute-start(bf16[2,32,4992]{2,1,0:T(8,128)(2,1)S(1)} %get-tuple-element.38), channel_id=1, source_target_pairs={{0,2},{1,3},{2,0},{3,1},{4,6},{5,7},{6,4},{7,5},{8,10},{9,11},{10,... | collective-permute-start | bytes 1916936 | tf_op jit(solution)/shard_map/ppermute | solution.py:131
  45.9 30.3 %collective-permute-start.9 = (bf16[2,32,4992]{2,1,0:T(8,128)(2,1)S(1)}, bf16[2,32,4992]{2,1,0:T(8,128)(2,1)S(1)}, u32[]{:S(2)}, u32[]{:S(2)}) collective-permute-start(bf16[2,32,4992]{2,1,0:T(8,128)(2,1)S(1)} %get-tuple-element.39), channel_id=1, source_target_pairs={{0,3},{1,2},{2,1},{3,0},{4,7},{5,6},{6,5},{7,4},{8,11},{9,10},{10,... | collective-permute-start | bytes 1916936 | tf_op jit(solution)/shard_map/ppermute | solution.py:131
  68.4 18.4 %collective-permute-start.11 = (bf16[8,80,512]{2,1,0:T(8,128)(2,1)S(1)}, bf16[8,80,512]{2,1,0:T(8,128)(2,1)}, u32[]{:S(2)}, u32[]{:S(2)}) collective-permute-start(bf16[8,80,512]{2,1,0:T(8,128)(2,1)S(1)} %bitcast.11), channel_id=1, source_target_pairs={{0,16},{8,24},{16,0},{24,8},{32,48},{40,56},{48,32},{56,40},{64,80... | collective-permute-start | bytes 1966088 | tf_op jit(solution)/shard_map/ppermute | solution.py:261
  68.7 7.6 %copy-start.2 = (bf16[2,32,4992]{2,1,0:T(8,128)(2,1)S(1)}, bf16[2,32,4992]{2,1,0:T(8,128)(2,1)}, u32[]{:S(2)}) copy-start(bf16[2,32,4992]{2,1,0:T(8,128)(2,1)} %get-tuple-element.30.kept_ref) | copy-start | bytes 1916932
  74.5 1.7 copy-start.4
  81.7 27.4 %all-to-all-start = ((bf16[8,2,32,1664]{3,2,1,0:T(8,128)(2,1)}), bf16[8,2,32,1664]{3,2,1,0:T(8,128)(2,1)S(1)}, u32[]{:S(2)}, u32[]{:S(2)}) async-start(bf16[8,2,32,1664]{3,2,1,0:T(8,128)(2,1)} %spatial_attention.1), calls=%async_computation | async-start | bytes 3407872 | tf_op jit(solution)/shard_map/all_to_all | solution.py:545
  89.1 20.1 %collective-permute-start.12 = (bf16[16,80,512]{2,1,0:T(8,128)(2,1)}, bf16[16,80,512]{2,1,0:T(8,128)(2,1)S(1)}, u32[]{:S(2)}, u32[]{:S(2)}) collective-permute-start(bf16[16,80,512]{2,1,0:T(8,128)(2,1)} %bitcast.6.mine_ref), channel_id=1, source_target_pairs={{0,8},{8,0},{16,24},{24,16},{32,40},{40,32},{48,56},{56,48},{64,72... | collective-permute-start | bytes 3932168 | tf_op jit(solution)/shard_map/ppermute | solution.py:261
  109.1 1.1 copy-start.6
  110.2 2.0 %copy-start.5 = (bf16[13,2,256,256]{3,2,1,0:T(8,128)(2,1)S(1)}, bf16[13,2,256,256]{3,2,1,0:T(8,128)(2,1)}, u32[]{:S(2)}) copy-start(bf16[13,2,256,256]{3,2,1,0:T(8,128)(2,1)} %copy-done.4) | copy-start | bytes 10223620
  112.2 1.3 copy-start.7
  121.5 10.3 %all-to-all-start.1 = ((f32[8,2,32,128]{3,2,1,0:T(8,128)}), f32[8,2,32,128]{3,2,1,0:T(8,128)S(1)}, u32[]{:S(2)}, u32[]{:S(2)}) async-start(f32[8,2,32,128]{3,2,1,0:T(8,128)} %get-tuple-element.43), calls=%async_computation.1 | async-start | bytes 524288 | tf_op jit(solution)/shard_map/all_to_all | solution.py:547
  134.2 3.1 %collective-permute-start.13 = (bf16[16,80,512]{2,1,0:T(8,128)(2,1)S(1)}, bf16[16,80,512]{2,1,0:T(8,128)(2,1)S(1)}, u32[]{:S(2)}, u32[]{:S(2)}) collective-permute-start(bf16[16,80,512]{2,1,0:T(8,128)(2,1)S(1)} %get-tuple-element.47), channel_id=1, source_target_pairs={{0,8},{8,0},{16,24},{24,16},{32,40},{40,32},{48,56},{56,48},{64,72... | collective-permute-start | bytes 3932168 | tf_op jit(solution)/shard_map/ppermute | solution.py:506
  137.7 9.8 %collective-permute-start.14 = (bf16[8,80,256]{2,1,0:T(8,128)(2,1)S(1)}, bf16[8,80,256]{2,1,0:T(8,128)(2,1)S(1)}, u32[]{:S(2)}, u32[]{:S(2)}) collective-permute-start(bf16[8,80,256]{2,1,0:T(8,128)(2,1)S(1)} %get-tuple-element.49), channel_id=1, source_target_pairs={{0,2},{1,3},{2,0},{3,1},{4,6},{5,7},{6,4},{7,5},{8,10},{9,11},{10,... | collective-permute-start | bytes 983048 | tf_op jit(solution)/shard_map/ppermute | solution.py:510
  138.1 10.8 %collective-permute-start.15 = (bf16[8,80,256]{2,1,0:T(8,128)(2,1)S(1)}, bf16[8,80,256]{2,1,0:T(8,128)(2,1)S(1)}, u32[]{:S(2)}, u32[]{:S(2)}) collective-permute-start(bf16[8,80,256]{2,1,0:T(8,128)(2,1)S(1)} %get-tuple-element.51), channel_id=1, source_target_pairs={{0,6},{1,7},{2,4},{3,5},{4,2},{5,3},{6,0},{7,1},{8,14},{9,15},{10,... | collective-permute-start | bytes 983048 | tf_op jit(solution)/shard_map/ppermute | solution.py:511
  149.0 6.6 %collective-permute-start.16 = (bf16[8,80,128]{2,1,0:T(8,128)(2,1)S(1)}, bf16[8,80,128]{2,1,0:T(8,128)(2,1)S(1)}, u32[]{:S(2)}, u32[]{:S(2)}) collective-permute-start(bf16[8,80,128]{2,1,0:T(8,128)(2,1)S(1)} %get-tuple-element.53), channel_id=1, source_target_pairs={{0,6},{1,7},{2,4},{3,5},{4,2},{5,3},{6,0},{7,1},{8,14},{9,15},{10,... | collective-permute-start | bytes 491528 | tf_op jit(solution)/shard_map/ppermute | solution.py:516
  150.7 5.3 %collective-permute-start.17 = (bf16[8,80,128]{2,1,0:T(8,128)(2,1)S(1)}, bf16[8,80,128]{2,1,0:T(8,128)(2,1)S(1)}, u32[]{:S(2)}, u32[]{:S(2)}) collective-permute-start(bf16[8,80,128]{2,1,0:T(8,128)(2,1)S(1)} %get-tuple-element.55), channel_id=1, source_target_pairs={{0,2},{1,3},{2,0},{3,1},{4,6},{5,7},{6,4},{7,5},{8,10},{9,11},{10,... | collective-permute-start | bytes 491528 | tf_op jit(solution)/shard_map/ppermute | solution.py:517

commit v13 on v12

--- a/solution.py
+++ b/solution.py
@@ -538,7 +538,7 @@
     pieces, started = bring_frames(clip_qkv[0], far)
     time, done = time_weights(temporal_qk[0], started)
     caps = doubled(caps, far)
-    caps = doubled(caps, flip(caps, 4), pieces[2])
+    caps = doubled(caps, flip(caps, 4), pieces[2], done)
     caps = doubled(caps, flip(caps, 2))
     other = flip(caps, 1)
     attended = spatial_attention(pieces, done)

time: 189 us -> 183 us (0.968)
  waiting for transfers between devices: 76.7 us -> 73.8 us
  blocking collectives: 31.8 us -> 29.7 us
    ppermute x4, waiting for transfers between devices: 8.9 us -> 1.9 us  [flip(): return lax.ppermute(value, 'dp', [(i, i ^ bit) for i in range(32)])]
    ppermute x8, waiting for transfers between devices: 21.5 us -> 26.7 us  [swap(): return lax.ppermute(value, 'space', [(s, s ^ bits) for s in range(8)])]
    all_to_all x1, blocking collectives: 22.4 us -> 20.3 us  [reduce_gradient(): lax.all_to_all(parts, 'dp', split_axis=0, concat_axis=0, tiled=True, axis...]
  transfers between devices with their start and end apart: 20 -> 20, of which waited for: 11 -> 13; matrix products, arithmetic and copies ran while one was open for 0% -> 0% of each run, Pallas kernels for 9% -> 9%
where the time goes in v13:
time: 183 us; the launch traced here: 182 us
  waiting for transfers between devices  73.8 us (40%)
  starting transfers between devices  36.7 us (20%)
  Pallas kernels  32.5 us (18%)
  blocking collectives  29.7 us (16%)
  local copies, waits for them, and re-layouts  7.26 us (4%)
  between operations  2.17 us (1%)
    ppermute x8, waiting for transfers between devices, swap(): return lax.ppermute(value, 'space', [(s, s ^ bits) for s in range(8)])  26.7 us
    all_to_all x1, blocking collectives, reduce_gradient(): lax.all_to_all(parts, 'dp', split_axis=0, concat_axis=0, tiled=True, axis...  20.3 us
    all_to_all x1, waiting for transfers between devices, on_device(): lax.all_to_all(attended, 'space', split_axis=0, concat_axis=0, tiled=True)  18.9 us
    ppermute x8, starting transfers between devices, swap(): return lax.ppermute(value, 'space', [(s, s ^ bits) for s in range(8)])  12.7 us
    ppermute x4, starting transfers between devices, flip(): return lax.ppermute(value, 'dp', [(i, i ^ bit) for i in range(32)])  10 us
    all_to_all x1, blocking collectives, reduce_gradient(): lax.all_to_all(parts, 'space', split_axis=0, concat_axis=0, tiled=True)  9.43 us
    pallas_call x1, Pallas kernels, token_part(): pl.pallas_call(token_kernel, in_specs=[VMEM, VMEM, FAR_OFF, FAR_OFF, VMEM...  8.06 us
    ppermute x1, waiting for transfers between devices, reduce_gradient(): a_got = lax.ppermute(a_send, 'space', one)  7.73 us
  transfers between devices with their start and end apart: 20, of which 13 were waited for; matrix products, arithmetic and copies ran while one was open for 0% of the time, Pallas kernels for 9%

profile of v13, /device:TPU:32, one launch (start us, length us, event | category | flops | bytes accessed | tf_op | source)
XLA Modules:
  0.0 182.2 jit_solution(2378010957232693459)
XLA Ops:
  0.6 2.8 %depart.1 = (bf16[2,32,4992]{2,1,0:T(8,128)(2,1)}, bf16[2,32,4992]{2,1,0:T(8,128)(2,1)}, bf16[2,32,4992]{2,1,0:T(8,128)(2,1)}, bf16[4,32,4992]{2,1,0:T(8,128)(2,1)}) custom-call(bf16[16,32,4992]{2,1,0:T(8,128)(2,1)} %bitcast.17), custom_call_target="tpu_custom_call" | custom-call | bytes 6000000 | tf_op jit(solution)/shard_map/depart/pallas_call | solution.py:81
  3.5 2.8 %collective-permute-start = (bf16[4,32,4992]{2,1,0:T(8,128)(2,1)}, bf16[4,32,4992]{2,1,0:T(8,128)(2,1)S(1)}, u32[]{:S(2)}, u32[]{:S(2)}) collective-permute-start(bf16[4,32,4992]{2,1,0:T(8,128)(2,1)} %get-tuple-element.31), channel_id=1, source_target_pairs={{0,6},{1,7},{2,4},{3,5},{4,2},{5,3},{6,0},{7,1},{8,14},{9,15},{10,... | collective-permute-start | bytes 3833864 | tf_op jit(solution)/shard_map/ppermute | solution.py:131
  6.3 1.6 collective-permute-start.1
  8.1 1.7 collective-permute-start.3
  10.5 3.1 %collective-permute-start.4 = (bf16[1,80,512]{2,1,0:T(8,128)(2,1)S(1)}, bf16[1,80,512]{2,1,0:T(8,128)(2,1)S(1)}, u32[]{:S(2)}, u32[]{:S(2)}) collective-permute-start(bf16[1,80,512]{2,1,0:T(8,128)(2,1)S(1)} %concatenate.3.refs_0_), channel_id=1, source_target_pairs={{0,129},{1,128},{2,131},{3,130},{4,133},{5,132},{6,135},{7,134},{8... | collective-permute-start | bytes 245768 | tf_op jit(solution)/shard_map/ppermute | solution.py:271
  13.6 2.6 %collective-permute-done.4.refs_1_ = bf16[1,80,512]{2,1,0:T(8,128)(2,1)S(1)} collective-permute-done((bf16[1,80,512]{2,1,0:T(8,128)(2,1)S(1)}, bf16[1,80,512]{2,1,0:T(8,128)(2,1)S(1)}, u32[]{:S(2)}, u32[]{:S(2)}) %collective-permute-start.4) | collective-permute-done | bytes 81952 | tf_op jit(solution)/shard_map/ppermute | solution.py:271
  16.3 6.4 %collective-permute-start.5 = (bf16[2,80,512]{2,1,0:T(8,128)(2,1)S(1)}, bf16[2,80,512]{2,1,0:T(8,128)(2,1)S(1)}, u32[]{:S(2)}, u32[]{:S(2)}) collective-permute-start(bf16[2,80,512]{2,1,0:T(8,128)(2,1)S(1)} %bitcast.15), channel_id=1, source_target_pairs={{0,64},{8,72},{16,80},{24,88},{32,96},{40,104},{48,112},{56,120},{... | collective-permute-start | bytes 491528 | tf_op jit(solution)/shard_map/ppermute | solution.py:261
  22.6 2.3 %own.1 = (bf16[1,32,4992]{2,1,0:T(8,128)(2,1)}, bf16[3,32,4992]{2,1,0:T(8,128)(2,1)}, bf16[2,32,4992]{2,1,0:T(8,128)(2,1)}) custom-call(bf16[16,32,4992]{2,1,0:T(8,128)(2,1)} %bitcast.18), custom_call_target="tpu_custom_call" | custom-call | bytes 6000000 | tf_op jit(solution)/shard_map/own/pallas_call | solution.py:81
  25.0 9.9 %collective-permute-done.across_ref = bf16[4,32,4992]{2,1,0:T(8,128)(2,1)S(1)} collective-permute-done((bf16[4,32,4992]{2,1,0:T(8,128)(2,1)}, bf16[4,32,4992]{2,1,0:T(8,128)(2,1)S(1)}, u32[]{:S(2)}, u32[]{:S(2)}) %collective-permute-start) | collective-permute-done | bytes 1277984 | tf_op jit(solution)/shard_map/ppermute | solution.py:131
  38.1 2.8 %collective-permute-start.6 = (bf16[4,32,4992]{2,1,0:T(8,128)(2,1)S(1)}, bf16[4,32,4992]{2,1,0:T(8,128)(2,1)S(1)}, u32[]{:S(2)}, u32[]{:S(2)}) collective-permute-start(bf16[4,32,4992]{2,1,0:T(8,128)(2,1)S(1)} %turn.1), channel_id=1, source_target_pairs={{0,6},{1,7},{2,4},{3,5},{4,2},{5,3},{6,0},{7,1},{8,14},{9,15},{10,... | collective-permute-start | bytes 3833864 | tf_op jit(solution)/shard_map/ppermute | solution.py:131
  41.0 3.4 %collective-permute-start.10 = (bf16[4,80,512]{2,1,0:T(8,128)(2,1)S(1)}, bf16[4,80,512]{2,1,0:T(8,128)(2,1)S(1)}, u32[]{:S(2)}, u32[]{:S(2)}) collective-permute-start(bf16[4,80,512]{2,1,0:T(8,128)(2,1)S(1)} %bitcast.13), channel_id=1, source_target_pairs={{0,32},{8,40},{16,48},{24,56},{32,0},{40,8},{48,16},{56,24},{64,96... | collective-permute-start | bytes 983048 | tf_op jit(solution)/shard_map/ppermute | solution.py:261
  45.9 1.9 %collective-permute-start.9 = (bf16[2,32,4992]{2,1,0:T(8,128)(2,1)S(1)}, bf16[2,32,4992]{2,1,0:T(8,128)(2,1)S(1)}, u32[]{:S(2)}, u32[]{:S(2)}) collective-permute-start(bf16[2,32,4992]{2,1,0:T(8,128)(2,1)S(1)} %get-tuple-element.39), channel_id=1, source_target_pairs={{0,3},{1,2},{2,1},{3,0},{4,7},{5,6},{6,5},{7,4},{8,11},{9,10},{10,... | collective-permute-start | bytes 1916936 | tf_op jit(solution)/shard_map/ppermute | solution.py:131
  47.8 5.8 %time_weights.1 = (bf16[13,2,256,256]{3,2,1,0:T(8,128)(2,1)S(1)}, f32[8,128]{1,0:T(8,128)S(1)}) custom-call(bf16[16,32,3328]{2,1,0:T(8,128)(2,1)S(1)} %bitcast.10, bf16[2,32,4992]{2,1,0:T(8,128)(2,1)S(1)} %get-tuple-element.37.started_ref.behind_ref), custom_call_target="tpu_custom_call" | custom-call | flops 436207616 | bytes 7000000 | tf_op jit(solution)/shard_map/time_weights/pallas_call | solution.py:236
  53.7 1.7 copy-done.4
  56.7 11.6 %collective-permute-done.6.turned_ref.refs_2_ = bf16[4,32,4992]{2,1,0:T(8,128)(2,1)S(1)} collective-permute-done((bf16[4,32,4992]{2,1,0:T(8,128)(2,1)S(1)}, bf16[4,32,4992]{2,1,0:T(8,128)(2,1)S(1)}, u32[]{:S(2)}, u32[]{:S(2)}) %collective-permute-start.6) | collective-permute-done | bytes 1277984 | tf_op jit(solution)/shard_map/ppermute | solution.py:131
  68.7 5.2 %collective-permute-done.9.refs_5_ = bf16[2,32,4992]{2,1,0:T(8,128)(2,1)S(1)} collective-permute-done((bf16[2,32,4992]{2,1,0:T(8,128)(2,1)S(1)}, bf16[2,32,4992]{2,1,0:T(8,128)(2,1)S(1)}, u32[]{:S(2)}, u32[]{:S(2)}) %collective-permute-start.9) | collective-permute-done | bytes 639008 | tf_op jit(solution)/shard_map/ppermute | solution.py:131
  73.9 5.4 %spatial_attention.1 = bf16[8,2,32,1664]{3,2,1,0:T(8,128)(2,1)} custom-call(bf16[2,32,4992]{2,1,0:T(8,128)(2,1)S(1)} %copy-done.2, bf16[4,32,4992]{2,1,0:T(8,128)(2,1)S(1)} %collective-permute-done.across_ref, bf16[4,32,4992]{2,1,0:T(8,128)(2,1)S(1)} %collective-permute-done.6.turned_ref.refs_2_, ...), custom_call_target="tpu_custom_call" | custom-call | flops 872415232 | bytes 6815744 | tf_op jit(solution)/shard_map/spatial_attention/pallas_call | solution.py:186
  79.3 3.6 %all-to-all-start = ((bf16[8,2,32,1664]{3,2,1,0:T(8,128)(2,1)}), bf16[8,2,32,1664]{3,2,1,0:T(8,128)(2,1)S(1)}, u32[]{:S(2)}, u32[]{:S(2)}) async-start(bf16[8,2,32,1664]{3,2,1,0:T(8,128)(2,1)} %spatial_attention.1), calls=%async_computation | async-start | bytes 3407872 | tf_op jit(solution)/shard_map/all_to_all | solution.py:545
  83.5 2.2 %join.7 = bf16[2,8,80,512]{3,2,1,0:T(8,128)(2,1)} custom-call(bf16[8,80,512]{2,1,0:T(8,128)(2,1)S(1)} %bitcast.12, bf16[8,80,512]{2,1,0:T(8,128)(2,1)} %collective-permute-done.11.refs_1_), custom_call_target="tpu_custom_call" | custom-call | bytes 1000000 | tf_op jit(solution)/shard_map/join/pallas_call | solution.py:275
  85.7 18.9 %all-to-all-done.value = bf16[8,2,32,1664]{3,2,1,0:T(8,128)(2,1)S(1)} async-done(((bf16[8,2,32,1664]{3,2,1,0:T(8,128)(2,1)}), bf16[8,2,32,1664]{3,2,1,0:T(8,128)(2,1)S(1)}, u32[]{:S(2)}, u32[]{:S(2)}) %all-to-all-start) | async-done | bytes 1703968 | tf_op jit(solution)/shard_map/all_to_all | solution.py:545
  105.7 2.0 %copy-done.5 = bf16[13,2,256,256]{3,2,1,0:T(8,128)(2,1)S(1)} copy-done((bf16[13,2,256,256]{3,2,1,0:T(8,128)(2,1)S(1)}, bf16[13,2,256,256]{3,2,1,0:T(8,128)(2,1)}, u32[]{:S(2)}) %copy-start.5) | copy-done | bytes 3407896
  109.0 8.1 %token_part.1 = (bf16[16,32,512]{2,1,0:T(8,128)(2,1)}, f32[8,2,32,128]{3,2,1,0:T(8,128)}, bf16[32,80,512]{2,1,0:T(8,128)(2,1)}, f32[32,128]{1,0:T(8,128)S(1)}) custom-call(bf16[8,2,32,1664]{3,2,1,0:T(8,128)(2,1)S(1)} %all-to-all-done.value, bf16[13,2,256,256]{3,2,1,0:T(8,128)(2,1)S(1)} %copy-done.5, bf16[1664,512]{1,0:T(8,128)(2,1)} %proj_ref.1, ...), custom_call_target="tpu_custom_call" | custom-call | flops 4499999744 | bytes 12000000 | tf_op jit(solution)/shard_map/token_part/pallas_call | solution.py:356
  117.1 3.4 %all-to-all-start.1 = ((f32[8,2,32,128]{3,2,1,0:T(8,128)}), f32[8,2,32,128]{3,2,1,0:T(8,128)S(1)}, u32[]{:S(2)}, u32[]{:S(2)}) async-start(f32[8,2,32,128]{3,2,1,0:T(8,128)} %get-tuple-element.43), calls=%async_computation.1 | async-start | bytes 524288 | tf_op jit(solution)/shard_map/all_to_all | solution.py:547
  121.1 6.2 %all-to-all-done.1.stats_ref = f32[8,2,32,128]{3,2,1,0:T(8,128)S(1)} async-done(((f32[8,2,32,128]{3,2,1,0:T(8,128)}), f32[8,2,32,128]{3,2,1,0:T(8,128)S(1)}, u32[]{:S(2)}, u32[]{:S(2)}) %all-to-all-start.1) | async-done | bytes 262176 | tf_op jit(solution)/shard_map/all_to_all | solution.py:547
  127.4 2.4 %coef_part.1 = (bf16[16,80,512]{2,1,0:T(8,128)(2,1)S(1)}, bf16[16,80,512]{2,1,0:T(8,128)(2,1)S(1)}, f32[1,1]{1,0:T(1,128)}) custom-call(s32[1]{0:T(128)S(6)} %copy.10.pos_ref, f32[8,2,32,128]{3,2,1,0:T(8,128)S(1)} %all-to-all-done.1.stats_ref, f32[32,128]{1,0:T(8,128)S(1)} %get-tuple-element.44.lens_ref, bf16[32,80,512]{2,1,0:T(8,128)(2,1)} %get-tuple-element.45.grad_ref), custom_call_target="tpu_custom_call" | custom-call | flops 4000000 | bytes 6000000 | tf_op jit(solution)/shard_map/coef_part/pallas_call | solution.py:430
  129.9 3.0 %collective-permute-done.13.got_ref = bf16[16,80,512]{2,1,0:T(8,128)(2,1)S(1)} collective-permute-done((bf16[16,80,512]{2,1,0:T(8,128)(2,1)S(1)}, bf16[16,80,512]{2,1,0:T(8,128)(2,1)S(1)}, u32[]{:S(2)}, u32[]{:S(2)}) %collective-permute-start.13) | collective-permute-done | bytes 1310752 | tf_op jit(solution)/shard_map/ppermute | solution.py:506
  133.6 1.7 collective-permute-start.15
  135.3 7.7 %collective-permute-done.14.a_got = bf16[8,80,256]{2,1,0:T(8,128)(2,1)S(1)} collective-permute-done((bf16[8,80,256]{2,1,0:T(8,128)(2,1)S(1)}, bf16[8,80,256]{2,1,0:T(8,128)(2,1)S(1)}, u32[]{:S(2)}, u32[]{:S(2)}) %collective-permute-start.14) | collective-permute-done | bytes 327712 | tf_op jit(solution)/shard_map/ppermute | solution.py:510
  144.5 1.7 collective-permute-start.16
  146.3 4.9 %collective-permute-done.16.a_got = bf16[8,80,128]{2,1,0:T(8,128)(2,1)S(1)} collective-permute-done((bf16[8,80,128]{2,1,0:T(8,128)(2,1)S(1)}, bf16[8,80,128]{2,1,0:T(8,128)(2,1)S(1)}, u32[]{:S(2)}, u32[]{:S(2)}) %collective-permute-start.16) | collective-permute-done | bytes 163872 | tf_op jit(solution)/shard_map/ppermute | solution.py:516
  151.7 20.3 %all_to_all.20.parts = bf16[16,80,128]{2,1,0:T(8,128)(2,1)S(1)} all-to-all(bf16[16,80,128]{2,1,0:T(8,128)(2,1)S(1)} %third_sum.1), channel_id=1, replica_groups={{0,16,32,48,64,80,96,112,128,144,160,176,192,208,224,240},{8,24,40,56,7..., dimensions={0} | all-to-all | bytes 655360 | tf_op jit(solution)/shard_map/all_to_all | solution.py:521
  172.0 9.4 %all_to_all.21.parts = bf16[8,80,128]{2,1,0:T(8,128)(2,1)S(1)} all-to-all(bf16[8,80,128]{2,1,0:T(8,128)(2,1)S(1)} %owned_sum.1), channel_id=1, replica_groups=mesh['dp'=32,'space'=8] {'space'}, dimensions={0} | all-to-all | bytes 327680 | tf_op jit(solution)/shard_map/all_to_all | solution.py:526
  (46 shorter events, 13.3 us)
Async XLA Ops:
  0.6 9.8 %copy-start.8 = (bf16[1,77,512]{2,1,0:T(8,128)(2,1)S(1)}, bf16[1,77,512]{2,1,0:T(8,128)(2,1)}, u32[]{:S(2)}) copy-start(bf16[1,77,512]{2,1,0:T(8,128)(2,1)} %param.9) | copy-start | bytes 236548
  3.5 31.3 %collective-permute-start = (bf16[4,32,4992]{2,1,0:T(8,128)(2,1)}, bf16[4,32,4992]{2,1,0:T(8,128)(2,1)S(1)}, u32[]{:S(2)}, u32[]{:S(2)}) collective-permute-start(bf16[4,32,4992]{2,1,0:T(8,128)(2,1)} %get-tuple-element.31), channel_id=1, source_target_pairs={{0,6},{1,7},{2,4},{3,5},{4,2},{5,3},{6,0},{7,1},{8,14},{9,15},{10,... | collective-permute-start | bytes 3833864 | tf_op jit(solution)/shard_map/ppermute | solution.py:131
  6.3 30.9 %collective-permute-start.1 = (bf16[2,32,4992]{2,1,0:T(8,128)(2,1)}, bf16[2,32,4992]{2,1,0:T(8,128)(2,1)S(1)}, u32[]{:S(2)}, u32[]{:S(2)}) collective-permute-start(bf16[2,32,4992]{2,1,0:T(8,128)(2,1)} %get-tuple-element.33), channel_id=1, source_target_pairs={{0,1},{1,0},{2,3},{3,2},{4,5},{5,4},{6,7},{7,6},{8,9},{9,8},{10,11... | collective-permute-start | bytes 1916936 | tf_op jit(solution)/shard_map/ppermute | solution.py:131
  7.9 29.3 %collective-permute-start.2 = (bf16[2,32,4992]{2,1,0:T(8,128)(2,1)}, bf16[2,32,4992]{2,1,0:T(8,128)(2,1)S(1)}, u32[]{:S(2)}, u32[]{:S(2)}) collective-permute-start(bf16[2,32,4992]{2,1,0:T(8,128)(2,1)} %get-tuple-element.34), channel_id=1, source_target_pairs={{0,2},{1,3},{2,0},{3,1},{4,6},{5,7},{6,4},{7,5},{8,10},{9,11},{10,... | collective-permute-start | bytes 1916936 | tf_op jit(solution)/shard_map/ppermute | solution.py:131
  8.1 29.1 %collective-permute-start.3 = (bf16[2,32,4992]{2,1,0:T(8,128)(2,1)}, bf16[2,32,4992]{2,1,0:T(8,128)(2,1)S(1)}, u32[]{:S(2)}, u32[]{:S(2)}) collective-permute-start(bf16[2,32,4992]{2,1,0:T(8,128)(2,1)} %get-tuple-element.35), channel_id=1, source_target_pairs={{0,3},{1,2},{2,1},{3,0},{4,7},{5,6},{6,5},{7,4},{8,11},{9,10},{10,... | collective-permute-start | bytes 1916936 | tf_op jit(solution)/shard_map/ppermute | solution.py:131
  10.5 5.7 %collective-permute-start.4 = (bf16[1,80,512]{2,1,0:T(8,128)(2,1)S(1)}, bf16[1,80,512]{2,1,0:T(8,128)(2,1)S(1)}, u32[]{:S(2)}, u32[]{:S(2)}) collective-permute-start(bf16[1,80,512]{2,1,0:T(8,128)(2,1)S(1)} %concatenate.3.refs_0_), channel_id=1, source_target_pairs={{0,129},{1,128},{2,131},{3,130},{4,133},{5,132},{6,135},{7,134},{8... | collective-permute-start | bytes 245768 | tf_op jit(solution)/shard_map/ppermute | solution.py:271
  16.3 21.0 %collective-permute-start.5 = (bf16[2,80,512]{2,1,0:T(8,128)(2,1)S(1)}, bf16[2,80,512]{2,1,0:T(8,128)(2,1)S(1)}, u32[]{:S(2)}, u32[]{:S(2)}) collective-permute-start(bf16[2,80,512]{2,1,0:T(8,128)(2,1)S(1)} %bitcast.15), channel_id=1, source_target_pairs={{0,64},{8,72},{16,80},{24,88},{32,96},{40,104},{48,112},{56,120},{... | collective-permute-start | bytes 491528 | tf_op jit(solution)/shard_map/ppermute | solution.py:261
  34.8 1.2 copy-start.1
  36.0 1.3 copy-start.3
  37.3 10.6 %copy-start = (bf16[1,16,32,3328]{3,2,1,0:T(8,128)(2,1)S(1)}, bf16[1,16,32,3328]{3,2,1,0:T(8,128)(2,1)}, u32[]{:S(2)}) copy-start(bf16[1,16,32,3328]{3,2,1,0:T(8,128)(2,1)} %param.7) | copy-start | bytes 10223620
  38.1 30.2 %collective-permute-start.6 = (bf16[4,32,4992]{2,1,0:T(8,128)(2,1)S(1)}, bf16[4,32,4992]{2,1,0:T(8,128)(2,1)S(1)}, u32[]{:S(2)}, u32[]{:S(2)}) collective-permute-start(bf16[4,32,4992]{2,1,0:T(8,128)(2,1)S(1)} %turn.1), channel_id=1, source_target_pairs={{0,6},{1,7},{2,4},{3,5},{4,2},{5,3},{6,0},{7,1},{8,14},{9,15},{10,... | collective-permute-start | bytes 3833864 | tf_op jit(solution)/shard_map/ppermute | solution.py:131
  41.0 15.7 %collective-permute-start.10 = (bf16[4,80,512]{2,1,0:T(8,128)(2,1)S(1)}, bf16[4,80,512]{2,1,0:T(8,128)(2,1)S(1)}, u32[]{:S(2)}, u32[]{:S(2)}) collective-permute-start(bf16[4,80,512]{2,1,0:T(8,128)(2,1)S(1)} %bitcast.13), channel_id=1, source_target_pairs={{0,32},{8,40},{16,48},{24,56},{32,0},{40,8},{48,16},{56,24},{64,96... | collective-permute-start | bytes 983048 | tf_op jit(solution)/shard_map/ppermute | solution.py:261
  44.4 24.3 %collective-permute-start.7 = (bf16[2,32,4992]{2,1,0:T(8,128)(2,1)S(1)}, bf16[2,32,4992]{2,1,0:T(8,128)(2,1)S(1)}, u32[]{:S(2)}, u32[]{:S(2)}) collective-permute-start(bf16[2,32,4992]{2,1,0:T(8,128)(2,1)S(1)} %get-tuple-element.37.started_ref.behind_ref), channel_id=1, source_target_pairs={{0,1},{1,0},{2,3},{3,2},{4,5},{5,4},{6,7},{7,6},{8,9},{9,8},{10,11... | collective-permute-start | bytes 1916936 | tf_op jit(solution)/shard_map/ppermute | solution.py:131
  45.9 22.8 %collective-permute-start.8 = (bf16[2,32,4992]{2,1,0:T(8,128)(2,1)S(1)}, bf16[2,32,4992]{2,1,0:T(8,128)(2,1)S(1)}, u32[]{:S(2)}, u32[]{:S(2)}) collective-permute-start(bf16[2,32,4992]{2,1,0:T(8,128)(2,1)S(1)} %get-tuple-element.38), channel_id=1, source_target_pairs={{0,2},{1,3},{2,0},{3,1},{4,6},{5,7},{6,4},{7,5},{8,10},{9,11},{10,... | collective-permute-start | bytes 1916936 | tf_op jit(solution)/shard_map/ppermute | solution.py:131
  45.9 28.0 %collective-permute-start.9 = (bf16[2,32,4992]{2,1,0:T(8,128)(2,1)S(1)}, bf16[2,32,4992]{2,1,0:T(8,128)(2,1)S(1)}, u32[]{:S(2)}, u32[]{:S(2)}) collective-permute-start(bf16[2,32,4992]{2,1,0:T(8,128)(2,1)S(1)} %get-tuple-element.39), channel_id=1, source_target_pairs={{0,3},{1,2},{2,1},{3,0},{4,7},{5,6},{6,5},{7,4},{8,11},{9,10},{10,... | collective-permute-start | bytes 1916936 | tf_op jit(solution)/shard_map/ppermute | solution.py:131
  53.7 1.7 copy-start.4
  55.4 18.5 %copy-start.2 = (bf16[2,32,4992]{2,1,0:T(8,128)(2,1)S(1)}, bf16[2,32,4992]{2,1,0:T(8,128)(2,1)}, u32[]{:S(2)}) copy-start(bf16[2,32,4992]{2,1,0:T(8,128)(2,1)} %get-tuple-element.30.kept_ref) | copy-start | bytes 1916932
  68.4 15.1 %collective-permute-start.11 = (bf16[8,80,512]{2,1,0:T(8,128)(2,1)S(1)}, bf16[8,80,512]{2,1,0:T(8,128)(2,1)}, u32[]{:S(2)}, u32[]{:S(2)}) collective-permute-start(bf16[8,80,512]{2,1,0:T(8,128)(2,1)S(1)} %bitcast.11), channel_id=1, source_target_pairs={{0,16},{8,24},{16,0},{24,8},{32,48},{40,56},{48,32},{56,40},{64,80... | collective-permute-start | bytes 1966088 | tf_op jit(solution)/shard_map/ppermute | solution.py:261
  79.3 25.3 %all-to-all-start = ((bf16[8,2,32,1664]{3,2,1,0:T(8,128)(2,1)}), bf16[8,2,32,1664]{3,2,1,0:T(8,128)(2,1)S(1)}, u32[]{:S(2)}, u32[]{:S(2)}) async-start(bf16[8,2,32,1664]{3,2,1,0:T(8,128)(2,1)} %spatial_attention.1), calls=%async_computation | async-start | bytes 3407872 | tf_op jit(solution)/shard_map/all_to_all | solution.py:545
  85.7 19.0 %collective-permute-start.12 = (bf16[16,80,512]{2,1,0:T(8,128)(2,1)}, bf16[16,80,512]{2,1,0:T(8,128)(2,1)S(1)}, u32[]{:S(2)}, u32[]{:S(2)}) collective-permute-start(bf16[16,80,512]{2,1,0:T(8,128)(2,1)} %bitcast.6.mine_ref), channel_id=1, source_target_pairs={{0,8},{8,0},{16,24},{24,16},{32,40},{40,32},{48,56},{56,48},{64,72... | collective-permute-start | bytes 3932168 | tf_op jit(solution)/shard_map/ppermute | solution.py:261
  104.7 1.1 copy-start.6
  105.7 2.0 %copy-start.5 = (bf16[13,2,256,256]{3,2,1,0:T(8,128)(2,1)S(1)}, bf16[13,2,256,256]{3,2,1,0:T(8,128)(2,1)}, u32[]{:S(2)}) copy-start(bf16[13,2,256,256]{3,2,1,0:T(8,128)(2,1)} %copy-done.4) | copy-start | bytes 10223620
  107.7 1.3 copy-start.7
  117.1 10.3 %all-to-all-start.1 = ((f32[8,2,32,128]{3,2,1,0:T(8,128)}), f32[8,2,32,128]{3,2,1,0:T(8,128)S(1)}, u32[]{:S(2)}, u32[]{:S(2)}) async-start(f32[8,2,32,128]{3,2,1,0:T(8,128)} %get-tuple-element.43), calls=%async_computation.1 | async-start | bytes 524288 | tf_op jit(solution)/shard_map/all_to_all | solution.py:547
  129.8 3.1 %collective-permute-start.13 = (bf16[16,80,512]{2,1,0:T(8,128)(2,1)S(1)}, bf16[16,80,512]{2,1,0:T(8,128)(2,1)S(1)}, u32[]{:S(2)}, u32[]{:S(2)}) collective-permute-start(bf16[16,80,512]{2,1,0:T(8,128)(2,1)S(1)} %get-tuple-element.47), channel_id=1, source_target_pairs={{0,8},{8,0},{16,24},{24,16},{32,40},{40,32},{48,56},{56,48},{64,72... | collective-permute-start | bytes 3932168 | tf_op jit(solution)/shard_map/ppermute | solution.py:506
  133.2 9.8 %collective-permute-start.14 = (bf16[8,80,256]{2,1,0:T(8,128)(2,1)S(1)}, bf16[8,80,256]{2,1,0:T(8,128)(2,1)S(1)}, u32[]{:S(2)}, u32[]{:S(2)}) collective-permute-start(bf16[8,80,256]{2,1,0:T(8,128)(2,1)S(1)} %get-tuple-element.49), channel_id=1, source_target_pairs={{0,2},{1,3},{2,0},{3,1},{4,6},{5,7},{6,4},{7,5},{8,10},{9,11},{10,... | collective-permute-start | bytes 983048 | tf_op jit(solution)/shard_map/ppermute | solution.py:510
  133.6 10.8 %collective-permute-start.15 = (bf16[8,80,256]{2,1,0:T(8,128)(2,1)S(1)}, bf16[8,80,256]{2,1,0:T(8,128)(2,1)S(1)}, u32[]{:S(2)}, u32[]{:S(2)}) collective-permute-start(bf16[8,80,256]{2,1,0:T(8,128)(2,1)S(1)} %get-tuple-element.51), channel_id=1, source_target_pairs={{0,6},{1,7},{2,4},{3,5},{4,2},{5,3},{6,0},{7,1},{8,14},{9,15},{10,... | collective-permute-start | bytes 983048 | tf_op jit(solution)/shard_map/ppermute | solution.py:511
  144.5 6.6 %collective-permute-start.16 = (bf16[8,80,128]{2,1,0:T(8,128)(2,1)S(1)}, bf16[8,80,128]{2,1,0:T(8,128)(2,1)S(1)}, u32[]{:S(2)}, u32[]{:S(2)}) collective-permute-start(bf16[8,80,128]{2,1,0:T(8,128)(2,1)S(1)} %get-tuple-element.53), channel_id=1, source_target_pairs={{0,6},{1,7},{2,4},{3,5},{4,2},{5,3},{6,0},{7,1},{8,14},{9,15},{10,... | collective-permute-start | bytes 491528 | tf_op jit(solution)/shard_map/ppermute | solution.py:516
  146.3 5.3 %collective-permute-start.17 = (bf16[8,80,128]{2,1,0:T(8,128)(2,1)S(1)}, bf16[8,80,128]{2,1,0:T(8,128)(2,1)S(1)}, u32[]{:S(2)}, u32[]{:S(2)}) collective-permute-start(bf16[8,80,128]{2,1,0:T(8,128)(2,1)S(1)} %get-tuple-element.55), channel_id=1, source_target_pairs={{0,2},{1,3},{2,0},{3,1},{4,6},{5,7},{6,4},{7,5},{8,10},{9,11},{10,... | collective-permute-start | bytes 491528 | tf_op jit(solution)/shard_map/ppermute | solution.py:517
